TPU v7x, 32 devices: a whole 2x2x4 slice. The times are simulated.
32 devices in a mesh: sector: 8 (over y, x, core), dof: 4 (over z).
Axes of the slice: x: 2, y: 2, z: 4, core: 2. Of those that a mesh axis runs over, the one named last changes fastest.
Arguments:
- rhs: float32 [8, 4096, 128], P('sector', 'dof')
- diagonal: float32 [8, 4096], P('sector', 'dof'), may hold values from 4 to 8
- coupling: bfloat16 [8, 4096, 2048], P('sector', 'dof'), may hold values from -0.125 to 0.125
- springs: float32 [8, 3072], P('sector', 'dof'), may hold values from 1 to 4
- precond: bfloat16 [4096, 4096], P('dof')
- hub_inverse: bfloat16 [3072, 3072], P('dof')
Outputs:
- solution: float32 [8, 4096, 128], P('sector', 'dof')
- residual: float32 [8, 4096, 128], P('sector', 'dof')
All inputs are finite; a program needn't handle non-finite values.
Results may differ from a plain program's by a relative error of at most 0.0056.
Values may be sent and summed in bfloat16 or wider, within the bound.
No kernel may reach another device: no remote copies, remote signals or barrier semaphores. Data moves between devices by JAX's collectives and lax.ppermute only.
A program may use at most 64 MiB of HBM per device.

v0:
```python
import jax
import jax.numpy as jnp
from jax import lax
from jax.sharding import PartitionSpec as P

ITERS = 3


def extended(cells, sides, width):
    for axis, dim in sides:
        count = lax.axis_size(axis)
        head = lax.slice_in_dim(cells, 0, width, axis=dim)
        tail = lax.slice_in_dim(cells, cells.shape[dim] - width, cells.shape[dim], axis=dim)
        cells = jnp.concatenate(
            [
                lax.ppermute(tail, axis, [(i, (i + 1) % count) for i in range(count)]),
                cells,
                lax.ppermute(head, axis, [((i + 1) % count, i) for i in range(count)]),
            ],
            axis=dim,
        )
    return cells


def fold_rows(field, update, start_value):
    return update(start_value, lax.all_gather(field, "dof", axis=0, tiled=True), jnp.int32(0))


def product_with(matrix):

    def update(total, piece, start):
        return jnp.dot(matrix, piece, preferred_element_type=jnp.float32)

    return update


def place_rows(total, piece, start):
    return piece


def body(rhs, diagonal, coupling, springs, precond, hub_inverse):
    residual = rhs[0]
    diag_rows = diagonal[0]
    couple_rows = coupling[0]
    spring_rows = springs[0][:, None]
    rows_dev = residual.shape[0]
    loads = residual.shape[1]
    quarter = rows_dev // 4
    parts = lax.axis_size("dof")
    solution = jnp.zeros_like(residual)
    for step in range(ITERS):
        precon = fold_rows(
            residual.astype(jnp.bfloat16),
            product_with(precond),
            jnp.zeros((rows_dev, loads), jnp.float32),
        )
        precon_low = precon.astype(jnp.bfloat16)
        own_faces = precon_low[: 2 * quarter]
        whole = fold_rows(
            own_faces, place_rows, jnp.zeros((parts * 2 * quarter, loads), jnp.bfloat16)
        )
        beside_all = extended(whole[None], (("sector", 0),), 1)
        prev_side = beside_all[0].reshape(parts, 2, quarter, loads)[:, 1]
        next_side = beside_all[2].reshape(parts, 2, quarter, loads)[:, 0]
        needed = jnp.stack([prev_side, next_side], axis=1).reshape(parts * 2 * quarter, loads)
        couple = jnp.dot(couple_rows, needed, preferred_element_type=jnp.float32)
        attached = precon[: 3 * quarter]
        load = lax.psum(spring_rows * attached, "sector")
        hub = fold_rows(
            load.astype(jnp.bfloat16),
            product_with(hub_inverse),
            jnp.zeros((3 * quarter, loads), jnp.float32),
        )
        hub_term = jnp.concatenate(
            [spring_rows * (attached - hub), jnp.zeros((quarter, loads), jnp.float32)], axis=0
        )
        image = diag_rows[:, None] * precon + couple + hub_term
        upper, lower = lax.psum(
            (jnp.sum(image * residual, axis=0), jnp.sum(image * image, axis=0)), ("sector", "dof")
        )
        alpha = upper / (lower + 1e-06)
        solution = solution + alpha * precon
        residual = residual - alpha * image
    return (solution[None], residual[None])


def solution(mesh):
    placed = (
        P("sector", "dof", None),
        P("sector", "dof"),
        P("sector", "dof", None),
        P("sector", "dof"),
        P("dof", None),
        P("dof", None),
    )
    return jax.shard_map(
        body,
        mesh=mesh,
        in_specs=placed,
        out_specs=(P("sector", "dof", None), P("sector", "dof", None)),
        check_vma=False,
    )
```

profile of v0, /device:TPU:0, one launch (start us, length us, event | category | flops | bytes accessed | tf_op | source)
XLA Modules:
  0.0 471.2 jit_solution(10762832128202610492)
XLA Ops:
  9.8 31.0 %all-gather.4.cloned.1.call-done = bf16[4096,128]{1,0:T(8,128)(2,1)} async-done(((bf16[1024,128]{1,0:T(8,128)(2,1)}), bf16[4096,128]{1,0:T(8,128)(2,1)}) %all-gather.4.cloned.1.call-update) | async-done | bytes 1048592 | tf_op jit(solution)/shard_map/all_gather | solution.py:26
  40.8 5.9 %fusion.42 = f32[1024,128]{1,0:T(8,128)S(1)} fusion(bf16[1024,4096]{1,0:T(8,128)(2,1)} %param.10, bf16[4096,128]{1,0:T(8,128)(2,1)} %all-gather.4.cloned.1.call-done), kind=kOutput, calls=%fused_computation.52 | convolution fusion | flops 1073741824 | bytes 9961472 | tf_op jit(solution)/shard_map/dot_general | solution.py:32
  46.8 15.4 %all_gather.28 = bf16[2048,128]{1,0:T(8,128)(2,1)S(1)} all-gather(bf16[512,128]{1,0:T(8,128)(2,1)S(1)} %slice.71), channel_id=1, replica_groups=mesh['sector'=8,'dof'=4] {'dof'}, dimensions={0}, use_global_device_ids=true | all-gather | bytes 655360 | tf_op jit(solution)/shard_map/all_gather | solution.py:26
  62.2 2.6 collective-permute-start.1
  65.0 34.3 %all-reduce.9 = bf16[768,128]{1,0:T(8,128)(2,1)S(1)} all-reduce(f32[768,128]{1,0:T(8,128)S(1)} %slice_multiply_fusion.2), channel_id=1, replica_groups=mesh['sector'=8,'dof'=4] {'sector'}, use_global_device_ids=true, to_apply=%region_0.0 | all-reduce | flops 98304 | bytes 589824 | tf_op jit(solution)/shard_map/psum | solution.py:68
  99.4 17.6 %all_gather.29 = bf16[3072,128]{1,0:T(8,128)(2,1)S(1)} all-gather(bf16[768,128]{1,0:T(8,128)(2,1)S(1)} %all-reduce.9), channel_id=1, replica_groups=mesh['sector'=8,'dof'=4] {'dof'}, dimensions={0}, use_global_device_ids=true | all-gather | bytes 983040 | tf_op jit(solution)/shard_map/all_gather | solution.py:26
  117.0 3.7 fusion.34
  122.2 38.3 %all-reduce.5 = (f32[128]{0:T(128)S(1)}, f32[128]{0:T(128)S(1)}) all-reduce(f32[128]{0:T(128)S(1)} %get-tuple-element.7, f32[128]{0:T(128)S(1)} %get-tuple-element.6), channel_id=1, replica_groups=mesh['sector'=8,'dof'=4] {'sector','dof'}, use_global_device_ids=true, to_apply=%region_2.0 | all-reduce | flops 256 | bytes 2048 | tf_op jit(solution)/shard_map/psum | solution.py:78
  161.3 29.1 %all-gather.6.cloned.1.call-done = bf16[4096,128]{1,0:T(8,128)(2,1)} async-done(((bf16[1024,128]{1,0:T(8,128)(2,1)}), bf16[4096,128]{1,0:T(8,128)(2,1)}) %all-gather.6.cloned.1.call-update) | async-done | bytes 1048592 | tf_op jit(solution)/shard_map/all_gather | solution.py:26
  190.4 5.9 %convolution_bitcast_fusion.1 = f32[1024,128]{1,0:T(8,128)S(1)} fusion(bf16[1024,4096]{1,0:T(8,128)(2,1)} %param.10, bf16[4096,128]{1,0:T(8,128)(2,1)} %all-gather.6.cloned.1.call-done), kind=kOutput, calls=%fused_computation.7 | convolution fusion | flops 1073741824 | bytes 9961472 | tf_op jit(solution)/shard_map/dot_general | solution.py:32
  196.4 15.4 %all_gather.31 = bf16[2048,128]{1,0:T(8,128)(2,1)S(1)} all-gather(bf16[512,128]{1,0:T(8,128)(2,1)S(1)} %slice.70), channel_id=1, replica_groups=mesh['sector'=8,'dof'=4] {'dof'}, dimensions={0}, use_global_device_ids=true | all-gather | bytes 655360 | tf_op jit(solution)/shard_map/all_gather | solution.py:26
  211.8 2.6 collective-permute-start.3
  214.6 34.4 %all-reduce.10 = bf16[768,128]{1,0:T(8,128)(2,1)S(1)} all-reduce(f32[768,128]{1,0:T(8,128)S(1)} %slice_multiply_fusion.1), channel_id=1, replica_groups=mesh['sector'=8,'dof'=4] {'sector'}, use_global_device_ids=true, to_apply=%region_5.0 | all-reduce | flops 98304 | bytes 589824 | tf_op jit(solution)/shard_map/psum | solution.py:68
  248.9 17.6 %all_gather.32 = bf16[3072,128]{1,0:T(8,128)(2,1)S(1)} all-gather(bf16[768,128]{1,0:T(8,128)(2,1)S(1)} %all-reduce.10), channel_id=1, replica_groups=mesh['sector'=8,'dof'=4] {'dof'}, dimensions={0}, use_global_device_ids=true | all-gather | bytes 983040 | tf_op jit(solution)/shard_map/all_gather | solution.py:26
  266.5 3.7 fusion.36
  273.7 38.5 %all-reduce.4 = (f32[128]{0:T(128)S(1)}, f32[128]{0:T(128)S(1)}) all-reduce(f32[128]{0:T(128)S(1)} %get-tuple-element.5, f32[128]{0:T(128)S(1)} %get-tuple-element.4), channel_id=1, replica_groups=mesh['sector'=8,'dof'=4] {'sector','dof'}, use_global_device_ids=true, to_apply=%region_7.0 | all-reduce | flops 256 | bytes 2048 | tf_op jit(solution)/shard_map/psum | solution.py:78
  312.9 29.1 %all-gather.8.cloned.1.call-done = bf16[4096,128]{1,0:T(8,128)(2,1)} async-done(((bf16[1024,128]{1,0:T(8,128)(2,1)}), bf16[4096,128]{1,0:T(8,128)(2,1)}) %all-gather.8.cloned.1.call-update) | async-done | bytes 1048592 | tf_op jit(solution)/shard_map/all_gather | solution.py:26
  342.1 5.9 %convolution_bitcast_fusion = f32[1024,128]{1,0:T(8,128)S(1)} fusion(bf16[1024,4096]{1,0:T(8,128)(2,1)} %param.10, bf16[4096,128]{1,0:T(8,128)(2,1)} %all-gather.8.cloned.1.call-done), kind=kOutput, calls=%fused_computation.6 | convolution fusion | flops 1073741824 | bytes 9961472 | tf_op jit(solution)/shard_map/dot_general | solution.py:32
  348.0 15.4 %all_gather.34 = bf16[2048,128]{1,0:T(8,128)(2,1)S(1)} all-gather(bf16[512,128]{1,0:T(8,128)(2,1)S(1)} %slice.69), channel_id=1, replica_groups=mesh['sector'=8,'dof'=4] {'dof'}, dimensions={0}, use_global_device_ids=true | all-gather | bytes 655360 | tf_op jit(solution)/shard_map/all_gather | solution.py:26
  363.4 2.6 collective-permute-start.5
  366.2 34.3 %all-reduce.11 = bf16[768,128]{1,0:T(8,128)(2,1)S(1)} all-reduce(f32[768,128]{1,0:T(8,128)S(1)} %slice_multiply_fusion), channel_id=1, replica_groups=mesh['sector'=8,'dof'=4] {'sector'}, use_global_device_ids=true, to_apply=%region_10.0 | all-reduce | flops 98304 | bytes 589824 | tf_op jit(solution)/shard_map/psum | solution.py:68
  400.6 17.6 %all_gather.35 = bf16[3072,128]{1,0:T(8,128)(2,1)S(1)} all-gather(bf16[768,128]{1,0:T(8,128)(2,1)S(1)} %all-reduce.11), channel_id=1, replica_groups=mesh['sector'=8,'dof'=4] {'dof'}, dimensions={0}, use_global_device_ids=true | all-gather | bytes 983040 | tf_op jit(solution)/shard_map/all_gather | solution.py:26
  418.2 3.7 fusion.38
  425.3 38.3 %all-reduce.3 = (f32[128]{0:T(128)S(1)}, f32[128]{0:T(128)S(1)}) all-reduce(f32[128]{0:T(128)S(1)} %get-tuple-element.3, f32[128]{0:T(128)S(1)} %get-tuple-element.2), channel_id=1, replica_groups=mesh['sector'=8,'dof'=4] {'sector','dof'}, use_global_device_ids=true, to_apply=%region_12.0 | all-reduce | flops 256 | bytes 2048 | tf_op jit(solution)/shard_map/psum | solution.py:78
  (51 shorter events, 14.1 us)
Async XLA Ops:
  7.2 33.6 %all-gather.4.cloned.1.call-start = ((), (), s32[]{:S(2)}) async-start(), calls=%async_computation | async-start | bytes 1310720 | tf_op jit(solution)/shard_map/all_gather | solution.py:26
  9.0 181.4 %all-gather.6.cloned.1.call-start = ((), (), s32[]{:S(2)}) async-start(), calls=%async_computation.1 | async-start | bytes 1310720 | tf_op jit(solution)/shard_map/all_gather | solution.py:26
  62.1 58.5 %collective-permute-start = (bf16[1,2048,128]{2,1,0:T(8,128)(2,1)S(1)}, bf16[1,2048,128]{2,1,0:T(8,128)(2,1)S(1)}, u32[]{:S(2)}, u32[]{:S(2)}) collective-permute-start(bf16[1,2048,128]{2,1,0:T(8,128)(2,1)S(1)} %bitcast.118), channel_id=1, source_target_pairs={{0,4},{4,8},{8,12},{12,16},{16,20},{20,24},{24,28},{28,0},{1,5},{5... | collective-permute-start | bytes 1572872 | tf_op jit(solution)/shard_map/ppermute | solution.py:16
  62.2 58.6 %collective-permute-start.1 = (bf16[1,2048,128]{2,1,0:T(8,128)(2,1)S(1)}, bf16[1,2048,128]{2,1,0:T(8,128)(2,1)S(1)}, u32[]{:S(2)}, u32[]{:S(2)}) collective-permute-start(bf16[1,2048,128]{2,1,0:T(8,128)(2,1)S(1)} %bitcast.119), channel_id=1, source_target_pairs={{4,0},{8,4},{12,8},{16,12},{20,16},{24,20},{28,24},{0,28},{5,1},{9... | collective-permute-start | bytes 1572872 | tf_op jit(solution)/shard_map/ppermute | solution.py:18
  99.3 21.5 %copy-start = (bf16[1,1024,2048]{2,1,0:T(8,128)(2,1)S(1)}, bf16[1,1024,2048]{2,1,0:T(8,128)(2,1)}, u32[]{:S(2)}) copy-start(bf16[1,1024,2048]{2,1,0:T(8,128)(2,1)} %param.8) | copy-start | bytes 12582916
  99.3 21.5 %copy-start.3 = (f32[1,1024,128]{2,1,0:T(8,128)S(1)}, f32[1,1024,128]{2,1,0:T(8,128)}, u32[]{:S(2)}) copy-start(f32[1,1024,128]{2,1,0:T(8,128)} %param.6) | copy-start | bytes 1572868
  99.3 21.5 %copy-start.4 = (f32[1,1024]{1,0:T(1,128)S(1)}, f32[1,1024]{1,0:T(1,128)}, u32[]{:S(2)}) copy-start(f32[1,1024]{1,0:T(1,128)} %param.7) | copy-start | bytes 12292
  161.3 180.8 %all-gather.8.cloned.1.call-start = ((), (), s32[]{:S(2)}) async-start(), calls=%async_computation.2 | async-start | bytes 1310720 | tf_op jit(solution)/shard_map/all_gather | solution.py:26
  211.8 58.5 %collective-permute-start.2 = (bf16[1,2048,128]{2,1,0:T(8,128)(2,1)S(1)}, bf16[1,2048,128]{2,1,0:T(8,128)(2,1)}, u32[]{:S(2)}, u32[]{:S(2)}) collective-permute-start(bf16[1,2048,128]{2,1,0:T(8,128)(2,1)S(1)} %bitcast.120), channel_id=1, source_target_pairs={{0,4},{4,8},{8,12},{12,16},{16,20},{20,24},{24,28},{28,0},{1,5},{5... | collective-permute-start | bytes 1572872 | tf_op jit(solution)/shard_map/ppermute | solution.py:16
  211.8 59.5 %collective-permute-start.3 = (bf16[1,2048,128]{2,1,0:T(8,128)(2,1)S(1)}, bf16[1,2048,128]{2,1,0:T(8,128)(2,1)}, u32[]{:S(2)}, u32[]{:S(2)}) collective-permute-start(bf16[1,2048,128]{2,1,0:T(8,128)(2,1)S(1)} %bitcast.121), channel_id=1, source_target_pairs={{4,0},{8,4},{12,8},{16,12},{20,16},{24,20},{28,24},{0,28},{5,1},{9... | collective-permute-start | bytes 1572872 | tf_op jit(solution)/shard_map/ppermute | solution.py:18
  248.9 23.4 %copy-start.1 = (bf16[1,1024,2048]{2,1,0:T(8,128)(2,1)S(1)}, bf16[1,1024,2048]{2,1,0:T(8,128)(2,1)}, u32[]{:S(2)}) copy-start(bf16[1,1024,2048]{2,1,0:T(8,128)(2,1)} %param.8) | copy-start | bytes 12582916
  363.4 58.5 %collective-permute-start.4 = (bf16[1,2048,128]{2,1,0:T(8,128)(2,1)S(1)}, bf16[1,2048,128]{2,1,0:T(8,128)(2,1)}, u32[]{:S(2)}, u32[]{:S(2)}) collective-permute-start(bf16[1,2048,128]{2,1,0:T(8,128)(2,1)S(1)} %bitcast.116), channel_id=1, source_target_pairs={{0,4},{4,8},{8,12},{12,16},{16,20},{20,24},{24,28},{28,0},{1,5},{5... | collective-permute-start | bytes 1572872 | tf_op jit(solution)/shard_map/ppermute | solution.py:16
  363.4 59.5 %collective-permute-start.5 = (bf16[1,2048,128]{2,1,0:T(8,128)(2,1)S(1)}, bf16[1,2048,128]{2,1,0:T(8,128)(2,1)}, u32[]{:S(2)}, u32[]{:S(2)}) collective-permute-start(bf16[1,2048,128]{2,1,0:T(8,128)(2,1)S(1)} %bitcast.117), channel_id=1, source_target_pairs={{4,0},{8,4},{12,8},{16,12},{20,16},{24,20},{28,24},{0,28},{5,1},{9... | collective-permute-start | bytes 1572872 | tf_op jit(solution)/shard_map/ppermute | solution.py:18
  400.6 23.4 %copy-start.2 = (bf16[1,1024,2048]{2,1,0:T(8,128)(2,1)S(1)}, bf16[1,1024,2048]{2,1,0:T(8,128)(2,1)}, u32[]{:S(2)}) copy-start(bf16[1,1024,2048]{2,1,0:T(8,128)(2,1)} %param.8) | copy-start | bytes 12582916
Sparse Core Ops, SparseCore 0:
  10.1 30.6 all-gather.3
  161.4 28.9 all-gather.5
  313.1 28.9 all-gather.7
where the time goes:
time: 472 us; the launch traced here: 471 us
  blocking collectives  317 us (67%)
  waiting for transfers between devices  89.3 us (19%)
  matrix products  33 us (7%)
  between operations  14 us (3%)
  starting transfers between devices  8.06 us (2%)
  other arithmetic  5.83 us (1%)
    psum x3, blocking collectives, body(): lax.psum((jnp.sum(image * residual, axis=0), jnp.sum(image * image, axis=...  115 us
    psum x3, blocking collectives, body(): load = lax.psum(spring_rows * attached, 'sector')  103 us
    all_gather x6, blocking collectives, fold_rows(): lax.all_gather(field, 'dof', axis=0, tiled=True)  98.9 us
    all_gather x3, waiting for transfers between devices, fold_rows(): lax.all_gather(field, 'dof', axis=0, tiled=True)  89.3 us
    dot_general x6, matrix products, update(): return jnp.dot(matrix, piece, preferred_element_type=jnp.float32)  29 us
  transfers between devices with their start and end apart: 9, of which 3 were waited for; matrix products, arithmetic and copies ran while one was open for 3% of the time, Pallas kernels for 0%

commit v1 on v0

v1 whole, which is shorter than its diff:
```python
import jax
import jax.numpy as jnp
from jax import lax
from jax.sharding import PartitionSpec as P

ITERS = 3


def from_ahead(cells, axis, distance):
    count = lax.axis_size(axis)
    return lax.ppermute(cells, axis, [((i + distance) % count, i) for i in range(count)])


def all_pieces(cells, axis):
    return [cells] + [from_ahead(cells, axis, d) for d in range(1, lax.axis_size(axis))]


def in_order(pieces, axis):
    count = len(pieces)
    stacked = jnp.stack(pieces + pieces[:-1])
    start = (count - lax.axis_index(axis)) % count
    placed = lax.dynamic_slice_in_dim(stacked, start, count, axis=0)
    return placed


def gathered(cells, axis):
    placed = in_order(all_pieces(cells, axis), axis)
    return placed.reshape((-1,) + cells.shape[1:])


def scattered_sum(cells, axis):
    count = lax.axis_size(axis)
    part = cells.shape[0] // count
    me = lax.axis_index(axis)
    total = None
    for d in range(count):
        target = (me + d) % count
        piece = lax.dynamic_slice_in_dim(cells, target * part, part, axis=0)
        if d:
            piece = from_ahead(piece, axis, count - d)
        piece = piece.astype(jnp.float32)
        total = piece if total is None else total + piece
    return total


def summed(cells, axis):
    return sum(all_pieces(cells, axis)[1:], cells)


def beside_faces(own_faces, quarter):
    sectors, parts = lax.axis_size("sector"), lax.axis_size("dof")
    both = []
    for step, cells in ((-1, own_faces[quarter:]), (1, own_faces[:quarter])):
        pieces = []
        for d in range(parts):
            perm = [
                (((s + step) % sectors) * parts + (z + d) % parts, s * parts + z)
                for s in range(sectors)
                for z in range(parts)
            ]
            pieces.append(lax.ppermute(cells, ("sector", "dof"), perm))
        both.append(in_order(pieces, "dof"))
    return jnp.stack(both, axis=1)


def body(rhs, diagonal, coupling, springs, precond, hub_inverse):
    residual = rhs[0]
    diag_rows = diagonal[0][:, None]
    couple_rows = coupling[0]
    spring_rows = springs[0][:, None]
    rows_dev, loads = residual.shape
    quarter = rows_dev // 4
    solution = jnp.zeros_like(residual)

    def precondition(field):
        return jnp.dot(
            precond,
            gathered(field.astype(jnp.bfloat16), "dof"),
            preferred_element_type=jnp.float32,
        )

    precon = precondition(residual)
    for step in range(ITERS):
        own_faces = precon[: 2 * quarter].astype(jnp.bfloat16)
        needed = beside_faces(own_faces, quarter).reshape(-1, loads)
        attached = precon[: 3 * quarter]
        load = (spring_rows * attached).astype(jnp.bfloat16).T
        load = scattered_sum(load, "sector").astype(jnp.bfloat16)
        load = in_order(all_pieces(load, "dof"), "dof")
        load = load.transpose(0, 2, 1).reshape(-1, load.shape[1])
        hub = jnp.dot(hub_inverse, load, preferred_element_type=jnp.float32)
        hub = gathered(hub.T, "sector").T
        couple = jnp.dot(couple_rows, needed, preferred_element_type=jnp.float32)
        hub_term = jnp.concatenate(
            [spring_rows * (attached - hub), jnp.zeros((quarter, loads), jnp.float32)], axis=0
        )
        image = diag_rows * precon + couple + hub_term
        sums = jnp.stack([jnp.sum(image * residual, axis=0), jnp.sum(image * image, axis=0)])
        sums = summed(summed(sums, "sector"), "dof")
        alpha = sums[0] / (sums[1] + 1e-06)
        solution = solution + alpha * precon
        residual = residual - alpha * image
        if step < ITERS - 1:
            precon = precon - alpha * precondition(image)
    return (solution[None], residual[None])


def solution(mesh):
    placed = (
        P("sector", "dof", None),
        P("sector", "dof"),
        P("sector", "dof", None),
        P("sector", "dof"),
        P("dof", None),
        P("dof", None),
    )
    return jax.shard_map(
        body,
        mesh=mesh,
        in_specs=placed,
        out_specs=(P("sector", "dof", None), P("sector", "dof", None)),
        check_vma=False,
    )
```

time: 472 us -> 371 us (0.79)
  blocking collectives: 317 us -> 0 us
  starting transfers between devices: 8.06 us -> 173 us
  waiting for transfers between devices: 89.3 us -> 133 us
  local copies, waits for them, and re-layouts: 4.01 us -> 26.8 us
  between operations: 14 us -> 2.01 us
    psum x6 -> x0, blocking collectives: 218 us -> none  [the longest x3 115 us: body(): lax.psum((jnp.sum(image * residual, axis=0), jnp.sum(image * image, axis=...]
    ppermute x6 -> x114, starting transfers between devices: 7.94 us -> 173 us  [the longest x90 136 us: from_ahead(): lax.ppermute(cells, axis, [((i + distance) % count, i) for i in range(cou...]
    ppermute x6 -> x114, waiting for transfers between devices: 0.02 us -> 133 us  [the longest x90 108 us: from_ahead(): lax.ppermute(cells, axis, [((i + distance) % count, i) for i in range(cou...]
    all_gather x6 -> x0, blocking collectives: 98.9 us -> none  [fold_rows(): lax.all_gather(field, 'dof', axis=0, tiled=True)]
    all_gather x3 -> x0, waiting for transfers between devices: 89.3 us -> none  [fold_rows(): lax.all_gather(field, 'dof', axis=0, tiled=True)]
    unnamed x10 -> x134, local copies, waits for them, and re-layouts: 0.03 us -> 16.2 us
    dynamic_slice x0 -> x23, local copies, waits for them, and re-layouts: none -> 9 us  [the longest x20 8.91 us: in_order(): placed = lax.dynamic_slice_in_dim(stacked, start, count, axis=0)]
  transfers between devices with their start and end apart: 9 -> 114, of which waited for: 3 -> 43; matrix products, arithmetic and copies ran while one was open for 3% -> 5% of each run, Pallas kernels for 0% -> 0%
where the time goes in v1:
time: 371 us; the launch traced here: 370 us
  starting transfers between devices  173 us (47%)
  waiting for transfers between devices  133 us (36%)
  matrix products  32.1 us (9%)
  local copies, waits for them, and re-layouts  26.8 us (7%)
    ppermute x90, starting transfers between devices, from_ahead(): lax.ppermute(cells, axis, [((i + distance) % count, i) for i in range(cou...  136 us
    ppermute x90, waiting for transfers between devices, from_ahead(): lax.ppermute(cells, axis, [((i + distance) % count, i) for i in range(cou...  108 us
    ppermute x24, starting transfers between devices, beside_faces(): pieces.append(lax.ppermute(cells, ('sector', 'dof'), perm))  37.2 us
    ppermute x24, waiting for transfers between devices, beside_faces(): pieces.append(lax.ppermute(cells, ('sector', 'dof'), perm))  24.4 us
    dot_general x3, matrix products, precondition(): jnp.dot(precond, gathered(field.astype(jnp.bfloat16), 'dof'), preferred_e...  19.8 us
    unnamed x134, local copies, waits for them, and re-layouts  16.2 us
    dynamic_slice x20, local copies, waits for them, and re-layouts, in_order(): placed = lax.dynamic_slice_in_dim(stacked, start, count, axis=0)  8.91 us
    dot_general x3, matrix products, body(): hub = jnp.dot(hub_inverse, load, preferred_element_type=jnp.float32)  7.55 us
  transfers between devices with their start and end apart: 114, of which 43 were waited for; matrix products, arithmetic and copies ran while one was open for 5% of the time, Pallas kernels for 0%

profile of v1, /device:TPU:0, one launch (start us, length us, event | category | flops | bytes accessed | tf_op | source)
XLA Modules:
  0.0 370.2 jit_solution(2223829396542548814)
XLA Ops:
  1.9 5.1 %collective-permute-start = (bf16[1024,128]{0,1:T(8,128)(2,1)S(1)}, bf16[1024,128]{0,1:T(8,128)(2,1)S(1)}, u32[]{:S(2)}, u32[]{:S(2)}) collective-permute-start(bf16[1024,128]{0,1:T(8,128)(2,1)S(1)} %bitcast_convert_fusion), channel_id=1, source_target_pairs={{1,0},{2,1},{3,2},{0,3},{5,4},{6,5},{7,6},{4,7},{9,8},{10,9},{11,1... | collective-permute-start | bytes 786440 | tf_op jit(solution)/shard_map/ppermute | solution.py:11
  8.8 4.9 %collective-permute-done = bf16[1024,128]{0,1:T(8,128)(2,1)S(1)} collective-permute-done((bf16[1024,128]{0,1:T(8,128)(2,1)S(1)}, bf16[1024,128]{0,1:T(8,128)(2,1)S(1)}, u32[]{:S(2)}, u32[]{:S(2)}) %collective-permute-start) | collective-permute-done | bytes 262176 | tf_op jit(solution)/shard_map/ppermute | solution.py:11
  14.5 14.9 %collective-permute-done.1 = bf16[1024,128]{0,1:T(8,128)(2,1)S(1)} collective-permute-done((bf16[1024,128]{0,1:T(8,128)(2,1)S(1)}, bf16[1024,128]{0,1:T(8,128)(2,1)S(1)}, u32[]{:S(2)}, u32[]{:S(2)}) %collective-permute-start.1) | collective-permute-done | bytes 262176 | tf_op jit(solution)/shard_map/ppermute | solution.py:11
  34.9 6.3 %fusion.69 = (bf16[1024,128]{0,1:T(8,128)(2,1)S(1)}, f32[1024,128]{0,1:T(8,128)S(1)}) fusion(bf16[4096,128]{1,0:T(8,128)(2,1)S(1)} %bitcast.433, bf16[1024,4096]{1,0:T(8,128)(2,1)} %param.10), kind=kOutput, calls=%fused_computation.251 | convolution fusion | flops 1073872896 | bytes 10223616 | tf_op jit(solution)/shard_map/dot_general | solution.py:76
  65.4 5.6 %collective-permute-done.20 = bf16[16,768]{1,0:T(8,128)(2,1)S(1)} collective-permute-done((bf16[16,768]{1,0:T(8,128)(2,1)S(1)}, bf16[16,768]{1,0:T(8,128)(2,1)S(1)}, u32[]{:S(2)}, u32[]{:S(2)}) %collective-permute-start.20) | collective-permute-done | bytes 24608 | tf_op jit(solution)/shard_map/ppermute | solution.py:11
  71.1 3.7 constant_dynamic-update-slice_fusion.42
  86.0 4.0 %collective-permute-done.10 = bf16[256,128]{0,1:T(8,128)(2,1)S(1)} collective-permute-done((bf16[256,128]{0,1:T(8,128)(2,1)S(1)}, bf16[256,128]{0,1:T(8,128)(2,1)S(1)}, u32[]{:S(2)}, u32[]{:S(2)}) %collective-permute-start.10) | collective-permute-done | bytes 65568 | tf_op jit(solution)/shard_map/ppermute | solution.py:61
  91.8 3.7 collective-permute-start.26
  128.9 12.2 %collective-permute-done.38 = bf16[1024,128]{0,1:T(8,128)(2,1)S(1)} collective-permute-done((bf16[1024,128]{0,1:T(8,128)(2,1)S(1)}, bf16[1024,128]{0,1:T(8,128)(2,1)S(1)}, u32[]{:S(2)}, u32[]{:S(2)}) %collective-permute-start.38) | collective-permute-done | bytes 262176 | tf_op jit(solution)/shard_map/ppermute | solution.py:11
  141.1 3.8 %collective-permute-done.39 = bf16[1024,128]{0,1:T(8,128)(2,1)S(1)} collective-permute-done((bf16[1024,128]{0,1:T(8,128)(2,1)S(1)}, bf16[1024,128]{0,1:T(8,128)(2,1)S(1)}, u32[]{:S(2)}, u32[]{:S(2)}) %collective-permute-start.39) | collective-permute-done | bytes 262176 | tf_op jit(solution)/shard_map/ppermute | solution.py:11
  146.6 6.8 %fusion.64 = (bf16[1024,128]{0,1:T(8,128)(2,1)S(1)}, f32[1024,128]{0,1:T(8,128)S(1)}) fusion(f32[1024,128]{0,1:T(8,128)S(1)} %get-tuple-element.59, f32[128]{0:T(128)S(1)} %fusion.58, bf16[4096,128]{1,0:T(8,128)(2,1)} %bitcast.434, bf16[1024,4096]{1,0:T(8,128)(2,1)} %param.10), kind=kOutput, calls=%fused_computation.247 | convolution fusion | flops 1074135040 | bytes 10748416 | tf_op jit(solution)/shard_map/dot_general | solution.py:76
  164.1 6.7 %collective-permute-start.56 = (bf16[16,768]{1,0:T(8,128)(2,1)S(1)}, bf16[16,768]{1,0:T(8,128)(2,1)S(1)}, u32[]{:S(2)}, u32[]{:S(2)}) collective-permute-start(bf16[16,768]{1,0:T(8,128)(2,1)S(1)} %get-tuple-element.22), channel_id=1, source_target_pairs={{1,0},{2,1},{3,2},{0,3},{5,4},{6,5},{7,6},{4,7},{9,8},{10,9},{11,1... | collective-permute-start | bytes 73736 | tf_op jit(solution)/shard_map/ppermute | solution.py:11
  181.3 5.6 %collective-permute-done.58 = bf16[16,768]{1,0:T(8,128)(2,1)S(1)} collective-permute-done((bf16[16,768]{1,0:T(8,128)(2,1)S(1)}, bf16[16,768]{1,0:T(8,128)(2,1)S(1)}, u32[]{:S(2)}, u32[]{:S(2)}) %collective-permute-start.58) | collective-permute-done | bytes 24608 | tf_op jit(solution)/shard_map/ppermute | solution.py:11
  192.7 3.8 %collective-permute-start.47 = (bf16[256,128]{0,1:T(8,128)(2,1)S(1)}, bf16[256,128]{0,1:T(8,128)(2,1)S(1)}, u32[]{:S(2)}, u32[]{:S(2)}) collective-permute-start(bf16[256,128]{0,1:T(8,128)(2,1)S(1)} %get-tuple-element.32), channel_id=1, source_target_pairs={{6,0},{7,1},{4,2},{5,3},{10,4},{11,5},{8,6},{9,7},{14,8},{15,9},{1... | collective-permute-start | bytes 196616 | tf_op jit(solution)/shard_map/ppermute | solution.py:61
  207.2 4.0 %collective-permute-start.64 = (f32[16,768]{1,0:T(8,128)S(1)}, f32[16,768]{1,0:T(8,128)S(1)}, u32[]{:S(2)}, u32[]{:S(2)}) collective-permute-start(f32[16,768]{1,0:T(8,128)S(1)} %get-tuple-element.64), channel_id=1, source_target_pairs={{24,0},{28,4},{0,8},{4,12},{8,16},{12,20},{16,24},{20,28},{25,1},{... | collective-permute-start | bytes 147464 | tf_op jit(solution)/shard_map/ppermute | solution.py:11
  227.5 3.8 %collective-permute-start.71 = (f32[2,128]{1,0:T(2,128)S(1)}, f32[2,128]{1,0:T(2,128)S(1)}, u32[]{:S(2)}, u32[]{:S(2)}) collective-permute-start(f32[2,128]{1,0:T(2,128)S(1)} %pad_maximum_fusion.4), channel_id=1, source_target_pairs={{24,0},{28,4},{0,8},{4,12},{8,16},{12,20},{16,24},{20,28},{25,1},{... | collective-permute-start | bytes 3080 | tf_op jit(solution)/shard_map/ppermute | solution.py:11
  247.1 12.3 %collective-permute-done.76 = bf16[1024,128]{0,1:T(8,128)(2,1)S(1)} collective-permute-done((bf16[1024,128]{0,1:T(8,128)(2,1)S(1)}, bf16[1024,128]{0,1:T(8,128)(2,1)S(1)}, u32[]{:S(2)}, u32[]{:S(2)}) %collective-permute-start.76) | collective-permute-done | bytes 262176 | tf_op jit(solution)/shard_map/ppermute | solution.py:11
  259.4 3.8 %collective-permute-done.77 = bf16[1024,128]{0,1:T(8,128)(2,1)S(1)} collective-permute-done((bf16[1024,128]{0,1:T(8,128)(2,1)S(1)}, bf16[1024,128]{0,1:T(8,128)(2,1)S(1)}, u32[]{:S(2)}, u32[]{:S(2)}) %collective-permute-start.77) | collective-permute-done | bytes 262176 | tf_op jit(solution)/shard_map/ppermute | solution.py:11
  266.7 6.8 %fusion.62 = (bf16[1024,128]{0,1:T(8,128)(2,1)S(1)}, f32[1024,128]{0,1:T(8,128)S(1)}) fusion(f32[1024,128]{0,1:T(8,128)S(1)} %get-tuple-element.24, f32[128]{0:T(128)S(1)} %fusion.59, bf16[4096,128]{1,0:T(8,128)(2,1)} %bitcast.435, bf16[1024,4096]{1,0:T(8,128)(2,1)} %param.10), kind=kOutput, calls=%fused_computation.246 | convolution fusion | flops 1074135040 | bytes 10748416 | tf_op jit(solution)/shard_map/dot_general | solution.py:76
  284.2 6.8 %collective-permute-start.94 = (bf16[16,768]{1,0:T(8,128)(2,1)S(1)}, bf16[16,768]{1,0:T(8,128)(2,1)S(1)}, u32[]{:S(2)}, u32[]{:S(2)}) collective-permute-start(bf16[16,768]{1,0:T(8,128)(2,1)S(1)} %get-tuple-element.15), channel_id=1, source_target_pairs={{1,0},{2,1},{3,2},{0,3},{5,4},{6,5},{7,6},{4,7},{9,8},{10,9},{11,1... | collective-permute-start | bytes 73736 | tf_op jit(solution)/shard_map/ppermute | solution.py:11
  301.4 5.6 %collective-permute-done.96 = bf16[16,768]{1,0:T(8,128)(2,1)S(1)} collective-permute-done((bf16[16,768]{1,0:T(8,128)(2,1)S(1)}, bf16[16,768]{1,0:T(8,128)(2,1)S(1)}, u32[]{:S(2)}, u32[]{:S(2)}) %collective-permute-start.96) | collective-permute-done | bytes 24608 | tf_op jit(solution)/shard_map/ppermute | solution.py:11
  312.8 3.8 %collective-permute-start.85 = (bf16[256,128]{0,1:T(8,128)(2,1)S(1)}, bf16[256,128]{0,1:T(8,128)(2,1)S(1)}, u32[]{:S(2)}, u32[]{:S(2)}) collective-permute-start(bf16[256,128]{0,1:T(8,128)(2,1)S(1)} %get-tuple-element.30), channel_id=1, source_target_pairs={{6,0},{7,1},{4,2},{5,3},{10,4},{11,5},{8,6},{9,7},{14,8},{15,9},{1... | collective-permute-start | bytes 196616 | tf_op jit(solution)/shard_map/ppermute | solution.py:61
  327.2 4.0 %collective-permute-start.102 = (f32[16,768]{1,0:T(8,128)S(1)}, f32[16,768]{1,0:T(8,128)S(1)}, u32[]{:S(2)}, u32[]{:S(2)}) collective-permute-start(f32[16,768]{1,0:T(8,128)S(1)} %get-tuple-element.67), channel_id=1, source_target_pairs={{24,0},{28,4},{0,8},{4,12},{8,16},{12,20},{16,24},{20,28},{25,1},{... | collective-permute-start | bytes 147464 | tf_op jit(solution)/shard_map/ppermute | solution.py:11
  360.5 3.5 collective-permute-start.111
  (427 shorter events, 226.7 us)
Async XLA Ops:
  7.0 23.0 %collective-permute-start.2 = (bf16[1024,128]{0,1:T(8,128)(2,1)S(1)}, bf16[1024,128]{0,1:T(8,128)(2,1)S(1)}, u32[]{:S(2)}, u32[]{:S(2)}) collective-permute-start(bf16[1024,128]{0,1:T(8,128)(2,1)S(1)} %bitcast_convert_fusion), channel_id=1, source_target_pairs={{3,0},{0,1},{1,2},{2,3},{7,4},{4,5},{5,6},{6,7},{11,8},{8,9},{9,10... | collective-permute-start | bytes 786440 | tf_op jit(solution)/shard_map/ppermute | solution.py:11
  7.0 22.3 %collective-permute-start.1 = (bf16[1024,128]{0,1:T(8,128)(2,1)S(1)}, bf16[1024,128]{0,1:T(8,128)(2,1)S(1)}, u32[]{:S(2)}, u32[]{:S(2)}) collective-permute-start(bf16[1024,128]{0,1:T(8,128)(2,1)S(1)} %bitcast_convert_fusion), channel_id=1, source_target_pairs={{2,0},{3,1},{0,2},{1,3},{6,4},{7,5},{4,6},{5,7},{10,8},{11,9},{8,1... | collective-permute-start | bytes 786440 | tf_op jit(solution)/shard_map/ppermute | solution.py:11
  55.0 41.5 %collective-permute-start.6 = (bf16[256,128]{0,1:T(8,128)(2,1)S(1)}, bf16[256,128]{0,1:T(8,128)(2,1)S(1)}, u32[]{:S(2)}, u32[]{:S(2)}) collective-permute-start(bf16[256,128]{0,1:T(8,128)(2,1)S(1)} %get-tuple-element.33), channel_id=1, source_target_pairs={{31,0},{28,1},{29,2},{30,3},{3,4},{0,5},{1,6},{2,7},{7,8},{4,9},{5... | collective-permute-start | bytes 196616 | tf_op jit(solution)/shard_map/ppermute | solution.py:61
  55.1 40.6 %collective-permute-start.5 = (bf16[256,128]{0,1:T(8,128)(2,1)S(1)}, bf16[256,128]{0,1:T(8,128)(2,1)S(1)}, u32[]{:S(2)}, u32[]{:S(2)}) collective-permute-start(bf16[256,128]{0,1:T(8,128)(2,1)S(1)} %get-tuple-element.33), channel_id=1, source_target_pairs={{30,0},{31,1},{28,2},{29,3},{2,4},{3,5},{0,6},{1,7},{6,8},{7,9},{4... | collective-permute-start | bytes 196616 | tf_op jit(solution)/shard_map/ppermute | solution.py:61
  56.3 39.3 %collective-permute-start.4 = (bf16[256,128]{0,1:T(8,128)(2,1)S(1)}, bf16[256,128]{0,1:T(8,128)(2,1)S(1)}, u32[]{:S(2)}, u32[]{:S(2)}) collective-permute-start(bf16[256,128]{0,1:T(8,128)(2,1)S(1)} %get-tuple-element.33), channel_id=1, source_target_pairs={{29,0},{30,1},{31,2},{28,3},{1,4},{2,5},{3,6},{0,7},{5,8},{6,9},{7... | collective-permute-start | bytes 196616 | tf_op jit(solution)/shard_map/ppermute | solution.py:61
  59.5 32.3 %collective-permute-start.3 = (bf16[256,128]{0,1:T(8,128)(2,1)S(1)}, bf16[256,128]{0,1:T(8,128)(2,1)S(1)}, u32[]{:S(2)}, u32[]{:S(2)}) collective-permute-start(bf16[256,128]{0,1:T(8,128)(2,1)S(1)} %get-tuple-element.33), channel_id=1, source_target_pairs={{28,0},{29,1},{30,2},{31,3},{0,4},{1,5},{2,6},{3,7},{4,8},{5,9},{6... | collective-permute-start | bytes 196616 | tf_op jit(solution)/shard_map/ppermute | solution.py:61
  90.0 18.2 %collective-permute-start.27 = (f32[16,768]{1,0:T(8,128)S(1)}, f32[16,768]{1,0:T(8,128)S(1)}, u32[]{:S(2)}, u32[]{:S(2)}) collective-permute-start(f32[16,768]{1,0:T(8,128)S(1)} %get-tuple-element.61), channel_id=1, source_target_pairs={{28,0},{0,4},{4,8},{8,12},{12,16},{16,20},{20,24},{24,28},{29,1},{... | collective-permute-start | bytes 147464 | tf_op jit(solution)/shard_map/ppermute | solution.py:11
  91.8 16.3 %collective-permute-start.26 = (f32[16,768]{1,0:T(8,128)S(1)}, f32[16,768]{1,0:T(8,128)S(1)}, u32[]{:S(2)}, u32[]{:S(2)}) collective-permute-start(f32[16,768]{1,0:T(8,128)S(1)} %get-tuple-element.61), channel_id=1, source_target_pairs={{24,0},{28,4},{0,8},{4,12},{8,16},{12,20},{16,24},{20,28},{25,1},{... | collective-permute-start | bytes 147464 | tf_op jit(solution)/shard_map/ppermute | solution.py:11
  123.9 21.1 %collective-permute-start.40 = (bf16[1024,128]{0,1:T(8,128)(2,1)S(1)}, bf16[1024,128]{0,1:T(8,128)(2,1)S(1)}, u32[]{:S(2)}, u32[]{:S(2)}) collective-permute-start(bf16[1024,128]{0,1:T(8,128)(2,1)S(1)} %get-tuple-element.26), channel_id=1, source_target_pairs={{3,0},{0,1},{1,2},{2,3},{7,4},{4,5},{5,6},{6,7},{11,8},{8,9},{9,10... | collective-permute-start | bytes 786440 | tf_op jit(solution)/shard_map/ppermute | solution.py:11
  124.5 20.5 %collective-permute-start.39 = (bf16[1024,128]{0,1:T(8,128)(2,1)S(1)}, bf16[1024,128]{0,1:T(8,128)(2,1)S(1)}, u32[]{:S(2)}, u32[]{:S(2)}) collective-permute-start(bf16[1024,128]{0,1:T(8,128)(2,1)S(1)} %get-tuple-element.26), channel_id=1, source_target_pairs={{2,0},{3,1},{0,2},{1,3},{6,4},{7,5},{4,6},{5,7},{10,8},{11,9},{8,1... | collective-permute-start | bytes 786440 | tf_op jit(solution)/shard_map/ppermute | solution.py:11
  170.8 42.1 %collective-permute-start.44 = (bf16[256,128]{0,1:T(8,128)(2,1)S(1)}, bf16[256,128]{0,1:T(8,128)(2,1)S(1)}, u32[]{:S(2)}, u32[]{:S(2)}) collective-permute-start(bf16[256,128]{0,1:T(8,128)(2,1)S(1)} %get-tuple-element.31), channel_id=1, source_target_pairs={{31,0},{28,1},{29,2},{30,3},{3,4},{0,5},{1,6},{2,7},{7,8},{4,9},{5... | collective-permute-start | bytes 196616 | tf_op jit(solution)/shard_map/ppermute | solution.py:61
  170.9 40.4 %collective-permute-start.43 = (bf16[256,128]{0,1:T(8,128)(2,1)S(1)}, bf16[256,128]{0,1:T(8,128)(2,1)S(1)}, u32[]{:S(2)}, u32[]{:S(2)}) collective-permute-start(bf16[256,128]{0,1:T(8,128)(2,1)S(1)} %get-tuple-element.31), channel_id=1, source_target_pairs={{30,0},{31,1},{28,2},{29,3},{2,4},{3,5},{0,6},{1,7},{6,8},{7,9},{4... | collective-permute-start | bytes 196616 | tf_op jit(solution)/shard_map/ppermute | solution.py:61
  172.0 39.2 %collective-permute-start.42 = (bf16[256,128]{0,1:T(8,128)(2,1)S(1)}, bf16[256,128]{0,1:T(8,128)(2,1)S(1)}, u32[]{:S(2)}, u32[]{:S(2)}) collective-permute-start(bf16[256,128]{0,1:T(8,128)(2,1)S(1)} %get-tuple-element.31), channel_id=1, source_target_pairs={{29,0},{30,1},{31,2},{28,3},{1,4},{2,5},{3,6},{0,7},{5,8},{6,9},{7... | collective-permute-start | bytes 196616 | tf_op jit(solution)/shard_map/ppermute | solution.py:61
  175.3 31.9 %collective-permute-start.41 = (bf16[256,128]{0,1:T(8,128)(2,1)S(1)}, bf16[256,128]{0,1:T(8,128)(2,1)S(1)}, u32[]{:S(2)}, u32[]{:S(2)}) collective-permute-start(bf16[256,128]{0,1:T(8,128)(2,1)S(1)} %get-tuple-element.31), channel_id=1, source_target_pairs={{28,0},{29,1},{30,2},{31,3},{0,4},{1,5},{2,6},{3,7},{4,8},{5,9},{6... | collective-permute-start | bytes 196616 | tf_op jit(solution)/shard_map/ppermute | solution.py:61
  204.7 20.8 %collective-permute-start.65 = (f32[16,768]{1,0:T(8,128)S(1)}, f32[16,768]{1,0:T(8,128)S(1)}, u32[]{:S(2)}, u32[]{:S(2)}) collective-permute-start(f32[16,768]{1,0:T(8,128)S(1)} %get-tuple-element.64), channel_id=1, source_target_pairs={{28,0},{0,4},{4,8},{8,12},{12,16},{16,20},{20,24},{24,28},{29,1},{... | collective-permute-start | bytes 147464 | tf_op jit(solution)/shard_map/ppermute | solution.py:11
  207.2 18.2 %collective-permute-start.64 = (f32[16,768]{1,0:T(8,128)S(1)}, f32[16,768]{1,0:T(8,128)S(1)}, u32[]{:S(2)}, u32[]{:S(2)}) collective-permute-start(f32[16,768]{1,0:T(8,128)S(1)} %get-tuple-element.64), channel_id=1, source_target_pairs={{24,0},{28,4},{0,8},{4,12},{8,16},{12,20},{16,24},{20,28},{25,1},{... | collective-permute-start | bytes 147464 | tf_op jit(solution)/shard_map/ppermute | solution.py:11
  242.1 21.2 %collective-permute-start.78 = (bf16[1024,128]{0,1:T(8,128)(2,1)S(1)}, bf16[1024,128]{0,1:T(8,128)(2,1)S(1)}, u32[]{:S(2)}, u32[]{:S(2)}) collective-permute-start(bf16[1024,128]{0,1:T(8,128)(2,1)S(1)} %get-tuple-element.20), channel_id=1, source_target_pairs={{3,0},{0,1},{1,2},{2,3},{7,4},{4,5},{5,6},{6,7},{11,8},{8,9},{9,10... | collective-permute-start | bytes 786440 | tf_op jit(solution)/shard_map/ppermute | solution.py:11
  242.7 20.6 %collective-permute-start.77 = (bf16[1024,128]{0,1:T(8,128)(2,1)S(1)}, bf16[1024,128]{0,1:T(8,128)(2,1)S(1)}, u32[]{:S(2)}, u32[]{:S(2)}) collective-permute-start(bf16[1024,128]{0,1:T(8,128)(2,1)S(1)} %get-tuple-element.20), channel_id=1, source_target_pairs={{2,0},{3,1},{0,2},{1,3},{6,4},{7,5},{4,6},{5,7},{10,8},{11,9},{8,1... | collective-permute-start | bytes 786440 | tf_op jit(solution)/shard_map/ppermute | solution.py:11
  291.0 41.0 %collective-permute-start.82 = (bf16[256,128]{0,1:T(8,128)(2,1)S(1)}, bf16[256,128]{0,1:T(8,128)(2,1)S(1)}, u32[]{:S(2)}, u32[]{:S(2)}) collective-permute-start(bf16[256,128]{0,1:T(8,128)(2,1)S(1)} %get-tuple-element.29), channel_id=1, source_target_pairs={{31,0},{28,1},{29,2},{30,3},{3,4},{0,5},{1,6},{2,7},{7,8},{4,9},{5... | collective-permute-start | bytes 196616 | tf_op jit(solution)/shard_map/ppermute | solution.py:61
  291.1 40.2 %collective-permute-start.81 = (bf16[256,128]{0,1:T(8,128)(2,1)S(1)}, bf16[256,128]{0,1:T(8,128)(2,1)S(1)}, u32[]{:S(2)}, u32[]{:S(2)}) collective-permute-start(bf16[256,128]{0,1:T(8,128)(2,1)S(1)} %get-tuple-element.29), channel_id=1, source_target_pairs={{30,0},{31,1},{28,2},{29,3},{2,4},{3,5},{0,6},{1,7},{6,8},{7,9},{4... | collective-permute-start | bytes 196616 | tf_op jit(solution)/shard_map/ppermute | solution.py:61
  292.1 39.2 %collective-permute-start.80 = (bf16[256,128]{0,1:T(8,128)(2,1)S(1)}, bf16[256,128]{0,1:T(8,128)(2,1)S(1)}, u32[]{:S(2)}, u32[]{:S(2)}) collective-permute-start(bf16[256,128]{0,1:T(8,128)(2,1)S(1)} %get-tuple-element.29), channel_id=1, source_target_pairs={{29,0},{30,1},{31,2},{28,3},{1,4},{2,5},{3,6},{0,7},{5,8},{6,9},{7... | collective-permute-start | bytes 196616 | tf_op jit(solution)/shard_map/ppermute | solution.py:61
  295.3 31.9 %collective-permute-start.79 = (bf16[256,128]{0,1:T(8,128)(2,1)S(1)}, bf16[256,128]{0,1:T(8,128)(2,1)S(1)}, u32[]{:S(2)}, u32[]{:S(2)}) collective-permute-start(bf16[256,128]{0,1:T(8,128)(2,1)S(1)} %get-tuple-element.29), channel_id=1, source_target_pairs={{28,0},{29,1},{30,2},{31,3},{0,4},{1,5},{2,6},{3,7},{4,8},{5,9},{6... | collective-permute-start | bytes 196616 | tf_op jit(solution)/shard_map/ppermute | solution.py:61
  324.7 20.4 %collective-permute-start.103 = (f32[16,768]{1,0:T(8,128)S(1)}, f32[16,768]{1,0:T(8,128)}, u32[]{:S(2)}, u32[]{:S(2)}) collective-permute-start(f32[16,768]{1,0:T(8,128)S(1)} %get-tuple-element.67), channel_id=1, source_target_pairs={{28,0},{0,4},{4,8},{8,12},{12,16},{16,20},{20,24},{24,28},{29,1},{... | collective-permute-start | bytes 147464 | tf_op jit(solution)/shard_map/ppermute | solution.py:11
  327.2 17.9 %collective-permute-start.102 = (f32[16,768]{1,0:T(8,128)S(1)}, f32[16,768]{1,0:T(8,128)S(1)}, u32[]{:S(2)}, u32[]{:S(2)}) collective-permute-start(f32[16,768]{1,0:T(8,128)S(1)} %get-tuple-element.67), channel_id=1, source_target_pairs={{24,0},{28,4},{0,8},{4,12},{8,16},{12,20},{16,24},{20,28},{25,1},{... | collective-permute-start | bytes 147464 | tf_op jit(solution)/shard_map/ppermute | solution.py:11
  (102 other events, 755.6 us)

commit v2 on v1

v2 whole, which is shorter than its diff:
```python
import jax
import jax.numpy as jnp
from jax import lax
from jax.sharding import PartitionSpec as P

ITERS = 3


def gathered(cells, axis):
    return lax.all_gather(cells, axis, axis=0, tiled=True)


def scattered_sum(cells, axis):
    count = lax.axis_size(axis)
    parts = cells.reshape((count, -1) + cells.shape[1:])
    parts = lax.all_to_all(parts, axis, split_axis=0, concat_axis=0)
    return jnp.sum(parts.astype(jnp.float32), axis=0)


def summed(cells, axes):
    count = lax.axis_size(axes)
    parts = jnp.broadcast_to(cells[None], (count,) + cells.shape)
    return jnp.sum(lax.all_to_all(parts, axes, split_axis=0, concat_axis=0), axis=0)


def beside_faces(own_faces, quarter):
    sectors = lax.axis_size("sector")
    before = lax.ppermute(
        own_faces[quarter:], "sector", [(s, (s + 1) % sectors) for s in range(sectors)]
    )
    after = lax.ppermute(
        own_faces[:quarter], "sector", [((s + 1) % sectors, s) for s in range(sectors)]
    )
    return gathered(jnp.concatenate([before, after]), "dof")


def body(rhs, diagonal, coupling, springs, precond, hub_inverse):
    residual = rhs[0]
    diag_rows = diagonal[0][:, None]
    couple_rows = coupling[0]
    spring_rows = springs[0][:, None]
    rows_dev, loads = residual.shape
    quarter = rows_dev // 4
    solution = jnp.zeros_like(residual)

    def precondition(field):
        return jnp.dot(
            precond,
            gathered(field.astype(jnp.bfloat16), "dof"),
            preferred_element_type=jnp.float32,
        )

    precon = precondition(residual)
    for step in range(ITERS):
        own_faces = precon[: 2 * quarter].astype(jnp.bfloat16)
        needed = beside_faces(own_faces, quarter)
        attached = precon[: 3 * quarter]
        load = (spring_rows * attached).astype(jnp.bfloat16).T
        load = scattered_sum(load, "sector").astype(jnp.bfloat16)
        load = lax.all_gather(load, "dof", axis=0)
        load = load.transpose(0, 2, 1).reshape(-1, load.shape[1])
        hub = jnp.dot(hub_inverse, load, preferred_element_type=jnp.float32)
        hub = gathered(hub.T, "sector").T
        couple = jnp.dot(couple_rows, needed, preferred_element_type=jnp.float32)
        hub_term = jnp.concatenate(
            [spring_rows * (attached - hub), jnp.zeros((quarter, loads), jnp.float32)], axis=0
        )
        image = diag_rows * precon + couple + hub_term
        sums = jnp.stack([jnp.sum(image * residual, axis=0), jnp.sum(image * image, axis=0)])
        sums = summed(sums, ("sector", "dof"))
        alpha = sums[0] / (sums[1] + 1e-06)
        solution = solution + alpha * precon
        residual = residual - alpha * image
        if step < ITERS - 1:
            precon = precon - alpha * precondition(image)
    return (solution[None], residual[None])


def solution(mesh):
    placed = (
        P("sector", "dof", None),
        P("sector", "dof"),
        P("sector", "dof", None),
        P("sector", "dof"),
        P("dof", None),
        P("dof", None),
    )
    return jax.shard_map(
        body,
        mesh=mesh,
        in_specs=placed,
        out_specs=(P("sector", "dof", None), P("sector", "dof", None)),
        check_vma=False,
    )
```

time: 371 us -> 296 us (0.80)
  starting transfers between devices: 173 us -> 18.4 us
  blocking collectives: 0 us -> 150 us
  waiting for transfers between devices: 133 us -> 63.6 us
  local copies, waits for them, and re-layouts: 26.8 us -> 4.38 us
  between operations: 2.01 us -> 14.1 us
  matrix products: 32.1 us -> 37.6 us
    ppermute x114 -> x6, starting transfers between devices: 173 us -> 8.07 us  [the longest x3 7.89 us: beside_faces(): lax.ppermute(own_faces[:quarter], 'sector', [((s + 1) % sectors, s) for s...]
    ppermute x114 -> x6, waiting for transfers between devices: 133 us -> 0.02 us  [the longest x3 0.01 us: beside_faces(): lax.ppermute(own_faces[:quarter], 'sector', [((s + 1) % sectors, s) for s...]
    all_gather x0 -> x9, blocking collectives: none -> 118 us  [the longest x6 78.1 us: gathered(): return lax.all_gather(cells, axis, axis=0, tiled=True)]
    all_gather x0 -> x3, waiting for transfers between devices: none -> 63.5 us  [gathered(): return lax.all_gather(cells, axis, axis=0, tiled=True)]
    all_to_all x0 -> x3, blocking collectives: none -> 32.1 us  [summed(): lax.all_to_all(parts, axes, split_axis=0, concat_axis=0)]
    unnamed x134 -> x13, local copies, waits for them, and re-layouts: 16.2 us -> 4.3 us
    all_to_all x0 -> x3, starting transfers between devices: none -> 10.2 us  [scattered_sum(): parts = lax.all_to_all(parts, axis, split_axis=0, concat_axis=0)]
    dynamic_slice x23 -> x0, local copies, waits for them, and re-layouts: 9 us -> none  [the longest x20 8.91 us: in_order(): placed = lax.dynamic_slice_in_dim(stacked, start, count, axis=0)]
  transfers between devices with their start and end apart: 114 -> 12, of which waited for: 43 -> 3; matrix products, arithmetic and copies ran while one was open for 5% -> 1% of each run, Pallas kernels for 0% -> 0%
where the time goes in v2:
time: 296 us; the launch traced here: 295 us
  blocking collectives  150 us (51%)
  waiting for transfers between devices  63.6 us (21%)
  matrix products  37.6 us (13%)
  starting transfers between devices  18.4 us (6%)
  between operations  14.1 us (5%)
  other arithmetic  6.18 us (2%)
  local copies, waits for them, and re-layouts  4.38 us (1%)
    all_gather x6, blocking collectives, gathered(): return lax.all_gather(cells, axis, axis=0, tiled=True)  78.1 us
    all_gather x3, waiting for transfers between devices, gathered(): return lax.all_gather(cells, axis, axis=0, tiled=True)  63.5 us
    all_gather x3, blocking collectives, body(): load = lax.all_gather(load, 'dof', axis=0)  40.2 us
    all_to_all x3, blocking collectives, summed(): lax.all_to_all(parts, axes, split_axis=0, concat_axis=0)  32.1 us
    dot_general x3, matrix products, precondition(): jnp.dot(precond, gathered(field.astype(jnp.bfloat16), 'dof'), preferred_e...  19.7 us
    dot_general x3, matrix products, body(): hub = jnp.dot(hub_inverse, load, preferred_element_type=jnp.float32)  11 us
    all_to_all x3, starting transfers between devices, scattered_sum(): parts = lax.all_to_all(parts, axis, split_axis=0, concat_axis=0)  10.2 us
    ppermute x3, starting transfers between devices, beside_faces(): lax.ppermute(own_faces[:quarter], 'sector', [((s + 1) % sectors, s) for s...  7.89 us
  transfers between devices with their start and end apart: 12, of which 3 were waited for; matrix products, arithmetic and copies ran while one was open for 1% of the time, Pallas kernels for 0%

profile of v2, /device:TPU:0, one launch (start us, length us, event | category | flops | bytes accessed | tf_op | source)
XLA Modules:
  0.0 294.7 jit_solution(12430687471568843845)
XLA Ops:
  9.9 30.9 %all-gather.7.cloned.1.call-done = bf16[4096,128]{0,1:T(8,128)(2,1)} async-done(((bf16[1024,128]{0,1:T(8,128)(2,1)}), bf16[4096,128]{0,1:T(8,128)(2,1)}) %all-gather.7.cloned.1.call-update) | async-done | bytes 1048592 | tf_op jit(solution)/shard_map/all_gather | solution.py:10
  40.8 6.5 %fusion.47 = (bf16[1024,128]{0,1:T(8,128)(2,1)S(1)}, f32[1024,128]{0,1:T(8,128)S(1)}) fusion(bf16[1024,4096]{1,0:T(8,128)(2,1)} %param.10, bf16[4096,128]{0,1:T(8,128)(2,1)} %all-gather.7.cloned.1.call-done), kind=kOutput, calls=%fused_computation.57 | convolution fusion | flops 1073872896 | bytes 10223616 | tf_op jit(solution)/shard_map/dot_general | solution.py:47
  50.8 3.4 %all-to-all-start = ((bf16[8,16,768]{2,1,0:T(8,128)(2,1)}), bf16[8,16,768]{2,1,0:T(8,128)(2,1)S(1)}, u32[]{:S(2)}, u32[]{:S(2)}) async-start(bf16[8,16,768]{2,1,0:T(8,128)(2,1)} %bitcast.5), calls=%async_computation | async-start | bytes 393216 | tf_op jit(solution)/shard_map/all_to_all | solution.py:16
  54.3 16.3 %all_gather.46 = bf16[2048,128]{0,1:T(8,128)(2,1)S(1)} all-gather(bf16[512,128]{0,1:T(8,128)(2,1)S(1)} %pad_maximum_fusion), channel_id=1, replica_groups=mesh['sector'=8,'dof'=4] {'dof'}, dimensions={0}, use_global_device_ids=true | all-gather | bytes 655360 | tf_op jit(solution)/shard_map/all_gather | solution.py:10
  70.6 13.4 %all-gather = bf16[64,768]{1,0:T(8,128)(2,1)S(1)} all-gather(bf16[16,768]{1,0:T(8,128)(2,1)S(1)} %reduce_sum.117), channel_id=2, replica_groups=mesh['sector'=8,'dof'=4] {'dof'}, dimensions={0}, use_global_device_ids=true | all-gather | bytes 122880 | tf_op jit(solution)/shard_map/all_gather | solution.py:60
  84.0 3.7 %fusion.50 = f32[16,768]{1,0:T(8,128)S(1)} fusion(bf16[3072,16]{0,1:T(8,128)(2,1)S(1)} %bitcast.135, bf16[768,3072]{1,0:T(8,128)(2,1)} %param.11), kind=kOutput, calls=%fused_computation.60 | convolution fusion | flops 75497472 | bytes 4866048 | tf_op jit(solution)/shard_map/dot_general | solution.py:62
  87.6 9.6 %all_gather.49 = f32[128,768]{1,0:T(8,128)S(1)} all-gather(f32[16,768]{1,0:T(8,128)S(1)} %fusion.50), channel_id=1, replica_groups=mesh['sector'=8,'dof'=4] {'sector'}, dimensions={0}, use_global_device_ids=true | all-gather | bytes 442368 | tf_op jit(solution)/shard_map/all_gather | solution.py:10
  99.7 10.7 %all_to_all.30 = f32[32,2,128]{2,1,0:T(2,128)S(1)} all-to-all(f32[32,2,128]{2,1,0:T(2,128)S(1)} %broadcast_in_dim.10), channel_id=1, replica_groups=mesh['sector'=8,'dof'=4] {'sector','dof'}, dimensions={0} | all-to-all | bytes 65536 | tf_op jit(solution)/shard_map/all_to_all | solution.py:23
  110.4 16.3 %all-gather.9.cloned.1.call-done = bf16[4096,128]{0,1:T(8,128)(2,1)} async-done(((bf16[1024,128]{0,1:T(8,128)(2,1)}), bf16[4096,128]{0,1:T(8,128)(2,1)}) %all-gather.9.cloned.1.call-update) | async-done | bytes 1048592 | tf_op jit(solution)/shard_map/all_gather | solution.py:10
  126.8 6.6 %fusion.48 = (bf16[1024,128]{0,1:T(8,128)(2,1)S(1)}, f32[1024,128]{0,1:T(8,128)S(1)}) fusion(f32[1024,128]{0,1:T(8,128)S(1)} %get-tuple-element.30, bf16[4096,128]{0,1:T(8,128)(2,1)} %all-gather.9.cloned.1.call-done, bf16[1024,4096]{1,0:T(8,128)(2,1)} %param.10, f32[128]{0:T(128)S(1)} %fusion.41), kind=kOutput, calls=%fused_computation.58 | convolution fusion | flops 1074135040 | bytes 10748416 | tf_op jit(solution)/shard_map/dot_general | solution.py:47
  136.8 3.4 %all-to-all-start.2 = ((bf16[8,16,768]{2,1,0:T(8,128)(2,1)}), bf16[8,16,768]{2,1,0:T(8,128)(2,1)S(1)}, u32[]{:S(2)}, u32[]{:S(2)}) async-start(bf16[8,16,768]{2,1,0:T(8,128)(2,1)} %bitcast.15), calls=%async_computation.2 | async-start | bytes 393216 | tf_op jit(solution)/shard_map/all_to_all | solution.py:16
  140.3 16.4 %all_gather.51 = bf16[2048,128]{0,1:T(8,128)(2,1)} all-gather(bf16[512,128]{0,1:T(8,128)(2,1)S(1)} %pad_maximum_fusion.1), channel_id=1, replica_groups=mesh['sector'=8,'dof'=4] {'dof'}, dimensions={0}, use_global_device_ids=true | all-gather | bytes 655360 | tf_op jit(solution)/shard_map/all_gather | solution.py:10
  156.8 13.4 %all-gather.1 = bf16[64,768]{1,0:T(8,128)(2,1)S(1)} all-gather(bf16[16,768]{1,0:T(8,128)(2,1)S(1)} %reduce_sum.121), channel_id=3, replica_groups=mesh['sector'=8,'dof'=4] {'dof'}, dimensions={0}, use_global_device_ids=true | all-gather | bytes 122880 | tf_op jit(solution)/shard_map/all_gather | solution.py:60
  170.2 3.7 %fusion.51 = f32[16,768]{1,0:T(8,128)S(1)} fusion(bf16[3072,16]{0,1:T(8,128)(2,1)S(1)} %bitcast.136, bf16[768,3072]{1,0:T(8,128)(2,1)} %param.11), kind=kOutput, calls=%fused_computation.61 | convolution fusion | flops 75497472 | bytes 4866048 | tf_op jit(solution)/shard_map/dot_general | solution.py:62
  173.8 9.9 %all_gather.54 = f32[128,768]{1,0:T(8,128)S(1)} all-gather(f32[16,768]{1,0:T(8,128)S(1)} %fusion.51), channel_id=1, replica_groups=mesh['sector'=8,'dof'=4] {'sector'}, dimensions={0}, use_global_device_ids=true | all-gather | bytes 442368 | tf_op jit(solution)/shard_map/all_gather | solution.py:10
  186.1 10.7 %all_to_all.31 = f32[32,2,128]{2,1,0:T(2,128)S(1)} all-to-all(f32[32,2,128]{2,1,0:T(2,128)S(1)} %broadcast_in_dim.11), channel_id=1, replica_groups=mesh['sector'=8,'dof'=4] {'sector','dof'}, dimensions={0} | all-to-all | bytes 65536 | tf_op jit(solution)/shard_map/all_to_all | solution.py:23
  196.9 16.3 %all-gather.11.cloned.1.call-done = bf16[4096,128]{0,1:T(8,128)(2,1)} async-done(((bf16[1024,128]{0,1:T(8,128)(2,1)}), bf16[4096,128]{0,1:T(8,128)(2,1)}) %all-gather.11.cloned.1.call-update) | async-done | bytes 1048592 | tf_op jit(solution)/shard_map/all_gather | solution.py:10
  213.3 6.6 %fusion.49 = (bf16[1024,128]{0,1:T(8,128)(2,1)S(1)}, f32[1024,128]{0,1:T(8,128)S(1)}) fusion(f32[1024,128]{0,1:T(8,128)S(1)} %get-tuple-element.33, bf16[4096,128]{0,1:T(8,128)(2,1)} %all-gather.11.cloned.1.call-done, bf16[1024,4096]{1,0:T(8,128)(2,1)} %param.10, f32[128]{0:T(128)S(1)} %fusion.42), kind=kOutput, calls=%fused_computation.59 | convolution fusion | flops 1074135040 | bytes 10748416 | tf_op jit(solution)/shard_map/dot_general | solution.py:47
  223.3 3.4 %all-to-all-start.4 = ((bf16[8,16,768]{2,1,0:T(8,128)(2,1)}), bf16[8,16,768]{2,1,0:T(8,128)(2,1)S(1)}, u32[]{:S(2)}, u32[]{:S(2)}) async-start(bf16[8,16,768]{2,1,0:T(8,128)(2,1)} %bitcast.25), calls=%async_computation.4 | async-start | bytes 393216 | tf_op jit(solution)/shard_map/all_to_all | solution.py:16
  226.7 16.3 %all_gather.56 = bf16[2048,128]{0,1:T(8,128)(2,1)S(1)} all-gather(bf16[512,128]{0,1:T(8,128)(2,1)S(1)} %pad_maximum_fusion.2), channel_id=1, replica_groups=mesh['sector'=8,'dof'=4] {'dof'}, dimensions={0}, use_global_device_ids=true | all-gather | bytes 655360 | tf_op jit(solution)/shard_map/all_gather | solution.py:10
  243.1 13.4 %all-gather.2 = bf16[64,768]{1,0:T(8,128)(2,1)S(1)} all-gather(bf16[16,768]{1,0:T(8,128)(2,1)S(1)} %reduce_sum.125), channel_id=4, replica_groups=mesh['sector'=8,'dof'=4] {'dof'}, dimensions={0}, use_global_device_ids=true | all-gather | bytes 122880 | tf_op jit(solution)/shard_map/all_gather | solution.py:60
  256.4 3.7 %fusion.52 = f32[16,768]{1,0:T(8,128)S(1)} fusion(bf16[3072,16]{0,1:T(8,128)(2,1)S(1)} %bitcast.137, bf16[768,3072]{1,0:T(8,128)(2,1)} %param.11), kind=kOutput, calls=%fused_computation.62 | convolution fusion | flops 75497472 | bytes 4866048 | tf_op jit(solution)/shard_map/dot_general | solution.py:62
  260.1 9.7 %all_gather.59 = f32[128,768]{1,0:T(8,128)S(1)} all-gather(f32[16,768]{1,0:T(8,128)S(1)} %fusion.52), channel_id=1, replica_groups=mesh['sector'=8,'dof'=4] {'sector'}, dimensions={0}, use_global_device_ids=true | all-gather | bytes 442368 | tf_op jit(solution)/shard_map/all_gather | solution.py:10
  272.2 10.7 %all_to_all.32 = f32[32,2,128]{2,1,0:T(2,128)S(1)} all-to-all(f32[32,2,128]{2,1,0:T(2,128)S(1)} %broadcast_in_dim.12), channel_id=1, replica_groups=mesh['sector'=8,'dof'=4] {'sector','dof'}, dimensions={0} | all-to-all | bytes 65536 | tf_op jit(solution)/shard_map/all_to_all | solution.py:23
  (70 shorter events, 25.8 us)
Async XLA Ops:
  7.2 33.6 %all-gather.7.cloned.1.call-start = ((), (), s32[]{:S(2)}) async-start(), calls=%async_computation.6 | async-start | bytes 1310720 | tf_op jit(solution)/shard_map/all_gather | solution.py:10
  47.3 50.0 %copy-start.4 = (f32[1,1024]{1,0:T(1,128)S(1)}, f32[1,1024]{1,0:T(1,128)}, u32[]{:S(2)}) copy-start(f32[1,1024]{1,0:T(1,128)} %param.7) | copy-start | bytes 12292
  47.4 6.9 %collective-permute-start = (bf16[256,128]{0,1:T(8,128)(2,1)S(1)}, bf16[256,128]{0,1:T(8,128)(2,1)S(1)}, u32[]{:S(2)}, u32[]{:S(2)}) collective-permute-start(bf16[256,128]{0,1:T(8,128)(2,1)S(1)} %get-tuple-element.25), channel_id=1, source_target_pairs={{0,4},{4,8},{8,12},{12,16},{16,20},{20,24},{24,28},{28,0},{1,5},{5... | collective-permute-start | bytes 196616 | tf_op jit(solution)/shard_map/ppermute | solution.py:28
  47.4 6.8 %collective-permute-start.1 = (bf16[256,128]{0,1:T(8,128)(2,1)S(1)}, bf16[256,128]{0,1:T(8,128)(2,1)S(1)}, u32[]{:S(2)}, u32[]{:S(2)}) collective-permute-start(bf16[256,128]{0,1:T(8,128)(2,1)S(1)} %get-tuple-element.26), channel_id=1, source_target_pairs={{4,0},{8,4},{12,8},{16,12},{20,16},{24,20},{28,24},{0,28},{5,1},{9... | collective-permute-start | bytes 196616 | tf_op jit(solution)/shard_map/ppermute | solution.py:31
  50.8 19.8 %all-to-all-start = ((bf16[8,16,768]{2,1,0:T(8,128)(2,1)}), bf16[8,16,768]{2,1,0:T(8,128)(2,1)S(1)}, u32[]{:S(2)}, u32[]{:S(2)}) async-start(bf16[8,16,768]{2,1,0:T(8,128)(2,1)} %bitcast.5), calls=%async_computation | async-start | bytes 393216 | tf_op jit(solution)/shard_map/all_to_all | solution.py:16
  54.2 72.6 %all-gather.9.cloned.1.call-start = ((), (), s32[]{:S(2)}) async-start(), calls=%async_computation.7 | async-start | bytes 1310720 | tf_op jit(solution)/shard_map/all_gather | solution.py:10
  70.6 26.8 %copy-start = (bf16[1,1024,2048]{2,1,0:T(8,128)(2,1)S(1)}, bf16[1,1024,2048]{2,1,0:T(8,128)(2,1)}, u32[]{:S(2)}) copy-start(bf16[1,1024,2048]{2,1,0:T(8,128)(2,1)} %param.8) | copy-start | bytes 12582916
  133.4 6.9 %collective-permute-start.2 = (bf16[256,128]{0,1:T(8,128)(2,1)S(1)}, bf16[256,128]{0,1:T(8,128)(2,1)S(1)}, u32[]{:S(2)}, u32[]{:S(2)}) collective-permute-start(bf16[256,128]{0,1:T(8,128)(2,1)S(1)} %get-tuple-element.23), channel_id=1, source_target_pairs={{0,4},{4,8},{8,12},{12,16},{16,20},{20,24},{24,28},{28,0},{1,5},{5... | collective-permute-start | bytes 196616 | tf_op jit(solution)/shard_map/ppermute | solution.py:28
  133.5 6.8 %collective-permute-start.3 = (bf16[256,128]{0,1:T(8,128)(2,1)S(1)}, bf16[256,128]{0,1:T(8,128)(2,1)S(1)}, u32[]{:S(2)}, u32[]{:S(2)}) collective-permute-start(bf16[256,128]{0,1:T(8,128)(2,1)S(1)} %get-tuple-element.24), channel_id=1, source_target_pairs={{4,0},{8,4},{12,8},{16,12},{20,16},{24,20},{28,24},{0,28},{5,1},{9... | collective-permute-start | bytes 196616 | tf_op jit(solution)/shard_map/ppermute | solution.py:31
  136.8 19.9 %all-to-all-start.2 = ((bf16[8,16,768]{2,1,0:T(8,128)(2,1)}), bf16[8,16,768]{2,1,0:T(8,128)(2,1)S(1)}, u32[]{:S(2)}, u32[]{:S(2)}) async-start(bf16[8,16,768]{2,1,0:T(8,128)(2,1)} %bitcast.15), calls=%async_computation.2 | async-start | bytes 393216 | tf_op jit(solution)/shard_map/all_to_all | solution.py:16
  140.2 73.1 %all-gather.11.cloned.1.call-start = ((), (), s32[]{:S(2)}) async-start(), calls=%async_computation.8 | async-start | bytes 1310720 | tf_op jit(solution)/shard_map/all_gather | solution.py:10
  156.7 27.1 %copy-start.1 = (bf16[1,1024,2048]{2,1,0:T(8,128)(2,1)S(1)}, bf16[1,1024,2048]{2,1,0:T(8,128)(2,1)}, u32[]{:S(2)}) copy-start(bf16[1,1024,2048]{2,1,0:T(8,128)(2,1)} %param.8) | copy-start | bytes 12582916
  156.8 27.1 %copy-start.3 = (bf16[2048,128]{0,1:T(8,128)(2,1)S(1)}, bf16[2048,128]{0,1:T(8,128)(2,1)}, u32[]{:S(2)}) copy-start(bf16[2048,128]{0,1:T(8,128)(2,1)} %all_gather.51) | copy-start | bytes 1572868
  219.9 6.8 %collective-permute-start.4 = (bf16[256,128]{0,1:T(8,128)(2,1)S(1)}, bf16[256,128]{0,1:T(8,128)(2,1)S(1)}, u32[]{:S(2)}, u32[]{:S(2)}) collective-permute-start(bf16[256,128]{0,1:T(8,128)(2,1)S(1)} %get-tuple-element.21), channel_id=1, source_target_pairs={{0,4},{4,8},{8,12},{12,16},{16,20},{20,24},{24,28},{28,0},{1,5},{5... | collective-permute-start | bytes 196616 | tf_op jit(solution)/shard_map/ppermute | solution.py:28
  220.0 6.7 %collective-permute-start.5 = (bf16[256,128]{0,1:T(8,128)(2,1)S(1)}, bf16[256,128]{0,1:T(8,128)(2,1)S(1)}, u32[]{:S(2)}, u32[]{:S(2)}) collective-permute-start(bf16[256,128]{0,1:T(8,128)(2,1)S(1)} %get-tuple-element.22), channel_id=1, source_target_pairs={{4,0},{8,4},{12,8},{16,12},{20,16},{24,20},{28,24},{0,28},{5,1},{9... | collective-permute-start | bytes 196616 | tf_op jit(solution)/shard_map/ppermute | solution.py:31
  223.3 19.7 %all-to-all-start.4 = ((bf16[8,16,768]{2,1,0:T(8,128)(2,1)}), bf16[8,16,768]{2,1,0:T(8,128)(2,1)S(1)}, u32[]{:S(2)}, u32[]{:S(2)}) async-start(bf16[8,16,768]{2,1,0:T(8,128)(2,1)} %bitcast.25), calls=%async_computation.4 | async-start | bytes 393216 | tf_op jit(solution)/shard_map/all_to_all | solution.py:16
  243.1 26.8 %copy-start.2 = (bf16[1,1024,2048]{2,1,0:T(8,128)(2,1)S(1)}, bf16[1,1024,2048]{2,1,0:T(8,128)(2,1)}, u32[]{:S(2)}) copy-start(bf16[1,1024,2048]{2,1,0:T(8,128)(2,1)} %param.8) | copy-start | bytes 12582916
Sparse Core Ops, SparseCore 0:
  10.1 30.6 all-gather.6
  99.7 26.9 all-gather.8
  186.2 26.9 all-gather.10

commit v3 on v2

--- a/solution.py
+++ b/solution.py
@@ -17,10 +17,10 @@
     return jnp.sum(parts.astype(jnp.float32), axis=0)
 
 
-def summed(cells, axes):
+def every_piece(cells, axes):
     count = lax.axis_size(axes)
     parts = jnp.broadcast_to(cells[None], (count,) + cells.shape)
-    return jnp.sum(lax.all_to_all(parts, axes, split_axis=0, concat_axis=0), axis=0)
+    return lax.all_to_all(parts, axes, split_axis=0, concat_axis=0)
 
 
 def beside_faces(own_faces, quarter):
@@ -31,7 +31,8 @@
     after = lax.ppermute(
         own_faces[:quarter], "sector", [((s + 1) % sectors, s) for s in range(sectors)]
     )
-    return gathered(jnp.concatenate([before, after]), "dof")
+    sides = every_piece(jnp.concatenate([before, after]), "dof")
+    return sides.reshape(-1, own_faces.shape[1])
 
 
 def body(rhs, diagonal, coupling, springs, precond, hub_inverse):
@@ -57,17 +58,17 @@
         attached = precon[: 3 * quarter]
         load = (spring_rows * attached).astype(jnp.bfloat16).T
         load = scattered_sum(load, "sector").astype(jnp.bfloat16)
-        load = lax.all_gather(load, "dof", axis=0)
+        load = every_piece(load, "dof")
         load = load.transpose(0, 2, 1).reshape(-1, load.shape[1])
         hub = jnp.dot(hub_inverse, load, preferred_element_type=jnp.float32)
-        hub = gathered(hub.T, "sector").T
+        hub = every_piece(hub.T, "sector").reshape(loads, -1).T
         couple = jnp.dot(couple_rows, needed, preferred_element_type=jnp.float32)
         hub_term = jnp.concatenate(
             [spring_rows * (attached - hub), jnp.zeros((quarter, loads), jnp.float32)], axis=0
         )
         image = diag_rows * precon + couple + hub_term
         sums = jnp.stack([jnp.sum(image * residual, axis=0), jnp.sum(image * image, axis=0)])
-        sums = summed(sums, ("sector", "dof"))
+        sums = jnp.sum(every_piece(sums, ("sector", "dof")), axis=0)
         alpha = sums[0] / (sums[1] + 1e-06)
         solution = solution + alpha * precon
         residual = residual - alpha * image

time: 296 us -> 315 us (1.064)
  blocking collectives: 150 us -> 84.2 us
  waiting for transfers between devices: 63.6 us -> 125 us
  starting transfers between devices: 18.4 us -> 29.1 us
  local copies, waits for them, and re-layouts: 4.38 us -> 12.4 us
  matrix products: 37.6 us -> 44.4 us
    all_gather x9 -> x0, blocking collectives: 118 us -> none  [the longest x6 78.1 us: gathered(): return lax.all_gather(cells, axis, axis=0, tiled=True)]
    all_to_all x3 -> x9, blocking collectives: 32.1 us -> 84.2 us  [the longest x6 55.1 us: every_piece(): return lax.all_to_all(parts, axes, split_axis=0, concat_axis=0)]
    all_to_all x3 -> x6, waiting for transfers between devices: 0.01 us -> 42.4 us  [every_piece(): return lax.all_to_all(parts, axes, split_axis=0, concat_axis=0)]
    ppermute x3, waiting for transfers between devices: 0.01 us -> 19.4 us  [beside_faces(): lax.ppermute(own_faces[quarter:], 'sector', [(s, (s + 1) % sectors) for s...]
    all_to_all x3 -> x6, starting transfers between devices: 10.2 us -> 20.8 us  [every_piece(): return lax.all_to_all(parts, axes, split_axis=0, concat_axis=0)]
    dot_general x3, matrix products: 6.93 us -> 13.7 us  [body(): couple = jnp.dot(couple_rows, needed, preferred_element_type=jnp.float32)]
    broadcast_in_dim x3 -> x12, local copies, waits for them, and re-layouts: 0.03 us -> 5.07 us  [every_piece(): parts = jnp.broadcast_to(cells[None], (count,) + cells.shape)]
    unnamed x13 -> x11, local copies, waits for them, and re-layouts: 4.3 us -> 6.9 us
  transfers between devices with their start and end apart: 12 -> 15, of which waited for: 3 -> 9; matrix products, arithmetic and copies ran while one was open for 1% -> 1% of each run, Pallas kernels for 0% -> 0%
where the time goes in v3:
time: 315 us; the launch traced here: 314 us
  waiting for transfers between devices  125 us (40%)
  blocking collectives  84.2 us (27%)
  matrix products  44.4 us (14%)
  starting transfers between devices  29.1 us (9%)
  between operations  14.1 us (4%)
  local copies, waits for them, and re-layouts  12.4 us (4%)
  other arithmetic  4.89 us (2%)
    all_gather x3, waiting for transfers between devices, gathered(): return lax.all_gather(cells, axis, axis=0, tiled=True)  62.8 us
    all_to_all x6, blocking collectives, every_piece(): return lax.all_to_all(parts, axes, split_axis=0, concat_axis=0)  55.1 us
    all_to_all x6, waiting for transfers between devices, every_piece(): return lax.all_to_all(parts, axes, split_axis=0, concat_axis=0)  42.4 us
    all_to_all x3, blocking collectives, scattered_sum(): parts = lax.all_to_all(parts, axis, split_axis=0, concat_axis=0)  29.1 us
    all_to_all x6, starting transfers between devices, every_piece(): return lax.all_to_all(parts, axes, split_axis=0, concat_axis=0)  20.8 us
    dot_general x3, matrix products, precondition(): jnp.dot(precond, gathered(field.astype(jnp.bfloat16), 'dof'), preferred_e...  19.7 us
    ppermute x3, waiting for transfers between devices, beside_faces(): lax.ppermute(own_faces[quarter:], 'sector', [(s, (s + 1) % sectors) for s...  19.4 us
    dot_general x3, matrix products, body(): couple = jnp.dot(couple_rows, needed, preferred_element_type=jnp.float32)  13.7 us
  transfers between devices with their start and end apart: 15, of which 9 were waited for; matrix products, arithmetic and copies ran while one was open for 1% of the time, Pallas kernels for 0%

profile of v3, /device:TPU:0, one launch (start us, length us, event | category | flops | bytes accessed | tf_op | source)
XLA Modules:
  0.0 313.6 jit_solution(1891920308516671388)
XLA Ops:
  9.9 30.9 %all-gather.4.cloned.1.call-done = bf16[4096,128]{0,1:T(8,128)(2,1)} async-done(((bf16[1024,128]{0,1:T(8,128)(2,1)}), bf16[4096,128]{0,1:T(8,128)(2,1)}) %all-gather.4.cloned.1.call-update) | async-done | bytes 1048592 | tf_op jit(solution)/shard_map/all_gather | solution.py:10
  40.8 6.5 %fusion.47 = (bf16[1024,128]{0,1:T(8,128)(2,1)S(1)}, f32[1024,128]{0,1:T(8,128)S(1)}) fusion(bf16[1024,4096]{1,0:T(8,128)(2,1)} %param.10, bf16[4096,128]{0,1:T(8,128)(2,1)} %all-gather.4.cloned.1.call-done), kind=kOutput, calls=%fused_computation.57 | convolution fusion | flops 1073872896 | bytes 10223616 | tf_op jit(solution)/shard_map/dot_general | solution.py:48
  47.4 9.7 %all_to_all.75 = bf16[8,16,768]{2,1,0:T(8,128)(2,1)S(1)} all-to-all(bf16[8,16,768]{2,1,0:T(8,128)(2,1)S(1)} %bitcast.138), channel_id=1, replica_groups=mesh['sector'=8,'dof'=4] {'sector'}, dimensions={0} | all-to-all | bytes 393216 | tf_op jit(solution)/shard_map/all_to_all | solution.py:16
  57.1 8.8 %all_to_all.76 = bf16[4,16,768]{2,1,0:T(8,128)(2,1)S(1)} all-to-all(bf16[4,16,768]{2,1,0:T(8,128)(2,1)S(1)} %broadcast_in_dim.29), channel_id=1, replica_groups=mesh['sector'=8,'dof'=4] {'dof'}, dimensions={0} | all-to-all | bytes 196608 | tf_op jit(solution)/shard_map/all_to_all | solution.py:23
  76.6 6.5 %collective-permute-done = bf16[256,128]{0,1:T(8,128)(2,1)S(1)} collective-permute-done((bf16[256,128]{0,1:T(8,128)(2,1)S(1)}, bf16[256,128]{0,1:T(8,128)(2,1)S(1)}, u32[]{:S(2)}, u32[]{:S(2)}) %collective-permute-start) | collective-permute-done | bytes 65568 | tf_op jit(solution)/shard_map/ppermute | solution.py:28
  87.6 14.5 %all-to-all-done = bf16[4,512,128]{2,1,0:T(8,128)(2,1)S(1)} async-done(((bf16[4,512,128]{2,1,0:T(8,128)(2,1)}), bf16[4,512,128]{2,1,0:T(8,128)(2,1)S(1)}, u32[]{:S(2)}, u32[]{:S(2)}) %all-to-all-start) | async-done | bytes 524320 | tf_op jit(solution)/shard_map/all_to_all | solution.py:23
  102.1 4.4 %fusion.37 = (f32[128]{0:T(128)S(1)}, f32[128]{0:T(128)S(1)}, bf16[1024,128]{0,1:T(8,128)(2,1)}, f32[1024,128]{0,1:T(8,128)S(1)}) fusion(f32[1,1024,128]{1,2,0:T(8,128)S(1)} %copy.38, f32[768,128]{0,1:T(8,128)S(1)} %fusion.40, bf16[2048,128]{1,0:T(8,128)(2,1)S(1)} %bitcast.136, bf16[1,1024,2048]{2,1,0:T(8,128)(2,1)} %param.8, ...), kind=kOutput, calls=%fused_computation.24 | convolution fusion | flops 537919232 | bytes 6951936 | tf_op jit(solution)/shard_map/dot_general | solution.py:65
  106.6 9.6 %all_to_all.77 = f32[32,2,128]{2,1,0:T(2,128)S(1)} all-to-all(f32[32,2,128]{2,1,0:T(2,128)S(1)} %broadcast_in_dim.31), channel_id=1, replica_groups=mesh['sector'=8,'dof'=4] {'sector','dof'}, dimensions={0} | all-to-all | bytes 65536 | tf_op jit(solution)/shard_map/all_to_all | solution.py:23
  116.2 16.3 %all-gather.6.cloned.1.call-done = bf16[4096,128]{0,1:T(8,128)(2,1)} async-done(((bf16[1024,128]{0,1:T(8,128)(2,1)}), bf16[4096,128]{0,1:T(8,128)(2,1)}) %all-gather.6.cloned.1.call-update) | async-done | bytes 1048592 | tf_op jit(solution)/shard_map/all_gather | solution.py:10
  132.5 6.6 %fusion.48 = (bf16[1024,128]{0,1:T(8,128)(2,1)S(1)}, f32[1024,128]{0,1:T(8,128)S(1)}) fusion(f32[1024,128]{0,1:T(8,128)S(1)} %get-tuple-element.30, bf16[4096,128]{0,1:T(8,128)(2,1)} %all-gather.6.cloned.1.call-done, bf16[1024,4096]{1,0:T(8,128)(2,1)} %param.10, f32[128]{0:T(128)S(1)} %fusion.41), kind=kOutput, calls=%fused_computation.58 | convolution fusion | flops 1074135040 | bytes 10748416 | tf_op jit(solution)/shard_map/dot_general | solution.py:48
  139.2 9.7 %all_to_all.78 = bf16[8,16,768]{2,1,0:T(8,128)(2,1)S(1)} all-to-all(bf16[8,16,768]{2,1,0:T(8,128)(2,1)S(1)} %bitcast.139), channel_id=1, replica_groups=mesh['sector'=8,'dof'=4] {'sector'}, dimensions={0} | all-to-all | bytes 393216 | tf_op jit(solution)/shard_map/all_to_all | solution.py:16
  148.9 8.8 %all_to_all.79 = bf16[4,16,768]{2,1,0:T(8,128)(2,1)S(1)} all-to-all(bf16[4,16,768]{2,1,0:T(8,128)(2,1)S(1)} %broadcast_in_dim.33), channel_id=1, replica_groups=mesh['sector'=8,'dof'=4] {'dof'}, dimensions={0} | all-to-all | bytes 196608 | tf_op jit(solution)/shard_map/all_to_all | solution.py:23
  168.4 6.5 %collective-permute-done.2 = bf16[256,128]{0,1:T(8,128)(2,1)S(1)} collective-permute-done((bf16[256,128]{0,1:T(8,128)(2,1)S(1)}, bf16[256,128]{0,1:T(8,128)(2,1)S(1)}, u32[]{:S(2)}, u32[]{:S(2)}) %collective-permute-start.2) | collective-permute-done | bytes 65568 | tf_op jit(solution)/shard_map/ppermute | solution.py:28
  179.4 14.5 %all-to-all-done.5 = bf16[4,512,128]{2,1,0:T(8,128)(2,1)S(1)} async-done(((bf16[4,512,128]{2,1,0:T(8,128)(2,1)}), bf16[4,512,128]{2,1,0:T(8,128)(2,1)S(1)}, u32[]{:S(2)}, u32[]{:S(2)}) %all-to-all-start.5) | async-done | bytes 524320 | tf_op jit(solution)/shard_map/all_to_all | solution.py:23
  194.7 5.2 %multiply_reduce_fusion.3 = (f32[128]{0:T(128)S(1)}, f32[128]{0:T(128)}, f32[1024,128]{0,1:T(8,128)S(1)}, bf16[1024,128]{0,1:T(8,128)(2,1)}, f32[1024,128]{0,1:T(8,128)S(1)}) fusion(f32[1024,128]{0,1:T(8,128)S(1)} %get-tuple-element.31, f32[128]{0:T(128)S(1)} %fusion.41, f32[1,1024,128]{1,2,0:T(8,128)S(1)} %copy.38, f32[768,128]{0,1:T(8,128)S(1)} %fusion.39, ...), kind=kOutput, calls=%fused_computation.31 | convolution fusion | flops 538181376 | bytes 8001024 | tf_op jit(solution)/shard_map/dot_general | solution.py:65
  200.6 9.6 %all_to_all.80 = f32[32,2,128]{2,1,0:T(2,128)S(1)} all-to-all(f32[32,2,128]{2,1,0:T(2,128)S(1)} %broadcast_in_dim.35), channel_id=1, replica_groups=mesh['sector'=8,'dof'=4] {'sector','dof'}, dimensions={0} | all-to-all | bytes 65536 | tf_op jit(solution)/shard_map/all_to_all | solution.py:23
  210.2 15.6 %all-gather.8.cloned.1.call-done = bf16[4096,128]{0,1:T(8,128)(2,1)} async-done(((bf16[1024,128]{0,1:T(8,128)(2,1)}), bf16[4096,128]{0,1:T(8,128)(2,1)}) %all-gather.8.cloned.1.call-update) | async-done | bytes 1048592 | tf_op jit(solution)/shard_map/all_gather | solution.py:10
  225.9 6.6 %fusion.49 = (bf16[1024,128]{0,1:T(8,128)(2,1)S(1)}, f32[1024,128]{0,1:T(8,128)S(1)}) fusion(f32[1024,128]{0,1:T(8,128)S(1)} %get-tuple-element.33, bf16[4096,128]{0,1:T(8,128)(2,1)} %all-gather.8.cloned.1.call-done, bf16[1024,4096]{1,0:T(8,128)(2,1)} %param.10, f32[128]{0:T(128)S(1)} %fusion.42), kind=kOutput, calls=%fused_computation.59 | convolution fusion | flops 1074135040 | bytes 10748416 | tf_op jit(solution)/shard_map/dot_general | solution.py:48
  232.5 9.7 %all_to_all.81 = bf16[8,16,768]{2,1,0:T(8,128)(2,1)S(1)} all-to-all(bf16[8,16,768]{2,1,0:T(8,128)(2,1)S(1)} %bitcast.140), channel_id=1, replica_groups=mesh['sector'=8,'dof'=4] {'sector'}, dimensions={0} | all-to-all | bytes 393216 | tf_op jit(solution)/shard_map/all_to_all | solution.py:16
  242.3 8.8 %all_to_all.82 = bf16[4,16,768]{2,1,0:T(8,128)(2,1)S(1)} all-to-all(bf16[4,16,768]{2,1,0:T(8,128)(2,1)S(1)} %broadcast_in_dim.37), channel_id=1, replica_groups=mesh['sector'=8,'dof'=4] {'dof'}, dimensions={0} | all-to-all | bytes 196608 | tf_op jit(solution)/shard_map/all_to_all | solution.py:23
  261.7 6.5 %collective-permute-done.4 = bf16[256,128]{0,1:T(8,128)(2,1)S(1)} collective-permute-done((bf16[256,128]{0,1:T(8,128)(2,1)S(1)}, bf16[256,128]{0,1:T(8,128)(2,1)S(1)}, u32[]{:S(2)}, u32[]{:S(2)}) %collective-permute-start.4) | collective-permute-done | bytes 65568 | tf_op jit(solution)/shard_map/ppermute | solution.py:28
  273.8 13.5 %all-to-all-done.10 = bf16[4,512,128]{2,1,0:T(8,128)(2,1)S(1)} async-done(((bf16[4,512,128]{2,1,0:T(8,128)(2,1)}), bf16[4,512,128]{2,1,0:T(8,128)(2,1)S(1)}, u32[]{:S(2)}, u32[]{:S(2)}) %all-to-all-start.10) | async-done | bytes 524320 | tf_op jit(solution)/shard_map/all_to_all | solution.py:23
  288.1 4.0 %multiply_reduce_fusion.1 = (f32[128]{0:T(128)S(1)}, f32[128]{0:T(128)S(1)}, f32[1024,128]{0,1:T(8,128)S(1)}) fusion(f32[1024,128]{0,1:T(8,128)S(1)} %get-tuple-element.18, f32[1024,128]{0,1:T(8,128)S(1)} %get-tuple-element.34, f32[128]{0:T(128)S(1)} %fusion.42, f32[768,128]{0,1:T(8,128)S(1)} %fusion.38, bf16[2048,128]{1,0:T(8,128)(2,1)} %bitcast.137, ...), kind=kOutput, calls=%fused_computation.28 | convolution fusion | flops 538050304 | bytes 7214592 | tf_op jit(solution)/shard_map/dot_general | solution.py:65
  292.1 9.6 %all_to_all.83 = f32[32,2,128]{2,1,0:T(2,128)S(1)} all-to-all(f32[32,2,128]{2,1,0:T(2,128)S(1)} %broadcast_in_dim.39), channel_id=1, replica_groups=mesh['sector'=8,'dof'=4] {'sector','dof'}, dimensions={0} | all-to-all | bytes 65536 | tf_op jit(solution)/shard_map/all_to_all | solution.py:23
  (83 shorter events, 57.4 us)
Async XLA Ops:
  7.2 33.6 %all-gather.4.cloned.1.call-start = ((), (), s32[]{:S(2)}) async-start(), calls=%async_computation.15 | async-start | bytes 1310720 | tf_op jit(solution)/shard_map/all_gather | solution.py:10
  65.9 36.2 %copy-start.3 = (f32[1,1024]{1,0:T(1,128)S(1)}, f32[1,1024]{1,0:T(1,128)}, u32[]{:S(2)}) copy-start(f32[1,1024]{1,0:T(1,128)} %param.7) | copy-start | bytes 12292
  70.4 12.8 %all-to-all-start.3 = ((f32[8,16,768]{2,1,0:T(8,128)}), f32[8,16,768]{2,1,0:T(8,128)S(1)}, u32[]{:S(2)}, u32[]{:S(2)}) async-start(f32[8,16,768]{2,1,0:T(8,128)} %broadcast_in_dim.30), calls=%async_computation.3 | async-start | bytes 786432 | tf_op jit(solution)/shard_map/all_to_all | solution.py:23
  73.9 9.2 %collective-permute-start = (bf16[256,128]{0,1:T(8,128)(2,1)S(1)}, bf16[256,128]{0,1:T(8,128)(2,1)S(1)}, u32[]{:S(2)}, u32[]{:S(2)}) collective-permute-start(bf16[256,128]{0,1:T(8,128)(2,1)S(1)} %get-tuple-element.25), channel_id=1, source_target_pairs={{0,4},{4,8},{8,12},{12,16},{16,20},{20,24},{24,28},{28,0},{1,5},{5... | collective-permute-start | bytes 196616 | tf_op jit(solution)/shard_map/ppermute | solution.py:28
  74.3 8.7 %collective-permute-start.1 = (bf16[256,128]{0,1:T(8,128)(2,1)S(1)}, bf16[256,128]{0,1:T(8,128)(2,1)S(1)}, u32[]{:S(2)}, u32[]{:S(2)}) collective-permute-start(bf16[256,128]{0,1:T(8,128)(2,1)S(1)} %get-tuple-element.26), channel_id=1, source_target_pairs={{4,0},{8,4},{12,8},{16,12},{20,16},{24,20},{28,24},{0,28},{5,1},{9... | collective-permute-start | bytes 196616 | tf_op jit(solution)/shard_map/ppermute | solution.py:31
  84.1 18.0 %all-to-all-start = ((bf16[4,512,128]{2,1,0:T(8,128)(2,1)}), bf16[4,512,128]{2,1,0:T(8,128)(2,1)S(1)}, u32[]{:S(2)}, u32[]{:S(2)}) async-start(bf16[4,512,128]{2,1,0:T(8,128)(2,1)} %broadcast_in_dim.28), calls=%async_computation | async-start | bytes 1048576 | tf_op jit(solution)/shard_map/all_to_all | solution.py:23
  87.5 45.0 %all-gather.6.cloned.1.call-start = ((), (), s32[]{:S(2)}) async-start(), calls=%async_computation.16 | async-start | bytes 1310720 | tf_op jit(solution)/shard_map/all_gather | solution.py:10
  162.2 12.8 %all-to-all-start.8 = ((f32[8,16,768]{2,1,0:T(8,128)}), f32[8,16,768]{2,1,0:T(8,128)S(1)}, u32[]{:S(2)}, u32[]{:S(2)}) async-start(f32[8,16,768]{2,1,0:T(8,128)} %broadcast_in_dim.34), calls=%async_computation.8 | async-start | bytes 786432 | tf_op jit(solution)/shard_map/all_to_all | solution.py:23
  165.6 9.2 %collective-permute-start.2 = (bf16[256,128]{0,1:T(8,128)(2,1)S(1)}, bf16[256,128]{0,1:T(8,128)(2,1)S(1)}, u32[]{:S(2)}, u32[]{:S(2)}) collective-permute-start(bf16[256,128]{0,1:T(8,128)(2,1)S(1)} %get-tuple-element.23), channel_id=1, source_target_pairs={{0,4},{4,8},{8,12},{12,16},{16,20},{20,24},{24,28},{28,0},{1,5},{5... | collective-permute-start | bytes 196616 | tf_op jit(solution)/shard_map/ppermute | solution.py:28
  166.1 8.7 %collective-permute-start.3 = (bf16[256,128]{0,1:T(8,128)(2,1)S(1)}, bf16[256,128]{0,1:T(8,128)(2,1)S(1)}, u32[]{:S(2)}, u32[]{:S(2)}) collective-permute-start(bf16[256,128]{0,1:T(8,128)(2,1)S(1)} %get-tuple-element.24), channel_id=1, source_target_pairs={{4,0},{8,4},{12,8},{16,12},{20,16},{24,20},{28,24},{0,28},{5,1},{9... | collective-permute-start | bytes 196616 | tf_op jit(solution)/shard_map/ppermute | solution.py:31
  175.8 18.0 %all-to-all-start.5 = ((bf16[4,512,128]{2,1,0:T(8,128)(2,1)}), bf16[4,512,128]{2,1,0:T(8,128)(2,1)S(1)}, u32[]{:S(2)}, u32[]{:S(2)}) async-start(bf16[4,512,128]{2,1,0:T(8,128)(2,1)} %broadcast_in_dim.32), calls=%async_computation.5 | async-start | bytes 1048576 | tf_op jit(solution)/shard_map/all_to_all | solution.py:23
  179.3 46.5 %all-gather.8.cloned.1.call-start = ((), (), s32[]{:S(2)}) async-start(), calls=%async_computation.17 | async-start | bytes 1310720 | tf_op jit(solution)/shard_map/all_gather | solution.py:10
  193.9 0.8 copy-start
  255.5 12.8 %all-to-all-start.13 = ((f32[8,16,768]{2,1,0:T(8,128)}), f32[8,16,768]{2,1,0:T(8,128)S(1)}, u32[]{:S(2)}, u32[]{:S(2)}) async-start(f32[8,16,768]{2,1,0:T(8,128)} %broadcast_in_dim.38), calls=%async_computation.13 | async-start | bytes 786432 | tf_op jit(solution)/shard_map/all_to_all | solution.py:23
  259.0 9.2 %collective-permute-start.4 = (bf16[256,128]{0,1:T(8,128)(2,1)S(1)}, bf16[256,128]{0,1:T(8,128)(2,1)S(1)}, u32[]{:S(2)}, u32[]{:S(2)}) collective-permute-start(bf16[256,128]{0,1:T(8,128)(2,1)S(1)} %get-tuple-element.21), channel_id=1, source_target_pairs={{0,4},{4,8},{8,12},{12,16},{16,20},{20,24},{24,28},{28,0},{1,5},{5... | collective-permute-start | bytes 196616 | tf_op jit(solution)/shard_map/ppermute | solution.py:28
  259.5 8.7 %collective-permute-start.5 = (bf16[256,128]{0,1:T(8,128)(2,1)S(1)}, bf16[256,128]{0,1:T(8,128)(2,1)S(1)}, u32[]{:S(2)}, u32[]{:S(2)}) collective-permute-start(bf16[256,128]{0,1:T(8,128)(2,1)S(1)} %get-tuple-element.22), channel_id=1, source_target_pairs={{4,0},{8,4},{12,8},{16,12},{20,16},{24,20},{28,24},{0,28},{5,1},{9... | collective-permute-start | bytes 196616 | tf_op jit(solution)/shard_map/ppermute | solution.py:31
  268.3 0.9 copy-start.2
  269.3 18.0 %all-to-all-start.10 = ((bf16[4,512,128]{2,1,0:T(8,128)(2,1)}), bf16[4,512,128]{2,1,0:T(8,128)(2,1)S(1)}, u32[]{:S(2)}, u32[]{:S(2)}) async-start(bf16[4,512,128]{2,1,0:T(8,128)(2,1)} %broadcast_in_dim.36), calls=%async_computation.10 | async-start | bytes 1048576 | tf_op jit(solution)/shard_map/all_to_all | solution.py:23
  287.3 0.8 copy-start.1
Sparse Core Ops, SparseCore 0:
  10.1 30.6 all-gather.3
  106.7 25.7 all-gather.5
  200.0 25.7 all-gather.7

commit v4 on v3

v4 whole, which is shorter than its diff:
```python
import functools

import jax
import jax.numpy as jnp
from jax import lax
from jax.experimental import pallas as pl
from jax.experimental.pallas import tpu as pltpu
from jax.sharding import PartitionSpec as P

ITERS = 3
VMEM_LIMIT = 32 * 1024 * 1024


def every_piece(cells, axes):
    count = lax.axis_size(axes)
    parts = jnp.broadcast_to(cells[None], (count,) + cells.shape)
    return lax.all_to_all(parts, axes, split_axis=0, concat_axis=0)


def product_kernel(first, matrix_ref, field_ref, *refs):
    if first:
        (out_ref,) = refs
    else:
        before_ref, sums_ref, out_ref = refs
    step = pl.program_id(0)
    product = jnp.dot(matrix_ref[...], field_ref[...], preferred_element_type=jnp.float32)

    @pl.when(step == 0)
    def _():
        out_ref[...] = product

    @pl.when(step > 0)
    def _():
        out_ref[...] += product

    if not first:

        @pl.when(step == pl.num_programs(0) - 1)
        def _():
            sums = jnp.sum(sums_ref[...], axis=0)
            alpha = sums[0:1] / (sums[1:2] + 1e-06)
            out_ref[...] = before_ref[...] - alpha * out_ref[...]


def preconditioned(matrix, field, before=None, sums=None):
    rows, depth = matrix.shape
    loads = field.shape[1]
    block = min(512, depth)
    first = before is None
    extra = [] if first else [before, sums]
    extra_specs = [pl.BlockSpec(a.shape, functools.partial(lambda n, k: (0,) * n, a.ndim)) for a in extra]
    return pl.pallas_call(
        functools.partial(product_kernel, first),
        grid=(depth // block,),
        in_specs=[
            pl.BlockSpec((rows, block), lambda k: (0, k)),
            pl.BlockSpec((block, loads), lambda k: (k, 0)),
        ]
        + extra_specs,
        out_specs=pl.BlockSpec((rows, loads), lambda k: (0, 0)),
        out_shape=jax.ShapeDtypeStruct((rows, loads), jnp.float32),
        compiler_params=pltpu.CompilerParams(vmem_limit_bytes=VMEM_LIMIT),
        cost_estimate=pl.CostEstimate(
            flops=2 * rows * depth * loads,
            bytes_accessed=2 * depth * (rows + loads) + 8 * rows * loads,
            transcendentals=0,
        ),
    )(matrix, field, *extra)


def send_kernel(precon_ref, springs_ref, before_ref, after_ref, faces_ref, load_ref):
    quarter = before_ref.shape[0]
    faces_ref[:quarter] = before_ref[...]
    faces_ref[quarter : 2 * quarter] = after_ref[...]
    faces_ref[2 * quarter :] = jnp.zeros_like(faces_ref[2 * quarter :])
    attached = precon_ref[: 3 * quarter]
    load_ref[...] = (attached.T * springs_ref[...]).astype(load_ref.dtype)


def faces_and_load(precon, springs, before, after):
    rows, loads = precon.shape
    return pl.pallas_call(
        send_kernel,
        out_shape=(
            jax.ShapeDtypeStruct((rows, loads), jnp.bfloat16),
            jax.ShapeDtypeStruct((loads, springs.shape[1]), jnp.bfloat16),
        ),
        compiler_params=pltpu.CompilerParams(vmem_limit_bytes=VMEM_LIMIT),
    )(precon, springs, before, after)


def hub_kernel(matrix_ref, load_ref, out_ref, total_ref):
    step = pl.program_id(0)
    product = lax.dot_general(
        load_ref[0], matrix_ref[...], (((1,), (1,)), ((), ())), preferred_element_type=jnp.float32
    )

    @pl.when(step == 0)
    def _():
        total_ref[...] = product

    @pl.when(step > 0)
    def _():
        total_ref[...] += product

    @pl.when(step == pl.num_programs(0) - 1)
    def _():
        out_ref[...] = jnp.broadcast_to(total_ref[...][None], out_ref.shape)


def hub_copies(matrix, load, count):
    parts, cases, depth = load.shape
    rows = matrix.shape[0]
    if depth % 128 or cases % 16:
        load = load.transpose(1, 0, 2).reshape(cases, -1)
        hub = lax.dot_general(
            load, matrix, (((1,), (1,)), ((), ())), preferred_element_type=jnp.float32
        )
        return jnp.broadcast_to(hub[None], (count,) + hub.shape)
    return pl.pallas_call(
        hub_kernel,
        grid=(parts,),
        in_specs=[
            pl.BlockSpec((rows, depth), lambda k: (0, k)),
            pl.BlockSpec((1, cases, depth), lambda k: (k, 0, 0)),
        ],
        out_specs=pl.BlockSpec((count, cases, rows), lambda k: (0, 0, 0)),
        out_shape=jax.ShapeDtypeStruct((count, cases, rows), jnp.float32),
        scratch_shapes=[pltpu.VMEM((cases, rows), jnp.float32)],
        compiler_params=pltpu.CompilerParams(vmem_limit_bytes=VMEM_LIMIT),
        cost_estimate=pl.CostEstimate(
            flops=2 * rows * depth * parts * cases,
            bytes_accessed=2 * rows * depth * parts,
            transcendentals=0,
        ),
    )(matrix, load)


def body(rhs, diagonal, coupling, springs, precond, hub_inverse):
    residual = rhs[0]
    diag_rows = diagonal[0][:, None]
    couple_rows = coupling[0]
    spring_rows = springs[0][:, None]
    rows_dev, loads = residual.shape
    quarter = rows_dev // 4
    sectors = lax.axis_size("sector")
    onward = [(s, (s + 1) % sectors) for s in range(sectors)]
    backward = [((s + 1) % sectors, s) for s in range(sectors)]
    solution = jnp.zeros_like(residual)

    def gathered(field):
        return lax.all_gather(field.astype(jnp.bfloat16), "dof", axis=0)

    precon = preconditioned(precond, gathered(residual).reshape(-1, loads))
    for step in range(ITERS):
        own_faces = precon[: 2 * quarter].astype(jnp.bfloat16)
        before = lax.ppermute(own_faces[quarter:], "sector", onward)
        after = lax.ppermute(own_faces[:quarter], "sector", backward)
        faces, load = faces_and_load(precon, springs, before, after)
        needed = gathered(faces)[:, : 2 * quarter].reshape(-1, loads)

        load = load.reshape(sectors, loads // sectors, -1)
        load = lax.all_to_all(load, "sector", split_axis=0, concat_axis=0)
        load = jnp.sum(load.astype(jnp.float32), axis=0).astype(jnp.bfloat16)
        hub = hub_copies(hub_inverse, every_piece(load, "dof"), sectors)
        hub = lax.all_to_all(hub, "sector", split_axis=0, concat_axis=0)
        hub = hub.reshape(loads, -1).T

        couple = jnp.dot(couple_rows, needed, preferred_element_type=jnp.float32)
        attached = precon[: 3 * quarter]
        hub_term = jnp.concatenate(
            [spring_rows * (attached - hub), jnp.zeros((quarter, loads), jnp.float32)], axis=0
        )
        image = diag_rows * precon + couple + hub_term
        sums = jnp.stack([jnp.sum(image * residual, axis=0), jnp.sum(image * image, axis=0)])
        sums = every_piece(sums, ("sector", "dof"))
        total = jnp.sum(sums, axis=0)
        alpha = total[0] / (total[1] + 1e-06)
        solution = solution + alpha * precon
        residual = residual - alpha * image
        if step < ITERS - 1:
            precon = preconditioned(precond, gathered(image).reshape(-1, loads), precon, sums)
    return (solution[None], residual[None])


def solution(mesh):
    placed = (
        P("sector", "dof", None),
        P("sector", "dof"),
        P("sector", "dof", None),
        P("sector", "dof"),
        P("dof", None),
        P("dof", None),
    )
    return jax.shard_map(
        body,
        mesh=mesh,
        in_specs=placed,
        out_specs=(P("sector", "dof", None), P("sector", "dof", None)),
        check_vma=False,
    )
```

time: 315 us -> 293 us (0.930)
  matrix products: 44.4 us -> 12.5 us
  Pallas kernels: 0 us -> 25.2 us
  waiting for transfers between devices: 125 us -> 102 us
  starting transfers between devices: 29.1 us -> 15.8 us
  local copies, waits for them, and re-layouts: 12.4 us -> 25.5 us
  blocking collectives: 84.2 us -> 90.6 us
    dot_general x6 -> x0, matrix products: 30.7 us -> none  [the longest x3 19.7 us: precondition(): jnp.dot(precond, gathered(field.astype(jnp.bfloat16), 'dof'), preferred_e...]
    pallas_call x0 -> x9, Pallas kernels: none -> 25.2 us  [the longest x3 14 us: preconditioned(): pl.pallas_call(functools.partial(product_kernel, first), grid=(depth // b...]
    all_to_all x6 -> x3, waiting for transfers between devices: 42.4 us -> 24.6 us  [body(): hub = lax.all_to_all(hub, 'sector', split_axis=0, concat_axis=0)]
    unnamed x11 -> x24, local copies, waits for them, and re-layouts: 6.9 us -> 20.9 us
    all_to_all x6 -> x3, starting transfers between devices: 20.8 us -> 10.4 us  [body(): hub = lax.all_to_all(hub, 'sector', split_axis=0, concat_axis=0)]
    all_to_all x6, blocking collectives: 55.1 us -> 64.7 us  [every_piece(): return lax.all_to_all(parts, axes, split_axis=0, concat_axis=0)]
    ppermute x6, waiting for transfers between devices: 19.4 us -> 13.8 us  [the longest x3 8.05 us: body(): before = lax.ppermute(own_faces[quarter:], 'sector', onward)]
    broadcast_in_dim x12 -> x6, local copies, waits for them, and re-layouts: 5.07 us -> 0.06 us  [every_piece(): parts = jnp.broadcast_to(cells[None], (count,) + cells.shape)]
  transfers between devices with their start and end apart: 15 -> 15, of which waited for: 9 -> 12; matrix products, arithmetic and copies ran while one was open for 1% -> 1% of each run, Pallas kernels for 0% -> 3%
where the time goes in v4:
time: 293 us; the launch traced here: 292 us
  waiting for transfers between devices  102 us (35%)
  blocking collectives  90.6 us (31%)
  local copies, waits for them, and re-layouts  25.5 us (9%)
  Pallas kernels  25.2 us (9%)
  starting transfers between devices  15.8 us (5%)
  between operations  14.4 us (5%)
  matrix products  12.5 us (4%)
  other arithmetic  5.55 us (2%)
    all_to_all x6, blocking collectives, every_piece(): return lax.all_to_all(parts, axes, split_axis=0, concat_axis=0)  64.7 us
    all_gather x6, waiting for transfers between devices, gathered(): return lax.all_gather(field.astype(jnp.bfloat16), 'dof', axis=0)  63.8 us
    all_to_all x3, blocking collectives, body(): load = lax.all_to_all(load, 'sector', split_axis=0, concat_axis=0)  25.9 us
    all_to_all x3, waiting for transfers between devices, body(): hub = lax.all_to_all(hub, 'sector', split_axis=0, concat_axis=0)  24.6 us
    unnamed x24, local copies, waits for them, and re-layouts  20.9 us
    pallas_call x3, Pallas kernels, preconditioned(): pl.pallas_call(functools.partial(product_kernel, first), grid=(depth // b...  14 us
    dot_general x3, matrix products, body(): couple = jnp.dot(couple_rows, needed, preferred_element_type=jnp.float32)  12.5 us
    all_to_all x3, starting transfers between devices, body(): hub = lax.all_to_all(hub, 'sector', split_axis=0, concat_axis=0)  10.4 us
  transfers between devices with their start and end apart: 15, of which 12 were waited for; matrix products, arithmetic and copies ran while one was open for 1% of the time, Pallas kernels for 3%

profile of v4, /device:TPU:0, one launch (start us, length us, event | category | flops | bytes accessed | tf_op | source)
XLA Modules:
  0.0 291.7 jit_solution(14271616370691459781)
XLA Ops:
  9.1 31.7 %all-gather.12.cloned.1.call-done = bf16[4,1024,128]{2,1,0:T(8,128)(2,1)} async-done(((bf16[1,1024,128]{2,1,0:T(8,128)(2,1)}), bf16[4,1024,128]{2,1,0:T(8,128)(2,1)}) %all-gather.12.cloned.1.call-update) | async-done | bytes 1048592 | tf_op jit(solution)/shard_map/all_gather | solution.py:152
  45.4 4.5 %shard_map.77.precon_ref.refs_0_ = f32[1024,128]{1,0:T(8,128)S(1)} custom-call(bf16[1024,4096]{1,0:T(8,128)(2,1)S(1)} %copy-done, bf16[4096,128]{1,0:T(8,128)(2,1)S(1)} %bitcast.94), custom_call_target="tpu_custom_call" | custom-call | flops 1073741824 | bytes 10485760 | tf_op jit(solution)/shard_map/pallas_call | solution.py:52
  57.2 8.6 %all_to_all.60 = bf16[8,16,768]{2,1,0:T(8,128)(2,1)S(1)} all-to-all(bf16[8,16,768]{2,1,0:T(8,128)(2,1)S(1)} %bitcast.95), channel_id=1, replica_groups=mesh['sector'=8,'dof'=4] {'sector'}, dimensions={0} | all-to-all | bytes 393216 | tf_op jit(solution)/shard_map/all_to_all | solution.py:163
  65.9 11.6 %all_to_all.61.load_ref = bf16[4,16,768]{2,1,0:T(8,128)(2,1)S(1)} all-to-all(bf16[4,16,768]{2,1,0:T(8,128)(2,1)S(1)} %broadcast_in_dim.16), channel_id=1, replica_groups=mesh['sector'=8,'dof'=4] {'dof'}, dimensions={0} | all-to-all | bytes 196608 | tf_op jit(solution)/shard_map/all_to_all | solution.py:17
  82.8 3.5 %all-to-all-start.2 = ((f32[8,16,768]{2,1,0:T(8,128)}), f32[8,16,768]{2,1,0:T(8,128)S(1)}, u32[]{:S(2)}, u32[]{:S(2)}) async-start(f32[8,16,768]{2,1,0:T(8,128)} %shard_map.79), calls=%async_computation.2 | async-start | bytes 786432 | tf_op jit(solution)/shard_map/all_to_all | solution.py:166
  86.3 8.2 %all-to-all-done.2 = f32[8,16,768]{2,1,0:T(8,128)S(1)} async-done(((f32[8,16,768]{2,1,0:T(8,128)}), f32[8,16,768]{2,1,0:T(8,128)S(1)}, u32[]{:S(2)}, u32[]{:S(2)}) %all-to-all-start.2) | async-done | bytes 393248 | tf_op jit(solution)/shard_map/all_to_all | solution.py:166
  96.0 4.2 %fusion.33 = (f32[128]{0:T(128)S(1)}, f32[128]{0:T(128)S(1)}, bf16[1024,128]{1,0:T(8,128)(2,1)}, f32[1024,128]{1,0:T(8,128)S(1)}) fusion(f32[1,1024,128]{2,1,0:T(8,128)S(1)} %copy-done.10, f32[768,128]{1,0:T(8,128)S(1)} %fusion.36, bf16[2048,128]{1,0:T(8,128)(2,1)S(1)} %bitcast.99, bf16[1,1024,2048]{2,1,0:T(8,128)(2,1)} %param.8, ...), kind=kOutput, calls=%fused_computation.17 | convolution fusion | flops 537919232 | bytes 6951936 | tf_op jit(solution)/shard_map/dot_general | solution.py:169
  100.3 9.9 %all_to_all.62.refs_1_ = f32[32,2,128]{2,1,0:T(2,128)S(1)} all-to-all(f32[32,2,128]{2,1,0:T(2,128)S(1)} %broadcast_in_dim.17), channel_id=1, replica_groups=mesh['sector'=8,'dof'=4] {'sector','dof'}, dimensions={0} | all-to-all | bytes 65536 | tf_op jit(solution)/shard_map/all_to_all | solution.py:17
  110.3 16.3 %all-gather.16.cloned.1.call-done.field_ref = bf16[4096,128]{1,0:T(8,128)(2,1)} async-done(((bf16[1024,128]{1,0:T(8,128)(2,1)}), bf16[4096,128]{1,0:T(8,128)(2,1)}) %all-gather.16.cloned.1.call-update) | async-done | bytes 1048592 | tf_op jit(solution)/shard_map/all_gather | solution.py:152
  131.2 4.7 %shard_map.80.precon_ref.refs_0_ = f32[1024,128]{1,0:T(8,128)S(1)} custom-call(bf16[1024,4096]{1,0:T(8,128)(2,1)S(1)} %copy-done.1, bf16[4096,128]{1,0:T(8,128)(2,1)S(1)} %copy-done.6, f32[1024,128]{1,0:T(8,128)S(1)} %shard_map.77.precon_ref.refs_0_, f32[32,2,128]{2,1,0:T(2,128)S(1)} %all_to_all.62.refs_1_), custom_call_target="tpu_custom_call" | custom-call | flops 1073741824 | bytes 10485760 | tf_op jit(solution)/shard_map/pallas_call | solution.py:52
  143.1 8.6 %all_to_all.63 = bf16[8,16,768]{2,1,0:T(8,128)(2,1)S(1)} all-to-all(bf16[8,16,768]{2,1,0:T(8,128)(2,1)S(1)} %bitcast.96), channel_id=1, replica_groups=mesh['sector'=8,'dof'=4] {'sector'}, dimensions={0} | all-to-all | bytes 393216 | tf_op jit(solution)/shard_map/all_to_all | solution.py:163
  151.8 11.6 %all_to_all.64.load_ref = bf16[4,16,768]{2,1,0:T(8,128)(2,1)S(1)} all-to-all(bf16[4,16,768]{2,1,0:T(8,128)(2,1)S(1)} %broadcast_in_dim.18), channel_id=1, replica_groups=mesh['sector'=8,'dof'=4] {'dof'}, dimensions={0} | all-to-all | bytes 196608 | tf_op jit(solution)/shard_map/all_to_all | solution.py:17
  168.7 3.5 %all-to-all-start.6 = ((f32[8,16,768]{2,1,0:T(8,128)}), f32[8,16,768]{2,1,0:T(8,128)S(1)}, u32[]{:S(2)}, u32[]{:S(2)}) async-start(f32[8,16,768]{2,1,0:T(8,128)} %shard_map.82), calls=%async_computation.6 | async-start | bytes 786432 | tf_op jit(solution)/shard_map/all_to_all | solution.py:166
  172.3 8.2 %all-to-all-done.6 = f32[8,16,768]{2,1,0:T(8,128)S(1)} async-done(((f32[8,16,768]{2,1,0:T(8,128)}), f32[8,16,768]{2,1,0:T(8,128)S(1)}, u32[]{:S(2)}, u32[]{:S(2)}) %all-to-all-start.6) | async-done | bytes 393248 | tf_op jit(solution)/shard_map/all_to_all | solution.py:166
  181.9 4.7 %multiply_reduce_fusion.3 = (f32[128]{0:T(128)}, f32[128]{0:T(128)}, f32[1024,128]{1,0:T(8,128)S(1)}, bf16[1024,128]{1,0:T(8,128)(2,1)}, f32[1024,128]{1,0:T(8,128)S(1)}) fusion(f32[1024,128]{1,0:T(8,128)S(1)} %get-tuple-element.31, f32[128]{0:T(128)S(1)} %fusion.37, f32[1,1024,128]{2,1,0:T(8,128)S(1)} %copy-done.10, f32[768,128]{1,0:T(8,128)S(1)} %fusion.35, ...), kind=kOutput, calls=%fused_computation.24 | convolution fusion | flops 538181376 | bytes 8001024 | tf_op jit(solution)/shard_map/dot_general | solution.py:169
  187.4 9.9 %all_to_all.65.refs_1_ = f32[32,2,128]{2,1,0:T(2,128)S(1)} all-to-all(f32[32,2,128]{2,1,0:T(2,128)S(1)} %broadcast_in_dim.19), channel_id=1, replica_groups=mesh['sector'=8,'dof'=4] {'sector','dof'}, dimensions={0} | all-to-all | bytes 65536 | tf_op jit(solution)/shard_map/all_to_all | solution.py:17
  197.4 15.7 %all-gather.20.cloned.1.call-done.field_ref = bf16[4096,128]{1,0:T(8,128)(2,1)} async-done(((bf16[1024,128]{1,0:T(8,128)(2,1)}), bf16[4096,128]{1,0:T(8,128)(2,1)}) %all-gather.20.cloned.1.call-update) | async-done | bytes 1048592 | tf_op jit(solution)/shard_map/all_gather | solution.py:152
  217.6 4.7 %shard_map.83.precon_ref = f32[1024,128]{1,0:T(8,128)S(1)} custom-call(bf16[1024,4096]{1,0:T(8,128)(2,1)S(1)} %copy-done.2, bf16[4096,128]{1,0:T(8,128)(2,1)S(1)} %copy-done.7, f32[1024,128]{1,0:T(8,128)S(1)} %shard_map.80.precon_ref.refs_0_, f32[32,2,128]{2,1,0:T(2,128)S(1)} %all_to_all.65.refs_1_), custom_call_target="tpu_custom_call" | custom-call | flops 1073741824 | bytes 10485760 | tf_op jit(solution)/shard_map/pallas_call | solution.py:52
  229.6 8.6 %all_to_all.66 = bf16[8,16,768]{2,1,0:T(8,128)(2,1)S(1)} all-to-all(bf16[8,16,768]{2,1,0:T(8,128)(2,1)S(1)} %bitcast.97), channel_id=1, replica_groups=mesh['sector'=8,'dof'=4] {'sector'}, dimensions={0} | all-to-all | bytes 393216 | tf_op jit(solution)/shard_map/all_to_all | solution.py:163
  238.3 11.6 %all_to_all.67.load_ref = bf16[4,16,768]{2,1,0:T(8,128)(2,1)S(1)} all-to-all(bf16[4,16,768]{2,1,0:T(8,128)(2,1)S(1)} %broadcast_in_dim.20), channel_id=1, replica_groups=mesh['sector'=8,'dof'=4] {'dof'}, dimensions={0} | all-to-all | bytes 196608 | tf_op jit(solution)/shard_map/all_to_all | solution.py:17
  255.2 3.5 %all-to-all-start.10 = ((f32[8,16,768]{2,1,0:T(8,128)}), f32[8,16,768]{2,1,0:T(8,128)S(1)}, u32[]{:S(2)}, u32[]{:S(2)}) async-start(f32[8,16,768]{2,1,0:T(8,128)} %shard_map.85), calls=%async_computation.10 | async-start | bytes 786432 | tf_op jit(solution)/shard_map/all_to_all | solution.py:166
  258.7 8.2 %all-to-all-done.10 = f32[8,16,768]{2,1,0:T(8,128)S(1)} async-done(((f32[8,16,768]{2,1,0:T(8,128)}), f32[8,16,768]{2,1,0:T(8,128)S(1)}, u32[]{:S(2)}, u32[]{:S(2)}) %all-to-all-start.10) | async-done | bytes 393248 | tf_op jit(solution)/shard_map/all_to_all | solution.py:166
  270.1 3.5 %multiply_reduce_fusion.1 = (f32[128]{0:T(128)S(1)}, f32[128]{0:T(128)S(1)}, f32[1024,128]{1,0:T(8,128)S(1)}) fusion(f32[1024,128]{1,0:T(8,128)S(1)} %get-tuple-element.20, f32[1024,128]{1,0:T(8,128)S(1)} %get-tuple-element.32, f32[128]{0:T(128)S(1)} %fusion.38, f32[768,128]{1,0:T(8,128)S(1)} %fusion.34, bf16[2048,128]{1,0:T(8,128)(2,1)S(1)} %bitcast.100, ...), kind=kOutput, calls=%fused_computation.21 | convolution fusion | flops 538050304 | bytes 7214592 | tf_op jit(solution)/shard_map/dot_general | solution.py:169
  273.7 9.9 %all_to_all.68 = f32[32,2,128]{2,1,0:T(2,128)S(1)} all-to-all(f32[32,2,128]{2,1,0:T(2,128)S(1)} %broadcast_in_dim.21), channel_id=1, replica_groups=mesh['sector'=8,'dof'=4] {'sector','dof'}, dimensions={0} | all-to-all | bytes 65536 | tf_op jit(solution)/shard_map/all_to_all | solution.py:17
  (93 shorter events, 61.6 us)
Async XLA Ops:
  7.2 33.6 %all-gather.12.cloned.1.call-start = ((), (), s32[]{:S(2)}) async-start(), calls=%async_computation.12 | async-start | bytes 1310720 | tf_op jit(solution)/shard_map/all_gather | solution.py:152
  9.0 85.9 %all-gather.14.cloned.1.call-start = ((), (), s32[]{:S(2)}) async-start(), calls=%async_computation.13 | async-start | bytes 1310720 | tf_op jit(solution)/shard_map/all_gather | solution.py:152
  40.8 3.4 %copy-start = (bf16[1024,4096]{1,0:T(8,128)(2,1)S(1)}, bf16[1024,4096]{1,0:T(8,128)(2,1)}, u32[]{:S(2)}) copy-start(bf16[1024,4096]{1,0:T(8,128)(2,1)} %matrix_ref.10) | copy-start | bytes 25165828
  45.4 10.9 %copy-start.9 = (f32[1,768]{1,0:T(1,128)S(1)}, f32[1,768]{1,0:T(1,128)}, u32[]{:S(2)}) copy-start(f32[1,768]{1,0:T(1,128)} %springs_ref.5) | copy-start | bytes 9220
  50.0 3.6 %collective-permute-start.1 = (bf16[256,128]{1,0:T(8,128)(2,1)S(1)}, bf16[256,128]{1,0:T(8,128)(2,1)S(1)}, u32[]{:S(2)}, u32[]{:S(2)}) collective-permute-start(bf16[256,128]{1,0:T(8,128)(2,1)S(1)} %get-tuple-element.27), channel_id=1, source_target_pairs={{4,0},{8,4},{12,8},{16,12},{20,16},{24,20},{28,24},{0,28},{5,1},{9... | collective-permute-start | bytes 196616 | tf_op jit(solution)/shard_map/ppermute | solution.py:158
  51.7 4.6 %collective-permute-start = (bf16[256,128]{1,0:T(8,128)(2,1)S(1)}, bf16[256,128]{1,0:T(8,128)(2,1)S(1)}, u32[]{:S(2)}, u32[]{:S(2)}) collective-permute-start(bf16[256,128]{1,0:T(8,128)(2,1)S(1)} %get-tuple-element.28), channel_id=1, source_target_pairs={{0,4},{4,8},{8,12},{12,16},{16,20},{20,24},{24,28},{28,0},{1,5},{5... | collective-permute-start | bytes 196616 | tf_op jit(solution)/shard_map/ppermute | solution.py:157
  77.5 2.4 copy-start.3
  79.8 16.2 %copy-start.10 = (f32[1,1024,128]{2,1,0:T(8,128)S(1)}, f32[1,1024,128]{2,1,0:T(8,128)}, u32[]{:S(2)}) copy-start(f32[1,1024,128]{2,1,0:T(8,128)} %param.6) | copy-start | bytes 1572868
  79.8 16.2 %copy-start.11 = (f32[1,1024]{1,0:T(1,128)S(1)}, f32[1,1024]{1,0:T(1,128)}, u32[]{:S(2)}) copy-start(f32[1,1024]{1,0:T(1,128)} %param.7) | copy-start | bytes 12292
  82.8 11.7 %all-to-all-start.2 = ((f32[8,16,768]{2,1,0:T(8,128)}), f32[8,16,768]{2,1,0:T(8,128)S(1)}, u32[]{:S(2)}, u32[]{:S(2)}) async-start(f32[8,16,768]{2,1,0:T(8,128)} %shard_map.79), calls=%async_computation.2 | async-start | bytes 786432 | tf_op jit(solution)/shard_map/all_to_all | solution.py:166
  86.2 40.4 %all-gather.16.cloned.1.call-start = ((), (), s32[]{:S(2)}) async-start(), calls=%async_computation.14 | async-start | bytes 1310720 | tf_op jit(solution)/shard_map/all_gather | solution.py:152
  100.3 80.6 %all-gather.18.cloned.1.call-start = ((), (), s32[]{:S(2)}) async-start(), calls=%async_computation.15 | async-start | bytes 1310720 | tf_op jit(solution)/shard_map/all_gather | solution.py:152
  126.6 3.4 %copy-start.1 = (bf16[1024,4096]{1,0:T(8,128)(2,1)S(1)}, bf16[1024,4096]{1,0:T(8,128)(2,1)}, u32[]{:S(2)}) copy-start(bf16[1024,4096]{1,0:T(8,128)(2,1)} %matrix_ref.10) | copy-start | bytes 25165828
  136.0 3.6 %collective-permute-start.3 = (bf16[256,128]{1,0:T(8,128)(2,1)S(1)}, bf16[256,128]{1,0:T(8,128)(2,1)S(1)}, u32[]{:S(2)}, u32[]{:S(2)}) collective-permute-start(bf16[256,128]{1,0:T(8,128)(2,1)S(1)} %get-tuple-element.25), channel_id=1, source_target_pairs={{4,0},{8,4},{12,8},{16,12},{20,16},{24,20},{28,24},{0,28},{5,1},{9... | collective-permute-start | bytes 196616 | tf_op jit(solution)/shard_map/ppermute | solution.py:158
  137.7 4.6 %collective-permute-start.2 = (bf16[256,128]{1,0:T(8,128)(2,1)S(1)}, bf16[256,128]{1,0:T(8,128)(2,1)S(1)}, u32[]{:S(2)}, u32[]{:S(2)}) collective-permute-start(bf16[256,128]{1,0:T(8,128)(2,1)S(1)} %get-tuple-element.26), channel_id=1, source_target_pairs={{0,4},{4,8},{8,12},{12,16},{16,20},{20,24},{24,28},{28,0},{1,5},{5... | collective-permute-start | bytes 196616 | tf_op jit(solution)/shard_map/ppermute | solution.py:157
  163.4 2.4 copy-start.4
  168.7 11.7 %all-to-all-start.6 = ((f32[8,16,768]{2,1,0:T(8,128)}), f32[8,16,768]{2,1,0:T(8,128)S(1)}, u32[]{:S(2)}, u32[]{:S(2)}) async-start(f32[8,16,768]{2,1,0:T(8,128)} %shard_map.82), calls=%async_computation.6 | async-start | bytes 786432 | tf_op jit(solution)/shard_map/all_to_all | solution.py:166
  172.2 40.8 %all-gather.20.cloned.1.call-start = ((), (), s32[]{:S(2)}) async-start(), calls=%async_computation.16 | async-start | bytes 1310720 | tf_op jit(solution)/shard_map/all_gather | solution.py:152
  186.7 82.3 %all-gather.22.cloned.1.call-start = ((), (), s32[]{:S(2)}) async-start(), calls=%async_computation.17 | async-start | bytes 1310720 | tf_op jit(solution)/shard_map/all_gather | solution.py:152
  213.0 3.4 %copy-start.2 = (bf16[1024,4096]{1,0:T(8,128)(2,1)S(1)}, bf16[1024,4096]{1,0:T(8,128)(2,1)}, u32[]{:S(2)}) copy-start(bf16[1024,4096]{1,0:T(8,128)(2,1)} %matrix_ref.10) | copy-start | bytes 25165828
  222.4 3.6 %collective-permute-start.5 = (bf16[256,128]{1,0:T(8,128)(2,1)S(1)}, bf16[256,128]{1,0:T(8,128)(2,1)S(1)}, u32[]{:S(2)}, u32[]{:S(2)}) collective-permute-start(bf16[256,128]{1,0:T(8,128)(2,1)S(1)} %get-tuple-element.23), channel_id=1, source_target_pairs={{4,0},{8,4},{12,8},{16,12},{20,16},{24,20},{28,24},{0,28},{5,1},{9... | collective-permute-start | bytes 196616 | tf_op jit(solution)/shard_map/ppermute | solution.py:158
  224.1 4.6 %collective-permute-start.4 = (bf16[256,128]{1,0:T(8,128)(2,1)S(1)}, bf16[256,128]{1,0:T(8,128)(2,1)S(1)}, u32[]{:S(2)}, u32[]{:S(2)}) collective-permute-start(bf16[256,128]{1,0:T(8,128)(2,1)S(1)} %get-tuple-element.24), channel_id=1, source_target_pairs={{0,4},{4,8},{8,12},{12,16},{16,20},{20,24},{24,28},{28,0},{1,5},{5... | collective-permute-start | bytes 196616 | tf_op jit(solution)/shard_map/ppermute | solution.py:157
  249.9 2.4 copy-start.5
  255.2 11.7 %all-to-all-start.10 = ((f32[8,16,768]{2,1,0:T(8,128)}), f32[8,16,768]{2,1,0:T(8,128)S(1)}, u32[]{:S(2)}, u32[]{:S(2)}) async-start(f32[8,16,768]{2,1,0:T(8,128)} %shard_map.85), calls=%async_computation.10 | async-start | bytes 786432 | tf_op jit(solution)/shard_map/all_to_all | solution.py:166
  (3 other events, 3.7 us)
Sparse Core Ops, SparseCore 0:
  10.1 30.6 all-gather.11
  57.3 28.5 all-gather.13
  100.4 26.1 all-gather.15
  143.3 28.5 all-gather.17
  186.8 26.1 all-gather.19
  229.7 28.5 all-gather.21

commit v5 on v2

v5 whole, which is shorter than its diff:
```python
import functools

import jax
import jax.numpy as jnp
from jax import lax
from jax.experimental import pallas as pl
from jax.experimental.pallas import tpu as pltpu
from jax.sharding import PartitionSpec as P

ITERS = 3
LANES = 128
VMEM_LIMIT = 30 * 1024 * 1024
WHOLE = pl.BlockSpec(memory_space=pltpu.VMEM)
UNREAD = pl.BlockSpec(memory_space=pl.ANY)
f32 = jnp.float32
bf16 = jnp.bfloat16


def call(kernel, outs, operands, unread=0, scratch=(), flops=0, traffic=0):
    count = len(operands)
    return pl.pallas_call(
        kernel,
        in_specs=[WHOLE] * (count - unread) + [UNREAD] * unread,
        out_specs=jax.tree.map(lambda _: WHOLE, outs),
        out_shape=outs,
        scratch_shapes=list(scratch),
        compiler_params=pltpu.CompilerParams(vmem_limit_bytes=VMEM_LIMIT),
        cost_estimate=pl.CostEstimate(flops=flops, bytes_accessed=traffic, transcendentals=0),
    )(*operands)


def shape(*dims, dtype=f32):
    return jax.ShapeDtypeStruct(dims, dtype)


def product_kernel(matrix_ref, tops_ref, ends_ref, *refs):
    before_ref, sums_ref, out_ref = refs if len(refs) == 3 else (None, None, refs[0])
    parts, top, _ = tops_ref.shape
    end = ends_ref.shape[1]
    out_ref[...] = jnp.zeros_like(out_ref)

    @pl.loop(0, parts)
    def _(part):
        start = pl.multiple_of(part * (top + end), LANES)
        out_ref[...] += jnp.dot(
            matrix_ref[:, pl.ds(start, top)], tops_ref[part], preferred_element_type=f32
        ) + jnp.dot(
            matrix_ref[:, pl.ds(pl.multiple_of(start + top, LANES), end)],
            ends_ref[part],
            preferred_element_type=f32,
        )

    if before_ref is not None:
        sums = jnp.sum(sums_ref[...], axis=0)
        alpha = sums[0:1] / (sums[1:2] + 1e-06)
        out_ref[...] = before_ref[...] - alpha * out_ref[...]


def preconditioned(matrix, tops, ends, *before_and_sums):
    rows, depth = matrix.shape
    loads = tops.shape[2]
    return call(
        product_kernel,
        shape(rows, loads),
        (matrix, tops, ends, *before_and_sums),
        flops=2 * rows * depth * loads,
        traffic=2 * depth * (rows + loads),
    )


def send_kernel(precon_ref, springs_ref, load_ref, right_ref, left_ref):
    sectors, height, _ = load_ref.shape
    cases = precon_ref.shape[1] // sectors
    quarter = right_ref.shape[0]
    left_ref[...] = precon_ref[:quarter].astype(bf16)
    right_ref[...] = precon_ref[quarter : 2 * quarter].astype(bf16)
    for at in range(height // cases):
        rows = precon_ref[at * LANES : (at + 1) * LANES]
        turned = (rows.T * springs_ref[:, at * LANES : (at + 1) * LANES]).astype(bf16)
        for s in range(sectors):
            load_ref[s, at * cases : (at + 1) * cases] = turned[s * cases : (s + 1) * cases]


def pack_kernel(before_ref, after_ref, parts_ref, out_ref):
    quarter = before_ref.shape[0]
    out_ref[:quarter] = before_ref[...]
    out_ref[quarter : 2 * quarter] = after_ref[...]
    out_ref[2 * quarter :] = jnp.sum(parts_ref[...].astype(f32), axis=0).astype(bf16)


def hub_kernel(cases, matrix_ref, pieces_ref, out_ref):
    parts = pieces_ref.shape[0]
    height = out_ref.shape[1]
    chunks = height // cases
    depth = chunks * LANES
    first = pieces_ref.shape[1] - height
    total = None
    for part in range(parts):
        load = jnp.concatenate(
            [pieces_ref[part, first + c * cases : first + (c + 1) * cases] for c in range(chunks)],
            axis=1,
        )
        product = lax.dot_general(
            load,
            matrix_ref[:, part * depth : (part + 1) * depth],
            (((1,), (1,)), ((), ())),
            preferred_element_type=f32,
        )
        total = product if total is None else total + product
    total = total.astype(bf16)
    for c in range(chunks):
        block = total[:, c * LANES : (c + 1) * LANES]
        for s in range(out_ref.shape[0]):
            out_ref[s, c * cases : (c + 1) * cases] = block


def base_kernel(matrix_ref, pieces_ref, precon_ref, stiffness_ref, base_ref, end_ref):
    parts = pieces_ref.shape[0]
    depth = matrix_ref.shape[1] // parts
    base_ref[...] = stiffness_ref[...] * precon_ref[...]

    @pl.loop(0, parts)
    def _(part):
        start = pl.multiple_of(part * depth, LANES)
        base_ref[...] += jnp.dot(
            matrix_ref[:, pl.ds(start, depth)], pieces_ref[part, :depth], preferred_element_type=f32
        )

    end = end_ref.shape[0]
    end_ref[...] = base_ref[base_ref.shape[0] - end :].astype(bf16)


def image_kernel(base_ref, hubs_ref, springs_ref, residual_ref, _, image_ref, top_ref, sums_ref):
    sectors, height, _ = hubs_ref.shape
    attached, loads = top_ref.shape
    chunks = attached // LANES
    cases = height // chunks
    for c in range(chunks):
        at = slice(c * LANES, (c + 1) * LANES)
        hub = jnp.concatenate([hubs_ref[s, c * cases : (c + 1) * cases] for s in range(sectors)], axis=0)
        pull = (hub.astype(f32) * springs_ref[:, at]).T
        image = base_ref[at] - pull
        image_ref[at] = image
        top_ref[at] = image.astype(bf16)
    image_ref[attached:] = base_ref[attached:]
    image = image_ref[...]
    upper = jnp.sum(image * residual_ref[...], axis=0, keepdims=True)
    lower = jnp.sum(image * image, axis=0, keepdims=True)
    sums = jnp.concatenate([upper, lower], axis=0)
    sums_ref[...] = jnp.broadcast_to(sums[None], sums_ref.shape)


def exchange(blocks, axes):
    return lax.all_to_all(blocks, axes, split_axis=0, concat_axis=0)


def gathered(field):
    return lax.all_gather(field, "dof", axis=0)


def around(sectors):
    onward = [(s, (s + 1) % sectors) for s in range(sectors)]
    return onward, [(b, a) for a, b in onward]


def alpha_of(sums):
    total = jnp.sum(sums, axis=0)
    return total[0] / (total[1] + 1e-06)


def round_kernel(field_ref, _, out_ref):
    out_ref[...] = field_ref[...].astype(bf16)


def tiled_body(rhs, diagonal, coupling, springs, precond, hub_inverse):
    residual = rhs[0]
    rows, loads = residual.shape
    attached = springs.shape[1]
    quarter = rows - attached
    sectors, parts = lax.axis_size("sector"), lax.axis_size("dof")
    cases = loads // sectors
    height = attached // LANES * cases
    onward, backward = around(sectors)

    stiffness = diagonal[0] + jnp.pad(springs[0], (0, quarter))
    stiffness = jnp.broadcast_to(stiffness[:, None], (rows, loads))
    solution = jnp.zeros_like(residual)

    ends = gathered(residual[attached:].astype(bf16))
    top = call(round_kernel, shape(attached, loads, dtype=bf16), (residual[:attached], ends), unread=1)
    precon = preconditioned(precond, gathered(top), ends)
    for step in range(ITERS):
        load, right, left = call(
            send_kernel,
            (
                shape(sectors, height, LANES, dtype=bf16),
                shape(quarter, loads, dtype=bf16),
                shape(quarter, loads, dtype=bf16),
            ),
            (precon, springs),
        )
        before = lax.ppermute(right, "sector", onward)
        after = lax.ppermute(left, "sector", backward)
        packed = call(
            pack_kernel,
            shape(2 * quarter + height, loads, dtype=bf16),
            (before, after, exchange(load, "sector")),
        )
        pieces = gathered(packed)
        hub = call(
            functools.partial(hub_kernel, cases),
            shape(sectors, height, LANES, dtype=bf16),
            (hub_inverse, pieces),
            flops=2 * hub_inverse.size * cases,
            traffic=2 * hub_inverse.size,
        )
        hubs = exchange(hub, "sector")
        base, end = call(
            base_kernel,
            (shape(rows, loads), shape(quarter, loads, dtype=bf16)),
            (coupling[0], pieces, precon, stiffness),
            flops=2 * coupling.size * loads,
            traffic=2 * coupling.size,
        )
        last = step == ITERS - 1
        ends = end if last else gathered(end)
        image, top, sums = call(
            image_kernel,
            (
                shape(rows, loads),
                shape(attached, loads, dtype=bf16),
                shape(sectors * parts, 2, loads),
            ),
            (base, hubs, springs, residual, ends),
            unread=1,
        )
        sums = exchange(sums, ("sector", "dof"))
        alpha = alpha_of(sums)
        solution = solution + alpha * precon
        residual = residual - alpha * image
        if not last:
            precon = preconditioned(precond, gathered(top), ends, precon, sums)
    return (solution[None], residual[None])


def plain_body(rhs, diagonal, coupling, springs, precond, hub_inverse):
    residual = rhs[0]
    spring_rows = springs[0][:, None]
    rows, loads = residual.shape
    quarter = rows // 4
    sectors = lax.axis_size("sector")
    onward, backward = around(sectors)
    solution = jnp.zeros_like(residual)

    def whole(field):
        return gathered(field.astype(bf16)).reshape(-1, loads)

    def copies(cells, axes):
        count = lax.axis_size(axes)
        return exchange(jnp.broadcast_to(cells[None], (count,) + cells.shape), axes)

    precon = jnp.dot(precond, whole(residual), preferred_element_type=f32)
    for step in range(ITERS):
        faces = precon[: 2 * quarter].astype(bf16)
        before = lax.ppermute(faces[quarter:], "sector", onward)
        after = lax.ppermute(faces[:quarter], "sector", backward)
        couple = jnp.dot(
            coupling[0], whole(jnp.concatenate([before, after])), preferred_element_type=f32
        )
        attached = precon[: 3 * quarter]
        load = (spring_rows * attached).T.reshape(sectors, loads // sectors, -1)
        load = jnp.sum(exchange(load, "sector"), axis=0).astype(bf16)
        load = copies(load, "dof").transpose(0, 2, 1).reshape(hub_inverse.shape[1], -1)
        hub = jnp.dot(hub_inverse, load, preferred_element_type=f32)
        hub = copies(hub.T, "sector").reshape(loads, -1).T
        pull = jnp.pad(spring_rows * (attached - hub), ((0, quarter), (0, 0)))
        image = diagonal[0][:, None] * precon + couple + pull
        sums = jnp.stack([jnp.sum(image * residual, axis=0), jnp.sum(image * image, axis=0)])
        alpha = alpha_of(copies(sums, ("sector", "dof")))
        solution = solution + alpha * precon
        residual = residual - alpha * image
        if step < ITERS - 1:
            change = jnp.dot(precond, whole(image), preferred_element_type=f32)
            precon = precon - alpha * change
    return (solution[None], residual[None])


def body(rhs, *rest):
    rows, loads = rhs.shape[1:]
    cases = loads // lax.axis_size("sector")
    tiled = loads == LANES and (rows // 4) % LANES == 0 and cases % 16 == 0
    return (tiled_body if tiled else plain_body)(rhs, *rest)


def solution(mesh):
    placed = (
        P("sector", "dof", None),
        P("sector", "dof"),
        P("sector", "dof", None),
        P("sector", "dof"),
        P("dof", None),
        P("dof", None),
    )
    return jax.shard_map(
        body,
        mesh=mesh,
        in_specs=placed,
        out_specs=(P("sector", "dof", None), P("sector", "dof", None)),
        check_vma=False,
    )
```

time: 296 us -> 279 us (0.943)
  waiting for transfers between devices: 63.6 us -> 13.3 us
  matrix products: 37.6 us -> 0 us
  local copies, waits for them, and re-layouts: 4.38 us -> 32.2 us
  Pallas kernels: 0 us -> 25.6 us
  starting transfers between devices: 18.4 us -> 38.4 us
  between operations: 14.1 us -> 0.84 us
  blocking collectives: 150 us -> 163 us
    all_gather x3 -> x0, waiting for transfers between devices: 63.5 us -> none  [gathered(): return lax.all_gather(cells, axis, axis=0, tiled=True)]
    dot_general x9 -> x0, matrix products: 37.6 us -> none  [the longest x3 19.7 us: precondition(): jnp.dot(precond, gathered(field.astype(jnp.bfloat16), 'dof'), preferred_e...]
    all_gather x9, blocking collectives: 118 us -> 151 us  [gathered(): return lax.all_gather(field, 'dof', axis=0)]
    unnamed x13 -> x40, local copies, waits for them, and re-layouts: 4.3 us -> 30.1 us
    pallas_call x0 -> x19, Pallas kernels: none -> 25.6 us  [call(): pl.pallas_call(kernel, in_specs=[WHOLE] * (count - unread) + [UNREAD] * u...]
    all_to_all x3 -> x8, starting transfers between devices: 10.2 us -> 30.3 us  [exchange(): return lax.all_to_all(blocks, axes, split_axis=0, concat_axis=0)]
    all_to_all x3 -> x1, blocking collectives: 32.1 us -> 12.2 us  [exchange(): return lax.all_to_all(blocks, axes, split_axis=0, concat_axis=0)]
    ppermute x6, waiting for transfers between devices: 0.02 us -> 13.3 us  [the longest x3 13.3 us: tiled_body(): before = lax.ppermute(right, 'sector', onward)]
  transfers between devices with their start and end apart: 12 -> 14, of which waited for: 3 -> 3; matrix products, arithmetic and copies ran while one was open for 1% -> 1% of each run, Pallas kernels for 0% -> 2%
where the time goes in v5:
time: 279 us; the launch traced here: 278 us
  blocking collectives  163 us (58%)
  starting transfers between devices  38.4 us (14%)
  local copies, waits for them, and re-layouts  32.2 us (12%)
  Pallas kernels  25.6 us (9%)
  waiting for transfers between devices  13.3 us (5%)
  other arithmetic  4.27 us (2%)
    all_gather x9, blocking collectives, gathered(): return lax.all_gather(field, 'dof', axis=0)  151 us
    all_to_all x8, starting transfers between devices, exchange(): return lax.all_to_all(blocks, axes, split_axis=0, concat_axis=0)  30.3 us
    unnamed x40, local copies, waits for them, and re-layouts  30.1 us
    pallas_call x19, Pallas kernels, call(): pl.pallas_call(kernel, in_specs=[WHOLE] * (count - unread) + [UNREAD] * u...  25.6 us
    ppermute x3, waiting for transfers between devices, tiled_body(): before = lax.ppermute(right, 'sector', onward)  13.3 us
    all_to_all x1, blocking collectives, exchange(): return lax.all_to_all(blocks, axes, split_axis=0, concat_axis=0)  12.2 us
    ppermute x3, starting transfers between devices, tiled_body(): after = lax.ppermute(left, 'sector', backward)  6.56 us
  transfers between devices with their start and end apart: 14, of which 3 were waited for; matrix products, arithmetic and copies ran while one was open for 1% of the time, Pallas kernels for 2%

profile of v5, /device:TPU:0, one launch (start us, length us, event | category | flops | bytes accessed | tf_op | source)
XLA Modules:
  0.0 277.8 jit_solution(10908362670704383044)
XLA Ops:
  2.6 15.6 %all_gather.52._.ends_ref = bf16[4,256,128]{2,1,0:T(8,128)(2,1)S(1)} all-gather(bf16[1,256,128]{2,1,0:T(8,128)(2,1)S(1)} %slice.59), channel_id=1, replica_groups=mesh['sector'=8,'dof'=4] {'dof'}, dimensions={0}, use_global_device_ids=true | all-gather | bytes 327680 | tf_op jit(solution)/shard_map/all_gather | solution.py:158
  18.2 18.3 %all-gather = bf16[3072,128]{1,0:T(8,128)(2,1)S(1)} all-gather(bf16[768,128]{1,0:T(8,128)(2,1)S(1)} %shard_map.77), channel_id=2, replica_groups=mesh['sector'=8,'dof'=4] {'dof'}, dimensions={0}, use_global_device_ids=true | all-gather | bytes 983040 | tf_op jit(solution)/shard_map/all_gather | solution.py:158
  36.5 3.4 %copy-done = bf16[1024,4096]{1,0:T(8,128)(2,1)S(1)} copy-done((bf16[1024,4096]{1,0:T(8,128)(2,1)S(1)}, bf16[1024,4096]{1,0:T(8,128)(2,1)}, u32[]{:S(2)}) %copy-start) | copy-done | bytes 8388632
  43.7 3.7 %all-to-all-start = ((bf16[8,96,128]{2,1,0:T(8,128)(2,1)}), bf16[8,96,128]{2,1,0:T(8,128)(2,1)S(1)}, u32[]{:S(2)}, u32[]{:S(2)}) async-start(bf16[8,96,128]{2,1,0:T(8,128)(2,1)} %get-tuple-element.27), calls=%async_computation | async-start | bytes 393216 | tf_op jit(solution)/shard_map/all_to_all | solution.py:154
  50.1 4.5 %collective-permute-done.before_ref = bf16[256,128]{1,0:T(8,128)(2,1)S(1)} collective-permute-done((bf16[256,128]{1,0:T(8,128)(2,1)S(1)}, bf16[256,128]{1,0:T(8,128)(2,1)S(1)}, u32[]{:S(2)}, u32[]{:S(2)}) %collective-permute-start) | collective-permute-done | bytes 65568 | tf_op jit(solution)/shard_map/ppermute | solution.py:202
  54.6 16.4 %all-gather.1 = bf16[2432,128]{1,0:T(8,128)(2,1)S(1)} all-gather(bf16[608,128]{1,0:T(8,128)(2,1)S(1)} %shard_map.80), channel_id=3, replica_groups=mesh['sector'=8,'dof'=4] {'dof'}, dimensions={0}, use_global_device_ids=true | all-gather | bytes 778240 | tf_op jit(solution)/shard_map/all_gather | solution.py:158
  75.3 3.5 %all-to-all-start.1 = ((bf16[8,96,128]{2,1,0:T(8,128)(2,1)}), bf16[8,96,128]{2,1,0:T(8,128)(2,1)S(1)}, u32[]{:S(2)}, u32[]{:S(2)}) async-start(bf16[8,96,128]{2,1,0:T(8,128)(2,1)} %shard_map.82), calls=%async_computation.1 | async-start | bytes 393216 | tf_op jit(solution)/shard_map/all_to_all | solution.py:154
  83.1 13.9 %all-gather.2 = bf16[1024,128]{1,0:T(8,128)(2,1)S(1)} all-gather(bf16[256,128]{1,0:T(8,128)(2,1)S(1)} %get-tuple-element.29), channel_id=4, replica_groups=mesh['sector'=8,'dof'=4] {'dof'}, dimensions={0}, use_global_device_ids=true | all-gather | bytes 327680 | tf_op jit(solution)/shard_map/all_gather | solution.py:158
  98.7 4.6 %all-to-all-start.2 = ((f32[32,2,128]{2,1,0:T(2,128)}), f32[32,2,128]{2,1,0:T(2,128)S(1)}, u32[]{:S(2)}, u32[]{:S(2)}) async-start(f32[32,2,128]{2,1,0:T(2,128)} %get-tuple-element.30), calls=%async_computation.2 | async-start | bytes 65536 | tf_op jit(solution)/shard_map/all_to_all | solution.py:154
  103.3 19.8 %all-gather.3 = bf16[3072,128]{1,0:T(8,128)(2,1)S(1)} all-gather(bf16[768,128]{1,0:T(8,128)(2,1)S(1)} %get-tuple-element.31), channel_id=5, replica_groups=mesh['sector'=8,'dof'=4] {'dof'}, dimensions={0}, use_global_device_ids=true | all-gather | bytes 983040 | tf_op jit(solution)/shard_map/all_gather | solution.py:158
  123.1 3.4 %copy-done.1 = bf16[1024,4096]{1,0:T(8,128)(2,1)S(1)} copy-done((bf16[1024,4096]{1,0:T(8,128)(2,1)S(1)}, bf16[1024,4096]{1,0:T(8,128)(2,1)}, u32[]{:S(2)}) %copy-start.1) | copy-done | bytes 8388632
  130.4 3.7 %all-to-all-start.3 = ((bf16[8,96,128]{2,1,0:T(8,128)(2,1)}), bf16[8,96,128]{2,1,0:T(8,128)(2,1)S(1)}, u32[]{:S(2)}, u32[]{:S(2)}) async-start(bf16[8,96,128]{2,1,0:T(8,128)(2,1)} %get-tuple-element.34), calls=%async_computation.3 | async-start | bytes 393216 | tf_op jit(solution)/shard_map/all_to_all | solution.py:154
  136.8 4.4 %collective-permute-done.2.before_ref = bf16[256,128]{1,0:T(8,128)(2,1)S(1)} collective-permute-done((bf16[256,128]{1,0:T(8,128)(2,1)S(1)}, bf16[256,128]{1,0:T(8,128)(2,1)S(1)}, u32[]{:S(2)}, u32[]{:S(2)}) %collective-permute-start.2) | collective-permute-done | bytes 65568 | tf_op jit(solution)/shard_map/ppermute | solution.py:202
  141.3 16.3 %all-gather.4 = bf16[2432,128]{1,0:T(8,128)(2,1)S(1)} all-gather(bf16[608,128]{1,0:T(8,128)(2,1)S(1)} %shard_map.86), channel_id=6, replica_groups=mesh['sector'=8,'dof'=4] {'dof'}, dimensions={0}, use_global_device_ids=true | all-gather | bytes 778240 | tf_op jit(solution)/shard_map/all_gather | solution.py:158
  161.9 3.4 %all-to-all-start.4 = ((bf16[8,96,128]{2,1,0:T(8,128)(2,1)}), bf16[8,96,128]{2,1,0:T(8,128)(2,1)S(1)}, u32[]{:S(2)}, u32[]{:S(2)}) async-start(bf16[8,96,128]{2,1,0:T(8,128)(2,1)} %shard_map.88), calls=%async_computation.4 | async-start | bytes 393216 | tf_op jit(solution)/shard_map/all_to_all | solution.py:154
  171.2 14.0 %all-gather.5 = bf16[1024,128]{1,0:T(8,128)(2,1)S(1)} all-gather(bf16[256,128]{1,0:T(8,128)(2,1)S(1)} %get-tuple-element.37), channel_id=7, replica_groups=mesh['sector'=8,'dof'=4] {'dof'}, dimensions={0}, use_global_device_ids=true | all-gather | bytes 327680 | tf_op jit(solution)/shard_map/all_gather | solution.py:158
  188.0 4.3 %all-to-all-start.5 = ((f32[32,2,128]{2,1,0:T(2,128)}), f32[32,2,128]{2,1,0:T(2,128)S(1)}, u32[]{:S(2)}, u32[]{:S(2)}) async-start(f32[32,2,128]{2,1,0:T(2,128)} %get-tuple-element.38), calls=%async_computation.5 | async-start | bytes 65536 | tf_op jit(solution)/shard_map/all_to_all | solution.py:154
  192.3 20.2 %all-gather.6 = bf16[3072,128]{1,0:T(8,128)(2,1)} all-gather(bf16[768,128]{1,0:T(8,128)(2,1)S(1)} %get-tuple-element.39), channel_id=8, replica_groups=mesh['sector'=8,'dof'=4] {'dof'}, dimensions={0}, use_global_device_ids=true | all-gather | bytes 983040 | tf_op jit(solution)/shard_map/all_gather | solution.py:158
  212.6 3.4 %copy-done.2 = bf16[1024,4096]{1,0:T(8,128)(2,1)S(1)} copy-done((bf16[1024,4096]{1,0:T(8,128)(2,1)S(1)}, bf16[1024,4096]{1,0:T(8,128)(2,1)}, u32[]{:S(2)}) %copy-start.2) | copy-done | bytes 8388632
  220.9 3.7 %all-to-all-start.6 = ((bf16[8,96,128]{2,1,0:T(8,128)(2,1)}), bf16[8,96,128]{2,1,0:T(8,128)(2,1)S(1)}, u32[]{:S(2)}, u32[]{:S(2)}) async-start(bf16[8,96,128]{2,1,0:T(8,128)(2,1)} %get-tuple-element.42), calls=%async_computation.6 | async-start | bytes 393216 | tf_op jit(solution)/shard_map/all_to_all | solution.py:154
  227.3 4.4 %collective-permute-done.4.before_ref = bf16[256,128]{1,0:T(8,128)(2,1)S(1)} collective-permute-done((bf16[256,128]{1,0:T(8,128)(2,1)S(1)}, bf16[256,128]{1,0:T(8,128)(2,1)S(1)}, u32[]{:S(2)}, u32[]{:S(2)}) %collective-permute-start.4) | collective-permute-done | bytes 65568 | tf_op jit(solution)/shard_map/ppermute | solution.py:202
  231.8 16.4 %all-gather.7 = bf16[2432,128]{1,0:T(8,128)(2,1)S(1)} all-gather(bf16[608,128]{1,0:T(8,128)(2,1)S(1)} %shard_map.92), channel_id=9, replica_groups=mesh['sector'=8,'dof'=4] {'dof'}, dimensions={0}, use_global_device_ids=true | all-gather | bytes 778240 | tf_op jit(solution)/shard_map/all_gather | solution.py:158
  252.5 3.4 %all-to-all-start.7 = ((bf16[8,96,128]{2,1,0:T(8,128)(2,1)}), bf16[8,96,128]{2,1,0:T(8,128)(2,1)S(1)}, u32[]{:S(2)}, u32[]{:S(2)}) async-start(bf16[8,96,128]{2,1,0:T(8,128)(2,1)} %shard_map.94), calls=%async_computation.7 | async-start | bytes 393216 | tf_op jit(solution)/shard_map/all_to_all | solution.py:154
  264.5 12.2 %all_to_all.45 = f32[32,2,128]{2,1,0:T(2,128)S(1)} all-to-all(f32[32,2,128]{2,1,0:T(2,128)S(1)} %get-tuple-element.46), channel_id=1, replica_groups=mesh['sector'=8,'dof'=4] {'sector','dof'}, dimensions={0} | all-to-all | bytes 65536 | tf_op jit(solution)/shard_map/all_to_all | solution.py:154
  (87 shorter events, 60.1 us)
Async XLA Ops:
  36.5 3.4 %copy-start = (bf16[1024,4096]{1,0:T(8,128)(2,1)S(1)}, bf16[1024,4096]{1,0:T(8,128)(2,1)}, u32[]{:S(2)}) copy-start(bf16[1024,4096]{1,0:T(8,128)(2,1)} %matrix_ref.10) | copy-start | bytes 25165828
  39.9 2.9 %copy-start.18 = (f32[1,768]{1,0:T(1,128)S(1)}, f32[1,768]{1,0:T(1,128)}, u32[]{:S(2)}) copy-start(f32[1,768]{1,0:T(1,128)} %springs_ref.11) | copy-start | bytes 9220
  42.8 36.1 %copy-start.19 = (f32[1,1024]{1,0:T(1,128)S(1)}, f32[1,1024]{1,0:T(1,128)}, u32[]{:S(2)}) copy-start(f32[1,1024]{1,0:T(1,128)} %param.7) | copy-start | bytes 12292
  43.7 10.9 %all-to-all-start = ((bf16[8,96,128]{2,1,0:T(8,128)(2,1)}), bf16[8,96,128]{2,1,0:T(8,128)(2,1)S(1)}, u32[]{:S(2)}, u32[]{:S(2)}) async-start(bf16[8,96,128]{2,1,0:T(8,128)(2,1)} %get-tuple-element.27), calls=%async_computation | async-start | bytes 393216 | tf_op jit(solution)/shard_map/all_to_all | solution.py:154
  47.4 7.2 %collective-permute-start = (bf16[256,128]{1,0:T(8,128)(2,1)S(1)}, bf16[256,128]{1,0:T(8,128)(2,1)S(1)}, u32[]{:S(2)}, u32[]{:S(2)}) collective-permute-start(bf16[256,128]{1,0:T(8,128)(2,1)S(1)} %get-tuple-element.25), channel_id=1, source_target_pairs={{0,4},{4,8},{8,12},{12,16},{16,20},{20,24},{24,28},{28,0},{1,5},{5... | collective-permute-start | bytes 196616 | tf_op jit(solution)/shard_map/ppermute | solution.py:202
  47.9 6.7 %collective-permute-start.1 = (bf16[256,128]{1,0:T(8,128)(2,1)S(1)}, bf16[256,128]{1,0:T(8,128)(2,1)S(1)}, u32[]{:S(2)}, u32[]{:S(2)}) collective-permute-start(bf16[256,128]{1,0:T(8,128)(2,1)S(1)} %get-tuple-element.26), channel_id=1, source_target_pairs={{4,0},{8,4},{12,8},{16,12},{20,16},{24,20},{28,24},{0,28},{5,1},{9... | collective-permute-start | bytes 196616 | tf_op jit(solution)/shard_map/ppermute | solution.py:203
  71.0 2.3 copy-start.3
  75.3 21.7 %copy-start.10 = (f32[1,1024,128]{2,1,0:T(8,128)S(1)}, f32[1,1024,128]{2,1,0:T(8,128)}, u32[]{:S(2)}) copy-start(f32[1,1024,128]{2,1,0:T(8,128)} %param.6) | copy-start | bytes 1572868
  75.3 21.7 %all-to-all-start.1 = ((bf16[8,96,128]{2,1,0:T(8,128)(2,1)}), bf16[8,96,128]{2,1,0:T(8,128)(2,1)S(1)}, u32[]{:S(2)}, u32[]{:S(2)}) async-start(bf16[8,96,128]{2,1,0:T(8,128)(2,1)} %shard_map.82), calls=%async_computation.1 | async-start | bytes 393216 | tf_op jit(solution)/shard_map/all_to_all | solution.py:154
  98.7 24.4 %all-to-all-start.2 = ((f32[32,2,128]{2,1,0:T(2,128)}), f32[32,2,128]{2,1,0:T(2,128)S(1)}, u32[]{:S(2)}, u32[]{:S(2)}) async-start(f32[32,2,128]{2,1,0:T(2,128)} %get-tuple-element.30), calls=%async_computation.2 | async-start | bytes 65536 | tf_op jit(solution)/shard_map/all_to_all | solution.py:154
  123.1 3.4 %copy-start.1 = (bf16[1024,4096]{1,0:T(8,128)(2,1)S(1)}, bf16[1024,4096]{1,0:T(8,128)(2,1)}, u32[]{:S(2)}) copy-start(bf16[1024,4096]{1,0:T(8,128)(2,1)} %matrix_ref.10) | copy-start | bytes 25165828
  130.4 10.9 %all-to-all-start.3 = ((bf16[8,96,128]{2,1,0:T(8,128)(2,1)}), bf16[8,96,128]{2,1,0:T(8,128)(2,1)S(1)}, u32[]{:S(2)}, u32[]{:S(2)}) async-start(bf16[8,96,128]{2,1,0:T(8,128)(2,1)} %get-tuple-element.34), calls=%async_computation.3 | async-start | bytes 393216 | tf_op jit(solution)/shard_map/all_to_all | solution.py:154
  134.0 7.2 %collective-permute-start.2 = (bf16[256,128]{1,0:T(8,128)(2,1)S(1)}, bf16[256,128]{1,0:T(8,128)(2,1)S(1)}, u32[]{:S(2)}, u32[]{:S(2)}) collective-permute-start(bf16[256,128]{1,0:T(8,128)(2,1)S(1)} %get-tuple-element.32), channel_id=1, source_target_pairs={{0,4},{4,8},{8,12},{12,16},{16,20},{20,24},{24,28},{28,0},{1,5},{5... | collective-permute-start | bytes 196616 | tf_op jit(solution)/shard_map/ppermute | solution.py:202
  134.5 6.7 %collective-permute-start.3 = (bf16[256,128]{1,0:T(8,128)(2,1)S(1)}, bf16[256,128]{1,0:T(8,128)(2,1)S(1)}, u32[]{:S(2)}, u32[]{:S(2)}) collective-permute-start(bf16[256,128]{1,0:T(8,128)(2,1)S(1)} %get-tuple-element.33), channel_id=1, source_target_pairs={{4,0},{8,4},{12,8},{16,12},{20,16},{24,20},{28,24},{0,28},{5,1},{9... | collective-permute-start | bytes 196616 | tf_op jit(solution)/shard_map/ppermute | solution.py:203
  157.6 2.3 copy-start.4
  161.9 23.4 %all-to-all-start.4 = ((bf16[8,96,128]{2,1,0:T(8,128)(2,1)}), bf16[8,96,128]{2,1,0:T(8,128)(2,1)S(1)}, u32[]{:S(2)}, u32[]{:S(2)}) async-start(bf16[8,96,128]{2,1,0:T(8,128)(2,1)} %shard_map.88), calls=%async_computation.4 | async-start | bytes 393216 | tf_op jit(solution)/shard_map/all_to_all | solution.py:154
  188.0 24.6 %all-to-all-start.5 = ((f32[32,2,128]{2,1,0:T(2,128)}), f32[32,2,128]{2,1,0:T(2,128)S(1)}, u32[]{:S(2)}, u32[]{:S(2)}) async-start(f32[32,2,128]{2,1,0:T(2,128)} %get-tuple-element.38), calls=%async_computation.5 | async-start | bytes 65536 | tf_op jit(solution)/shard_map/all_to_all | solution.py:154
  212.6 3.4 %copy-start.2 = (bf16[1024,4096]{1,0:T(8,128)(2,1)S(1)}, bf16[1024,4096]{1,0:T(8,128)(2,1)}, u32[]{:S(2)}) copy-start(bf16[1024,4096]{1,0:T(8,128)(2,1)} %matrix_ref.10) | copy-start | bytes 25165828
  220.9 10.9 %all-to-all-start.6 = ((bf16[8,96,128]{2,1,0:T(8,128)(2,1)}), bf16[8,96,128]{2,1,0:T(8,128)(2,1)S(1)}, u32[]{:S(2)}, u32[]{:S(2)}) async-start(bf16[8,96,128]{2,1,0:T(8,128)(2,1)} %get-tuple-element.42), calls=%async_computation.6 | async-start | bytes 393216 | tf_op jit(solution)/shard_map/all_to_all | solution.py:154
  224.6 7.2 %collective-permute-start.4 = (bf16[256,128]{1,0:T(8,128)(2,1)S(1)}, bf16[256,128]{1,0:T(8,128)(2,1)S(1)}, u32[]{:S(2)}, u32[]{:S(2)}) collective-permute-start(bf16[256,128]{1,0:T(8,128)(2,1)S(1)} %get-tuple-element.40), channel_id=1, source_target_pairs={{0,4},{4,8},{8,12},{12,16},{16,20},{20,24},{24,28},{28,0},{1,5},{5... | collective-permute-start | bytes 196616 | tf_op jit(solution)/shard_map/ppermute | solution.py:202
  225.1 6.7 %collective-permute-start.5 = (bf16[256,128]{1,0:T(8,128)(2,1)S(1)}, bf16[256,128]{1,0:T(8,128)(2,1)S(1)}, u32[]{:S(2)}, u32[]{:S(2)}) collective-permute-start(bf16[256,128]{1,0:T(8,128)(2,1)S(1)} %get-tuple-element.41), channel_id=1, source_target_pairs={{4,0},{8,4},{12,8},{16,12},{20,16},{24,20},{28,24},{0,28},{5,1},{9... | collective-permute-start | bytes 196616 | tf_op jit(solution)/shard_map/ppermute | solution.py:203
  248.2 2.3 copy-start.5
  252.5 10.1 %all-to-all-start.7 = ((bf16[8,96,128]{2,1,0:T(8,128)(2,1)}), bf16[8,96,128]{2,1,0:T(8,128)(2,1)S(1)}, u32[]{:S(2)}, u32[]{:S(2)}) async-start(bf16[8,96,128]{2,1,0:T(8,128)(2,1)} %shard_map.94), calls=%async_computation.7 | async-start | bytes 393216 | tf_op jit(solution)/shard_map/all_to_all | solution.py:154
  260.0 2.6 copy-start.9
  (10 other events, 13.0 us)

commit v6 on v5

v6 whole, which is shorter than its diff:
```python
import functools

import jax
import jax.numpy as jnp
from jax import lax
from jax.experimental import pallas as pl
from jax.experimental.pallas import tpu as pltpu
from jax.sharding import PartitionSpec as P

ITERS = 3
LANES = 128
MIB = 1024 * 1024
WHOLE = pl.BlockSpec(memory_space=pltpu.VMEM)
UNREAD = pl.BlockSpec(memory_space=pl.ANY)
f32 = jnp.float32
bf16 = jnp.bfloat16


def shape(*dims, dtype=f32):
    return jax.ShapeDtypeStruct(dims, dtype)


def call(kernel, outs, operands, streamed=False, unread=0, flops=0):
    matrix = operands[0]
    specs = [WHOLE] * (len(operands) - unread) + [UNREAD] * unread
    scratch = []
    if streamed:
        specs[0] = pl.BlockSpec(memory_space=pltpu.HBM)
        scratch = [pltpu.VMEM(matrix.shape, matrix.dtype), pltpu.SemaphoreType.DMA((streamed,))]
    return pl.pallas_call(
        kernel,
        in_specs=specs,
        out_specs=jax.tree.map(lambda _: WHOLE, outs),
        out_shape=outs,
        scratch_shapes=scratch,
        compiler_params=pltpu.CompilerParams(vmem_limit_bytes=(60 if streamed else 16) * MIB),
        cost_estimate=pl.CostEstimate(
            flops=flops, bytes_accessed=sum(x.size * x.dtype.itemsize for x in operands), transcendentals=0
        ),
    )(*operands)


def columns(parts, width, source, buffer, sems):
    copies = []
    for part in range(parts):
        at = (slice(None), pl.ds(part * width, width))
        copy = pltpu.make_async_copy(source.at[at], buffer.at[at], sems.at[part])
        copy.start()
        copies.append((copy, at))

    def block(part):
        copy, at = copies[part]
        copy.wait()
        return buffer[at]

    return block


def product_kernel(change, matrix_ref, springs_ref, *refs):
    *refs, out_ref, load_ref, right_ref, left_ref, buffer, sems = refs
    field_refs = refs[:-2] if change else refs
    parts = field_refs[0].shape[0]
    count = len(field_refs)
    block = columns(parts * count, field_refs[0].shape[1], matrix_ref, buffer, sems)
    for part in range(parts):
        for at, ref in enumerate(field_refs):
            product = jnp.dot(block(part * count + at), ref[part], preferred_element_type=f32)
            if part + at == 0:
                out_ref[...] = product
            else:
                out_ref[...] += product
    if change:
        before_ref, alpha_ref = refs[-2:]
        out_ref[...] = before_ref[...] - alpha_ref[0:1] * out_ref[...]

    sectors, height, _ = load_ref.shape
    cases = out_ref.shape[1] // sectors
    quarter = right_ref.shape[0]
    left_ref[...] = out_ref[:quarter].astype(bf16)
    right_ref[...] = out_ref[quarter : 2 * quarter].astype(bf16)
    for at in range(height // cases):
        rows = slice(at * LANES, (at + 1) * LANES)
        turned = out_ref[rows].T * springs_ref[:, rows]
        for s in range(sectors):
            load_ref[s, at * cases : (at + 1) * cases] = turned[s * cases : (s + 1) * cases]


def preconditioned(sectors, matrix, springs, fields, *before_and_alpha):
    rows, depth = matrix.shape
    parts, _, loads = fields[0].shape
    attached = springs.shape[1]
    height = attached // LANES * (loads // sectors)
    face = shape(rows - attached, loads, dtype=bf16)
    return call(
        functools.partial(product_kernel, bool(before_and_alpha)),
        (shape(rows, loads), shape(sectors, height, LANES), face, face),
        (matrix, springs, *fields, *before_and_alpha),
        streamed=parts * len(fields),
        flops=2 * rows * depth * loads,
    )


def pack_kernel(before_ref, after_ref, parts_ref, out_ref):
    quarter = before_ref.shape[0]
    out_ref[:quarter] = before_ref[...]
    out_ref[quarter : 2 * quarter] = after_ref[...]
    out_ref[2 * quarter :] = jnp.sum(parts_ref[...], axis=0).astype(bf16)


def hub_kernel(cases, matrix_ref, pieces_ref, out_ref, buffer, sems):
    parts = pieces_ref.shape[0]
    height = out_ref.shape[1]
    chunks = height // cases
    depth = chunks * LANES
    first = pieces_ref.shape[1] - height
    matrix_block = columns(parts, depth, matrix_ref, buffer, sems)
    total = None
    for part in range(parts):
        load = jnp.concatenate(
            [pieces_ref[part, first + c * cases : first + (c + 1) * cases] for c in range(chunks)],
            axis=1,
        )
        product = lax.dot_general(
            load,
            matrix_block(part),
            (((1,), (1,)), ((), ())),
            preferred_element_type=f32,
        )
        total = product if total is None else total + product
    for c in range(chunks):
        block = total[:, c * LANES : (c + 1) * LANES]
        for s in range(out_ref.shape[0]):
            out_ref[s, c * cases : (c + 1) * cases] = block


def base_kernel(matrix_ref, pieces_ref, precon_ref, stiffness_ref, base_ref, buffer, sems):
    parts = pieces_ref.shape[0]
    depth = matrix_ref.shape[1] // parts
    block = columns(parts, depth, matrix_ref, buffer, sems)
    base_ref[...] = stiffness_ref[...] * precon_ref[...]
    for part in range(parts):
        base_ref[...] += jnp.dot(block(part), pieces_ref[part, :depth], preferred_element_type=f32)


def image_kernel(base_ref, hubs_ref, springs_ref, residual_ref, image_ref, low_ref, sums_ref):
    sectors, height, _ = hubs_ref.shape
    attached = springs_ref.shape[1]
    chunks = attached // LANES
    cases = height // chunks
    for c in range(chunks):
        at = slice(c * LANES, (c + 1) * LANES)
        hub = jnp.concatenate([hubs_ref[s, c * cases : (c + 1) * cases] for s in range(sectors)], axis=0)
        image_ref[at] = base_ref[at] - (hub * springs_ref[:, at]).T
    image_ref[attached:] = base_ref[attached:]
    image = image_ref[...]
    low_ref[...] = image.astype(bf16)
    upper = jnp.sum(image * residual_ref[...], axis=0, keepdims=True)
    lower = jnp.sum(image * image, axis=0, keepdims=True)
    sums = jnp.concatenate([upper, lower], axis=0)
    sums_ref[...] = jnp.broadcast_to(sums[None], sums_ref.shape)


def step_kernel(sums_ref, precon_ref, image_ref, solution_ref, residual_ref, alpha_ref, newer_ref, left_ref):
    sums = jnp.sum(sums_ref[...], axis=0)
    alpha = sums[0:1] / (sums[1:2] + 1e-06)
    alpha_ref[...] = jnp.broadcast_to(alpha, alpha_ref.shape)
    newer_ref[...] = solution_ref[...] + alpha * precon_ref[...]
    left_ref[...] = residual_ref[...] - alpha * image_ref[...]


def halves_kernel(field_ref, upper_ref, lower_ref):
    half = upper_ref.shape[0]
    upper_ref[...] = field_ref[0, :half].astype(bf16)
    lower_ref[...] = field_ref[0, half:].astype(bf16)


def after_kernel(field_ref, _, out_ref):
    out_ref[...] = field_ref[...]


def exchange(blocks, axes):
    return lax.all_to_all(blocks, axes, split_axis=0, concat_axis=0)


def gathered(field):
    return lax.all_gather(field, "dof", axis=0)


def around(sectors):
    onward = [(s, (s + 1) % sectors) for s in range(sectors)]
    return onward, [(b, a) for a, b in onward]


def alpha_of(sums):
    total = jnp.sum(sums, axis=0)
    return total[0] / (total[1] + 1e-06)


def tiled_body(rhs, diagonal, coupling, springs, precond, hub_inverse):
    residual = rhs[0]
    rows, loads = residual.shape
    attached = springs.shape[1]
    quarter = rows - attached
    sectors, parts = lax.axis_size("sector"), lax.axis_size("dof")
    cases = loads // sectors
    height = attached // LANES * cases
    onward, backward = around(sectors)

    stiffness = diagonal[0] + jnp.pad(springs[0], (0, quarter))
    stiffness = jnp.broadcast_to(stiffness[:, None], (rows, loads))
    solution = jnp.zeros_like(residual)

    half = shape(rows // 2, loads, dtype=bf16)
    upper, lower = call(halves_kernel, (half, half), (rhs,))
    upper = gathered(upper)
    lower = gathered(call(after_kernel, half, (lower, upper), unread=1))
    precon, load, right, left = preconditioned(sectors, precond, springs, (upper, lower))
    for step in range(ITERS):
        before = lax.ppermute(right, "sector", onward)
        after = lax.ppermute(left, "sector", backward)
        packed = call(
            pack_kernel,
            shape(2 * quarter + height, loads, dtype=bf16),
            (before, after, exchange(load, "sector")),
        )
        pieces = gathered(packed)
        hub = call(
            functools.partial(hub_kernel, cases),
            shape(sectors, height, LANES),
            (hub_inverse, pieces),
            streamed=parts,
            flops=2 * hub_inverse.size * cases,
        )
        hubs = exchange(hub, "sector")
        base = call(
            base_kernel,
            shape(rows, loads),
            (coupling[0], pieces, precon, stiffness),
            streamed=parts,
            flops=2 * coupling.size * loads,
        )
        image, low, sums = call(
            image_kernel,
            (shape(rows, loads), shape(rows, loads, dtype=bf16), shape(sectors * parts, 2, loads)),
            (base, hubs, springs, residual),
        )
        sums = exchange(sums, ("sector", "dof"))
        alpha, solution, residual = call(
            step_kernel,
            (shape(8, loads), shape(rows, loads), shape(rows, loads)),
            (sums, precon, image, solution, residual),
        )
        if step < ITERS - 1:
            precon, load, right, left = preconditioned(
                sectors, precond, springs, (gathered(low),), precon, alpha
            )
    return (solution[None], residual[None])


def plain_body(rhs, diagonal, coupling, springs, precond, hub_inverse):
    residual = rhs[0]
    spring_rows = springs[0][:, None]
    rows, loads = residual.shape
    quarter = rows // 4
    sectors = lax.axis_size("sector")
    onward, backward = around(sectors)
    solution = jnp.zeros_like(residual)

    def whole(field):
        return gathered(field.astype(bf16)).reshape(-1, loads)

    def copies(cells, axes):
        count = lax.axis_size(axes)
        return exchange(jnp.broadcast_to(cells[None], (count,) + cells.shape), axes)

    precon = jnp.dot(precond, whole(residual), preferred_element_type=f32)
    for step in range(ITERS):
        faces = precon[: 2 * quarter].astype(bf16)
        before = lax.ppermute(faces[quarter:], "sector", onward)
        after = lax.ppermute(faces[:quarter], "sector", backward)
        couple = jnp.dot(
            coupling[0], whole(jnp.concatenate([before, after])), preferred_element_type=f32
        )
        attached = precon[: 3 * quarter]
        load = (spring_rows * attached).T.reshape(sectors, loads // sectors, -1)
        load = jnp.sum(exchange(load, "sector"), axis=0).astype(bf16)
        load = copies(load, "dof").transpose(0, 2, 1).reshape(hub_inverse.shape[1], -1)
        hub = jnp.dot(hub_inverse, load, preferred_element_type=f32)
        hub = copies(hub.T, "sector").reshape(loads, -1).T
        pull = jnp.pad(spring_rows * (attached - hub), ((0, quarter), (0, 0)))
        image = diagonal[0][:, None] * precon + couple + pull
        sums = jnp.stack([jnp.sum(image * residual, axis=0), jnp.sum(image * image, axis=0)])
        alpha = alpha_of(copies(sums, ("sector", "dof")))
        solution = solution + alpha * precon
        residual = residual - alpha * image
        if step < ITERS - 1:
            change = jnp.dot(precond, whole(image), preferred_element_type=f32)
            precon = precon - alpha * change
    return (solution[None], residual[None])


def body(rhs, *rest):
    rows, loads = rhs.shape[1:]
    cases = loads // lax.axis_size("sector")
    tiled = loads == LANES and (rows // 4) % LANES == 0 and cases % 16 == 0
    return (tiled_body if tiled else plain_body)(rhs, *rest)


def solution(mesh):
    placed = (
        P("sector", "dof", None),
        P("sector", "dof"),
        P("sector", "dof", None),
        P("sector", "dof"),
        P("dof", None),
        P("dof", None),
    )
    return jax.shard_map(
        body,
        mesh=mesh,
        in_specs=placed,
        out_specs=(P("sector", "dof", None), P("sector", "dof", None)),
        check_vma=False,
    )
```

time: 279 us -> 289 us (1.036)
  blocking collectives: 163 us -> 116 us
  waiting for transfers between devices: 13.3 us -> 56.5 us
  Pallas kernels: 25.6 us -> 63.6 us
  local copies, waits for them, and re-layouts: 32.2 us -> 6.42 us
  between operations: 0.84 us -> 14.3 us
  starting transfers between devices: 38.4 us -> 30 us
  other arithmetic: 4.27 us -> 0.02 us
    all_gather x9 -> x5, blocking collectives: 151 us -> 85 us  [gathered(): return lax.all_gather(field, 'dof', axis=0)]
    pallas_call x19 -> x20, Pallas kernels: 25.6 us -> 63.6 us  [call(): pl.pallas_call(kernel, in_specs=specs, out_specs=jax.tree.map(lambda _: W...]
    all_gather x0 -> x2, waiting for transfers between devices: none -> 31.2 us  [gathered(): return lax.all_gather(field, 'dof', axis=0)]
    unnamed x40 -> x30, local copies, waits for them, and re-layouts: 30.1 us -> 5.39 us
    all_to_all x1 -> x3, blocking collectives: 12.2 us -> 31.4 us  [exchange(): return lax.all_to_all(blocks, axes, split_axis=0, concat_axis=0)]
    all_to_all x8 -> x6, starting transfers between devices: 30.3 us -> 21.9 us  [exchange(): return lax.all_to_all(blocks, axes, split_axis=0, concat_axis=0)]
    ppermute x3, waiting for transfers between devices: 13.3 us -> 19.7 us  [tiled_body(): before = lax.ppermute(right, 'sector', onward)]
    all_to_all x8 -> x6, waiting for transfers between devices: 0.02 us -> 5.49 us  [exchange(): return lax.all_to_all(blocks, axes, split_axis=0, concat_axis=0)]
  transfers between devices with their start and end apart: 14 -> 14, of which waited for: 3 -> 8; matrix products, arithmetic and copies ran while one was open for 1% -> 0% of each run, Pallas kernels for 2% -> 6%
where the time goes in v6:
time: 289 us; the launch traced here: 287 us
  blocking collectives  116 us (40%)
  Pallas kernels  63.6 us (22%)
  waiting for transfers between devices  56.5 us (20%)
  starting transfers between devices  30 us (10%)
  between operations  14.3 us (5%)
  local copies, waits for them, and re-layouts  6.42 us (2%)
    all_gather x5, blocking collectives, gathered(): return lax.all_gather(field, 'dof', axis=0)  85 us
    pallas_call x20, Pallas kernels, call(): pl.pallas_call(kernel, in_specs=specs, out_specs=jax.tree.map(lambda _: W...  63.6 us
    all_to_all x3, blocking collectives, exchange(): return lax.all_to_all(blocks, axes, split_axis=0, concat_axis=0)  31.4 us
    all_gather x2, waiting for transfers between devices, gathered(): return lax.all_gather(field, 'dof', axis=0)  31.2 us
    all_to_all x6, starting transfers between devices, exchange(): return lax.all_to_all(blocks, axes, split_axis=0, concat_axis=0)  21.9 us
    ppermute x3, waiting for transfers between devices, tiled_body(): before = lax.ppermute(right, 'sector', onward)  19.7 us
    ppermute x3, starting transfers between devices, tiled_body(): after = lax.ppermute(left, 'sector', backward)  6.56 us
  transfers between devices with their start and end apart: 14, of which 8 were waited for; matrix products, arithmetic and copies ran while one was open for 0% of the time, Pallas kernels for 6%

profile of v6, /device:TPU:0, one launch (start us, length us, event | category | flops | bytes accessed | tf_op | source)
XLA Modules:
  0.0 287.3 jit_solution(7964533347637749480)
XLA Ops:
  8.2 17.4 %all-gather = bf16[2048,128]{1,0:T(8,128)(2,1)S(1)} all-gather(bf16[512,128]{1,0:T(8,128)(2,1)S(1)} %get-tuple-element.32), channel_id=2, replica_groups=mesh['sector'=8,'dof'=4] {'dof'}, dimensions={0}, use_global_device_ids=true | all-gather | bytes 655360 | tf_op jit(solution)/shard_map/all_gather | solution.py:186
  25.6 17.1 %all-gather.1 = bf16[2048,128]{1,0:T(8,128)(2,1)} all-gather(bf16[512,128]{1,0:T(8,128)(2,1)S(1)} %shard_map.78), channel_id=3, replica_groups=mesh['sector'=8,'dof'=4] {'dof'}, dimensions={0}, use_global_device_ids=true | all-gather | bytes 655360 | tf_op jit(solution)/shard_map/all_gather | solution.py:186
  42.7 8.3 %shard_map.79 = (f32[1024,128]{1,0:T(8,128)}, f32[8,96,128]{2,1,0:T(8,128)}, bf16[256,128]{1,0:T(8,128)(2,1)}, bf16[256,128]{1,0:T(8,128)(2,1)}) custom-call(bf16[1024,4096]{1,0:T(8,128)(2,1)} %matrix_ref.10, f32[1,768]{1,0:T(1,128)} %springs_ref.11, bf16[4,512,128]{2,1,0:T(8,128)(2,1)} %bitcast.13, bf16[4,512,128]{2,1,0:T(8,128)(2,1)} %bitcast.25), custom_call_target="tpu_custom_call" | custom-call | flops 1073741824 | bytes 9440256 | tf_op jit(solution)/shard_map/pallas_call | solution.py:30
  51.0 3.7 %all-to-all-start = ((f32[8,96,128]{2,1,0:T(8,128)}), f32[8,96,128]{2,1,0:T(8,128)S(1)}, u32[]{:S(2)}, u32[]{:S(2)}) async-start(f32[8,96,128]{2,1,0:T(8,128)} %get-tuple-element.36), calls=%async_computation | async-start | bytes 786432 | tf_op jit(solution)/shard_map/all_to_all | solution.py:182
  57.4 6.6 %collective-permute-done.before_ref = bf16[256,128]{1,0:T(8,128)(2,1)S(1)} collective-permute-done((bf16[256,128]{1,0:T(8,128)(2,1)}, bf16[256,128]{1,0:T(8,128)(2,1)S(1)}, u32[]{:S(2)}, u32[]{:S(2)}) %collective-permute-start) | collective-permute-done | bytes 65568 | tf_op jit(solution)/shard_map/ppermute | solution.py:219
  64.0 16.5 %all-gather.2 = bf16[2432,128]{1,0:T(8,128)(2,1)} all-gather(bf16[608,128]{1,0:T(8,128)(2,1)S(1)} %shard_map.80), channel_id=4, replica_groups=mesh['sector'=8,'dof'=4] {'dof'}, dimensions={0}, use_global_device_ids=true | all-gather | bytes 778240 | tf_op jit(solution)/shard_map/all_gather | solution.py:186
  80.5 5.3 %shard_map.82 = f32[8,96,128]{2,1,0:T(8,128)} custom-call(bf16[768,3072]{1,0:T(8,128)(2,1)} %matrix_ref.11, bf16[4,608,128]{2,1,0:T(8,128)(2,1)} %bitcast.19), custom_call_target="tpu_custom_call" | custom-call | flops 75497472 | bytes 5341184 | tf_op jit(solution)/shard_map/pallas_call | solution.py:30
  90.5 6.1 %shard_map.81.base_ref = f32[1024,128]{1,0:T(8,128)} custom-call(bf16[1024,2048]{1,0:T(8,128)(2,1)} %bitcast.16, bf16[4,608,128]{2,1,0:T(8,128)(2,1)} %bitcast.20, f32[1024,128]{1,0:T(8,128)} %get-tuple-element.37.precon_ref.refs_1_, f32[1024,128]{1,0:T(8,128)} %broadcast_in_dim.15.stiffness_ref), custom_call_target="tpu_custom_call" | custom-call | flops 536870912 | bytes 5865472 | tf_op jit(solution)/shard_map/pallas_call | solution.py:30
  99.7 12.5 %all_to_all.45.sums_ref = f32[32,2,128]{2,1,0:T(2,128)S(1)} all-to-all(f32[32,2,128]{2,1,0:T(2,128)S(1)} %get-tuple-element.39), channel_id=1, replica_groups=mesh['sector'=8,'dof'=4] {'sector','dof'}, dimensions={0} | all-to-all | bytes 65536 | tf_op jit(solution)/shard_map/all_to_all | solution.py:182
  113.0 15.6 %all-gather.10.cloned.1.call-done = bf16[4096,128]{1,0:T(8,128)(2,1)} async-done(((bf16[1024,128]{1,0:T(8,128)(2,1)}), bf16[4096,128]{1,0:T(8,128)(2,1)}) %all-gather.10.cloned.1.call-update) | async-done | bytes 1048592 | tf_op jit(solution)/shard_map/all_gather | solution.py:186
  128.6 8.6 %shard_map.85 = (f32[1024,128]{1,0:T(8,128)}, f32[8,96,128]{2,1,0:T(8,128)}, bf16[256,128]{1,0:T(8,128)(2,1)}, bf16[256,128]{1,0:T(8,128)(2,1)}) custom-call(bf16[1024,4096]{1,0:T(8,128)(2,1)} %matrix_ref.10, f32[1,768]{1,0:T(1,128)} %springs_ref.11, bf16[4,1024,128]{2,1,0:T(8,128)(2,1)} %bitcast.26, f32[1024,128]{1,0:T(8,128)} %get-tuple-element.37.precon_ref.refs_1_, ...), custom_call_target="tpu_custom_call" | custom-call | flops 1073741824 | bytes 9968640 | tf_op jit(solution)/shard_map/pallas_call | solution.py:30
  143.6 6.6 %collective-permute-done.2.before_ref = bf16[256,128]{1,0:T(8,128)(2,1)S(1)} collective-permute-done((bf16[256,128]{1,0:T(8,128)(2,1)}, bf16[256,128]{1,0:T(8,128)(2,1)S(1)}, u32[]{:S(2)}, u32[]{:S(2)}) %collective-permute-start.2) | collective-permute-done | bytes 65568 | tf_op jit(solution)/shard_map/ppermute | solution.py:219
  150.2 17.1 %all-gather.4 = bf16[2432,128]{1,0:T(8,128)(2,1)} all-gather(bf16[608,128]{1,0:T(8,128)(2,1)S(1)} %shard_map.86), channel_id=6, replica_groups=mesh['sector'=8,'dof'=4] {'dof'}, dimensions={0}, use_global_device_ids=true | all-gather | bytes 778240 | tf_op jit(solution)/shard_map/all_gather | solution.py:186
  167.2 5.3 %shard_map.88 = f32[8,96,128]{2,1,0:T(8,128)} custom-call(bf16[768,3072]{1,0:T(8,128)(2,1)} %matrix_ref.11, bf16[4,608,128]{2,1,0:T(8,128)(2,1)} %bitcast.21), custom_call_target="tpu_custom_call" | custom-call | flops 75497472 | bytes 5341184 | tf_op jit(solution)/shard_map/pallas_call | solution.py:30
  176.2 6.0 %shard_map.87.base_ref = f32[1024,128]{1,0:T(8,128)} custom-call(bf16[1024,2048]{1,0:T(8,128)(2,1)} %bitcast.17, bf16[4,608,128]{2,1,0:T(8,128)(2,1)} %bitcast.22, f32[1024,128]{1,0:T(8,128)} %get-tuple-element.45.precon_ref.refs_1_, f32[1024,128]{1,0:T(8,128)} %broadcast_in_dim.15.stiffness_ref), custom_call_target="tpu_custom_call" | custom-call | flops 536870912 | bytes 5865472 | tf_op jit(solution)/shard_map/pallas_call | solution.py:30
  186.4 9.5 %all_to_all.46.sums_ref = f32[32,2,128]{2,1,0:T(2,128)S(1)} all-to-all(f32[32,2,128]{2,1,0:T(2,128)S(1)} %get-tuple-element.48), channel_id=1, replica_groups=mesh['sector'=8,'dof'=4] {'sector','dof'}, dimensions={0} | all-to-all | bytes 65536 | tf_op jit(solution)/shard_map/all_to_all | solution.py:182
  196.6 15.6 %all-gather.12.cloned.1.call-done = bf16[4096,128]{1,0:T(8,128)(2,1)} async-done(((bf16[1024,128]{1,0:T(8,128)(2,1)}), bf16[4096,128]{1,0:T(8,128)(2,1)}) %all-gather.12.cloned.1.call-update) | async-done | bytes 1048592 | tf_op jit(solution)/shard_map/all_gather | solution.py:186
  212.2 8.6 %shard_map.91 = (f32[1024,128]{1,0:T(8,128)}, f32[8,96,128]{2,1,0:T(8,128)}, bf16[256,128]{1,0:T(8,128)(2,1)}, bf16[256,128]{1,0:T(8,128)(2,1)}) custom-call(bf16[1024,4096]{1,0:T(8,128)(2,1)} %matrix_ref.10, f32[1,768]{1,0:T(1,128)} %springs_ref.11, bf16[4,1024,128]{2,1,0:T(8,128)(2,1)} %bitcast.27, f32[1024,128]{1,0:T(8,128)} %get-tuple-element.45.precon_ref.refs_1_, ...), custom_call_target="tpu_custom_call" | custom-call | flops 1073741824 | bytes 9968640 | tf_op jit(solution)/shard_map/pallas_call | solution.py:30
  220.8 3.7 %all-to-all-start.6 = ((f32[8,96,128]{2,1,0:T(8,128)}), f32[8,96,128]{2,1,0:T(8,128)S(1)}, u32[]{:S(2)}, u32[]{:S(2)}) async-start(f32[8,96,128]{2,1,0:T(8,128)} %get-tuple-element.54), calls=%async_computation.6 | async-start | bytes 786432 | tf_op jit(solution)/shard_map/all_to_all | solution.py:182
  227.2 6.6 %collective-permute-done.4.before_ref = bf16[256,128]{1,0:T(8,128)(2,1)S(1)} collective-permute-done((bf16[256,128]{1,0:T(8,128)(2,1)}, bf16[256,128]{1,0:T(8,128)(2,1)S(1)}, u32[]{:S(2)}, u32[]{:S(2)}) %collective-permute-start.4) | collective-permute-done | bytes 65568 | tf_op jit(solution)/shard_map/ppermute | solution.py:219
  233.8 17.1 %all-gather.6 = bf16[2432,128]{1,0:T(8,128)(2,1)} all-gather(bf16[608,128]{1,0:T(8,128)(2,1)S(1)} %shard_map.92), channel_id=8, replica_groups=mesh['sector'=8,'dof'=4] {'dof'}, dimensions={0}, use_global_device_ids=true | all-gather | bytes 778240 | tf_op jit(solution)/shard_map/all_gather | solution.py:186
  250.9 5.3 %shard_map.94 = f32[8,96,128]{2,1,0:T(8,128)} custom-call(bf16[768,3072]{1,0:T(8,128)(2,1)} %matrix_ref.11, bf16[4,608,128]{2,1,0:T(8,128)(2,1)} %bitcast.23), custom_call_target="tpu_custom_call" | custom-call | flops 75497472 | bytes 5341184 | tf_op jit(solution)/shard_map/pallas_call | solution.py:30
  259.8 6.1 %shard_map.93.base_ref = f32[1024,128]{1,0:T(8,128)} custom-call(bf16[1024,2048]{1,0:T(8,128)(2,1)} %bitcast.18, bf16[4,608,128]{2,1,0:T(8,128)(2,1)} %bitcast.24, f32[1024,128]{1,0:T(8,128)} %get-tuple-element.55.precon_ref, f32[1024,128]{1,0:T(8,128)} %broadcast_in_dim.15.stiffness_ref), custom_call_target="tpu_custom_call" | custom-call | flops 536870912 | bytes 5865472 | tf_op jit(solution)/shard_map/pallas_call | solution.py:30
  270.0 9.5 %all_to_all.47.sums_ref = f32[32,2,128]{2,1,0:T(2,128)S(1)} all-to-all(f32[32,2,128]{2,1,0:T(2,128)S(1)} %get-tuple-element.57), channel_id=1, replica_groups=mesh['sector'=8,'dof'=4] {'sector','dof'}, dimensions={0} | all-to-all | bytes 65536 | tf_op jit(solution)/shard_map/all_to_all | solution.py:182
  (68 shorter events, 38.7 us)
Async XLA Ops:
  7.2 1.0 copy-start.1
  25.6 17.1 %copy-start = (bf16[2048,128]{1,0:T(8,128)(2,1)}, bf16[2048,128]{1,0:T(8,128)(2,1)S(1)}, u32[]{:S(2)}) copy-start(bf16[2048,128]{1,0:T(8,128)(2,1)S(1)} %all-gather) | copy-start | bytes 1572868
  51.0 38.5 %copy-start.9 = (f32[1,768]{1,0:T(1,128)S(1)}, f32[1,768]{1,0:T(1,128)}, u32[]{:S(2)}) copy-start(f32[1,768]{1,0:T(1,128)} %springs_ref.11) | copy-start | bytes 9220
  51.0 38.5 %copy-start.14 = (f32[1,1024]{1,0:T(1,128)S(1)}, f32[1,1024]{1,0:T(1,128)}, u32[]{:S(2)}) copy-start(f32[1,1024]{1,0:T(1,128)} %param.7) | copy-start | bytes 12292
  51.0 13.0 %all-to-all-start = ((f32[8,96,128]{2,1,0:T(8,128)}), f32[8,96,128]{2,1,0:T(8,128)S(1)}, u32[]{:S(2)}, u32[]{:S(2)}) async-start(f32[8,96,128]{2,1,0:T(8,128)} %get-tuple-element.36), calls=%async_computation | async-start | bytes 786432 | tf_op jit(solution)/shard_map/all_to_all | solution.py:182
  54.7 9.3 %collective-permute-start = (bf16[256,128]{1,0:T(8,128)(2,1)}, bf16[256,128]{1,0:T(8,128)(2,1)S(1)}, u32[]{:S(2)}, u32[]{:S(2)}) collective-permute-start(bf16[256,128]{1,0:T(8,128)(2,1)} %get-tuple-element.34), channel_id=1, source_target_pairs={{0,4},{4,8},{8,12},{12,16},{16,20},{20,24},{24,28},{28,0},{1,5},{5... | collective-permute-start | bytes 196616 | tf_op jit(solution)/shard_map/ppermute | solution.py:219
  55.2 8.8 %collective-permute-start.1 = (bf16[256,128]{1,0:T(8,128)(2,1)}, bf16[256,128]{1,0:T(8,128)(2,1)S(1)}, u32[]{:S(2)}, u32[]{:S(2)}) collective-permute-start(bf16[256,128]{1,0:T(8,128)(2,1)} %get-tuple-element.35), channel_id=1, source_target_pairs={{4,0},{8,4},{12,8},{16,12},{20,16},{24,20},{28,24},{0,28},{5,1},{9... | collective-permute-start | bytes 196616 | tf_op jit(solution)/shard_map/ppermute | solution.py:220
  85.8 11.9 %copy-start.2 = (f32[1,1024,128]{2,1,0:T(8,128)S(1)}, f32[1,1024,128]{2,1,0:T(8,128)}, u32[]{:S(2)}) copy-start(f32[1,1024,128]{2,1,0:T(8,128)} %field_ref.1) | copy-start | bytes 1572868
  85.8 11.9 %all-to-all-start.1 = ((f32[8,96,128]{2,1,0:T(8,128)}), f32[8,96,128]{2,1,0:T(8,128)S(1)}, u32[]{:S(2)}, u32[]{:S(2)}) async-start(f32[8,96,128]{2,1,0:T(8,128)} %shard_map.82), calls=%async_computation.1 | async-start | bytes 786432 | tf_op jit(solution)/shard_map/all_to_all | solution.py:182
  89.4 22.8 %copy-start.3 = (f32[1024,128]{1,0:T(8,128)S(1)}, f32[1024,128]{1,0:T(8,128)}, u32[]{:S(2)}) copy-start(f32[1024,128]{1,0:T(8,128)} %get-tuple-element.37.precon_ref.refs_1_) | copy-start | bytes 1572868
  89.4 39.1 %all-gather.10.cloned.1.call-start = ((), (), s32[]{:S(2)}) async-start(), calls=%async_computation.9 | async-start | bytes 1310720 | tf_op jit(solution)/shard_map/all_gather | solution.py:186
  137.2 12.9 %all-to-all-start.3 = ((f32[8,96,128]{2,1,0:T(8,128)}), f32[8,96,128]{2,1,0:T(8,128)S(1)}, u32[]{:S(2)}, u32[]{:S(2)}) async-start(f32[8,96,128]{2,1,0:T(8,128)} %get-tuple-element.44), calls=%async_computation.3 | async-start | bytes 786432 | tf_op jit(solution)/shard_map/all_to_all | solution.py:182
  140.9 9.3 %collective-permute-start.2 = (bf16[256,128]{1,0:T(8,128)(2,1)}, bf16[256,128]{1,0:T(8,128)(2,1)S(1)}, u32[]{:S(2)}, u32[]{:S(2)}) collective-permute-start(bf16[256,128]{1,0:T(8,128)(2,1)} %get-tuple-element.42), channel_id=1, source_target_pairs={{0,4},{4,8},{8,12},{12,16},{16,20},{20,24},{24,28},{28,0},{1,5},{5... | collective-permute-start | bytes 196616 | tf_op jit(solution)/shard_map/ppermute | solution.py:219
  141.4 8.8 %collective-permute-start.3 = (bf16[256,128]{1,0:T(8,128)(2,1)}, bf16[256,128]{1,0:T(8,128)(2,1)S(1)}, u32[]{:S(2)}, u32[]{:S(2)}) collective-permute-start(bf16[256,128]{1,0:T(8,128)(2,1)} %get-tuple-element.43), channel_id=1, source_target_pairs={{4,0},{8,4},{12,8},{16,12},{20,16},{24,20},{28,24},{0,28},{5,1},{9... | collective-permute-start | bytes 196616 | tf_op jit(solution)/shard_map/ppermute | solution.py:220
  172.5 11.9 %copy-start.10 = (f32[1,768]{1,0:T(1,128)S(1)}, f32[1,768]{1,0:T(1,128)}, u32[]{:S(2)}) copy-start(f32[1,768]{1,0:T(1,128)} %springs_ref.11) | copy-start | bytes 9220
  172.5 23.3 %copy-start.4 = (f32[1024,128]{1,0:T(8,128)S(1)}, f32[1024,128]{1,0:T(8,128)}, u32[]{:S(2)}) copy-start(f32[1024,128]{1,0:T(8,128)} %get-tuple-element.45.precon_ref.refs_1_) | copy-start | bytes 1572868
  172.5 11.9 %all-to-all-start.4 = ((f32[8,96,128]{2,1,0:T(8,128)}), f32[8,96,128]{2,1,0:T(8,128)S(1)}, u32[]{:S(2)}, u32[]{:S(2)}) async-start(f32[8,96,128]{2,1,0:T(8,128)} %shard_map.88), calls=%async_computation.4 | async-start | bytes 786432 | tf_op jit(solution)/shard_map/all_to_all | solution.py:182
  176.1 36.1 %all-gather.12.cloned.1.call-start = ((), (), s32[]{:S(2)}) async-start(), calls=%async_computation.10 | async-start | bytes 1310720 | tf_op jit(solution)/shard_map/all_gather | solution.py:186
  220.8 12.9 %all-to-all-start.6 = ((f32[8,96,128]{2,1,0:T(8,128)}), f32[8,96,128]{2,1,0:T(8,128)S(1)}, u32[]{:S(2)}, u32[]{:S(2)}) async-start(f32[8,96,128]{2,1,0:T(8,128)} %get-tuple-element.54), calls=%async_computation.6 | async-start | bytes 786432 | tf_op jit(solution)/shard_map/all_to_all | solution.py:182
  224.5 9.3 %collective-permute-start.4 = (bf16[256,128]{1,0:T(8,128)(2,1)}, bf16[256,128]{1,0:T(8,128)(2,1)S(1)}, u32[]{:S(2)}, u32[]{:S(2)}) collective-permute-start(bf16[256,128]{1,0:T(8,128)(2,1)} %get-tuple-element.52), channel_id=1, source_target_pairs={{0,4},{4,8},{8,12},{12,16},{16,20},{20,24},{24,28},{28,0},{1,5},{5... | collective-permute-start | bytes 196616 | tf_op jit(solution)/shard_map/ppermute | solution.py:219
  225.0 8.8 %collective-permute-start.5 = (bf16[256,128]{1,0:T(8,128)(2,1)}, bf16[256,128]{1,0:T(8,128)(2,1)S(1)}, u32[]{:S(2)}, u32[]{:S(2)}) collective-permute-start(bf16[256,128]{1,0:T(8,128)(2,1)} %get-tuple-element.53), channel_id=1, source_target_pairs={{4,0},{8,4},{12,8},{16,12},{20,16},{24,20},{28,24},{0,28},{5,1},{9... | collective-permute-start | bytes 196616 | tf_op jit(solution)/shard_map/ppermute | solution.py:220
  256.1 11.9 %copy-start.11 = (f32[1,768]{1,0:T(1,128)S(1)}, f32[1,768]{1,0:T(1,128)}, u32[]{:S(2)}) copy-start(f32[1,768]{1,0:T(1,128)} %springs_ref.11) | copy-start | bytes 9220
  256.2 23.3 %copy-start.8 = (f32[1024,128]{1,0:T(8,128)S(1)}, f32[1024,128]{1,0:T(8,128)}, u32[]{:S(2)}) copy-start(f32[1024,128]{1,0:T(8,128)} %get-tuple-element.55.precon_ref) | copy-start | bytes 1572868
  256.2 11.9 %all-to-all-start.7 = ((f32[8,96,128]{2,1,0:T(8,128)}), f32[8,96,128]{2,1,0:T(8,128)S(1)}, u32[]{:S(2)}, u32[]{:S(2)}) async-start(f32[8,96,128]{2,1,0:T(8,128)} %shard_map.94), calls=%async_computation.7 | async-start | bytes 786432 | tf_op jit(solution)/shard_map/all_to_all | solution.py:182
  (5 other events, 4.3 us)
Sparse Core Ops, SparseCore 0:
  99.8 28.7 all-gather.9
  186.5 25.6 all-gather.11

commit v7 on v6

v7 whole, which is shorter than its diff:
```python
import functools

import jax
import jax.numpy as jnp
from jax import lax
from jax.experimental import pallas as pl
from jax.experimental.pallas import tpu as pltpu
from jax.sharding import PartitionSpec as P

ITERS = 3
LANES = 128
MIB = 1024 * 1024
IN_FLIGHT = 3
SUM_ROWS = 8
WHOLE = pl.BlockSpec(memory_space=pltpu.VMEM)
f32 = jnp.float32
bf16 = jnp.bfloat16


def shape(*dims, dtype=f32):
    return jax.ShapeDtypeStruct(dims, dtype)


def call(kernel, outs, operands, parts=0, flops=0):
    matrix = operands[0]
    specs = [WHOLE] * len(operands)
    scratch = []
    if parts:
        specs[0] = pl.BlockSpec(memory_space=pltpu.HBM)
        scratch = [pltpu.VMEM(matrix.shape, matrix.dtype), pltpu.SemaphoreType.DMA((parts,))]
    return pl.pallas_call(
        kernel,
        in_specs=specs,
        out_specs=jax.tree.map(lambda _: WHOLE, outs),
        out_shape=outs,
        scratch_shapes=scratch,
        compiler_params=pltpu.CompilerParams(vmem_limit_bytes=(60 if parts else 16) * MIB),
        cost_estimate=pl.CostEstimate(
            flops=flops, bytes_accessed=sum(x.size * x.dtype.itemsize for x in operands), transcendentals=0
        ),
    )(*operands)


def columns(widths, source, buffer, sems):
    copies = []
    start = 0
    for at, width in enumerate(widths):
        block = (slice(None), pl.ds(start, width))
        copies.append((pltpu.make_async_copy(source.at[block], buffer.at[block], sems.at[at]), block))
        start += width
    for copy, _ in copies[:IN_FLIGHT]:
        copy.start()

    def block(at):
        copy, columns_at = copies[at]
        copy.wait()
        if at + IN_FLIGHT < len(copies):
            copies[at + IN_FLIGHT][0].start()
        return buffer[columns_at]

    return block


def product_kernel(matrix_ref, springs_ref, sums_ref, *refs):
    *field_refs, out_ref, load_ref, right_ref, left_ref, buffer, sems = refs
    count = len(field_refs)
    parts = field_refs[0].shape[0]
    block = columns([ref.shape[1] for ref in field_refs] * parts, matrix_ref, buffer, sems)
    for at in range(parts * count):
        field = field_refs[at % count][at // count]
        product = jnp.dot(block(at), field, preferred_element_type=f32)
        if at == 0:
            out_ref[...] = product
        else:
            out_ref[...] += product

    sectors, height, _ = load_ref.shape
    cases = out_ref.shape[1] // sectors
    quarter = right_ref.shape[0]
    left_ref[...] = out_ref[:quarter].astype(bf16)
    right_ref[...] = out_ref[quarter : 2 * quarter].astype(bf16)
    for at in range((height - SUM_ROWS) // cases):
        rows = slice(at * LANES, (at + 1) * LANES)
        turned = out_ref[rows].T * springs_ref[:, rows]
        for s in range(sectors):
            load_ref[s, at * cases : (at + 1) * cases] = turned[s * cases : (s + 1) * cases]
    for s in range(sectors):
        load_ref[s, height - SUM_ROWS :] = sums_ref[...]


def pack_kernel(before_ref, after_ref, parts_ref, out_ref):
    quarter = before_ref.shape[0]
    height = parts_ref.shape[1] - SUM_ROWS
    out_ref[:quarter] = before_ref[...]
    out_ref[quarter : 2 * quarter] = after_ref[...]
    total = jnp.sum(parts_ref[...], axis=0)
    out_ref[2 * quarter : 2 * quarter + height] = total[:height].astype(bf16)
    rest = total[height:]
    terms = []
    for _ in range(3):
        term = rest.astype(bf16)
        terms.append(term.astype(f32))
        rest = rest - terms[-1]
    terms.append(jnp.zeros_like(rest))
    out_ref[2 * quarter + height :] = jnp.concatenate(terms, axis=0).astype(bf16)


def alpha_from(sums):
    return sums[0:1] / (sums[1:2] + 1e-06)


def hub_kernel(cases, matrix_ref, pieces_ref, out_ref, buffer, sems):
    parts = pieces_ref.shape[0]
    height = out_ref.shape[1]
    chunks = height // cases
    depth = chunks * LANES
    first = pieces_ref.shape[1] - 4 * SUM_ROWS - height
    block = columns([depth] * parts, matrix_ref, buffer, sems)
    total = None
    for part in range(parts):
        load = jnp.concatenate(
            [pieces_ref[part, first + c * cases : first + (c + 1) * cases] for c in range(chunks)],
            axis=1,
        )
        product = lax.dot_general(
            load, block(part), (((1,), (1,)), ((), ())), preferred_element_type=f32
        )
        total = product if total is None else total + product
    for c in range(chunks):
        for s in range(out_ref.shape[0]):
            out_ref[s, c * cases : (c + 1) * cases] = total[:, c * LANES : (c + 1) * LANES]


def base_kernel(first, matrix_ref, pieces_ref, product_ref, stiffness_ref, *refs):
    if first:
        base_ref, ends_ref, factor_ref, buffer, sems = refs
    else:
        image_ref, residual_ref, precon_ref, solution_ref, *refs = refs
        base_ref, ends_ref, factor_ref, left_ref, newer_ref, better_ref, buffer, sems = refs
    parts = pieces_ref.shape[0]
    depth = matrix_ref.shape[1] // parts
    block = columns([depth] * parts, matrix_ref, buffer, sems)
    base_ref[...] = stiffness_ref[...] * product_ref[...]
    for part in range(parts):
        base_ref[...] += jnp.dot(block(part), pieces_ref[part, :depth], preferred_element_type=f32)
    if first:
        factor_ref[...] = jnp.ones_like(factor_ref)
    else:
        sums = None
        height = pieces_ref.shape[1]
        for part in range(parts):
            terms = pieces_ref[part, height - 4 * SUM_ROWS :].astype(f32)
            terms = terms[:SUM_ROWS] + terms[SUM_ROWS : 2 * SUM_ROWS] + terms[2 * SUM_ROWS : 3 * SUM_ROWS]
            sums = terms if sums is None else sums + terms
        alpha = alpha_from(sums)
        factor_ref[...] = jnp.broadcast_to(-alpha, factor_ref.shape)
        base_ref[...] = image_ref[...] - alpha * base_ref[...]
        left_ref[...] = residual_ref[...] - alpha * image_ref[...]
        better_ref[...] = solution_ref[...] + alpha * precon_ref[...]
        newer_ref[...] = precon_ref[...] - alpha * product_ref[...]
    end = base_ref[base_ref.shape[0] - ends_ref.shape[1] :].astype(bf16)
    ends_ref[...] = jnp.broadcast_to(end[None], ends_ref.shape)


def image_kernel(base_ref, hubs_ref, springs_ref, factor_ref, residual_ref, image_ref, top_ref, sums_ref):
    sectors, height, _ = hubs_ref.shape
    attached = top_ref.shape[0]
    chunks = attached // LANES
    cases = height // chunks
    factor = factor_ref[0:1]
    for c in range(chunks):
        at = slice(c * LANES, (c + 1) * LANES)
        hub = jnp.concatenate([hubs_ref[s, c * cases : (c + 1) * cases] for s in range(sectors)], axis=0)
        image = base_ref[at] - factor * (hub * springs_ref[:, at]).T
        image_ref[at] = image
        top_ref[at] = image.astype(bf16)
    image_ref[attached:] = base_ref[attached:]
    image = image_ref[...]
    upper = jnp.sum(image * residual_ref[...], axis=0, keepdims=True)
    lower = jnp.sum(image * image, axis=0, keepdims=True)
    rest = jnp.zeros((SUM_ROWS - 2, image.shape[1]), f32)
    sums = jnp.concatenate([upper, lower, rest], axis=0)
    sums_ref[...] = jnp.broadcast_to(sums[None], sums_ref.shape)


def last_kernel(sums_ref, precon_ref, image_ref, solution_ref, residual_ref, newer_ref, left_ref):
    alpha = alpha_from(jnp.sum(sums_ref[...], axis=0))
    newer_ref[0] = solution_ref[...] + alpha * precon_ref[...]
    left_ref[0] = residual_ref[...] - alpha * image_ref[...]


def round_kernel(field_ref, top_ref, ends_ref):
    attached = top_ref.shape[0]
    top_ref[...] = field_ref[0, :attached].astype(bf16)
    end = field_ref[0, attached:].astype(bf16)
    ends_ref[...] = jnp.broadcast_to(end[None], ends_ref.shape)


def exchange(blocks, axes):
    return lax.all_to_all(blocks, axes, split_axis=0, concat_axis=0)


def gathered(field):
    return lax.all_gather(field, "dof", axis=0)


def around(sectors):
    onward = [(s, (s + 1) % sectors) for s in range(sectors)]
    return onward, [(b, a) for a, b in onward]


def alpha_of(sums):
    return alpha_from(jnp.sum(sums, axis=0))[0]


def tiled_body(rhs, diagonal, coupling, springs, precond, hub_inverse):
    residual = rhs[0]
    rows, loads = residual.shape
    attached = springs.shape[1]
    quarter = rows - attached
    sectors, parts = lax.axis_size("sector"), lax.axis_size("dof")
    cases = loads // sectors
    height = attached // LANES * cases
    onward, backward = around(sectors)
    full, face = shape(rows, loads), shape(quarter, loads, dtype=bf16)
    top_shape, ends_shape = shape(attached, loads, dtype=bf16), shape(parts, quarter, loads, dtype=bf16)

    stiffness = diagonal[0] + jnp.pad(springs[0], (0, quarter))
    stiffness = jnp.broadcast_to(stiffness[:, None], (rows, loads))
    solution = jnp.zeros_like(residual)
    image = precon = None
    sums = jnp.zeros((1, SUM_ROWS, loads), f32)

    top, ends = call(round_kernel, (top_shape, ends_shape), (rhs,))
    for step in range(ITERS):
        first, last = step == 0, step == ITERS - 1
        product, load, right, left = call(
            product_kernel,
            (full, shape(sectors, height + SUM_ROWS, LANES), face, face),
            (precond, springs, sums[0], gathered(top), exchange(ends, "dof")),
            parts=2 * parts,
            flops=2 * precond.size * loads,
        )
        before = lax.ppermute(right, "sector", onward)
        after = lax.ppermute(left, "sector", backward)
        packed = call(
            pack_kernel,
            shape(2 * quarter + height + 4 * SUM_ROWS, loads, dtype=bf16),
            (before, after, exchange(load, "sector")),
        )
        pieces = gathered(packed)
        hub = call(
            functools.partial(hub_kernel, cases),
            shape(sectors, height, LANES),
            (hub_inverse, pieces),
            parts=parts,
            flops=2 * hub_inverse.size * cases,
        )
        hubs = exchange(hub, "sector")
        state = () if first else (image, residual, precon, solution)
        base, ends, factor, *state = call(
            functools.partial(base_kernel, first),
            (full, ends_shape, shape(SUM_ROWS, loads)) + (() if first else (full, full, full)),
            (coupling[0], pieces, product, stiffness, *state),
            parts=parts,
            flops=2 * coupling.size * loads,
        )
        if first:
            precon = product
        else:
            residual, precon, solution = state
        image, top, sums = call(
            image_kernel,
            (full, top_shape, shape(sectors * parts if last else 1, SUM_ROWS, loads)),
            (base, hubs, springs, factor, residual),
        )
    out = shape(1, rows, loads)
    return call(
        last_kernel, (out, out), (exchange(sums, ("sector", "dof")), precon, image, solution, residual)
    )


def plain_body(rhs, diagonal, coupling, springs, precond, hub_inverse):
    residual = rhs[0]
    spring_rows = springs[0][:, None]
    rows, loads = residual.shape
    quarter = rows // 4
    sectors = lax.axis_size("sector")
    onward, backward = around(sectors)
    solution = jnp.zeros_like(residual)

    def whole(field):
        return gathered(field.astype(bf16)).reshape(-1, loads)

    def copies(cells, axes):
        count = lax.axis_size(axes)
        return exchange(jnp.broadcast_to(cells[None], (count,) + cells.shape), axes)

    precon = jnp.dot(precond, whole(residual), preferred_element_type=f32)
    for step in range(ITERS):
        faces = precon[: 2 * quarter].astype(bf16)
        before = lax.ppermute(faces[quarter:], "sector", onward)
        after = lax.ppermute(faces[:quarter], "sector", backward)
        couple = jnp.dot(
            coupling[0], whole(jnp.concatenate([before, after])), preferred_element_type=f32
        )
        attached = precon[: 3 * quarter]
        load = (spring_rows * attached).T.reshape(sectors, loads // sectors, -1)
        load = jnp.sum(exchange(load, "sector"), axis=0).astype(bf16)
        load = copies(load, "dof").transpose(0, 2, 1).reshape(hub_inverse.shape[1], -1)
        hub = jnp.dot(hub_inverse, load, preferred_element_type=f32)
        hub = copies(hub.T, "sector").reshape(loads, -1).T
        pull = jnp.pad(spring_rows * (attached - hub), ((0, quarter), (0, 0)))
        image = diagonal[0][:, None] * precon + couple + pull
        sums = jnp.stack([jnp.sum(image * residual, axis=0), jnp.sum(image * image, axis=0)])
        alpha = alpha_of(copies(sums, ("sector", "dof")))
        solution = solution + alpha * precon
        residual = residual - alpha * image
        if step < ITERS - 1:
            change = jnp.dot(precond, whole(image), preferred_element_type=f32)
            precon = precon - alpha * change
    return (solution[None], residual[None])


def body(rhs, *rest):
    rows, loads = rhs.shape[1:]
    cases = loads // lax.axis_size("sector")
    tiled = loads == LANES and (rows // 4) % LANES == 0 and cases % 16 == 0
    return (tiled_body if tiled else plain_body)(rhs, *rest)


def solution(mesh):
    placed = (
        P("sector", "dof", None),
        P("sector", "dof"),
        P("sector", "dof", None),
        P("sector", "dof"),
        P("dof", None),
        P("dof", None),
    )
    return jax.shard_map(
        body,
        mesh=mesh,
        in_specs=placed,
        out_specs=(P("sector", "dof", None), P("sector", "dof", None)),
        check_vma=False,
    )
```

time: 289 us -> 280 us (0.969)
  waiting for transfers between devices: 56.5 us -> 22.9 us
  starting transfers between devices: 30 us -> 45.2 us
  between operations: 14.3 us -> 0.87 us
  local copies, waits for them, and re-layouts: 6.42 us -> 18.1 us
  blocking collectives: 116 us -> 126 us
    all_gather x2 -> x0, waiting for transfers between devices: 31.2 us -> none  [gathered(): return lax.all_gather(field, 'dof', axis=0)]
    all_gather x5 -> x6, blocking collectives: 85 us -> 114 us  [gathered(): return lax.all_gather(field, 'dof', axis=0)]
    all_to_all x3 -> x1, blocking collectives: 31.4 us -> 11.9 us  [exchange(): return lax.all_to_all(blocks, axes, split_axis=0, concat_axis=0)]
    all_to_all x6 -> x9, starting transfers between devices: 21.9 us -> 37.1 us  [exchange(): return lax.all_to_all(blocks, axes, split_axis=0, concat_axis=0)]
    unnamed x30 -> x48, local copies, waits for them, and re-layouts: 5.39 us -> 15.6 us
    all_to_all x6 -> x9, waiting for transfers between devices: 5.49 us -> 2.19 us  [exchange(): return lax.all_to_all(blocks, axes, split_axis=0, concat_axis=0)]
    pallas_call x20 -> x17, Pallas kernels: 63.6 us -> 65.1 us  [call(): pl.pallas_call(kernel, in_specs=specs, out_specs=jax.tree.map(lambda _: W...]
  transfers between devices with their start and end apart: 14 -> 15, of which waited for: 8 -> 6; matrix products, arithmetic and copies ran while one was open for 0% -> 1% of each run, Pallas kernels for 6% -> 8%
where the time goes in v7:
time: 280 us; the launch traced here: 278 us
  blocking collectives  126 us (45%)
  Pallas kernels  65.1 us (23%)
  starting transfers between devices  45.2 us (16%)
  waiting for transfers between devices  22.9 us (8%)
  local copies, waits for them, and re-layouts  18.1 us (6%)
    all_gather x6, blocking collectives, gathered(): return lax.all_gather(field, 'dof', axis=0)  114 us
    pallas_call x17, Pallas kernels, call(): pl.pallas_call(kernel, in_specs=specs, out_specs=jax.tree.map(lambda _: W...  65.1 us
    all_to_all x9, starting transfers between devices, exchange(): return lax.all_to_all(blocks, axes, split_axis=0, concat_axis=0)  37.1 us
    ppermute x3, waiting for transfers between devices, tiled_body(): before = lax.ppermute(right, 'sector', onward)  20.7 us
    unnamed x48, local copies, waits for them, and re-layouts  15.6 us
    all_to_all x1, blocking collectives, exchange(): return lax.all_to_all(blocks, axes, split_axis=0, concat_axis=0)  11.9 us
    ppermute x3, starting transfers between devices, tiled_body(): after = lax.ppermute(left, 'sector', backward)  6.59 us
  transfers between devices with their start and end apart: 15, of which 6 were waited for; matrix products, arithmetic and copies ran while one was open for 1% of the time, Pallas kernels for 8%

profile of v7, /device:TPU:0, one launch (start us, length us, event | category | flops | bytes accessed | tf_op | source)
XLA Modules:
  0.0 278.3 jit_solution(15945291453806093125)
XLA Ops:
  2.4 6.3 %all-to-all-start = ((bf16[4,256,128]{2,1,0:T(8,128)(2,1)}), bf16[4,256,128]{2,1,0:T(8,128)(2,1)S(1)}, u32[]{:S(2)}, u32[]{:S(2)}) async-start(bf16[4,256,128]{2,1,0:T(8,128)(2,1)} %get-tuple-element.39), calls=%async_computation | async-start | bytes 524288 | tf_op jit(solution)/shard_map/all_to_all | solution.py:200
  8.7 22.8 %all-gather = bf16[3072,128]{1,0:T(8,128)(2,1)} all-gather(bf16[768,128]{1,0:T(8,128)(2,1)S(1)} %get-tuple-element.38), channel_id=2, replica_groups=mesh['sector'=8,'dof'=4] {'dof'}, dimensions={0}, use_global_device_ids=true | all-gather | bytes 983040 | tf_op jit(solution)/shard_map/all_gather | solution.py:204
  32.2 8.4 %shard_map.78 = (f32[1024,128]{1,0:T(8,128)}, f32[8,104,128]{2,1,0:T(8,128)}, bf16[256,128]{1,0:T(8,128)(2,1)}, bf16[256,128]{1,0:T(8,128)(2,1)}) custom-call(bf16[1024,4096]{1,0:T(8,128)(2,1)} %matrix_ref.10, f32[1,768]{1,0:T(1,128)} %springs_ref.11, f32[8,128]{1,0:T(8,128)} %squeeze.24.sums_ref, bf16[4,768,128]{2,1,0:T(8,128)(2,1)} %bitcast.24, ...), custom_call_target="tpu_custom_call" | custom-call | flops 1073741824 | bytes 9444352 | tf_op jit(solution)/shard_map/pallas_call | solution.py:31
  40.7 3.7 %all-to-all-start.1 = ((f32[8,104,128]{2,1,0:T(8,128)}), f32[8,104,128]{2,1,0:T(8,128)S(1)}, u32[]{:S(2)}, u32[]{:S(2)}) async-start(f32[8,104,128]{2,1,0:T(8,128)} %get-tuple-element.42), calls=%async_computation.1 | async-start | bytes 851968 | tf_op jit(solution)/shard_map/all_to_all | solution.py:200
  47.1 6.9 %collective-permute-done.before_ref = bf16[256,128]{1,0:T(8,128)(2,1)S(1)} collective-permute-done((bf16[256,128]{1,0:T(8,128)(2,1)}, bf16[256,128]{1,0:T(8,128)(2,1)S(1)}, u32[]{:S(2)}, u32[]{:S(2)}) %collective-permute-start) | collective-permute-done | bytes 65568 | tf_op jit(solution)/shard_map/ppermute | solution.py:244
  54.1 16.7 %all-gather.1 = bf16[2560,128]{1,0:T(8,128)(2,1)} all-gather(bf16[640,128]{1,0:T(8,128)(2,1)S(1)} %shard_map.79), channel_id=3, replica_groups=mesh['sector'=8,'dof'=4] {'dof'}, dimensions={0}, use_global_device_ids=true | all-gather | bytes 819200 | tf_op jit(solution)/shard_map/all_gather | solution.py:204
  70.8 5.3 %shard_map.81 = f32[8,96,128]{2,1,0:T(8,128)} custom-call(bf16[768,3072]{1,0:T(8,128)(2,1)} %matrix_ref.11, bf16[4,640,128]{2,1,0:T(8,128)(2,1)} %bitcast.22), custom_call_target="tpu_custom_call" | custom-call | flops 75497472 | bytes 5373952 | tf_op jit(solution)/shard_map/pallas_call | solution.py:31
  80.8 6.1 %shard_map.80 = (f32[1024,128]{1,0:T(8,128)}, bf16[4,256,128]{2,1,0:T(8,128)(2,1)}, f32[8,128]{1,0:T(8,128)}) custom-call(bf16[1024,2048]{1,0:T(8,128)(2,1)} %bitcast.15, bf16[4,640,128]{2,1,0:T(8,128)(2,1)} %bitcast.23, f32[1024,128]{1,0:T(8,128)} %get-tuple-element.43.product_ref.refs_2_, f32[1024,128]{1,0:T(8,128)} %broadcast_in_dim.4.stiffness_ref), custom_call_target="tpu_custom_call" | custom-call | flops 536870912 | bytes 5898240 | tf_op jit(solution)/shard_map/pallas_call | solution.py:31
  88.0 4.5 %all-to-all-start.3 = ((bf16[4,256,128]{2,1,0:T(8,128)(2,1)}), bf16[4,256,128]{2,1,0:T(8,128)(2,1)S(1)}, u32[]{:S(2)}, u32[]{:S(2)}) async-start(bf16[4,256,128]{2,1,0:T(8,128)(2,1)} %get-tuple-element.48), calls=%async_computation.3 | async-start | bytes 524288 | tf_op jit(solution)/shard_map/all_to_all | solution.py:200
  95.8 20.1 %all-gather.2 = bf16[3072,128]{1,0:T(8,128)(2,1)} all-gather(bf16[768,128]{1,0:T(8,128)(2,1)S(1)} %get-tuple-element.47), channel_id=4, replica_groups=mesh['sector'=8,'dof'=4] {'dof'}, dimensions={0}, use_global_device_ids=true | all-gather | bytes 983040 | tf_op jit(solution)/shard_map/all_gather | solution.py:204
  116.6 8.5 %shard_map.83 = (f32[1024,128]{1,0:T(8,128)}, f32[8,104,128]{2,1,0:T(8,128)}, bf16[256,128]{1,0:T(8,128)(2,1)}, bf16[256,128]{1,0:T(8,128)(2,1)}) custom-call(bf16[1024,4096]{1,0:T(8,128)(2,1)} %matrix_ref.10, f32[1,768]{1,0:T(1,128)} %springs_ref.11, f32[8,128]{1,0:T(8,128)} %bitcast.13, bf16[4,768,128]{2,1,0:T(8,128)(2,1)} %bitcast.25, ...), custom_call_target="tpu_custom_call" | custom-call | flops 1073741824 | bytes 9444352 | tf_op jit(solution)/shard_map/pallas_call | solution.py:31
  131.3 6.9 %collective-permute-done.2.before_ref = bf16[256,128]{1,0:T(8,128)(2,1)S(1)} collective-permute-done((bf16[256,128]{1,0:T(8,128)(2,1)}, bf16[256,128]{1,0:T(8,128)(2,1)S(1)}, u32[]{:S(2)}, u32[]{:S(2)}) %collective-permute-start.2) | collective-permute-done | bytes 65568 | tf_op jit(solution)/shard_map/ppermute | solution.py:244
  138.2 16.7 %all-gather.3 = bf16[2560,128]{1,0:T(8,128)(2,1)} all-gather(bf16[640,128]{1,0:T(8,128)(2,1)S(1)} %shard_map.84), channel_id=5, replica_groups=mesh['sector'=8,'dof'=4] {'dof'}, dimensions={0}, use_global_device_ids=true | all-gather | bytes 819200 | tf_op jit(solution)/shard_map/all_gather | solution.py:204
  155.0 5.3 %shard_map.86 = f32[8,96,128]{2,1,0:T(8,128)} custom-call(bf16[768,3072]{1,0:T(8,128)(2,1)} %matrix_ref.11, bf16[4,640,128]{2,1,0:T(8,128)(2,1)} %bitcast.20), custom_call_target="tpu_custom_call" | custom-call | flops 75497472 | bytes 5373952 | tf_op jit(solution)/shard_map/pallas_call | solution.py:31
  164.6 7.3 %shard_map.85 = (f32[1024,128]{1,0:T(8,128)}, bf16[4,256,128]{2,1,0:T(8,128)(2,1)}, f32[8,128]{1,0:T(8,128)}, f32[1024,128]{1,0:T(8,128)}, f32[1024,128]{1,0:T(8,128)}, /*index=5*/f32[1024,128]{1,0:T(8,128)}) custom-call(bf16[1024,2048]{1,0:T(8,128)(2,1)} %bitcast.16, bf16[4,640,128]{2,1,0:T(8,128)(2,1)} %bitcast.21, ...), custom_call_target="tpu_custom_call" | custom-call | flops 536870912 | bytes 7995392 | tf_op jit(solution)/shard_map/pallas_call | solution.py:31
  172.0 4.5 %all-to-all-start.6 = ((bf16[4,256,128]{2,1,0:T(8,128)(2,1)}), bf16[4,256,128]{2,1,0:T(8,128)(2,1)S(1)}, u32[]{:S(2)}, u32[]{:S(2)}) async-start(bf16[4,256,128]{2,1,0:T(8,128)(2,1)} %get-tuple-element.59), calls=%async_computation.6 | async-start | bytes 524288 | tf_op jit(solution)/shard_map/all_to_all | solution.py:200
  180.8 20.7 %all-gather.4 = bf16[3072,128]{1,0:T(8,128)(2,1)} all-gather(bf16[768,128]{1,0:T(8,128)(2,1)S(1)} %get-tuple-element.58), channel_id=6, replica_groups=mesh['sector'=8,'dof'=4] {'dof'}, dimensions={0}, use_global_device_ids=true | all-gather | bytes 983040 | tf_op jit(solution)/shard_map/all_gather | solution.py:204
  202.2 8.4 %shard_map.88 = (f32[1024,128]{1,0:T(8,128)}, f32[8,104,128]{2,1,0:T(8,128)}, bf16[256,128]{1,0:T(8,128)(2,1)}, bf16[256,128]{1,0:T(8,128)(2,1)}) custom-call(bf16[1024,4096]{1,0:T(8,128)(2,1)} %matrix_ref.10, f32[1,768]{1,0:T(1,128)} %springs_ref.11, f32[8,128]{1,0:T(8,128)} %bitcast.14, bf16[4,768,128]{2,1,0:T(8,128)(2,1)} %bitcast.26, ...), custom_call_target="tpu_custom_call" | custom-call | flops 1073741824 | bytes 9444352 | tf_op jit(solution)/shard_map/pallas_call | solution.py:31
  210.7 4.1 %all-to-all-start.7 = ((f32[8,104,128]{2,1,0:T(8,128)}), f32[8,104,128]{2,1,0:T(8,128)S(1)}, u32[]{:S(2)}, u32[]{:S(2)}) async-start(f32[8,104,128]{2,1,0:T(8,128)} %get-tuple-element.62), calls=%async_computation.7 | async-start | bytes 851968 | tf_op jit(solution)/shard_map/all_to_all | solution.py:200
  217.4 6.9 %collective-permute-done.4.before_ref = bf16[256,128]{1,0:T(8,128)(2,1)S(1)} collective-permute-done((bf16[256,128]{1,0:T(8,128)(2,1)}, bf16[256,128]{1,0:T(8,128)(2,1)S(1)}, u32[]{:S(2)}, u32[]{:S(2)}) %collective-permute-start.4) | collective-permute-done | bytes 65568 | tf_op jit(solution)/shard_map/ppermute | solution.py:244
  224.4 17.2 %all-gather.5 = bf16[2560,128]{1,0:T(8,128)(2,1)} all-gather(bf16[640,128]{1,0:T(8,128)(2,1)S(1)} %shard_map.89), channel_id=7, replica_groups=mesh['sector'=8,'dof'=4] {'dof'}, dimensions={0}, use_global_device_ids=true | all-gather | bytes 819200 | tf_op jit(solution)/shard_map/all_gather | solution.py:204
  241.6 5.3 %shard_map.91 = f32[8,96,128]{2,1,0:T(8,128)} custom-call(bf16[768,3072]{1,0:T(8,128)(2,1)} %matrix_ref.11, bf16[4,640,128]{2,1,0:T(8,128)(2,1)} %bitcast.18), custom_call_target="tpu_custom_call" | custom-call | flops 75497472 | bytes 5373952 | tf_op jit(solution)/shard_map/pallas_call | solution.py:31
  250.4 7.3 %shard_map.90 = (f32[1024,128]{1,0:T(8,128)}, bf16[4,256,128]{2,1,0:T(8,128)(2,1)}, f32[8,128]{1,0:T(8,128)}, f32[1024,128]{1,0:T(8,128)}, f32[1024,128]{1,0:T(8,128)}, /*index=5*/f32[1024,128]{1,0:T(8,128)}) custom-call(bf16[1024,2048]{1,0:T(8,128)(2,1)} %bitcast.17, bf16[4,640,128]{2,1,0:T(8,128)(2,1)} %bitcast.19, ...), custom_call_target="tpu_custom_call" | custom-call | flops 536870912 | bytes 7995392 | tf_op jit(solution)/shard_map/pallas_call | solution.py:31
  262.3 11.9 %all_to_all.50.sums_ref = f32[32,8,128]{2,1,0:T(8,128)S(1)} all-to-all(f32[32,8,128]{2,1,0:T(8,128)S(1)} %get-tuple-element.70), channel_id=1, replica_groups=mesh['sector'=8,'dof'=4] {'sector','dof'}, dimensions={0} | all-to-all | bytes 262144 | tf_op jit(solution)/shard_map/all_to_all | solution.py:200
  (83 shorter events, 45.7 us)
Async XLA Ops:
  0.6 1.0 copy-start
  2.4 29.1 %all-to-all-start = ((bf16[4,256,128]{2,1,0:T(8,128)(2,1)}), bf16[4,256,128]{2,1,0:T(8,128)(2,1)S(1)}, u32[]{:S(2)}, u32[]{:S(2)}) async-start(bf16[4,256,128]{2,1,0:T(8,128)(2,1)} %get-tuple-element.39), calls=%async_computation | async-start | bytes 524288 | tf_op jit(solution)/shard_map/all_to_all | solution.py:200
  40.7 39.0 %copy-start.12 = (f32[1,768]{1,0:T(1,128)S(1)}, f32[1,768]{1,0:T(1,128)}, u32[]{:S(2)}) copy-start(f32[1,768]{1,0:T(1,128)} %springs_ref.11) | copy-start | bytes 9220
  40.7 39.1 %copy-start.23 = (f32[1,1024]{1,0:T(1,128)S(1)}, f32[1,1024]{1,0:T(1,128)}, u32[]{:S(2)}) copy-start(f32[1,1024]{1,0:T(1,128)} %param.7) | copy-start | bytes 12292
  40.7 13.4 %all-to-all-start.1 = ((f32[8,104,128]{2,1,0:T(8,128)}), f32[8,104,128]{2,1,0:T(8,128)S(1)}, u32[]{:S(2)}, u32[]{:S(2)}) async-start(f32[8,104,128]{2,1,0:T(8,128)} %get-tuple-element.42), calls=%async_computation.1 | async-start | bytes 851968 | tf_op jit(solution)/shard_map/all_to_all | solution.py:200
  44.4 9.6 %collective-permute-start = (bf16[256,128]{1,0:T(8,128)(2,1)}, bf16[256,128]{1,0:T(8,128)(2,1)S(1)}, u32[]{:S(2)}, u32[]{:S(2)}) collective-permute-start(bf16[256,128]{1,0:T(8,128)(2,1)} %get-tuple-element.40), channel_id=1, source_target_pairs={{0,4},{4,8},{8,12},{12,16},{16,20},{20,24},{24,28},{28,0},{1,5},{5... | collective-permute-start | bytes 196616 | tf_op jit(solution)/shard_map/ppermute | solution.py:244
  44.9 9.1 %collective-permute-start.1 = (bf16[256,128]{1,0:T(8,128)(2,1)}, bf16[256,128]{1,0:T(8,128)(2,1)S(1)}, u32[]{:S(2)}, u32[]{:S(2)}) collective-permute-start(bf16[256,128]{1,0:T(8,128)(2,1)} %get-tuple-element.41), channel_id=1, source_target_pairs={{4,0},{8,4},{12,8},{16,12},{20,16},{24,20},{28,24},{0,28},{5,1},{9... | collective-permute-start | bytes 196616 | tf_op jit(solution)/shard_map/ppermute | solution.py:245
  76.1 16.4 %copy-start.1 = (f32[1,1024,128]{2,1,0:T(8,128)S(1)}, f32[1,1024,128]{2,1,0:T(8,128)}, u32[]{:S(2)}) copy-start(f32[1,1024,128]{2,1,0:T(8,128)} %field_ref.1) | copy-start | bytes 1572868
  76.1 11.9 %all-to-all-start.2 = ((f32[8,96,128]{2,1,0:T(8,128)}), f32[8,96,128]{2,1,0:T(8,128)S(1)}, u32[]{:S(2)}, u32[]{:S(2)}) async-start(f32[8,96,128]{2,1,0:T(8,128)} %shard_map.81), calls=%async_computation.2 | async-start | bytes 786432 | tf_op jit(solution)/shard_map/all_to_all | solution.py:200
  88.0 28.0 %all-to-all-start.3 = ((bf16[4,256,128]{2,1,0:T(8,128)(2,1)}), bf16[4,256,128]{2,1,0:T(8,128)(2,1)S(1)}, u32[]{:S(2)}, u32[]{:S(2)}) async-start(bf16[4,256,128]{2,1,0:T(8,128)(2,1)} %get-tuple-element.48), calls=%async_computation.3 | async-start | bytes 524288 | tf_op jit(solution)/shard_map/all_to_all | solution.py:200
  92.5 1.0 copy-start.9
  125.1 13.1 %all-to-all-start.4 = ((f32[8,104,128]{2,1,0:T(8,128)}), f32[8,104,128]{2,1,0:T(8,128)S(1)}, u32[]{:S(2)}, u32[]{:S(2)}) async-start(f32[8,104,128]{2,1,0:T(8,128)} %get-tuple-element.51), calls=%async_computation.4 | async-start | bytes 851968 | tf_op jit(solution)/shard_map/all_to_all | solution.py:200
  128.6 9.6 %collective-permute-start.2 = (bf16[256,128]{1,0:T(8,128)(2,1)}, bf16[256,128]{1,0:T(8,128)(2,1)S(1)}, u32[]{:S(2)}, u32[]{:S(2)}) collective-permute-start(bf16[256,128]{1,0:T(8,128)(2,1)} %get-tuple-element.49), channel_id=1, source_target_pairs={{0,4},{4,8},{8,12},{12,16},{16,20},{20,24},{24,28},{28,0},{1,5},{5... | collective-permute-start | bytes 196616 | tf_op jit(solution)/shard_map/ppermute | solution.py:244
  129.1 9.1 %collective-permute-start.3 = (bf16[256,128]{1,0:T(8,128)(2,1)}, bf16[256,128]{1,0:T(8,128)(2,1)S(1)}, u32[]{:S(2)}, u32[]{:S(2)}) collective-permute-start(bf16[256,128]{1,0:T(8,128)(2,1)} %get-tuple-element.50), channel_id=1, source_target_pairs={{4,0},{8,4},{12,8},{16,12},{20,16},{24,20},{28,24},{0,28},{5,1},{9... | collective-permute-start | bytes 196616 | tf_op jit(solution)/shard_map/ppermute | solution.py:245
  160.3 11.7 %all-to-all-start.5 = ((f32[8,96,128]{2,1,0:T(8,128)}), f32[8,96,128]{2,1,0:T(8,128)S(1)}, u32[]{:S(2)}, u32[]{:S(2)}) async-start(f32[8,96,128]{2,1,0:T(8,128)} %shard_map.86), calls=%async_computation.5 | async-start | bytes 786432 | tf_op jit(solution)/shard_map/all_to_all | solution.py:200
  163.7 12.7 %copy-start.13 = (f32[1,768]{1,0:T(1,128)S(1)}, f32[1,768]{1,0:T(1,128)}, u32[]{:S(2)}) copy-start(f32[1,768]{1,0:T(1,128)} %springs_ref.11) | copy-start | bytes 9220
  172.0 29.5 %all-to-all-start.6 = ((bf16[4,256,128]{2,1,0:T(8,128)(2,1)}), bf16[4,256,128]{2,1,0:T(8,128)(2,1)S(1)}, u32[]{:S(2)}, u32[]{:S(2)}) async-start(bf16[4,256,128]{2,1,0:T(8,128)(2,1)} %get-tuple-element.59), calls=%async_computation.6 | async-start | bytes 524288 | tf_op jit(solution)/shard_map/all_to_all | solution.py:200
  176.5 1.0 copy-start.4
  210.7 13.7 %all-to-all-start.7 = ((f32[8,104,128]{2,1,0:T(8,128)}), f32[8,104,128]{2,1,0:T(8,128)S(1)}, u32[]{:S(2)}, u32[]{:S(2)}) async-start(f32[8,104,128]{2,1,0:T(8,128)} %get-tuple-element.62), calls=%async_computation.7 | async-start | bytes 851968 | tf_op jit(solution)/shard_map/all_to_all | solution.py:200
  214.7 9.6 %collective-permute-start.4 = (bf16[256,128]{1,0:T(8,128)(2,1)}, bf16[256,128]{1,0:T(8,128)(2,1)S(1)}, u32[]{:S(2)}, u32[]{:S(2)}) collective-permute-start(bf16[256,128]{1,0:T(8,128)(2,1)} %get-tuple-element.60), channel_id=1, source_target_pairs={{0,4},{4,8},{8,12},{12,16},{16,20},{20,24},{24,28},{28,0},{1,5},{5... | collective-permute-start | bytes 196616 | tf_op jit(solution)/shard_map/ppermute | solution.py:244
  215.2 9.1 %collective-permute-start.5 = (bf16[256,128]{1,0:T(8,128)(2,1)}, bf16[256,128]{1,0:T(8,128)(2,1)S(1)}, u32[]{:S(2)}, u32[]{:S(2)}) collective-permute-start(bf16[256,128]{1,0:T(8,128)(2,1)} %get-tuple-element.61), channel_id=1, source_target_pairs={{4,0},{8,4},{12,8},{16,12},{20,16},{24,20},{28,24},{0,28},{5,1},{9... | collective-permute-start | bytes 196616 | tf_op jit(solution)/shard_map/ppermute | solution.py:245
  246.9 11.8 %copy-start.14 = (f32[1,768]{1,0:T(1,128)S(1)}, f32[1,768]{1,0:T(1,128)}, u32[]{:S(2)}) copy-start(f32[1,768]{1,0:T(1,128)} %springs_ref.11) | copy-start | bytes 9220
  246.9 11.7 %all-to-all-start.8 = ((f32[8,96,128]{2,1,0:T(8,128)}), f32[8,96,128]{2,1,0:T(8,128)S(1)}, u32[]{:S(2)}, u32[]{:S(2)}) async-start(f32[8,96,128]{2,1,0:T(8,128)} %shard_map.91), calls=%async_computation.8 | async-start | bytes 786432 | tf_op jit(solution)/shard_map/all_to_all | solution.py:200
  258.6 1.0 copy-start.2
  (15 other events, 12.1 us)

commit v8 on v7

--- a/solution.py
+++ b/solution.py
@@ -10,7 +10,7 @@
 ITERS = 3
 LANES = 128
 MIB = 1024 * 1024
-IN_FLIGHT = 3
+IN_FLIGHT = 2
 SUM_ROWS = 8
 WHOLE = pl.BlockSpec(memory_space=pltpu.VMEM)
 f32 = jnp.float32
@@ -21,7 +21,7 @@
     return jax.ShapeDtypeStruct(dims, dtype)
 
 
-def call(kernel, outs, operands, parts=0, flops=0):
+def call(kernel, outs, operands, parts=0, flops=0, small=False):
     matrix = operands[0]
     specs = [WHOLE] * len(operands)
     scratch = []
@@ -34,45 +34,46 @@
         out_specs=jax.tree.map(lambda _: WHOLE, outs),
         out_shape=outs,
         scratch_shapes=scratch,
-        compiler_params=pltpu.CompilerParams(vmem_limit_bytes=(60 if parts else 16) * MIB),
+        compiler_params=pltpu.CompilerParams(vmem_limit_bytes=(16 if small else 60) * MIB),
         cost_estimate=pl.CostEstimate(
             flops=flops, bytes_accessed=sum(x.size * x.dtype.itemsize for x in operands), transcendentals=0
         ),
     )(*operands)
 
 
-def columns(widths, source, buffer, sems):
-    copies = []
-    start = 0
-    for at, width in enumerate(widths):
-        block = (slice(None), pl.ds(start, width))
-        copies.append((pltpu.make_async_copy(source.at[block], buffer.at[block], sems.at[at]), block))
-        start += width
-    for copy, _ in copies[:IN_FLIGHT]:
+def row_blocks(source, buffer, sems):
+    count = sems.shape[0]
+    height = source.shape[0] // count
+    blocks = [pl.ds(at * height, height) for at in range(count)]
+    copies = [
+        pltpu.make_async_copy(source.at[rows], buffer.at[rows], sems.at[at])
+        for at, rows in enumerate(blocks)
+    ]
+    for copy in copies[:IN_FLIGHT]:
         copy.start()
-
-    def block(at):
-        copy, columns_at = copies[at]
-        copy.wait()
-        if at + IN_FLIGHT < len(copies):
-            copies[at + IN_FLIGHT][0].start()
-        return buffer[columns_at]
-
-    return block
-
-
-def product_kernel(matrix_ref, springs_ref, sums_ref, *refs):
-    *field_refs, out_ref, load_ref, right_ref, left_ref, buffer, sems = refs
-    count = len(field_refs)
-    parts = field_refs[0].shape[0]
-    block = columns([ref.shape[1] for ref in field_refs] * parts, matrix_ref, buffer, sems)
-    for at in range(parts * count):
-        field = field_refs[at % count][at // count]
-        product = jnp.dot(block(at), field, preferred_element_type=f32)
-        if at == 0:
-            out_ref[...] = product
-        else:
-            out_ref[...] += product
+    for at in range(count):
+        copies[at].wait()
+        if at + IN_FLIGHT < count:
+            copies[at + IN_FLIGHT].start()
+        yield slice(at * height, (at + 1) * height)
+
+
+def product_kernel(summed, matrix_ref, springs_ref, *refs):
+    *refs, out_ref, load_ref, right_ref, left_ref, buffer, sems = refs
+    tops_ref, ends_ref = refs[-2:]
+    parts, top, _ = tops_ref.shape
+    end = ends_ref.shape[1]
+    for rows in row_blocks(matrix_ref, buffer, sems):
+        total = None
+        for part in range(parts):
+            start = part * (top + end)
+            for width, field in ((top, tops_ref[part]), (end, ends_ref[part])):
+                product = jnp.dot(
+                    buffer[rows, start : start + width], field, preferred_element_type=f32
+                )
+                total = product if total is None else total + product
+                start += width
+        out_ref[rows] = total
 
     sectors, height, _ = load_ref.shape
     cases = out_ref.shape[1] // sectors
@@ -85,7 +86,7 @@
         for s in range(sectors):
             load_ref[s, at * cases : (at + 1) * cases] = turned[s * cases : (s + 1) * cases]
     for s in range(sectors):
-        load_ref[s, height - SUM_ROWS :] = sums_ref[...]
+        load_ref[s, height - SUM_ROWS :] = refs[0][...] if summed else jnp.zeros((SUM_ROWS, LANES), f32)
 
 
 def pack_kernel(before_ref, after_ref, parts_ref, out_ref):
@@ -113,36 +114,42 @@
     parts = pieces_ref.shape[0]
     height = out_ref.shape[1]
     chunks = height // cases
-    depth = chunks * LANES
     first = pieces_ref.shape[1] - 4 * SUM_ROWS - height
-    block = columns([depth] * parts, matrix_ref, buffer, sems)
-    total = None
-    for part in range(parts):
-        load = jnp.concatenate(
-            [pieces_ref[part, first + c * cases : first + (c + 1) * cases] for c in range(chunks)],
-            axis=1,
-        )
-        product = lax.dot_general(
-            load, block(part), (((1,), (1,)), ((), ())), preferred_element_type=f32
-        )
-        total = product if total is None else total + product
-    for c in range(chunks):
-        for s in range(out_ref.shape[0]):
-            out_ref[s, c * cases : (c + 1) * cases] = total[:, c * LANES : (c + 1) * LANES]
+    load = jnp.concatenate(
+        [
+            pieces_ref[part, first + c * cases : first + (c + 1) * cases]
+            for part in range(parts)
+            for c in range(chunks)
+        ],
+        axis=1,
+    )
+    for rows in row_blocks(matrix_ref, buffer, sems):
+        hub = lax.dot_general(
+            load, buffer[rows], (((1,), (1,)), ((), ())), preferred_element_type=f32
+        )
+        for c in range(rows.start // LANES, rows.stop // LANES):
+            at = c * LANES - rows.start
+            for s in range(out_ref.shape[0]):
+                out_ref[s, c * cases : (c + 1) * cases] = hub[:, at : at + LANES]
 
 
 def base_kernel(first, matrix_ref, pieces_ref, product_ref, stiffness_ref, *refs):
     if first:
         base_ref, ends_ref, factor_ref, buffer, sems = refs
     else:
-        image_ref, residual_ref, precon_ref, solution_ref, *refs = refs
-        base_ref, ends_ref, factor_ref, left_ref, newer_ref, better_ref, buffer, sems = refs
+        *refs, base_ref, ends_ref, factor_ref, left_ref, newer_ref, better_ref, buffer, sems = refs
+        image_ref, residual_ref, precon_ref = refs[:3]
     parts = pieces_ref.shape[0]
     depth = matrix_ref.shape[1] // parts
-    block = columns([depth] * parts, matrix_ref, buffer, sems)
-    base_ref[...] = stiffness_ref[...] * product_ref[...]
-    for part in range(parts):
-        base_ref[...] += jnp.dot(block(part), pieces_ref[part, :depth], preferred_element_type=f32)
+    for rows in row_blocks(matrix_ref, buffer, sems):
+        total = stiffness_ref[rows] * product_ref[rows]
+        for part in range(parts):
+            total += jnp.dot(
+                buffer[rows, part * depth : (part + 1) * depth],
+                pieces_ref[part, :depth],
+                preferred_element_type=f32,
+            )
+        base_ref[rows] = total
     if first:
         factor_ref[...] = jnp.ones_like(factor_ref)
     else:
@@ -156,7 +163,8 @@
         factor_ref[...] = jnp.broadcast_to(-alpha, factor_ref.shape)
         base_ref[...] = image_ref[...] - alpha * base_ref[...]
         left_ref[...] = residual_ref[...] - alpha * image_ref[...]
-        better_ref[...] = solution_ref[...] + alpha * precon_ref[...]
+        gain = alpha * precon_ref[...]
+        better_ref[...] = refs[3][...] + gain if len(refs) > 3 else gain
         newer_ref[...] = precon_ref[...] - alpha * product_ref[...]
     end = base_ref[base_ref.shape[0] - ends_ref.shape[1] :].astype(bf16)
     ends_ref[...] = jnp.broadcast_to(end[None], ends_ref.shape)
@@ -180,10 +188,10 @@
     lower = jnp.sum(image * image, axis=0, keepdims=True)
     rest = jnp.zeros((SUM_ROWS - 2, image.shape[1]), f32)
     sums = jnp.concatenate([upper, lower, rest], axis=0)
-    sums_ref[...] = jnp.broadcast_to(sums[None], sums_ref.shape)
-
-
-def last_kernel(sums_ref, precon_ref, image_ref, solution_ref, residual_ref, newer_ref, left_ref):
+    sums_ref[...] = jnp.broadcast_to(sums, sums_ref.shape)
+
+
+def last_kernel(sums_ref, image_ref, residual_ref, precon_ref, solution_ref, newer_ref, left_ref):
     alpha = alpha_from(jnp.sum(sums_ref[...], axis=0))
     newer_ref[0] = solution_ref[...] + alpha * precon_ref[...]
     left_ref[0] = residual_ref[...] - alpha * image_ref[...]
@@ -227,18 +235,16 @@
 
     stiffness = diagonal[0] + jnp.pad(springs[0], (0, quarter))
     stiffness = jnp.broadcast_to(stiffness[:, None], (rows, loads))
-    solution = jnp.zeros_like(residual)
-    image = precon = None
-    sums = jnp.zeros((1, SUM_ROWS, loads), f32)
+    state = sums = ()
 
     top, ends = call(round_kernel, (top_shape, ends_shape), (rhs,))
     for step in range(ITERS):
         first, last = step == 0, step == ITERS - 1
         product, load, right, left = call(
-            product_kernel,
+            functools.partial(product_kernel, not first),
             (full, shape(sectors, height + SUM_ROWS, LANES), face, face),
-            (precond, springs, sums[0], gathered(top), exchange(ends, "dof")),
-            parts=2 * parts,
+            (precond, springs, *sums, gathered(top), exchange(ends, "dof")),
+            parts=rows // (2 * LANES),
             flops=2 * precond.size * loads,
         )
         before = lax.ppermute(right, "sector", onward)
@@ -247,37 +253,38 @@
             pack_kernel,
             shape(2 * quarter + height + 4 * SUM_ROWS, loads, dtype=bf16),
             (before, after, exchange(load, "sector")),
+            small=True,
         )
         pieces = gathered(packed)
         hub = call(
             functools.partial(hub_kernel, cases),
             shape(sectors, height, LANES),
             (hub_inverse, pieces),
-            parts=parts,
+            parts=attached // LANES // 2 if attached % (2 * LANES) == 0 else attached // LANES,
             flops=2 * hub_inverse.size * cases,
         )
         hubs = exchange(hub, "sector")
-        state = () if first else (image, residual, precon, solution)
         base, ends, factor, *state = call(
             functools.partial(base_kernel, first),
             (full, ends_shape, shape(SUM_ROWS, loads)) + (() if first else (full, full, full)),
             (coupling[0], pieces, product, stiffness, *state),
-            parts=parts,
+            parts=rows // (2 * LANES),
             flops=2 * coupling.size * loads,
         )
-        if first:
-            precon = product
-        else:
-            residual, precon, solution = state
+        residual, precon, *solution = (residual, product) if first else state
         image, top, sums = call(
             image_kernel,
-            (full, top_shape, shape(sectors * parts if last else 1, SUM_ROWS, loads)),
+            (
+                full,
+                top_shape,
+                shape(sectors * parts, SUM_ROWS, loads) if last else shape(SUM_ROWS, loads),
+            ),
             (base, hubs, springs, factor, residual),
         )
+        state = (image, residual, precon, *solution)
+        sums = (sums,)
     out = shape(1, rows, loads)
-    return call(
-        last_kernel, (out, out), (exchange(sums, ("sector", "dof")), precon, image, solution, residual)
-    )
+    return call(last_kernel, (out, out), (exchange(*sums, ("sector", "dof")), *state))
 
 
 def plain_body(rhs, diagonal, coupling, springs, precond, hub_inverse):

time: 280 us -> 270 us (0.964)
  local copies, waits for them, and re-layouts: 18.1 us -> 3.86 us
  Pallas kernels: 65.1 us -> 69 us
    unnamed x48 -> x16, local copies, waits for them, and re-layouts: 15.6 us -> 2.87 us
    pallas_call x17, Pallas kernels: 65.1 us -> 69 us  [call(): pl.pallas_call(kernel, in_specs=specs, out_specs=jax.tree.map(lambda _: W...]
  transfers between devices with their start and end apart: 15 -> 15, of which waited for: 6 -> 6; matrix products, arithmetic and copies ran while one was open for 1% -> 0% of each run, Pallas kernels for 8% -> 9%
where the time goes in v8:
time: 270 us; the launch traced here: 268 us
  blocking collectives  126 us (47%)
  Pallas kernels  69 us (26%)
  starting transfers between devices  43.5 us (16%)
  waiting for transfers between devices  24.9 us (9%)
  local copies, waits for them, and re-layouts  3.86 us (1%)
    all_gather x6, blocking collectives, gathered(): return lax.all_gather(field, 'dof', axis=0)  114 us
    pallas_call x17, Pallas kernels, call(): pl.pallas_call(kernel, in_specs=specs, out_specs=jax.tree.map(lambda _: W...  69 us
    all_to_all x9, starting transfers between devices, exchange(): return lax.all_to_all(blocks, axes, split_axis=0, concat_axis=0)  35.4 us
    ppermute x3, waiting for transfers between devices, tiled_body(): before = lax.ppermute(right, 'sector', onward)  20.6 us
    all_to_all x1, blocking collectives, exchange(): return lax.all_to_all(blocks, axes, split_axis=0, concat_axis=0)  12.6 us
    ppermute x3, starting transfers between devices, tiled_body(): after = lax.ppermute(left, 'sector', backward)  6.74 us
  transfers between devices with their start and end apart: 15, of which 6 were waited for; matrix products, arithmetic and copies ran while one was open for 0% of the time, Pallas kernels for 9%

profile of v8, /device:TPU:0, one launch (start us, length us, event | category | flops | bytes accessed | tf_op | source)
XLA Modules:
  0.0 268.5 jit_solution(16676514579077492936)
XLA Ops:
  2.5 6.3 %all-to-all-start = ((bf16[4,256,128]{2,1,0:T(8,128)(2,1)}), bf16[4,256,128]{2,1,0:T(8,128)(2,1)S(1)}, u32[]{:S(2)}, u32[]{:S(2)}) async-start(bf16[4,256,128]{2,1,0:T(8,128)(2,1)} %get-tuple-element.39), calls=%async_computation | async-start | bytes 524288 | tf_op jit(solution)/shard_map/all_to_all | solution.py:208
  8.8 22.8 %all-gather = bf16[3072,128]{1,0:T(8,128)(2,1)} all-gather(bf16[768,128]{1,0:T(8,128)(2,1)} %get-tuple-element.38), channel_id=2, replica_groups=mesh['sector'=8,'dof'=4] {'dof'}, dimensions={0}, use_global_device_ids=true | all-gather | bytes 983040 | tf_op jit(solution)/shard_map/all_gather | solution.py:212
  32.3 6.9 %shard_map.78 = (f32[1024,128]{1,0:T(8,128)}, f32[8,104,128]{2,1,0:T(8,128)}, bf16[256,128]{1,0:T(8,128)(2,1)}, bf16[256,128]{1,0:T(8,128)(2,1)}) custom-call(bf16[1024,4096]{1,0:T(8,128)(2,1)} %matrix_ref.10, f32[1,768]{1,0:T(1,128)} %springs_ref.11, bf16[4,768,128]{2,1,0:T(8,128)(2,1)} %bitcast.22, bf16[4,256,128]{2,1,0:T(8,128)(2,1)} %copy-done.5), custom_call_target="tpu_custom_call" | custom-call | flops 1073741824 | bytes 9440256 | tf_op jit(solution)/shard_map/pallas_call | solution.py:31
  39.2 3.7 %all-to-all-start.1 = ((f32[8,104,128]{2,1,0:T(8,128)}), f32[8,104,128]{2,1,0:T(8,128)S(1)}, u32[]{:S(2)}, u32[]{:S(2)}) async-start(f32[8,104,128]{2,1,0:T(8,128)} %get-tuple-element.42), calls=%async_computation.1 | async-start | bytes 851968 | tf_op jit(solution)/shard_map/all_to_all | solution.py:208
  45.7 6.9 %collective-permute-done.before_ref = bf16[256,128]{1,0:T(8,128)(2,1)S(1)} collective-permute-done((bf16[256,128]{1,0:T(8,128)(2,1)}, bf16[256,128]{1,0:T(8,128)(2,1)S(1)}, u32[]{:S(2)}, u32[]{:S(2)}) %collective-permute-start) | collective-permute-done | bytes 65568 | tf_op jit(solution)/shard_map/ppermute | solution.py:250
  52.6 16.8 %all-gather.1 = bf16[2560,128]{1,0:T(8,128)(2,1)} all-gather(bf16[640,128]{1,0:T(8,128)(2,1)S(1)} %shard_map.79), channel_id=3, replica_groups=mesh['sector'=8,'dof'=4] {'dof'}, dimensions={0}, use_global_device_ids=true | all-gather | bytes 819200 | tf_op jit(solution)/shard_map/all_gather | solution.py:212
  69.4 5.7 %shard_map.81 = f32[8,96,128]{2,1,0:T(8,128)} custom-call(bf16[768,3072]{1,0:T(8,128)(2,1)} %matrix_ref.11, bf16[4,640,128]{2,1,0:T(8,128)(2,1)} %bitcast.16), custom_call_target="tpu_custom_call" | custom-call | flops 75497472 | bytes 5373952 | tf_op jit(solution)/shard_map/pallas_call | solution.py:31
  79.6 5.7 %shard_map.80 = (f32[1024,128]{1,0:T(8,128)}, bf16[4,256,128]{2,1,0:T(8,128)(2,1)}, f32[8,128]{1,0:T(8,128)}) custom-call(bf16[1024,2048]{1,0:T(8,128)(2,1)} %bitcast.9, bf16[4,640,128]{2,1,0:T(8,128)(2,1)} %bitcast.17, f32[1024,128]{1,0:T(8,128)} %get-tuple-element.43.product_ref.refs_2_, f32[1024,128]{1,0:T(8,128)} %broadcast_in_dim.2.stiffness_ref), custom_call_target="tpu_custom_call" | custom-call | flops 536870912 | bytes 5898240 | tf_op jit(solution)/shard_map/pallas_call | solution.py:31
  86.9 4.5 %all-to-all-start.3 = ((bf16[4,256,128]{2,1,0:T(8,128)(2,1)}), bf16[4,256,128]{2,1,0:T(8,128)(2,1)S(1)}, u32[]{:S(2)}, u32[]{:S(2)}) async-start(bf16[4,256,128]{2,1,0:T(8,128)(2,1)} %get-tuple-element.48), calls=%async_computation.3 | async-start | bytes 524288 | tf_op jit(solution)/shard_map/all_to_all | solution.py:208
  93.7 20.4 %all-gather.2 = bf16[3072,128]{1,0:T(8,128)(2,1)} all-gather(bf16[768,128]{1,0:T(8,128)(2,1)} %get-tuple-element.47), channel_id=4, replica_groups=mesh['sector'=8,'dof'=4] {'dof'}, dimensions={0}, use_global_device_ids=true | all-gather | bytes 983040 | tf_op jit(solution)/shard_map/all_gather | solution.py:212
  114.8 6.9 %shard_map.83 = (f32[1024,128]{1,0:T(8,128)}, f32[8,104,128]{2,1,0:T(8,128)}, bf16[256,128]{1,0:T(8,128)(2,1)}, bf16[256,128]{1,0:T(8,128)(2,1)}) custom-call(bf16[1024,4096]{1,0:T(8,128)(2,1)} %matrix_ref.10, f32[1,768]{1,0:T(1,128)} %springs_ref.11, f32[8,128]{1,0:T(8,128)} %get-tuple-element.46.refs_0_, bf16[4,768,128]{2,1,0:T(8,128)(2,1)} %bitcast.20, ...), custom_call_target="tpu_custom_call" | custom-call | flops 1073741824 | bytes 9444352 | tf_op jit(solution)/shard_map/pallas_call | solution.py:31
  121.8 3.5 %all-to-all-start.4 = ((f32[8,104,128]{2,1,0:T(8,128)}), f32[8,104,128]{2,1,0:T(8,128)S(1)}, u32[]{:S(2)}, u32[]{:S(2)}) async-start(f32[8,104,128]{2,1,0:T(8,128)} %get-tuple-element.51), calls=%async_computation.4 | async-start | bytes 851968 | tf_op jit(solution)/shard_map/all_to_all | solution.py:208
  127.9 6.9 %collective-permute-done.2.before_ref = bf16[256,128]{1,0:T(8,128)(2,1)S(1)} collective-permute-done((bf16[256,128]{1,0:T(8,128)(2,1)}, bf16[256,128]{1,0:T(8,128)(2,1)S(1)}, u32[]{:S(2)}, u32[]{:S(2)}) %collective-permute-start.2) | collective-permute-done | bytes 65568 | tf_op jit(solution)/shard_map/ppermute | solution.py:250
  134.8 17.1 %all-gather.3 = bf16[2560,128]{1,0:T(8,128)(2,1)} all-gather(bf16[640,128]{1,0:T(8,128)(2,1)S(1)} %shard_map.84), channel_id=5, replica_groups=mesh['sector'=8,'dof'=4] {'dof'}, dimensions={0}, use_global_device_ids=true | all-gather | bytes 819200 | tf_op jit(solution)/shard_map/all_gather | solution.py:212
  152.0 5.7 %shard_map.86 = f32[8,96,128]{2,1,0:T(8,128)} custom-call(bf16[768,3072]{1,0:T(8,128)(2,1)} %matrix_ref.11, bf16[4,640,128]{2,1,0:T(8,128)(2,1)} %bitcast.12), custom_call_target="tpu_custom_call" | custom-call | flops 75497472 | bytes 5373952 | tf_op jit(solution)/shard_map/pallas_call | solution.py:31
  157.7 3.6 %all-to-all-start.5 = ((f32[8,96,128]{2,1,0:T(8,128)}), f32[8,96,128]{2,1,0:T(8,128)S(1)}, u32[]{:S(2)}, u32[]{:S(2)}) async-start(f32[8,96,128]{2,1,0:T(8,128)} %shard_map.86), calls=%async_computation.5 | async-start | bytes 786432 | tf_op jit(solution)/shard_map/all_to_all | solution.py:208
  161.4 6.7 %shard_map.85 = (f32[1024,128]{1,0:T(8,128)}, bf16[4,256,128]{2,1,0:T(8,128)(2,1)}, f32[8,128]{1,0:T(8,128)}, f32[1024,128]{1,0:T(8,128)}, f32[1024,128]{1,0:T(8,128)}, /*index=5*/f32[1024,128]{1,0:T(8,128)}) custom-call(bf16[1024,2048]{1,0:T(8,128)(2,1)} %bitcast.10, bf16[4,640,128]{2,1,0:T(8,128)(2,1)} %bitcast.13, ...), custom_call_target="tpu_custom_call" | custom-call | flops 536870912 | bytes 7471104 | tf_op jit(solution)/shard_map/pallas_call | solution.py:31
  175.2 19.8 %all-gather.4 = bf16[3072,128]{1,0:T(8,128)(2,1)} all-gather(bf16[768,128]{1,0:T(8,128)(2,1)} %get-tuple-element.58), channel_id=6, replica_groups=mesh['sector'=8,'dof'=4] {'dof'}, dimensions={0}, use_global_device_ids=true | all-gather | bytes 983040 | tf_op jit(solution)/shard_map/all_gather | solution.py:212
  195.7 6.9 %shard_map.88 = (f32[1024,128]{1,0:T(8,128)}, f32[8,104,128]{2,1,0:T(8,128)}, bf16[256,128]{1,0:T(8,128)(2,1)}, bf16[256,128]{1,0:T(8,128)(2,1)}) custom-call(bf16[1024,4096]{1,0:T(8,128)(2,1)} %matrix_ref.10, f32[1,768]{1,0:T(1,128)} %springs_ref.11, f32[8,128]{1,0:T(8,128)} %get-tuple-element.57.refs_0_, bf16[4,768,128]{2,1,0:T(8,128)(2,1)} %bitcast.21, ...), custom_call_target="tpu_custom_call" | custom-call | flops 1073741824 | bytes 9444352 | tf_op jit(solution)/shard_map/pallas_call | solution.py:31
  208.8 6.9 %collective-permute-done.4.before_ref = bf16[256,128]{1,0:T(8,128)(2,1)S(1)} collective-permute-done((bf16[256,128]{1,0:T(8,128)(2,1)}, bf16[256,128]{1,0:T(8,128)(2,1)S(1)}, u32[]{:S(2)}, u32[]{:S(2)}) %collective-permute-start.4) | collective-permute-done | bytes 65568 | tf_op jit(solution)/shard_map/ppermute | solution.py:250
  215.7 16.9 %all-gather.5 = bf16[2560,128]{1,0:T(8,128)(2,1)} all-gather(bf16[640,128]{1,0:T(8,128)(2,1)S(1)} %shard_map.89), channel_id=7, replica_groups=mesh['sector'=8,'dof'=4] {'dof'}, dimensions={0}, use_global_device_ids=true | all-gather | bytes 819200 | tf_op jit(solution)/shard_map/all_gather | solution.py:212
  232.6 5.8 %shard_map.91 = f32[8,96,128]{2,1,0:T(8,128)} custom-call(bf16[768,3072]{1,0:T(8,128)(2,1)} %matrix_ref.11, bf16[4,640,128]{2,1,0:T(8,128)(2,1)} %bitcast.14), custom_call_target="tpu_custom_call" | custom-call | flops 75497472 | bytes 5373952 | tf_op jit(solution)/shard_map/pallas_call | solution.py:31
  241.9 6.9 %shard_map.90 = (f32[1024,128]{1,0:T(8,128)}, bf16[4,256,128]{2,1,0:T(8,128)(2,1)}, f32[8,128]{1,0:T(8,128)}, f32[1024,128]{1,0:T(8,128)}, f32[1024,128]{1,0:T(8,128)}, /*index=5*/f32[1024,128]{1,0:T(8,128)}) custom-call(bf16[1024,2048]{1,0:T(8,128)(2,1)} %bitcast.11, bf16[4,640,128]{2,1,0:T(8,128)(2,1)} %bitcast.15, ...), custom_call_target="tpu_custom_call" | custom-call | flops 536870912 | bytes 7995392 | tf_op jit(solution)/shard_map/pallas_call | solution.py:31
  253.3 12.6 %all_to_all.50.sums_ref = f32[32,8,128]{2,1,0:T(8,128)} all-to-all(f32[32,8,128]{2,1,0:T(8,128)} %get-tuple-element.70), channel_id=1, replica_groups=mesh['sector'=8,'dof'=4] {'sector','dof'}, dimensions={0} | all-to-all | bytes 262144 | tf_op jit(solution)/shard_map/all_to_all | solution.py:208
  (49 shorter events, 41.7 us)
Async XLA Ops:
  2.5 29.1 %all-to-all-start = ((bf16[4,256,128]{2,1,0:T(8,128)(2,1)}), bf16[4,256,128]{2,1,0:T(8,128)(2,1)S(1)}, u32[]{:S(2)}, u32[]{:S(2)}) async-start(bf16[4,256,128]{2,1,0:T(8,128)(2,1)} %get-tuple-element.39), calls=%async_computation | async-start | bytes 524288 | tf_op jit(solution)/shard_map/all_to_all | solution.py:208
  31.6 0.7 copy-start.5
  39.2 39.4 %copy-start.6 = (f32[1,768]{1,0:T(1,128)S(1)}, f32[1,768]{1,0:T(1,128)}, u32[]{:S(2)}) copy-start(f32[1,768]{1,0:T(1,128)} %springs_ref.11) | copy-start | bytes 9220
  39.2 39.4 %copy-start.7 = (f32[1,1024]{1,0:T(1,128)S(1)}, f32[1,1024]{1,0:T(1,128)}, u32[]{:S(2)}) copy-start(f32[1,1024]{1,0:T(1,128)} %param.7) | copy-start | bytes 12292
  39.2 13.4 %all-to-all-start.1 = ((f32[8,104,128]{2,1,0:T(8,128)}), f32[8,104,128]{2,1,0:T(8,128)S(1)}, u32[]{:S(2)}, u32[]{:S(2)}) async-start(f32[8,104,128]{2,1,0:T(8,128)} %get-tuple-element.42), calls=%async_computation.1 | async-start | bytes 851968 | tf_op jit(solution)/shard_map/all_to_all | solution.py:208
  43.0 9.6 %collective-permute-start = (bf16[256,128]{1,0:T(8,128)(2,1)}, bf16[256,128]{1,0:T(8,128)(2,1)S(1)}, u32[]{:S(2)}, u32[]{:S(2)}) collective-permute-start(bf16[256,128]{1,0:T(8,128)(2,1)} %get-tuple-element.40), channel_id=1, source_target_pairs={{0,4},{4,8},{8,12},{12,16},{16,20},{20,24},{24,28},{28,0},{1,5},{5... | collective-permute-start | bytes 196616 | tf_op jit(solution)/shard_map/ppermute | solution.py:250
  43.5 9.1 %collective-permute-start.1 = (bf16[256,128]{1,0:T(8,128)(2,1)}, bf16[256,128]{1,0:T(8,128)(2,1)S(1)}, u32[]{:S(2)}, u32[]{:S(2)}) collective-permute-start(bf16[256,128]{1,0:T(8,128)(2,1)} %get-tuple-element.41), channel_id=1, source_target_pairs={{4,0},{8,4},{12,8},{16,12},{20,16},{24,20},{28,24},{0,28},{5,1},{9... | collective-permute-start | bytes 196616 | tf_op jit(solution)/shard_map/ppermute | solution.py:251
  75.1 11.7 %all-to-all-start.2 = ((f32[8,96,128]{2,1,0:T(8,128)}), f32[8,96,128]{2,1,0:T(8,128)S(1)}, u32[]{:S(2)}, u32[]{:S(2)}) async-start(f32[8,96,128]{2,1,0:T(8,128)} %shard_map.81), calls=%async_computation.2 | async-start | bytes 786432 | tf_op jit(solution)/shard_map/all_to_all | solution.py:208
  86.9 4.5 %copy-start = (f32[8,96,128]{2,1,0:T(8,128)}, f32[8,96,128]{2,1,0:T(8,128)S(1)}, u32[]{:S(2)}) copy-start(f32[8,96,128]{2,1,0:T(8,128)S(1)} %all-to-all-done.2.hubs_ref) | copy-start | bytes 1179652
  86.9 27.2 %all-to-all-start.3 = ((bf16[4,256,128]{2,1,0:T(8,128)(2,1)}), bf16[4,256,128]{2,1,0:T(8,128)(2,1)S(1)}, u32[]{:S(2)}, u32[]{:S(2)}) async-start(bf16[4,256,128]{2,1,0:T(8,128)(2,1)} %get-tuple-element.48), calls=%async_computation.3 | async-start | bytes 524288 | tf_op jit(solution)/shard_map/all_to_all | solution.py:208
  114.1 0.7 copy-start.3
  121.8 13.0 %all-to-all-start.4 = ((f32[8,104,128]{2,1,0:T(8,128)}), f32[8,104,128]{2,1,0:T(8,128)S(1)}, u32[]{:S(2)}, u32[]{:S(2)}) async-start(f32[8,104,128]{2,1,0:T(8,128)} %get-tuple-element.51), calls=%async_computation.4 | async-start | bytes 851968 | tf_op jit(solution)/shard_map/all_to_all | solution.py:208
  125.2 9.5 %collective-permute-start.2 = (bf16[256,128]{1,0:T(8,128)(2,1)}, bf16[256,128]{1,0:T(8,128)(2,1)S(1)}, u32[]{:S(2)}, u32[]{:S(2)}) collective-permute-start(bf16[256,128]{1,0:T(8,128)(2,1)} %get-tuple-element.49), channel_id=1, source_target_pairs={{0,4},{4,8},{8,12},{12,16},{16,20},{20,24},{24,28},{28,0},{1,5},{5... | collective-permute-start | bytes 196616 | tf_op jit(solution)/shard_map/ppermute | solution.py:250
  125.6 9.1 %collective-permute-start.3 = (bf16[256,128]{1,0:T(8,128)(2,1)}, bf16[256,128]{1,0:T(8,128)(2,1)S(1)}, u32[]{:S(2)}, u32[]{:S(2)}) collective-permute-start(bf16[256,128]{1,0:T(8,128)(2,1)} %get-tuple-element.50), channel_id=1, source_target_pairs={{4,0},{8,4},{12,8},{16,12},{20,16},{24,20},{28,24},{0,28},{5,1},{9... | collective-permute-start | bytes 196616 | tf_op jit(solution)/shard_map/ppermute | solution.py:251
  157.7 11.7 %all-to-all-start.5 = ((f32[8,96,128]{2,1,0:T(8,128)}), f32[8,96,128]{2,1,0:T(8,128)S(1)}, u32[]{:S(2)}, u32[]{:S(2)}) async-start(f32[8,96,128]{2,1,0:T(8,128)} %shard_map.86), calls=%async_computation.5 | async-start | bytes 786432 | tf_op jit(solution)/shard_map/all_to_all | solution.py:208
  169.5 3.4 %copy-start.1 = (f32[8,96,128]{2,1,0:T(8,128)}, f32[8,96,128]{2,1,0:T(8,128)S(1)}, u32[]{:S(2)}) copy-start(f32[8,96,128]{2,1,0:T(8,128)S(1)} %all-to-all-done.5.hubs_ref) | copy-start | bytes 1179652
  169.5 25.6 %all-to-all-start.6 = ((bf16[4,256,128]{2,1,0:T(8,128)(2,1)}), bf16[4,256,128]{2,1,0:T(8,128)(2,1)S(1)}, u32[]{:S(2)}, u32[]{:S(2)}) async-start(bf16[4,256,128]{2,1,0:T(8,128)(2,1)} %get-tuple-element.59), calls=%async_computation.6 | async-start | bytes 524288 | tf_op jit(solution)/shard_map/all_to_all | solution.py:208
  195.0 0.7 copy-start.4
  202.7 13.0 %all-to-all-start.7 = ((f32[8,104,128]{2,1,0:T(8,128)}), f32[8,104,128]{2,1,0:T(8,128)S(1)}, u32[]{:S(2)}, u32[]{:S(2)}) async-start(f32[8,104,128]{2,1,0:T(8,128)} %get-tuple-element.62), calls=%async_computation.7 | async-start | bytes 851968 | tf_op jit(solution)/shard_map/all_to_all | solution.py:208
  206.2 9.5 %collective-permute-start.4 = (bf16[256,128]{1,0:T(8,128)(2,1)}, bf16[256,128]{1,0:T(8,128)(2,1)S(1)}, u32[]{:S(2)}, u32[]{:S(2)}) collective-permute-start(bf16[256,128]{1,0:T(8,128)(2,1)} %get-tuple-element.60), channel_id=1, source_target_pairs={{0,4},{4,8},{8,12},{12,16},{16,20},{20,24},{24,28},{28,0},{1,5},{5... | collective-permute-start | bytes 196616 | tf_op jit(solution)/shard_map/ppermute | solution.py:250
  206.6 9.1 %collective-permute-start.5 = (bf16[256,128]{1,0:T(8,128)(2,1)}, bf16[256,128]{1,0:T(8,128)(2,1)S(1)}, u32[]{:S(2)}, u32[]{:S(2)}) collective-permute-start(bf16[256,128]{1,0:T(8,128)(2,1)} %get-tuple-element.61), channel_id=1, source_target_pairs={{4,0},{8,4},{12,8},{16,12},{20,16},{24,20},{28,24},{0,28},{5,1},{9... | collective-permute-start | bytes 196616 | tf_op jit(solution)/shard_map/ppermute | solution.py:251
  238.4 11.7 %all-to-all-start.8 = ((f32[8,96,128]{2,1,0:T(8,128)}), f32[8,96,128]{2,1,0:T(8,128)S(1)}, u32[]{:S(2)}, u32[]{:S(2)}) async-start(f32[8,96,128]{2,1,0:T(8,128)} %shard_map.91), calls=%async_computation.8 | async-start | bytes 786432 | tf_op jit(solution)/shard_map/all_to_all | solution.py:208
  250.1 0.7 copy-start.2

commit v9 on v8

--- a/solution.py
+++ b/solution.py
@@ -10,7 +10,9 @@
 ITERS = 3
 LANES = 128
 MIB = 1024 * 1024
-IN_FLIGHT = 2
+IN_FLIGHT = 8
+PIECE_ROWS = 64
+BLOCK_ROWS = 256
 SUM_ROWS = 8
 WHOLE = pl.BlockSpec(memory_space=pltpu.VMEM)
 f32 = jnp.float32
@@ -21,13 +23,13 @@
     return jax.ShapeDtypeStruct(dims, dtype)
 
 
-def call(kernel, outs, operands, parts=0, flops=0, small=False):
+def call(kernel, outs, operands, streamed=False, flops=0, small=False):
     matrix = operands[0]
     specs = [WHOLE] * len(operands)
     scratch = []
-    if parts:
+    if streamed:
         specs[0] = pl.BlockSpec(memory_space=pltpu.HBM)
-        scratch = [pltpu.VMEM(matrix.shape, matrix.dtype), pltpu.SemaphoreType.DMA((parts,))]
+        scratch = [pltpu.VMEM(matrix.shape, matrix.dtype), pltpu.SemaphoreType.DMA((matrix.shape[0] // PIECE_ROWS,))]
     return pl.pallas_call(
         kernel,
         in_specs=specs,
@@ -44,10 +46,10 @@
 def row_blocks(source, buffer, sems):
     count = sems.shape[0]
     height = source.shape[0] // count
-    blocks = [pl.ds(at * height, height) for at in range(count)]
+    pieces = [pl.ds(at * height, height) for at in range(count)]
     copies = [
         pltpu.make_async_copy(source.at[rows], buffer.at[rows], sems.at[at])
-        for at, rows in enumerate(blocks)
+        for at, rows in enumerate(pieces)
     ]
     for copy in copies[:IN_FLIGHT]:
         copy.start()
@@ -55,12 +57,12 @@
         copies[at].wait()
         if at + IN_FLIGHT < count:
             copies[at + IN_FLIGHT].start()
-        yield slice(at * height, (at + 1) * height)
-
-
-def product_kernel(summed, matrix_ref, springs_ref, *refs):
-    *refs, out_ref, load_ref, right_ref, left_ref, buffer, sems = refs
-    tops_ref, ends_ref = refs[-2:]
+        stop = (at + 1) * height
+        if stop % BLOCK_ROWS == 0:
+            yield slice(stop - BLOCK_ROWS, stop)
+
+
+def product_kernel(matrix_ref, tops_ref, ends_ref, out_ref, right_ref, left_ref, buffer, sems):
     parts, top, _ = tops_ref.shape
     end = ends_ref.shape[1]
     for rows in row_blocks(matrix_ref, buffer, sems):
@@ -74,19 +76,22 @@
                 total = product if total is None else total + product
                 start += width
         out_ref[rows] = total
-
-    sectors, height, _ = load_ref.shape
-    cases = out_ref.shape[1] // sectors
     quarter = right_ref.shape[0]
     left_ref[...] = out_ref[:quarter].astype(bf16)
     right_ref[...] = out_ref[quarter : 2 * quarter].astype(bf16)
+
+
+def load_kernel(product_ref, springs_ref, *refs):
+    load_ref = refs[-1]
+    sectors, height, loads = load_ref.shape
+    cases = loads // sectors
     for at in range((height - SUM_ROWS) // cases):
         rows = slice(at * LANES, (at + 1) * LANES)
-        turned = out_ref[rows].T * springs_ref[:, rows]
+        turned = product_ref[rows].T * springs_ref[:, rows]
         for s in range(sectors):
             load_ref[s, at * cases : (at + 1) * cases] = turned[s * cases : (s + 1) * cases]
     for s in range(sectors):
-        load_ref[s, height - SUM_ROWS :] = refs[0][...] if summed else jnp.zeros((SUM_ROWS, LANES), f32)
+        load_ref[s, height - SUM_ROWS :] = refs[0][...] if refs[1:] else jnp.zeros((SUM_ROWS, LANES), f32)
 
 
 def pack_kernel(before_ref, after_ref, parts_ref, out_ref):
@@ -240,15 +245,18 @@
     top, ends = call(round_kernel, (top_shape, ends_shape), (rhs,))
     for step in range(ITERS):
         first, last = step == 0, step == ITERS - 1
-        product, load, right, left = call(
-            functools.partial(product_kernel, not first),
-            (full, shape(sectors, height + SUM_ROWS, LANES), face, face),
-            (precond, springs, *sums, gathered(top), exchange(ends, "dof")),
-            parts=rows // (2 * LANES),
+        product, right, left = call(
+            product_kernel,
+            (full, face, face),
+            (precond, gathered(top), exchange(ends, "dof")),
+            streamed=True,
             flops=2 * precond.size * loads,
         )
         before = lax.ppermute(right, "sector", onward)
         after = lax.ppermute(left, "sector", backward)
+        load = call(
+            load_kernel, shape(sectors, height + SUM_ROWS, LANES), (product, springs, *sums), small=True
+        )
         packed = call(
             pack_kernel,
             shape(2 * quarter + height + 4 * SUM_ROWS, loads, dtype=bf16),
@@ -260,7 +268,7 @@
             functools.partial(hub_kernel, cases),
             shape(sectors, height, LANES),
             (hub_inverse, pieces),
-            parts=attached // LANES // 2 if attached % (2 * LANES) == 0 else attached // LANES,
+            streamed=True,
             flops=2 * hub_inverse.size * cases,
         )
         hubs = exchange(hub, "sector")
@@ -268,7 +276,7 @@
             functools.partial(base_kernel, first),
             (full, ends_shape, shape(SUM_ROWS, loads)) + (() if first else (full, full, full)),
             (coupling[0], pieces, product, stiffness, *state),
-            parts=rows // (2 * LANES),
+            streamed=True,
             flops=2 * coupling.size * loads,
         )
         residual, precon, *solution = (residual, product) if first else state
@@ -332,7 +340,7 @@
 def body(rhs, *rest):
     rows, loads = rhs.shape[1:]
     cases = loads // lax.axis_size("sector")
-    tiled = loads == LANES and (rows // 4) % LANES == 0 and cases % 16 == 0
+    tiled = loads == LANES and (rows // 4) % BLOCK_ROWS == 0 and cases % 16 == 0
     return (tiled_body if tiled else plain_body)(rhs, *rest)
 
 

time: 270 us -> 276 us (1.022)
  local copies, waits for them, and re-layouts: 3.86 us -> 7.01 us
    unnamed x16 -> x30, local copies, waits for them, and re-layouts: 2.87 us -> 6.01 us
    pallas_call x17 -> x20, Pallas kernels: 69 us -> 71.3 us  [call(): pl.pallas_call(kernel, in_specs=specs, out_specs=jax.tree.map(lambda _: W...]
where the time goes in v9:
time: 276 us; the launch traced here: 274 us
  blocking collectives  126 us (46%)
  Pallas kernels  71.3 us (26%)
  starting transfers between devices  43.7 us (16%)
  waiting for transfers between devices  24.8 us (9%)
  local copies, waits for them, and re-layouts  7.01 us (3%)
    all_gather x6, blocking collectives, gathered(): return lax.all_gather(field, 'dof', axis=0)  114 us
    pallas_call x20, Pallas kernels, call(): pl.pallas_call(kernel, in_specs=specs, out_specs=jax.tree.map(lambda _: W...  71.3 us
    all_to_all x9, starting transfers between devices, exchange(): return lax.all_to_all(blocks, axes, split_axis=0, concat_axis=0)  35.6 us
    ppermute x3, waiting for transfers between devices, tiled_body(): before = lax.ppermute(right, 'sector', onward)  20.7 us
    all_to_all x1, blocking collectives, exchange(): return lax.all_to_all(blocks, axes, split_axis=0, concat_axis=0)  12.5 us
    ppermute x3, starting transfers between devices, tiled_body(): after = lax.ppermute(left, 'sector', backward)  6.67 us
    unnamed x30, local copies, waits for them, and re-layouts  6.01 us
  transfers between devices with their start and end apart: 15, of which 6 were waited for; matrix products, arithmetic and copies ran while one was open for 0% of the time, Pallas kernels for 9%

profile of v9, /device:TPU:0, one launch (start us, length us, event | category | flops | bytes accessed | tf_op | source)
XLA Modules:
  0.0 273.8 jit_solution(3702078780270361370)
XLA Ops:
  2.5 6.3 %all-to-all-start = ((bf16[4,256,128]{2,1,0:T(8,128)(2,1)}), bf16[4,256,128]{2,1,0:T(8,128)(2,1)S(1)}, u32[]{:S(2)}, u32[]{:S(2)}) async-start(bf16[4,256,128]{2,1,0:T(8,128)(2,1)} %get-tuple-element.36), calls=%async_computation | async-start | bytes 524288 | tf_op jit(solution)/shard_map/all_to_all | solution.py:213
  8.8 22.8 %all-gather = bf16[3072,128]{1,0:T(8,128)(2,1)} all-gather(bf16[768,128]{1,0:T(8,128)(2,1)} %get-tuple-element.35), channel_id=2, replica_groups=mesh['sector'=8,'dof'=4] {'dof'}, dimensions={0}, use_global_device_ids=true | all-gather | bytes 983040 | tf_op jit(solution)/shard_map/all_gather | solution.py:217
  32.3 6.7 %shard_map.78 = (f32[1024,128]{1,0:T(8,128)}, bf16[256,128]{1,0:T(8,128)(2,1)}, bf16[256,128]{1,0:T(8,128)(2,1)}) custom-call(bf16[1024,4096]{1,0:T(8,128)(2,1)} %matrix_ref.10, bf16[4,768,128]{2,1,0:T(8,128)(2,1)} %bitcast.20, bf16[4,256,128]{2,1,0:T(8,128)(2,1)} %copy-done.13), custom_call_target="tpu_custom_call" | custom-call | flops 1073741824 | bytes 9437184 | tf_op jit(solution)/shard_map/pallas_call | solution.py:33
  41.0 3.9 %all-to-all-start.1 = ((f32[8,104,128]{2,1,0:T(8,128)}), f32[8,104,128]{2,1,0:T(8,128)S(1)}, u32[]{:S(2)}, u32[]{:S(2)}) async-start(f32[8,104,128]{2,1,0:T(8,128)} %shard_map.79), calls=%async_computation.1 | async-start | bytes 851968 | tf_op jit(solution)/shard_map/all_to_all | solution.py:213
  47.6 6.9 %collective-permute-done.before_ref = bf16[256,128]{1,0:T(8,128)(2,1)S(1)} collective-permute-done((bf16[256,128]{1,0:T(8,128)(2,1)}, bf16[256,128]{1,0:T(8,128)(2,1)S(1)}, u32[]{:S(2)}, u32[]{:S(2)}) %collective-permute-start) | collective-permute-done | bytes 65568 | tf_op jit(solution)/shard_map/ppermute | solution.py:255
  54.5 16.7 %all-gather.1 = bf16[2560,128]{1,0:T(8,128)(2,1)} all-gather(bf16[640,128]{1,0:T(8,128)(2,1)S(1)} %shard_map.80), channel_id=3, replica_groups=mesh['sector'=8,'dof'=4] {'dof'}, dimensions={0}, use_global_device_ids=true | all-gather | bytes 819200 | tf_op jit(solution)/shard_map/all_gather | solution.py:217
  71.3 5.7 %shard_map.82 = f32[8,96,128]{2,1,0:T(8,128)} custom-call(bf16[768,3072]{1,0:T(8,128)(2,1)} %matrix_ref.11, bf16[4,640,128]{2,1,0:T(8,128)(2,1)} %bitcast.16), custom_call_target="tpu_custom_call" | custom-call | flops 75497472 | bytes 5373952 | tf_op jit(solution)/shard_map/pallas_call | solution.py:33
  81.5 5.7 %shard_map.81 = (f32[1024,128]{1,0:T(8,128)}, bf16[4,256,128]{2,1,0:T(8,128)(2,1)}, f32[8,128]{1,0:T(8,128)}) custom-call(bf16[1024,2048]{1,0:T(8,128)(2,1)} %bitcast.9, bf16[4,640,128]{2,1,0:T(8,128)(2,1)} %bitcast.17, f32[1024,128]{1,0:T(8,128)} %get-tuple-element.39.product_ref.refs_2_, f32[1024,128]{1,0:T(8,128)} %broadcast_in_dim.2.stiffness_ref), custom_call_target="tpu_custom_call" | custom-call | flops 536870912 | bytes 5898240 | tf_op jit(solution)/shard_map/pallas_call | solution.py:33
  88.7 4.5 %all-to-all-start.3 = ((bf16[4,256,128]{2,1,0:T(8,128)(2,1)}), bf16[4,256,128]{2,1,0:T(8,128)(2,1)S(1)}, u32[]{:S(2)}, u32[]{:S(2)}) async-start(bf16[4,256,128]{2,1,0:T(8,128)(2,1)} %get-tuple-element.43), calls=%async_computation.3 | async-start | bytes 524288 | tf_op jit(solution)/shard_map/all_to_all | solution.py:213
  95.6 20.3 %all-gather.2 = bf16[3072,128]{1,0:T(8,128)(2,1)} all-gather(bf16[768,128]{1,0:T(8,128)(2,1)} %get-tuple-element.42), channel_id=4, replica_groups=mesh['sector'=8,'dof'=4] {'dof'}, dimensions={0}, use_global_device_ids=true | all-gather | bytes 983040 | tf_op jit(solution)/shard_map/all_gather | solution.py:217
  116.6 6.7 %shard_map.84 = (f32[1024,128]{1,0:T(8,128)}, bf16[256,128]{1,0:T(8,128)(2,1)}, bf16[256,128]{1,0:T(8,128)(2,1)}) custom-call(bf16[1024,4096]{1,0:T(8,128)(2,1)} %matrix_ref.10, bf16[4,768,128]{2,1,0:T(8,128)(2,1)} %bitcast.21, bf16[4,256,128]{2,1,0:T(8,128)(2,1)} %copy-done.11), custom_call_target="tpu_custom_call" | custom-call | flops 1073741824 | bytes 9437184 | tf_op jit(solution)/shard_map/pallas_call | solution.py:33
  131.5 6.9 %collective-permute-done.2.before_ref = bf16[256,128]{1,0:T(8,128)(2,1)S(1)} collective-permute-done((bf16[256,128]{1,0:T(8,128)(2,1)}, bf16[256,128]{1,0:T(8,128)(2,1)S(1)}, u32[]{:S(2)}, u32[]{:S(2)}) %collective-permute-start.2) | collective-permute-done | bytes 65568 | tf_op jit(solution)/shard_map/ppermute | solution.py:255
  138.4 17.1 %all-gather.3 = bf16[2560,128]{1,0:T(8,128)(2,1)} all-gather(bf16[640,128]{1,0:T(8,128)(2,1)S(1)} %shard_map.86), channel_id=5, replica_groups=mesh['sector'=8,'dof'=4] {'dof'}, dimensions={0}, use_global_device_ids=true | all-gather | bytes 819200 | tf_op jit(solution)/shard_map/all_gather | solution.py:217
  155.6 5.7 %shard_map.88 = f32[8,96,128]{2,1,0:T(8,128)} custom-call(bf16[768,3072]{1,0:T(8,128)(2,1)} %matrix_ref.11, bf16[4,640,128]{2,1,0:T(8,128)(2,1)} %bitcast.12), custom_call_target="tpu_custom_call" | custom-call | flops 75497472 | bytes 5373952 | tf_op jit(solution)/shard_map/pallas_call | solution.py:33
  161.3 3.6 %all-to-all-start.5 = ((f32[8,96,128]{2,1,0:T(8,128)}), f32[8,96,128]{2,1,0:T(8,128)S(1)}, u32[]{:S(2)}, u32[]{:S(2)}) async-start(f32[8,96,128]{2,1,0:T(8,128)} %shard_map.88), calls=%async_computation.5 | async-start | bytes 786432 | tf_op jit(solution)/shard_map/all_to_all | solution.py:213
  164.9 6.8 %shard_map.87 = (f32[1024,128]{1,0:T(8,128)}, bf16[4,256,128]{2,1,0:T(8,128)(2,1)}, f32[8,128]{1,0:T(8,128)}, f32[1024,128]{1,0:T(8,128)}, f32[1024,128]{1,0:T(8,128)}, /*index=5*/f32[1024,128]{1,0:T(8,128)}) custom-call(bf16[1024,2048]{1,0:T(8,128)(2,1)} %bitcast.10, bf16[4,640,128]{2,1,0:T(8,128)(2,1)} %bitcast.13, ...), custom_call_target="tpu_custom_call" | custom-call | flops 536870912 | bytes 7471104 | tf_op jit(solution)/shard_map/pallas_call | solution.py:33
  178.8 19.7 %all-gather.4 = bf16[3072,128]{1,0:T(8,128)(2,1)} all-gather(bf16[768,128]{1,0:T(8,128)(2,1)} %get-tuple-element.52), channel_id=6, replica_groups=mesh['sector'=8,'dof'=4] {'dof'}, dimensions={0}, use_global_device_ids=true | all-gather | bytes 983040 | tf_op jit(solution)/shard_map/all_gather | solution.py:217
  199.3 6.7 %shard_map.90 = (f32[1024,128]{1,0:T(8,128)}, bf16[256,128]{1,0:T(8,128)(2,1)}, bf16[256,128]{1,0:T(8,128)(2,1)}) custom-call(bf16[1024,4096]{1,0:T(8,128)(2,1)} %matrix_ref.10, bf16[4,768,128]{2,1,0:T(8,128)(2,1)} %bitcast.22, bf16[4,256,128]{2,1,0:T(8,128)(2,1)} %copy-done.12), custom_call_target="tpu_custom_call" | custom-call | flops 1073741824 | bytes 9437184 | tf_op jit(solution)/shard_map/pallas_call | solution.py:33
  208.0 3.5 %all-to-all-start.7 = ((f32[8,104,128]{2,1,0:T(8,128)}), f32[8,104,128]{2,1,0:T(8,128)S(1)}, u32[]{:S(2)}, u32[]{:S(2)}) async-start(f32[8,104,128]{2,1,0:T(8,128)} %shard_map.91), calls=%async_computation.7 | async-start | bytes 851968 | tf_op jit(solution)/shard_map/all_to_all | solution.py:213
  214.2 6.9 %collective-permute-done.4.before_ref = bf16[256,128]{1,0:T(8,128)(2,1)S(1)} collective-permute-done((bf16[256,128]{1,0:T(8,128)(2,1)}, bf16[256,128]{1,0:T(8,128)(2,1)S(1)}, u32[]{:S(2)}, u32[]{:S(2)}) %collective-permute-start.4) | collective-permute-done | bytes 65568 | tf_op jit(solution)/shard_map/ppermute | solution.py:255
  221.2 16.9 %all-gather.5 = bf16[2560,128]{1,0:T(8,128)(2,1)} all-gather(bf16[640,128]{1,0:T(8,128)(2,1)S(1)} %shard_map.92), channel_id=7, replica_groups=mesh['sector'=8,'dof'=4] {'dof'}, dimensions={0}, use_global_device_ids=true | all-gather | bytes 819200 | tf_op jit(solution)/shard_map/all_gather | solution.py:217
  238.1 5.7 %shard_map.94 = f32[8,96,128]{2,1,0:T(8,128)} custom-call(bf16[768,3072]{1,0:T(8,128)(2,1)} %matrix_ref.11, bf16[4,640,128]{2,1,0:T(8,128)(2,1)} %bitcast.14), custom_call_target="tpu_custom_call" | custom-call | flops 75497472 | bytes 5373952 | tf_op jit(solution)/shard_map/pallas_call | solution.py:33
  247.3 6.9 %shard_map.93 = (f32[1024,128]{1,0:T(8,128)}, bf16[4,256,128]{2,1,0:T(8,128)(2,1)}, f32[8,128]{1,0:T(8,128)}, f32[1024,128]{1,0:T(8,128)}, f32[1024,128]{1,0:T(8,128)}, /*index=5*/f32[1024,128]{1,0:T(8,128)}) custom-call(bf16[1024,2048]{1,0:T(8,128)(2,1)} %bitcast.11, bf16[4,640,128]{2,1,0:T(8,128)(2,1)} %bitcast.15, ...), custom_call_target="tpu_custom_call" | custom-call | flops 536870912 | bytes 7995392 | tf_op jit(solution)/shard_map/pallas_call | solution.py:33
  258.7 12.5 %all_to_all.50.sums_ref = f32[32,8,128]{2,1,0:T(8,128)} all-to-all(f32[32,8,128]{2,1,0:T(8,128)} %get-tuple-element.64), channel_id=1, replica_groups=mesh['sector'=8,'dof'=4] {'sector','dof'}, dimensions={0} | all-to-all | bytes 262144 | tf_op jit(solution)/shard_map/all_to_all | solution.py:213
  (66 shorter events, 47.6 us)
Async XLA Ops:
  2.5 29.1 %all-to-all-start = ((bf16[4,256,128]{2,1,0:T(8,128)(2,1)}), bf16[4,256,128]{2,1,0:T(8,128)(2,1)S(1)}, u32[]{:S(2)}, u32[]{:S(2)}) async-start(bf16[4,256,128]{2,1,0:T(8,128)(2,1)} %get-tuple-element.36), calls=%async_computation | async-start | bytes 524288 | tf_op jit(solution)/shard_map/all_to_all | solution.py:213
  32.3 6.7 %copy-start.3 = (f32[1,768]{1,0:T(1,128)S(1)}, f32[1,768]{1,0:T(1,128)}, u32[]{:S(2)}) copy-start(f32[1,768]{1,0:T(1,128)} %springs_ref.11) | copy-start | bytes 9220
  39.0 1.0 copy-start
  41.0 39.5 %copy-start.14 = (f32[1,1024]{1,0:T(1,128)S(1)}, f32[1,1024]{1,0:T(1,128)}, u32[]{:S(2)}) copy-start(f32[1,1024]{1,0:T(1,128)} %param.7) | copy-start | bytes 12292
  41.0 13.5 %all-to-all-start.1 = ((f32[8,104,128]{2,1,0:T(8,128)}), f32[8,104,128]{2,1,0:T(8,128)S(1)}, u32[]{:S(2)}, u32[]{:S(2)}) async-start(f32[8,104,128]{2,1,0:T(8,128)} %shard_map.79), calls=%async_computation.1 | async-start | bytes 851968 | tf_op jit(solution)/shard_map/all_to_all | solution.py:213
  44.9 9.6 %collective-permute-start = (bf16[256,128]{1,0:T(8,128)(2,1)}, bf16[256,128]{1,0:T(8,128)(2,1)S(1)}, u32[]{:S(2)}, u32[]{:S(2)}) collective-permute-start(bf16[256,128]{1,0:T(8,128)(2,1)} %get-tuple-element.37), channel_id=1, source_target_pairs={{0,4},{4,8},{8,12},{12,16},{16,20},{20,24},{24,28},{28,0},{1,5},{5... | collective-permute-start | bytes 196616 | tf_op jit(solution)/shard_map/ppermute | solution.py:255
  45.4 9.1 %collective-permute-start.1 = (bf16[256,128]{1,0:T(8,128)(2,1)}, bf16[256,128]{1,0:T(8,128)(2,1)S(1)}, u32[]{:S(2)}, u32[]{:S(2)}) collective-permute-start(bf16[256,128]{1,0:T(8,128)(2,1)} %get-tuple-element.38), channel_id=1, source_target_pairs={{4,0},{8,4},{12,8},{16,12},{20,16},{24,20},{28,24},{0,28},{5,1},{9... | collective-permute-start | bytes 196616 | tf_op jit(solution)/shard_map/ppermute | solution.py:256
  77.0 11.7 %all-to-all-start.2 = ((f32[8,96,128]{2,1,0:T(8,128)}), f32[8,96,128]{2,1,0:T(8,128)S(1)}, u32[]{:S(2)}, u32[]{:S(2)}) async-start(f32[8,96,128]{2,1,0:T(8,128)} %shard_map.82), calls=%async_computation.2 | async-start | bytes 786432 | tf_op jit(solution)/shard_map/all_to_all | solution.py:213
  88.7 4.5 %copy-start.8 = (f32[8,96,128]{2,1,0:T(8,128)}, f32[8,96,128]{2,1,0:T(8,128)S(1)}, u32[]{:S(2)}) copy-start(f32[8,96,128]{2,1,0:T(8,128)S(1)} %all-to-all-done.2.hubs_ref) | copy-start | bytes 1179652
  88.7 27.1 %all-to-all-start.3 = ((bf16[4,256,128]{2,1,0:T(8,128)(2,1)}), bf16[4,256,128]{2,1,0:T(8,128)(2,1)S(1)}, u32[]{:S(2)}, u32[]{:S(2)}) async-start(bf16[4,256,128]{2,1,0:T(8,128)(2,1)} %get-tuple-element.43), calls=%async_computation.3 | async-start | bytes 524288 | tf_op jit(solution)/shard_map/all_to_all | solution.py:213
  116.6 6.7 %copy-start.4 = (f32[1,768]{1,0:T(1,128)S(1)}, f32[1,768]{1,0:T(1,128)}, u32[]{:S(2)}) copy-start(f32[1,768]{1,0:T(1,128)} %springs_ref.11) | copy-start | bytes 9220
  116.6 6.7 %copy-start.6 = (f32[8,128]{1,0:T(8,128)S(1)}, f32[8,128]{1,0:T(8,128)}, u32[]{:S(2)}) copy-start(f32[8,128]{1,0:T(8,128)} %get-tuple-element.47.refs_0_) | copy-start | bytes 12292
  125.3 13.0 %all-to-all-start.4 = ((f32[8,104,128]{2,1,0:T(8,128)}), f32[8,104,128]{2,1,0:T(8,128)S(1)}, u32[]{:S(2)}, u32[]{:S(2)}) async-start(f32[8,104,128]{2,1,0:T(8,128)} %shard_map.85), calls=%async_computation.4 | async-start | bytes 851968 | tf_op jit(solution)/shard_map/all_to_all | solution.py:213
  128.8 9.5 %collective-permute-start.2 = (bf16[256,128]{1,0:T(8,128)(2,1)}, bf16[256,128]{1,0:T(8,128)(2,1)S(1)}, u32[]{:S(2)}, u32[]{:S(2)}) collective-permute-start(bf16[256,128]{1,0:T(8,128)(2,1)} %get-tuple-element.44), channel_id=1, source_target_pairs={{0,4},{4,8},{8,12},{12,16},{16,20},{20,24},{24,28},{28,0},{1,5},{5... | collective-permute-start | bytes 196616 | tf_op jit(solution)/shard_map/ppermute | solution.py:255
  129.2 9.1 %collective-permute-start.3 = (bf16[256,128]{1,0:T(8,128)(2,1)}, bf16[256,128]{1,0:T(8,128)(2,1)S(1)}, u32[]{:S(2)}, u32[]{:S(2)}) collective-permute-start(bf16[256,128]{1,0:T(8,128)(2,1)} %get-tuple-element.45), channel_id=1, source_target_pairs={{4,0},{8,4},{12,8},{16,12},{20,16},{24,20},{28,24},{0,28},{5,1},{9... | collective-permute-start | bytes 196616 | tf_op jit(solution)/shard_map/ppermute | solution.py:256
  161.3 11.7 %all-to-all-start.5 = ((f32[8,96,128]{2,1,0:T(8,128)}), f32[8,96,128]{2,1,0:T(8,128)S(1)}, u32[]{:S(2)}, u32[]{:S(2)}) async-start(f32[8,96,128]{2,1,0:T(8,128)} %shard_map.88), calls=%async_computation.5 | async-start | bytes 786432 | tf_op jit(solution)/shard_map/all_to_all | solution.py:213
  173.0 3.4 %copy-start.9 = (f32[8,96,128]{2,1,0:T(8,128)}, f32[8,96,128]{2,1,0:T(8,128)S(1)}, u32[]{:S(2)}) copy-start(f32[8,96,128]{2,1,0:T(8,128)S(1)} %all-to-all-done.5.hubs_ref) | copy-start | bytes 1179652
  173.0 25.5 %all-to-all-start.6 = ((bf16[4,256,128]{2,1,0:T(8,128)(2,1)}), bf16[4,256,128]{2,1,0:T(8,128)(2,1)S(1)}, u32[]{:S(2)}, u32[]{:S(2)}) async-start(bf16[4,256,128]{2,1,0:T(8,128)(2,1)} %get-tuple-element.53), calls=%async_computation.6 | async-start | bytes 524288 | tf_op jit(solution)/shard_map/all_to_all | solution.py:213
  199.3 6.7 %copy-start.5 = (f32[1,768]{1,0:T(1,128)S(1)}, f32[1,768]{1,0:T(1,128)}, u32[]{:S(2)}) copy-start(f32[1,768]{1,0:T(1,128)} %springs_ref.11) | copy-start | bytes 9220
  199.3 6.7 %copy-start.7 = (f32[8,128]{1,0:T(8,128)S(1)}, f32[8,128]{1,0:T(8,128)}, u32[]{:S(2)}) copy-start(f32[8,128]{1,0:T(8,128)} %get-tuple-element.57.refs_0_) | copy-start | bytes 12292
  208.0 13.1 %all-to-all-start.7 = ((f32[8,104,128]{2,1,0:T(8,128)}), f32[8,104,128]{2,1,0:T(8,128)S(1)}, u32[]{:S(2)}, u32[]{:S(2)}) async-start(f32[8,104,128]{2,1,0:T(8,128)} %shard_map.91), calls=%async_computation.7 | async-start | bytes 851968 | tf_op jit(solution)/shard_map/all_to_all | solution.py:213
  211.5 9.6 %collective-permute-start.4 = (bf16[256,128]{1,0:T(8,128)(2,1)}, bf16[256,128]{1,0:T(8,128)(2,1)S(1)}, u32[]{:S(2)}, u32[]{:S(2)}) collective-permute-start(bf16[256,128]{1,0:T(8,128)(2,1)} %get-tuple-element.54), channel_id=1, source_target_pairs={{0,4},{4,8},{8,12},{12,16},{16,20},{20,24},{24,28},{28,0},{1,5},{5... | collective-permute-start | bytes 196616 | tf_op jit(solution)/shard_map/ppermute | solution.py:255
  212.0 9.1 %collective-permute-start.5 = (bf16[256,128]{1,0:T(8,128)(2,1)}, bf16[256,128]{1,0:T(8,128)(2,1)S(1)}, u32[]{:S(2)}, u32[]{:S(2)}) collective-permute-start(bf16[256,128]{1,0:T(8,128)(2,1)} %get-tuple-element.55), channel_id=1, source_target_pairs={{4,0},{8,4},{12,8},{16,12},{20,16},{24,20},{28,24},{0,28},{5,1},{9... | collective-permute-start | bytes 196616 | tf_op jit(solution)/shard_map/ppermute | solution.py:256
  243.8 11.7 %all-to-all-start.8 = ((f32[8,96,128]{2,1,0:T(8,128)}), f32[8,96,128]{2,1,0:T(8,128)S(1)}, u32[]{:S(2)}, u32[]{:S(2)}) async-start(f32[8,96,128]{2,1,0:T(8,128)} %shard_map.94), calls=%async_computation.8 | async-start | bytes 786432 | tf_op jit(solution)/shard_map/all_to_all | solution.py:213
  (6 other events, 5.0 us)

commit v10 on v8

--- a/solution.py
+++ b/solution.py
@@ -10,9 +10,7 @@
 ITERS = 3
 LANES = 128
 MIB = 1024 * 1024
-IN_FLIGHT = 2
 SUM_ROWS = 8
-WHOLE = pl.BlockSpec(memory_space=pltpu.VMEM)
 f32 = jnp.float32
 bf16 = jnp.bfloat16
 
@@ -21,19 +19,26 @@
     return jax.ShapeDtypeStruct(dims, dtype)
 
 
-def call(kernel, outs, operands, parts=0, flops=0, small=False):
-    matrix = operands[0]
-    specs = [WHOLE] * len(operands)
-    scratch = []
-    if parts:
-        specs[0] = pl.BlockSpec(memory_space=pltpu.HBM)
-        scratch = [pltpu.VMEM(matrix.shape, matrix.dtype), pltpu.SemaphoreType.DMA((parts,))]
+def call(kernel, outs, operands, parted=(), steps=1, scratch=(), flops=0, small=False):
+    specs = []
+    for at, operand in enumerate(operands):
+        block, dim = list(operand.shape), operand.ndim
+        if at not in parted:
+            specs.append(pl.BlockSpec(block, lambda k, dim=dim: (0,) * dim))
+        elif dim == 2:
+            specs.append(pl.BlockSpec([block[0], block[1] // steps], lambda k: (0, k)))
+        else:
+            specs.append(pl.BlockSpec([1] + block[1:], lambda k: (k, 0, 0)))
+    out_specs = jax.tree.map(
+        lambda out: pl.BlockSpec(out.shape, lambda k, dim=len(out.shape): (0,) * dim), outs
+    )
     return pl.pallas_call(
         kernel,
+        grid=(steps,),
         in_specs=specs,
-        out_specs=jax.tree.map(lambda _: WHOLE, outs),
+        out_specs=out_specs,
         out_shape=outs,
-        scratch_shapes=scratch,
+        scratch_shapes=list(scratch),
         compiler_params=pltpu.CompilerParams(vmem_limit_bytes=(16 if small else 60) * MIB),
         cost_estimate=pl.CostEstimate(
             flops=flops, bytes_accessed=sum(x.size * x.dtype.itemsize for x in operands), transcendentals=0
@@ -41,52 +46,45 @@
     )(*operands)
 
 
-def row_blocks(source, buffer, sems):
-    count = sems.shape[0]
-    height = source.shape[0] // count
-    blocks = [pl.ds(at * height, height) for at in range(count)]
-    copies = [
-        pltpu.make_async_copy(source.at[rows], buffer.at[rows], sems.at[at])
-        for at, rows in enumerate(blocks)
-    ]
-    for copy in copies[:IN_FLIGHT]:
-        copy.start()
-    for at in range(count):
-        copies[at].wait()
-        if at + IN_FLIGHT < count:
-            copies[at + IN_FLIGHT].start()
-        yield slice(at * height, (at + 1) * height)
-
-
-def product_kernel(summed, matrix_ref, springs_ref, *refs):
-    *refs, out_ref, load_ref, right_ref, left_ref, buffer, sems = refs
-    tops_ref, ends_ref = refs[-2:]
-    parts, top, _ = tops_ref.shape
-    end = ends_ref.shape[1]
-    for rows in row_blocks(matrix_ref, buffer, sems):
-        total = None
-        for part in range(parts):
-            start = part * (top + end)
-            for width, field in ((top, tops_ref[part]), (end, ends_ref[part])):
-                product = jnp.dot(
-                    buffer[rows, start : start + width], field, preferred_element_type=f32
-                )
-                total = product if total is None else total + product
-                start += width
-        out_ref[rows] = total
-
-    sectors, height, _ = load_ref.shape
-    cases = out_ref.shape[1] // sectors
-    quarter = right_ref.shape[0]
-    left_ref[...] = out_ref[:quarter].astype(bf16)
-    right_ref[...] = out_ref[quarter : 2 * quarter].astype(bf16)
-    for at in range((height - SUM_ROWS) // cases):
-        rows = slice(at * LANES, (at + 1) * LANES)
-        turned = out_ref[rows].T * springs_ref[:, rows]
+def add_product(ref, product):
+    first = pl.program_id(0) == 0
+
+    @pl.when(first)
+    def _():
+        ref[...] = product
+
+    @pl.when(jnp.logical_not(first))
+    def _():
+        ref[...] += product
+
+
+def at_end(run):
+    pl.when(pl.program_id(0) == pl.num_programs(0) - 1)(run)
+
+
+def product_kernel(summed, matrix_ref, tops_ref, ends_ref, springs_ref, *refs):
+    *refs, out_ref, load_ref, right_ref, left_ref = refs
+    top = tops_ref.shape[1]
+    add_product(
+        out_ref,
+        jnp.dot(matrix_ref[:, :top], tops_ref[0], preferred_element_type=f32)
+        + jnp.dot(matrix_ref[:, top:], ends_ref[0], preferred_element_type=f32),
+    )
+
+    @at_end
+    def _():
+        sectors, height, _ = load_ref.shape
+        cases = out_ref.shape[1] // sectors
+        quarter = right_ref.shape[0]
+        left_ref[...] = out_ref[:quarter].astype(bf16)
+        right_ref[...] = out_ref[quarter : 2 * quarter].astype(bf16)
+        for at in range((height - SUM_ROWS) // cases):
+            rows = slice(at * LANES, (at + 1) * LANES)
+            turned = out_ref[rows].T * springs_ref[:, rows]
+            for s in range(sectors):
+                load_ref[s, at * cases : (at + 1) * cases] = turned[s * cases : (s + 1) * cases]
         for s in range(sectors):
-            load_ref[s, at * cases : (at + 1) * cases] = turned[s * cases : (s + 1) * cases]
-    for s in range(sectors):
-        load_ref[s, height - SUM_ROWS :] = refs[0][...] if summed else jnp.zeros((SUM_ROWS, LANES), f32)
+            load_ref[s, height - SUM_ROWS :] = refs[0][...] if summed else jnp.zeros((SUM_ROWS, LANES), f32)
 
 
 def pack_kernel(before_ref, after_ref, parts_ref, out_ref):
@@ -110,64 +108,59 @@
     return sums[0:1] / (sums[1:2] + 1e-06)
 
 
-def hub_kernel(cases, matrix_ref, pieces_ref, out_ref, buffer, sems):
-    parts = pieces_ref.shape[0]
+def hub_kernel(cases, matrix_ref, pieces_ref, out_ref, total_ref):
     height = out_ref.shape[1]
     chunks = height // cases
     first = pieces_ref.shape[1] - 4 * SUM_ROWS - height
     load = jnp.concatenate(
-        [
-            pieces_ref[part, first + c * cases : first + (c + 1) * cases]
-            for part in range(parts)
-            for c in range(chunks)
-        ],
-        axis=1,
-    )
-    for rows in row_blocks(matrix_ref, buffer, sems):
-        hub = lax.dot_general(
-            load, buffer[rows], (((1,), (1,)), ((), ())), preferred_element_type=f32
-        )
-        for c in range(rows.start // LANES, rows.stop // LANES):
-            at = c * LANES - rows.start
+        [pieces_ref[0, first + c * cases : first + (c + 1) * cases] for c in range(chunks)], axis=1
+    )
+    add_product(
+        total_ref,
+        lax.dot_general(
+            load, matrix_ref[...], (((1,), (1,)), ((), ())), preferred_element_type=f32
+        ),
+    )
+
+    @at_end
+    def _():
+        for c in range(chunks):
+            block = total_ref[:, c * LANES : (c + 1) * LANES]
             for s in range(out_ref.shape[0]):
-                out_ref[s, c * cases : (c + 1) * cases] = hub[:, at : at + LANES]
+                out_ref[s, c * cases : (c + 1) * cases] = block
 
 
 def base_kernel(first, matrix_ref, pieces_ref, product_ref, stiffness_ref, *refs):
     if first:
-        base_ref, ends_ref, factor_ref, buffer, sems = refs
+        base_ref, ends_ref, factor_ref, sums_ref = refs
     else:
-        *refs, base_ref, ends_ref, factor_ref, left_ref, newer_ref, better_ref, buffer, sems = refs
+        *refs, base_ref, ends_ref, factor_ref, left_ref, newer_ref, better_ref, sums_ref = refs
         image_ref, residual_ref, precon_ref = refs[:3]
-    parts = pieces_ref.shape[0]
-    depth = matrix_ref.shape[1] // parts
-    for rows in row_blocks(matrix_ref, buffer, sems):
-        total = stiffness_ref[rows] * product_ref[rows]
-        for part in range(parts):
-            total += jnp.dot(
-                buffer[rows, part * depth : (part + 1) * depth],
-                pieces_ref[part, :depth],
-                preferred_element_type=f32,
-            )
-        base_ref[rows] = total
-    if first:
-        factor_ref[...] = jnp.ones_like(factor_ref)
-    else:
-        sums = None
-        height = pieces_ref.shape[1]
-        for part in range(parts):
-            terms = pieces_ref[part, height - 4 * SUM_ROWS :].astype(f32)
-            terms = terms[:SUM_ROWS] + terms[SUM_ROWS : 2 * SUM_ROWS] + terms[2 * SUM_ROWS : 3 * SUM_ROWS]
-            sums = terms if sums is None else sums + terms
-        alpha = alpha_from(sums)
-        factor_ref[...] = jnp.broadcast_to(-alpha, factor_ref.shape)
-        base_ref[...] = image_ref[...] - alpha * base_ref[...]
-        left_ref[...] = residual_ref[...] - alpha * image_ref[...]
-        gain = alpha * precon_ref[...]
-        better_ref[...] = refs[3][...] + gain if len(refs) > 3 else gain
-        newer_ref[...] = precon_ref[...] - alpha * product_ref[...]
-    end = base_ref[base_ref.shape[0] - ends_ref.shape[1] :].astype(bf16)
-    ends_ref[...] = jnp.broadcast_to(end[None], ends_ref.shape)
+    depth = matrix_ref.shape[1]
+    add_product(
+        base_ref, jnp.dot(matrix_ref[...], pieces_ref[0, :depth], preferred_element_type=f32)
+    )
+    terms = pieces_ref[0, pieces_ref.shape[1] - 4 * SUM_ROWS :].astype(f32)
+    add_product(
+        sums_ref, terms[:SUM_ROWS] + terms[SUM_ROWS : 2 * SUM_ROWS] + terms[2 * SUM_ROWS : 3 * SUM_ROWS]
+    )
+
+    @at_end
+    def _():
+        base = base_ref[...] + stiffness_ref[...] * product_ref[...]
+        if first:
+            factor_ref[...] = jnp.ones_like(factor_ref)
+        else:
+            alpha = alpha_from(sums_ref[...])
+            factor_ref[...] = jnp.broadcast_to(-alpha, factor_ref.shape)
+            base = image_ref[...] - alpha * base
+            left_ref[...] = residual_ref[...] - alpha * image_ref[...]
+            gain = alpha * precon_ref[...]
+            better_ref[...] = refs[3][...] + gain if len(refs) > 3 else gain
+            newer_ref[...] = precon_ref[...] - alpha * product_ref[...]
+        base_ref[...] = base
+        end = base[base.shape[0] - ends_ref.shape[1] :].astype(bf16)
+        ends_ref[...] = jnp.broadcast_to(end[None], ends_ref.shape)
 
 
 def image_kernel(base_ref, hubs_ref, springs_ref, factor_ref, residual_ref, image_ref, top_ref, sums_ref):
@@ -243,8 +236,9 @@
         product, load, right, left = call(
             functools.partial(product_kernel, not first),
             (full, shape(sectors, height + SUM_ROWS, LANES), face, face),
-            (precond, springs, *sums, gathered(top), exchange(ends, "dof")),
-            parts=rows // (2 * LANES),
+            (precond, gathered(top), exchange(ends, "dof"), springs, *sums),
+            parted=(0, 1, 2),
+            steps=parts,
             flops=2 * precond.size * loads,
         )
         before = lax.ppermute(right, "sector", onward)
@@ -260,7 +254,9 @@
             functools.partial(hub_kernel, cases),
             shape(sectors, height, LANES),
             (hub_inverse, pieces),
-            parts=attached // LANES // 2 if attached % (2 * LANES) == 0 else attached // LANES,
+            parted=(0, 1),
+            steps=parts,
+            scratch=(pltpu.VMEM((cases, attached), f32),),
             flops=2 * hub_inverse.size * cases,
         )
         hubs = exchange(hub, "sector")
@@ -268,7 +264,9 @@
             functools.partial(base_kernel, first),
             (full, ends_shape, shape(SUM_ROWS, loads)) + (() if first else (full, full, full)),
             (coupling[0], pieces, product, stiffness, *state),
-            parts=rows // (2 * LANES),
+            parted=(0, 1),
+            steps=parts,
+            scratch=(pltpu.VMEM((SUM_ROWS, loads), f32),),
             flops=2 * coupling.size * loads,
         )
         residual, precon, *solution = (residual, product) if first else state

time: 270 us -> 268 us (level)
  Pallas kernels: 69 us -> 66 us
    pallas_call x17, Pallas kernels: 69 us -> 66 us  [call(): pl.pallas_call(kernel, grid=(steps,), in_specs=specs, out_specs=out_specs...]
where the time goes in v10:
time: 268 us; the launch traced here: 266 us
  blocking collectives  126 us (47%)
  Pallas kernels  66 us (25%)
  starting transfers between devices  43.4 us (16%)
  waiting for transfers between devices  25.6 us (10%)
  local copies, waits for them, and re-layouts  3.86 us (1%)
    all_gather x6, blocking collectives, gathered(): return lax.all_gather(field, 'dof', axis=0)  114 us
    pallas_call x17, Pallas kernels, call(): pl.pallas_call(kernel, grid=(steps,), in_specs=specs, out_specs=out_specs...  66 us
    all_to_all x9, starting transfers between devices, exchange(): return lax.all_to_all(blocks, axes, split_axis=0, concat_axis=0)  35.3 us
    ppermute x3, waiting for transfers between devices, tiled_body(): before = lax.ppermute(right, 'sector', onward)  20.6 us
    all_to_all x1, blocking collectives, exchange(): return lax.all_to_all(blocks, axes, split_axis=0, concat_axis=0)  12.3 us
    ppermute x3, starting transfers between devices, tiled_body(): after = lax.ppermute(left, 'sector', backward)  6.77 us
  transfers between devices with their start and end apart: 15, of which 6 were waited for; matrix products, arithmetic and copies ran while one was open for 0% of the time, Pallas kernels for 9%

profile of v10, /device:TPU:0, one launch (start us, length us, event | category | flops | bytes accessed | tf_op | source)
XLA Modules:
  0.0 265.9 jit_solution(961608323899895442)
XLA Ops:
  2.5 6.3 %all-to-all-start = ((bf16[4,256,128]{2,1,0:T(8,128)(2,1)}), bf16[4,256,128]{2,1,0:T(8,128)(2,1)S(1)}, u32[]{:S(2)}, u32[]{:S(2)}) async-start(bf16[4,256,128]{2,1,0:T(8,128)(2,1)} %get-tuple-element.39), calls=%async_computation | async-start | bytes 524288 | tf_op jit(solution)/shard_map/all_to_all | solution.py:201
  8.8 22.8 %all-gather = bf16[3072,128]{1,0:T(8,128)(2,1)} all-gather(bf16[768,128]{1,0:T(8,128)(2,1)} %get-tuple-element.38), channel_id=2, replica_groups=mesh['sector'=8,'dof'=4] {'dof'}, dimensions={0}, use_global_device_ids=true | all-gather | bytes 983040 | tf_op jit(solution)/shard_map/all_gather | solution.py:205
  32.3 7.0 %shard_map.78 = (f32[1024,128]{1,0:T(8,128)}, f32[8,104,128]{2,1,0:T(8,128)}, bf16[256,128]{1,0:T(8,128)(2,1)}, bf16[256,128]{1,0:T(8,128)(2,1)}) custom-call(bf16[1024,4096]{1,0:T(8,128)(2,1)} %matrix_ref.10, bf16[4,768,128]{2,1,0:T(8,128)(2,1)} %bitcast.22, bf16[4,256,128]{2,1,0:T(8,128)(2,1)} %copy-done.5, f32[1,768]{1,0:T(1,128)} %springs_ref.11), custom_call_target="tpu_custom_call" | custom-call | flops 1073741824 | bytes 9440256 | tf_op jit(solution)/shard_map/pallas_call | solution.py:35
  39.3 3.9 %all-to-all-start.1 = ((f32[8,104,128]{2,1,0:T(8,128)}), f32[8,104,128]{2,1,0:T(8,128)S(1)}, u32[]{:S(2)}, u32[]{:S(2)}) async-start(f32[8,104,128]{2,1,0:T(8,128)} %get-tuple-element.42), calls=%async_computation.1 | async-start | bytes 851968 | tf_op jit(solution)/shard_map/all_to_all | solution.py:201
  45.8 6.9 %collective-permute-done.before_ref = bf16[256,128]{1,0:T(8,128)(2,1)S(1)} collective-permute-done((bf16[256,128]{1,0:T(8,128)(2,1)}, bf16[256,128]{1,0:T(8,128)(2,1)S(1)}, u32[]{:S(2)}, u32[]{:S(2)}) %collective-permute-start) | collective-permute-done | bytes 65568 | tf_op jit(solution)/shard_map/ppermute | solution.py:244
  52.8 16.8 %all-gather.1 = bf16[2560,128]{1,0:T(8,128)(2,1)} all-gather(bf16[640,128]{1,0:T(8,128)(2,1)S(1)} %shard_map.79), channel_id=3, replica_groups=mesh['sector'=8,'dof'=4] {'dof'}, dimensions={0}, use_global_device_ids=true | all-gather | bytes 819200 | tf_op jit(solution)/shard_map/all_gather | solution.py:205
  69.5 4.8 %shard_map.81 = f32[8,96,128]{2,1,0:T(8,128)} custom-call(bf16[768,3072]{1,0:T(8,128)(2,1)} %matrix_ref.11, bf16[4,640,128]{2,1,0:T(8,128)(2,1)} %bitcast.16), custom_call_target="tpu_custom_call" | custom-call | flops 75497472 | bytes 5373952 | tf_op jit(solution)/shard_map/pallas_call | solution.py:35
  78.9 5.4 %shard_map.80 = (f32[1024,128]{1,0:T(8,128)}, bf16[4,256,128]{2,1,0:T(8,128)(2,1)}, f32[8,128]{1,0:T(8,128)}) custom-call(bf16[1024,2048]{1,0:T(8,128)(2,1)} %bitcast.9, bf16[4,640,128]{2,1,0:T(8,128)(2,1)} %bitcast.17, f32[1024,128]{1,0:T(8,128)} %get-tuple-element.43.product_ref.refs_2_, f32[1024,128]{1,0:T(8,128)} %broadcast_in_dim.2.stiffness_ref), custom_call_target="tpu_custom_call" | custom-call | flops 536870912 | bytes 5898240 | tf_op jit(solution)/shard_map/pallas_call | solution.py:35
  86.1 4.5 %all-to-all-start.3 = ((bf16[4,256,128]{2,1,0:T(8,128)(2,1)}), bf16[4,256,128]{2,1,0:T(8,128)(2,1)S(1)}, u32[]{:S(2)}, u32[]{:S(2)}) async-start(bf16[4,256,128]{2,1,0:T(8,128)(2,1)} %get-tuple-element.47), calls=%async_computation.3 | async-start | bytes 524288 | tf_op jit(solution)/shard_map/all_to_all | solution.py:201
  92.9 20.4 %all-gather.2 = bf16[3072,128]{1,0:T(8,128)(2,1)} all-gather(bf16[768,128]{1,0:T(8,128)(2,1)} %get-tuple-element.46), channel_id=4, replica_groups=mesh['sector'=8,'dof'=4] {'dof'}, dimensions={0}, use_global_device_ids=true | all-gather | bytes 983040 | tf_op jit(solution)/shard_map/all_gather | solution.py:205
  114.0 7.0 %shard_map.83 = (f32[1024,128]{1,0:T(8,128)}, f32[8,104,128]{2,1,0:T(8,128)}, bf16[256,128]{1,0:T(8,128)(2,1)}, bf16[256,128]{1,0:T(8,128)(2,1)}) custom-call(bf16[1024,4096]{1,0:T(8,128)(2,1)} %matrix_ref.10, bf16[4,768,128]{2,1,0:T(8,128)(2,1)} %bitcast.20, bf16[4,256,128]{2,1,0:T(8,128)(2,1)} %copy-done.3, f32[1,768]{1,0:T(1,128)} %springs_ref.11, ...), custom_call_target="tpu_custom_call" | custom-call | flops 1073741824 | bytes 9444352 | tf_op jit(solution)/shard_map/pallas_call | solution.py:35
  121.1 3.5 %all-to-all-start.4 = ((f32[8,104,128]{2,1,0:T(8,128)}), f32[8,104,128]{2,1,0:T(8,128)S(1)}, u32[]{:S(2)}, u32[]{:S(2)}) async-start(f32[8,104,128]{2,1,0:T(8,128)} %get-tuple-element.51), calls=%async_computation.4 | async-start | bytes 851968 | tf_op jit(solution)/shard_map/all_to_all | solution.py:201
  127.2 6.9 %collective-permute-done.2.before_ref = bf16[256,128]{1,0:T(8,128)(2,1)S(1)} collective-permute-done((bf16[256,128]{1,0:T(8,128)(2,1)}, bf16[256,128]{1,0:T(8,128)(2,1)S(1)}, u32[]{:S(2)}, u32[]{:S(2)}) %collective-permute-start.2) | collective-permute-done | bytes 65568 | tf_op jit(solution)/shard_map/ppermute | solution.py:244
  134.1 17.1 %all-gather.3 = bf16[2560,128]{1,0:T(8,128)(2,1)} all-gather(bf16[640,128]{1,0:T(8,128)(2,1)S(1)} %shard_map.84), channel_id=5, replica_groups=mesh['sector'=8,'dof'=4] {'dof'}, dimensions={0}, use_global_device_ids=true | all-gather | bytes 819200 | tf_op jit(solution)/shard_map/all_gather | solution.py:205
  151.2 4.8 %shard_map.86 = f32[8,96,128]{2,1,0:T(8,128)} custom-call(bf16[768,3072]{1,0:T(8,128)(2,1)} %matrix_ref.11, bf16[4,640,128]{2,1,0:T(8,128)(2,1)} %bitcast.12), custom_call_target="tpu_custom_call" | custom-call | flops 75497472 | bytes 5373952 | tf_op jit(solution)/shard_map/pallas_call | solution.py:35
  159.5 6.6 %shard_map.85 = (f32[1024,128]{1,0:T(8,128)}, bf16[4,256,128]{2,1,0:T(8,128)(2,1)}, f32[8,128]{1,0:T(8,128)}, f32[1024,128]{1,0:T(8,128)}, f32[1024,128]{1,0:T(8,128)}, /*index=5*/f32[1024,128]{1,0:T(8,128)}) custom-call(bf16[1024,2048]{1,0:T(8,128)(2,1)} %bitcast.10, bf16[4,640,128]{2,1,0:T(8,128)(2,1)} %bitcast.13, ...), custom_call_target="tpu_custom_call" | custom-call | flops 536870912 | bytes 7471104 | tf_op jit(solution)/shard_map/pallas_call | solution.py:35
  173.6 20.0 %all-gather.4 = bf16[3072,128]{1,0:T(8,128)(2,1)} all-gather(bf16[768,128]{1,0:T(8,128)(2,1)} %get-tuple-element.57), channel_id=6, replica_groups=mesh['sector'=8,'dof'=4] {'dof'}, dimensions={0}, use_global_device_ids=true | all-gather | bytes 983040 | tf_op jit(solution)/shard_map/all_gather | solution.py:205
  194.3 7.0 %shard_map.88 = (f32[1024,128]{1,0:T(8,128)}, f32[8,104,128]{2,1,0:T(8,128)}, bf16[256,128]{1,0:T(8,128)(2,1)}, bf16[256,128]{1,0:T(8,128)(2,1)}) custom-call(bf16[1024,4096]{1,0:T(8,128)(2,1)} %matrix_ref.10, bf16[4,768,128]{2,1,0:T(8,128)(2,1)} %bitcast.21, bf16[4,256,128]{2,1,0:T(8,128)(2,1)} %copy-done.4, f32[1,768]{1,0:T(1,128)} %springs_ref.11, ...), custom_call_target="tpu_custom_call" | custom-call | flops 1073741824 | bytes 9444352 | tf_op jit(solution)/shard_map/pallas_call | solution.py:35
  201.3 3.5 %all-to-all-start.7 = ((f32[8,104,128]{2,1,0:T(8,128)}), f32[8,104,128]{2,1,0:T(8,128)S(1)}, u32[]{:S(2)}, u32[]{:S(2)}) async-start(f32[8,104,128]{2,1,0:T(8,128)} %get-tuple-element.62), calls=%async_computation.7 | async-start | bytes 851968 | tf_op jit(solution)/shard_map/all_to_all | solution.py:201
  207.5 6.9 %collective-permute-done.4.before_ref = bf16[256,128]{1,0:T(8,128)(2,1)S(1)} collective-permute-done((bf16[256,128]{1,0:T(8,128)(2,1)}, bf16[256,128]{1,0:T(8,128)(2,1)S(1)}, u32[]{:S(2)}, u32[]{:S(2)}) %collective-permute-start.4) | collective-permute-done | bytes 65568 | tf_op jit(solution)/shard_map/ppermute | solution.py:244
  214.4 16.9 %all-gather.5 = bf16[2560,128]{1,0:T(8,128)(2,1)} all-gather(bf16[640,128]{1,0:T(8,128)(2,1)S(1)} %shard_map.89), channel_id=7, replica_groups=mesh['sector'=8,'dof'=4] {'dof'}, dimensions={0}, use_global_device_ids=true | all-gather | bytes 819200 | tf_op jit(solution)/shard_map/all_gather | solution.py:205
  231.3 4.8 %shard_map.91 = f32[8,96,128]{2,1,0:T(8,128)} custom-call(bf16[768,3072]{1,0:T(8,128)(2,1)} %matrix_ref.11, bf16[4,640,128]{2,1,0:T(8,128)(2,1)} %bitcast.14), custom_call_target="tpu_custom_call" | custom-call | flops 75497472 | bytes 5373952 | tf_op jit(solution)/shard_map/pallas_call | solution.py:35
  239.6 6.8 %shard_map.90 = (f32[1024,128]{1,0:T(8,128)}, bf16[4,256,128]{2,1,0:T(8,128)(2,1)}, f32[8,128]{1,0:T(8,128)}, f32[1024,128]{1,0:T(8,128)}, f32[1024,128]{1,0:T(8,128)}, /*index=5*/f32[1024,128]{1,0:T(8,128)}) custom-call(bf16[1024,2048]{1,0:T(8,128)(2,1)} %bitcast.11, bf16[4,640,128]{2,1,0:T(8,128)(2,1)} %bitcast.15, ...), custom_call_target="tpu_custom_call" | custom-call | flops 536870912 | bytes 7995392 | tf_op jit(solution)/shard_map/pallas_call | solution.py:35
  251.0 12.3 %all_to_all.50.sums_ref = f32[32,8,128]{2,1,0:T(8,128)} all-to-all(f32[32,8,128]{2,1,0:T(8,128)} %get-tuple-element.70), channel_id=1, replica_groups=mesh['sector'=8,'dof'=4] {'sector','dof'}, dimensions={0} | all-to-all | bytes 262144 | tf_op jit(solution)/shard_map/all_to_all | solution.py:201
  (49 shorter events, 42.4 us)
Async XLA Ops:
  2.5 29.1 %all-to-all-start = ((bf16[4,256,128]{2,1,0:T(8,128)(2,1)}), bf16[4,256,128]{2,1,0:T(8,128)(2,1)S(1)}, u32[]{:S(2)}, u32[]{:S(2)}) async-start(bf16[4,256,128]{2,1,0:T(8,128)(2,1)} %get-tuple-element.39), calls=%async_computation | async-start | bytes 524288 | tf_op jit(solution)/shard_map/all_to_all | solution.py:201
  31.6 0.7 copy-start.5
  39.3 38.6 %copy-start.6 = (f32[1,768]{1,0:T(1,128)S(1)}, f32[1,768]{1,0:T(1,128)}, u32[]{:S(2)}) copy-start(f32[1,768]{1,0:T(1,128)} %springs_ref.11) | copy-start | bytes 9220
  39.3 38.6 %copy-start.7 = (f32[1,1024]{1,0:T(1,128)S(1)}, f32[1,1024]{1,0:T(1,128)}, u32[]{:S(2)}) copy-start(f32[1,1024]{1,0:T(1,128)} %param.7) | copy-start | bytes 12292
  39.3 13.5 %all-to-all-start.1 = ((f32[8,104,128]{2,1,0:T(8,128)}), f32[8,104,128]{2,1,0:T(8,128)S(1)}, u32[]{:S(2)}, u32[]{:S(2)}) async-start(f32[8,104,128]{2,1,0:T(8,128)} %get-tuple-element.42), calls=%async_computation.1 | async-start | bytes 851968 | tf_op jit(solution)/shard_map/all_to_all | solution.py:201
  43.1 9.6 %collective-permute-start = (bf16[256,128]{1,0:T(8,128)(2,1)}, bf16[256,128]{1,0:T(8,128)(2,1)S(1)}, u32[]{:S(2)}, u32[]{:S(2)}) collective-permute-start(bf16[256,128]{1,0:T(8,128)(2,1)} %get-tuple-element.40), channel_id=1, source_target_pairs={{0,4},{4,8},{8,12},{12,16},{16,20},{20,24},{24,28},{28,0},{1,5},{5... | collective-permute-start | bytes 196616 | tf_op jit(solution)/shard_map/ppermute | solution.py:244
  43.6 9.1 %collective-permute-start.1 = (bf16[256,128]{1,0:T(8,128)(2,1)}, bf16[256,128]{1,0:T(8,128)(2,1)S(1)}, u32[]{:S(2)}, u32[]{:S(2)}) collective-permute-start(bf16[256,128]{1,0:T(8,128)(2,1)} %get-tuple-element.41), channel_id=1, source_target_pairs={{4,0},{8,4},{12,8},{16,12},{20,16},{24,20},{28,24},{0,28},{5,1},{9... | collective-permute-start | bytes 196616 | tf_op jit(solution)/shard_map/ppermute | solution.py:245
  74.4 11.7 %all-to-all-start.2 = ((f32[8,96,128]{2,1,0:T(8,128)}), f32[8,96,128]{2,1,0:T(8,128)S(1)}, u32[]{:S(2)}, u32[]{:S(2)}) async-start(f32[8,96,128]{2,1,0:T(8,128)} %shard_map.81), calls=%async_computation.2 | async-start | bytes 786432 | tf_op jit(solution)/shard_map/all_to_all | solution.py:201
  86.1 4.5 %copy-start = (f32[8,96,128]{2,1,0:T(8,128)}, f32[8,96,128]{2,1,0:T(8,128)S(1)}, u32[]{:S(2)}) copy-start(f32[8,96,128]{2,1,0:T(8,128)S(1)} %all-to-all-done.2.hubs_ref) | copy-start | bytes 1179652
  86.1 27.2 %all-to-all-start.3 = ((bf16[4,256,128]{2,1,0:T(8,128)(2,1)}), bf16[4,256,128]{2,1,0:T(8,128)(2,1)S(1)}, u32[]{:S(2)}, u32[]{:S(2)}) async-start(bf16[4,256,128]{2,1,0:T(8,128)(2,1)} %get-tuple-element.47), calls=%async_computation.3 | async-start | bytes 524288 | tf_op jit(solution)/shard_map/all_to_all | solution.py:201
  113.3 0.7 copy-start.3
  121.1 13.0 %all-to-all-start.4 = ((f32[8,104,128]{2,1,0:T(8,128)}), f32[8,104,128]{2,1,0:T(8,128)S(1)}, u32[]{:S(2)}, u32[]{:S(2)}) async-start(f32[8,104,128]{2,1,0:T(8,128)} %get-tuple-element.51), calls=%async_computation.4 | async-start | bytes 851968 | tf_op jit(solution)/shard_map/all_to_all | solution.py:201
  124.5 9.5 %collective-permute-start.2 = (bf16[256,128]{1,0:T(8,128)(2,1)}, bf16[256,128]{1,0:T(8,128)(2,1)S(1)}, u32[]{:S(2)}, u32[]{:S(2)}) collective-permute-start(bf16[256,128]{1,0:T(8,128)(2,1)} %get-tuple-element.49), channel_id=1, source_target_pairs={{0,4},{4,8},{8,12},{12,16},{16,20},{20,24},{24,28},{28,0},{1,5},{5... | collective-permute-start | bytes 196616 | tf_op jit(solution)/shard_map/ppermute | solution.py:244
  124.9 9.1 %collective-permute-start.3 = (bf16[256,128]{1,0:T(8,128)(2,1)}, bf16[256,128]{1,0:T(8,128)(2,1)S(1)}, u32[]{:S(2)}, u32[]{:S(2)}) collective-permute-start(bf16[256,128]{1,0:T(8,128)(2,1)} %get-tuple-element.50), channel_id=1, source_target_pairs={{4,0},{8,4},{12,8},{16,12},{20,16},{24,20},{28,24},{0,28},{5,1},{9... | collective-permute-start | bytes 196616 | tf_op jit(solution)/shard_map/ppermute | solution.py:245
  156.1 11.7 %all-to-all-start.5 = ((f32[8,96,128]{2,1,0:T(8,128)}), f32[8,96,128]{2,1,0:T(8,128)S(1)}, u32[]{:S(2)}, u32[]{:S(2)}) async-start(f32[8,96,128]{2,1,0:T(8,128)} %shard_map.86), calls=%async_computation.5 | async-start | bytes 786432 | tf_op jit(solution)/shard_map/all_to_all | solution.py:201
  167.8 3.4 %copy-start.1 = (f32[8,96,128]{2,1,0:T(8,128)}, f32[8,96,128]{2,1,0:T(8,128)S(1)}, u32[]{:S(2)}) copy-start(f32[8,96,128]{2,1,0:T(8,128)S(1)} %all-to-all-done.5.hubs_ref) | copy-start | bytes 1179652
  167.8 25.8 %all-to-all-start.6 = ((bf16[4,256,128]{2,1,0:T(8,128)(2,1)}), bf16[4,256,128]{2,1,0:T(8,128)(2,1)S(1)}, u32[]{:S(2)}, u32[]{:S(2)}) async-start(bf16[4,256,128]{2,1,0:T(8,128)(2,1)} %get-tuple-element.58), calls=%async_computation.6 | async-start | bytes 524288 | tf_op jit(solution)/shard_map/all_to_all | solution.py:201
  193.6 0.7 copy-start.4
  201.3 13.0 %all-to-all-start.7 = ((f32[8,104,128]{2,1,0:T(8,128)}), f32[8,104,128]{2,1,0:T(8,128)S(1)}, u32[]{:S(2)}, u32[]{:S(2)}) async-start(f32[8,104,128]{2,1,0:T(8,128)} %get-tuple-element.62), calls=%async_computation.7 | async-start | bytes 851968 | tf_op jit(solution)/shard_map/all_to_all | solution.py:201
  204.8 9.5 %collective-permute-start.4 = (bf16[256,128]{1,0:T(8,128)(2,1)}, bf16[256,128]{1,0:T(8,128)(2,1)S(1)}, u32[]{:S(2)}, u32[]{:S(2)}) collective-permute-start(bf16[256,128]{1,0:T(8,128)(2,1)} %get-tuple-element.60), channel_id=1, source_target_pairs={{0,4},{4,8},{8,12},{12,16},{16,20},{20,24},{24,28},{28,0},{1,5},{5... | collective-permute-start | bytes 196616 | tf_op jit(solution)/shard_map/ppermute | solution.py:244
  205.2 9.1 %collective-permute-start.5 = (bf16[256,128]{1,0:T(8,128)(2,1)}, bf16[256,128]{1,0:T(8,128)(2,1)S(1)}, u32[]{:S(2)}, u32[]{:S(2)}) collective-permute-start(bf16[256,128]{1,0:T(8,128)(2,1)} %get-tuple-element.61), channel_id=1, source_target_pairs={{4,0},{8,4},{12,8},{16,12},{20,16},{24,20},{28,24},{0,28},{5,1},{9... | collective-permute-start | bytes 196616 | tf_op jit(solution)/shard_map/ppermute | solution.py:245
  236.1 11.7 %all-to-all-start.8 = ((f32[8,96,128]{2,1,0:T(8,128)}), f32[8,96,128]{2,1,0:T(8,128)S(1)}, u32[]{:S(2)}, u32[]{:S(2)}) async-start(f32[8,96,128]{2,1,0:T(8,128)} %shard_map.91), calls=%async_computation.8 | async-start | bytes 786432 | tf_op jit(solution)/shard_map/all_to_all | solution.py:201
  247.9 0.7 copy-start.2

commit v11 on v10

--- a/solution.py
+++ b/solution.py
@@ -11,6 +11,7 @@
 LANES = 128
 MIB = 1024 * 1024
 SUM_ROWS = 8
+TERM_ROWS = 16
 f32 = jnp.float32
 bf16 = jnp.bfloat16
 
@@ -62,6 +63,21 @@
     pl.when(pl.program_id(0) == pl.num_programs(0) - 1)(run)
 
 
+def in_terms(sums):
+    terms = None
+    for at in range(3):
+        term = sums.astype(bf16).astype(f32)
+        sums = sums - term
+        terms = term if at == 0 else terms + pltpu.roll(term, 2 * at, 0)
+    return jnp.concatenate([terms, jnp.zeros_like(terms)], axis=0)
+
+
+def from_terms(terms):
+    terms = terms[:SUM_ROWS].astype(f32)
+    sums = terms + pltpu.roll(terms, SUM_ROWS - 2, 0) + pltpu.roll(terms, SUM_ROWS - 4, 0)
+    return jnp.where(lax.broadcasted_iota(jnp.int32, sums.shape, 0) < 2, sums, 0.0)
+
+
 def product_kernel(summed, matrix_ref, tops_ref, ends_ref, springs_ref, *refs):
     *refs, out_ref, load_ref, right_ref, left_ref = refs
     top = tops_ref.shape[1]
@@ -78,30 +94,24 @@
         quarter = right_ref.shape[0]
         left_ref[...] = out_ref[:quarter].astype(bf16)
         right_ref[...] = out_ref[quarter : 2 * quarter].astype(bf16)
-        for at in range((height - SUM_ROWS) // cases):
+        for at in range((height - TERM_ROWS) // cases):
             rows = slice(at * LANES, (at + 1) * LANES)
-            turned = out_ref[rows].T * springs_ref[:, rows]
+            turned = (out_ref[rows].T * springs_ref[:, rows]).astype(load_ref.dtype)
             for s in range(sectors):
                 load_ref[s, at * cases : (at + 1) * cases] = turned[s * cases : (s + 1) * cases]
+        terms = in_terms(refs[0][...]) if summed else jnp.zeros((TERM_ROWS, LANES), f32)
         for s in range(sectors):
-            load_ref[s, height - SUM_ROWS :] = refs[0][...] if summed else jnp.zeros((SUM_ROWS, LANES), f32)
+            load_ref[s, height - TERM_ROWS :] = terms.astype(load_ref.dtype)
 
 
 def pack_kernel(before_ref, after_ref, parts_ref, out_ref):
     quarter = before_ref.shape[0]
-    height = parts_ref.shape[1] - SUM_ROWS
+    height = parts_ref.shape[1] - TERM_ROWS
     out_ref[:quarter] = before_ref[...]
     out_ref[quarter : 2 * quarter] = after_ref[...]
-    total = jnp.sum(parts_ref[...], axis=0)
+    total = jnp.sum(parts_ref[...].astype(f32), axis=0)
     out_ref[2 * quarter : 2 * quarter + height] = total[:height].astype(bf16)
-    rest = total[height:]
-    terms = []
-    for _ in range(3):
-        term = rest.astype(bf16)
-        terms.append(term.astype(f32))
-        rest = rest - terms[-1]
-    terms.append(jnp.zeros_like(rest))
-    out_ref[2 * quarter + height :] = jnp.concatenate(terms, axis=0).astype(bf16)
+    out_ref[2 * quarter + height :] = in_terms(from_terms(total[height:])).astype(bf16)
 
 
 def alpha_from(sums):
@@ -111,7 +121,7 @@
 def hub_kernel(cases, matrix_ref, pieces_ref, out_ref, total_ref):
     height = out_ref.shape[1]
     chunks = height // cases
-    first = pieces_ref.shape[1] - 4 * SUM_ROWS - height
+    first = pieces_ref.shape[1] - TERM_ROWS - height
     load = jnp.concatenate(
         [pieces_ref[0, first + c * cases : first + (c + 1) * cases] for c in range(chunks)], axis=1
     )
@@ -125,7 +135,7 @@
     @at_end
     def _():
         for c in range(chunks):
-            block = total_ref[:, c * LANES : (c + 1) * LANES]
+            block = total_ref[:, c * LANES : (c + 1) * LANES].astype(out_ref.dtype)
             for s in range(out_ref.shape[0]):
                 out_ref[s, c * cases : (c + 1) * cases] = block
 
@@ -140,10 +150,7 @@
     add_product(
         base_ref, jnp.dot(matrix_ref[...], pieces_ref[0, :depth], preferred_element_type=f32)
     )
-    terms = pieces_ref[0, pieces_ref.shape[1] - 4 * SUM_ROWS :].astype(f32)
-    add_product(
-        sums_ref, terms[:SUM_ROWS] + terms[SUM_ROWS : 2 * SUM_ROWS] + terms[2 * SUM_ROWS : 3 * SUM_ROWS]
-    )
+    add_product(sums_ref, from_terms(pieces_ref[0, pieces_ref.shape[1] - TERM_ROWS :]))
 
     @at_end
     def _():
@@ -172,7 +179,7 @@
     for c in range(chunks):
         at = slice(c * LANES, (c + 1) * LANES)
         hub = jnp.concatenate([hubs_ref[s, c * cases : (c + 1) * cases] for s in range(sectors)], axis=0)
-        image = base_ref[at] - factor * (hub * springs_ref[:, at]).T
+        image = base_ref[at] - factor * (hub.astype(f32) * springs_ref[:, at]).T
         image_ref[at] = image
         top_ref[at] = image.astype(bf16)
     image_ref[attached:] = base_ref[attached:]
@@ -188,6 +195,22 @@
     alpha = alpha_from(jnp.sum(sums_ref[...], axis=0))
     newer_ref[0] = solution_ref[...] + alpha * precon_ref[...]
     left_ref[0] = residual_ref[...] - alpha * image_ref[...]
+
+
+def last_update(sums, *state):
+    rows, loads = state[0].shape
+    height = rows // 4
+    block = pl.BlockSpec((height, loads), lambda k: (k, 0))
+    out_block = pl.BlockSpec((1, height, loads), lambda k: (0, k, 0))
+    out = shape(1, rows, loads)
+    return pl.pallas_call(
+        last_kernel,
+        grid=(4,),
+        in_specs=[pl.BlockSpec(sums.shape, lambda k: (0, 0, 0))] + [block] * len(state),
+        out_specs=(out_block, out_block),
+        out_shape=(out, out),
+        compiler_params=pltpu.CompilerParams(vmem_limit_bytes=60 * MIB),
+    )(sums, *state)
 
 
 def round_kernel(field_ref, top_ref, ends_ref):
@@ -233,9 +256,10 @@
     top, ends = call(round_kernel, (top_shape, ends_shape), (rhs,))
     for step in range(ITERS):
         first, last = step == 0, step == ITERS - 1
+        sent = f32 if first else bf16
         product, load, right, left = call(
             functools.partial(product_kernel, not first),
-            (full, shape(sectors, height + SUM_ROWS, LANES), face, face),
+            (full, shape(sectors, height + TERM_ROWS, LANES, dtype=sent), face, face),
             (precond, gathered(top), exchange(ends, "dof"), springs, *sums),
             parted=(0, 1, 2),
             steps=parts,
@@ -245,14 +269,14 @@
         after = lax.ppermute(left, "sector", backward)
         packed = call(
             pack_kernel,
-            shape(2 * quarter + height + 4 * SUM_ROWS, loads, dtype=bf16),
+            shape(2 * quarter + height + TERM_ROWS, loads, dtype=bf16),
             (before, after, exchange(load, "sector")),
             small=True,
         )
         pieces = gathered(packed)
         hub = call(
             functools.partial(hub_kernel, cases),
-            shape(sectors, height, LANES),
+            shape(sectors, height, LANES, dtype=sent),
             (hub_inverse, pieces),
             parted=(0, 1),
             steps=parts,
@@ -281,8 +305,7 @@
         )
         state = (image, residual, precon, *solution)
         sums = (sums,)
-    out = shape(1, rows, loads)
-    return call(last_kernel, (out, out), (exchange(*sums, ("sector", "dof")), *state))
+    return last_update(exchange(*sums, ("sector", "dof")), *state)
 
 
 def plain_body(rhs, diagonal, coupling, springs, precond, hub_inverse):

time: 268 us -> 264 us (0.985)
  waiting for transfers between devices: 25.6 us -> 18.7 us
    pallas_call x0 -> x1, Pallas kernels: none -> 3.85 us  [last_update(): pl.pallas_call(last_kernel, grid=(4,), in_specs=[pl.BlockSpec(sums.shape,...]
    ppermute x3, waiting for transfers between devices: 20.6 us -> 16.8 us  [tiled_body(): before = lax.ppermute(right, 'sector', onward)]
    all_to_all x9, waiting for transfers between devices: 4.94 us -> 1.86 us  [exchange(): return lax.all_to_all(blocks, axes, split_axis=0, concat_axis=0)]
    pallas_call x17 -> x16, Pallas kernels: 66 us -> 63.1 us  [call(): pl.pallas_call(kernel, grid=(steps,), in_specs=specs, out_specs=out_specs...]
  transfers between devices with their start and end apart: 15 -> 15, of which waited for: 6 -> 4; matrix products, arithmetic and copies ran while one was open for 0% -> 0% of each run, Pallas kernels for 9% -> 9%
where the time goes in v11:
time: 264 us; the launch traced here: 262 us
  blocking collectives  128 us (48%)
  Pallas kernels  66.9 us (25%)
  starting transfers between devices  43.9 us (17%)
  waiting for transfers between devices  18.7 us (7%)
  local copies, waits for them, and re-layouts  3.79 us (1%)
    all_gather x6, blocking collectives, gathered(): return lax.all_gather(field, 'dof', axis=0)  114 us
    pallas_call x16, Pallas kernels, call(): pl.pallas_call(kernel, grid=(steps,), in_specs=specs, out_specs=out_specs...  63.1 us
    all_to_all x9, starting transfers between devices, exchange(): return lax.all_to_all(blocks, axes, split_axis=0, concat_axis=0)  35.8 us
    ppermute x3, waiting for transfers between devices, tiled_body(): before = lax.ppermute(right, 'sector', onward)  16.8 us
    all_to_all x1, blocking collectives, exchange(): return lax.all_to_all(blocks, axes, split_axis=0, concat_axis=0)  13.4 us
    ppermute x3, starting transfers between devices, tiled_body(): after = lax.ppermute(left, 'sector', backward)  6.67 us
  transfers between devices with their start and end apart: 15, of which 4 were waited for; matrix products, arithmetic and copies ran while one was open for 0% of the time, Pallas kernels for 9%

profile of v11, /device:TPU:0, one launch (start us, length us, event | category | flops | bytes accessed | tf_op | source)
XLA Modules:
  0.0 261.8 jit_solution(13488056465611491452)
XLA Ops:
  2.5 6.3 %all-to-all-start = ((bf16[4,256,128]{2,1,0:T(8,128)(2,1)}), bf16[4,256,128]{2,1,0:T(8,128)(2,1)S(1)}, u32[]{:S(2)}, u32[]{:S(2)}) async-start(bf16[4,256,128]{2,1,0:T(8,128)(2,1)} %get-tuple-element.39), calls=%async_computation | async-start | bytes 524288 | tf_op jit(solution)/shard_map/all_to_all | solution.py:224
  8.8 22.8 %all-gather = bf16[3072,128]{1,0:T(8,128)(2,1)} all-gather(bf16[768,128]{1,0:T(8,128)(2,1)} %get-tuple-element.38), channel_id=2, replica_groups=mesh['sector'=8,'dof'=4] {'dof'}, dimensions={0}, use_global_device_ids=true | all-gather | bytes 983040 | tf_op jit(solution)/shard_map/all_gather | solution.py:228
  32.3 7.0 %shard_map.78 = (f32[1024,128]{1,0:T(8,128)}, f32[8,112,128]{2,1,0:T(8,128)}, bf16[256,128]{1,0:T(8,128)(2,1)}, bf16[256,128]{1,0:T(8,128)(2,1)}) custom-call(bf16[1024,4096]{1,0:T(8,128)(2,1)} %matrix_ref.10, bf16[4,768,128]{2,1,0:T(8,128)(2,1)} %bitcast.22, bf16[4,256,128]{2,1,0:T(8,128)(2,1)} %copy-done.3, f32[1,768]{1,0:T(1,128)} %springs_ref.11), custom_call_target="tpu_custom_call" | custom-call | flops 1073741824 | bytes 9440256 | tf_op jit(solution)/shard_map/pallas_call | solution.py:36
  39.3 3.9 %all-to-all-start.1 = ((f32[8,112,128]{2,1,0:T(8,128)}), f32[8,112,128]{2,1,0:T(8,128)S(1)}, u32[]{:S(2)}, u32[]{:S(2)}) async-start(f32[8,112,128]{2,1,0:T(8,128)} %get-tuple-element.42), calls=%async_computation.1 | async-start | bytes 917504 | tf_op jit(solution)/shard_map/all_to_all | solution.py:224
  45.8 7.3 %collective-permute-done.before_ref = bf16[256,128]{1,0:T(8,128)(2,1)S(1)} collective-permute-done((bf16[256,128]{1,0:T(8,128)(2,1)}, bf16[256,128]{1,0:T(8,128)(2,1)S(1)}, u32[]{:S(2)}, u32[]{:S(2)}) %collective-permute-start) | collective-permute-done | bytes 65568 | tf_op jit(solution)/shard_map/ppermute | solution.py:268
  53.2 16.6 %all-gather.1 = bf16[2496,128]{1,0:T(8,128)(2,1)} all-gather(bf16[624,128]{1,0:T(8,128)(2,1)S(1)} %shard_map.79), channel_id=3, replica_groups=mesh['sector'=8,'dof'=4] {'dof'}, dimensions={0}, use_global_device_ids=true | all-gather | bytes 798720 | tf_op jit(solution)/shard_map/all_gather | solution.py:228
  69.7 4.8 %shard_map.81 = f32[8,96,128]{2,1,0:T(8,128)} custom-call(bf16[768,3072]{1,0:T(8,128)(2,1)} %matrix_ref.11, bf16[4,624,128]{2,1,0:T(8,128)(2,1)} %bitcast.16), custom_call_target="tpu_custom_call" | custom-call | flops 75497472 | bytes 5357568 | tf_op jit(solution)/shard_map/pallas_call | solution.py:36
  79.1 5.4 %shard_map.80 = (f32[1024,128]{1,0:T(8,128)}, bf16[4,256,128]{2,1,0:T(8,128)(2,1)}, f32[8,128]{1,0:T(8,128)}) custom-call(bf16[1024,2048]{1,0:T(8,128)(2,1)} %bitcast.9, bf16[4,624,128]{2,1,0:T(8,128)(2,1)} %bitcast.17, f32[1024,128]{1,0:T(8,128)} %get-tuple-element.43.product_ref.refs_2_, f32[1024,128]{1,0:T(8,128)} %broadcast_in_dim.2.stiffness_ref), custom_call_target="tpu_custom_call" | custom-call | flops 536870912 | bytes 5881856 | tf_op jit(solution)/shard_map/pallas_call | solution.py:36
  86.3 4.6 %all-to-all-start.3 = ((bf16[4,256,128]{2,1,0:T(8,128)(2,1)}), bf16[4,256,128]{2,1,0:T(8,128)(2,1)S(1)}, u32[]{:S(2)}, u32[]{:S(2)}) async-start(bf16[4,256,128]{2,1,0:T(8,128)(2,1)} %get-tuple-element.47), calls=%async_computation.3 | async-start | bytes 524288 | tf_op jit(solution)/shard_map/all_to_all | solution.py:224
  93.3 20.4 %all-gather.2 = bf16[3072,128]{1,0:T(8,128)(2,1)} all-gather(bf16[768,128]{1,0:T(8,128)(2,1)} %get-tuple-element.46), channel_id=4, replica_groups=mesh['sector'=8,'dof'=4] {'dof'}, dimensions={0}, use_global_device_ids=true | all-gather | bytes 983040 | tf_op jit(solution)/shard_map/all_gather | solution.py:228
  114.4 6.9 %shard_map.83 = (f32[1024,128]{1,0:T(8,128)}, bf16[8,112,128]{2,1,0:T(8,128)(2,1)}, bf16[256,128]{1,0:T(8,128)(2,1)}, bf16[256,128]{1,0:T(8,128)(2,1)}) custom-call(bf16[1024,4096]{1,0:T(8,128)(2,1)} %matrix_ref.10, bf16[4,768,128]{2,1,0:T(8,128)(2,1)} %bitcast.20, bf16[4,256,128]{2,1,0:T(8,128)(2,1)} %copy-done.1, f32[1,768]{1,0:T(1,128)} %springs_ref.11, ...), custom_call_target="tpu_custom_call" | custom-call | flops 1073741824 | bytes 9444352 | tf_op jit(solution)/shard_map/pallas_call | solution.py:36
  127.4 4.7 %collective-permute-done.2.before_ref = bf16[256,128]{1,0:T(8,128)(2,1)S(1)} collective-permute-done((bf16[256,128]{1,0:T(8,128)(2,1)}, bf16[256,128]{1,0:T(8,128)(2,1)S(1)}, u32[]{:S(2)}, u32[]{:S(2)}) %collective-permute-start.2) | collective-permute-done | bytes 65568 | tf_op jit(solution)/shard_map/ppermute | solution.py:268
  132.2 17.0 %all-gather.3 = bf16[2496,128]{1,0:T(8,128)(2,1)} all-gather(bf16[624,128]{1,0:T(8,128)(2,1)S(1)} %shard_map.84), channel_id=5, replica_groups=mesh['sector'=8,'dof'=4] {'dof'}, dimensions={0}, use_global_device_ids=true | all-gather | bytes 798720 | tf_op jit(solution)/shard_map/all_gather | solution.py:228
  149.2 4.7 %shard_map.86 = bf16[8,96,128]{2,1,0:T(8,128)(2,1)} custom-call(bf16[768,3072]{1,0:T(8,128)(2,1)} %matrix_ref.11, bf16[4,624,128]{2,1,0:T(8,128)(2,1)} %bitcast.12), custom_call_target="tpu_custom_call" | custom-call | flops 75497472 | bytes 5357568 | tf_op jit(solution)/shard_map/pallas_call | solution.py:36
  157.3 6.6 %shard_map.85 = (f32[1024,128]{1,0:T(8,128)}, bf16[4,256,128]{2,1,0:T(8,128)(2,1)}, f32[8,128]{1,0:T(8,128)}, f32[1024,128]{1,0:T(8,128)}, f32[1024,128]{1,0:T(8,128)}, /*index=5*/f32[1024,128]{1,0:T(8,128)}) custom-call(bf16[1024,2048]{1,0:T(8,128)(2,1)} %bitcast.10, bf16[4,624,128]{2,1,0:T(8,128)(2,1)} %bitcast.13, ...), custom_call_target="tpu_custom_call" | custom-call | flops 536870912 | bytes 7454720 | tf_op jit(solution)/shard_map/pallas_call | solution.py:36
  169.8 20.7 %all-gather.4 = bf16[3072,128]{1,0:T(8,128)(2,1)} all-gather(bf16[768,128]{1,0:T(8,128)(2,1)} %get-tuple-element.57), channel_id=6, replica_groups=mesh['sector'=8,'dof'=4] {'dof'}, dimensions={0}, use_global_device_ids=true | all-gather | bytes 983040 | tf_op jit(solution)/shard_map/all_gather | solution.py:228
  191.1 6.9 %shard_map.88 = (f32[1024,128]{1,0:T(8,128)}, bf16[8,112,128]{2,1,0:T(8,128)(2,1)}, bf16[256,128]{1,0:T(8,128)(2,1)}, bf16[256,128]{1,0:T(8,128)(2,1)}) custom-call(bf16[1024,4096]{1,0:T(8,128)(2,1)} %matrix_ref.10, bf16[4,768,128]{2,1,0:T(8,128)(2,1)} %bitcast.21, bf16[4,256,128]{2,1,0:T(8,128)(2,1)} %copy-done.2, f32[1,768]{1,0:T(1,128)} %springs_ref.11, ...), custom_call_target="tpu_custom_call" | custom-call | flops 1073741824 | bytes 9444352 | tf_op jit(solution)/shard_map/pallas_call | solution.py:36
  198.1 4.0 %all-to-all-start.7 = ((bf16[8,112,128]{2,1,0:T(8,128)(2,1)}), bf16[8,112,128]{2,1,0:T(8,128)(2,1)S(1)}, u32[]{:S(2)}, u32[]{:S(2)}) async-start(bf16[8,112,128]{2,1,0:T(8,128)(2,1)} %get-tuple-element.62), calls=%async_computation.7 | async-start | bytes 458752 | tf_op jit(solution)/shard_map/all_to_all | solution.py:224
  204.8 4.8 %collective-permute-done.4.before_ref = bf16[256,128]{1,0:T(8,128)(2,1)S(1)} collective-permute-done((bf16[256,128]{1,0:T(8,128)(2,1)}, bf16[256,128]{1,0:T(8,128)(2,1)S(1)}, u32[]{:S(2)}, u32[]{:S(2)}) %collective-permute-start.4) | collective-permute-done | bytes 65568 | tf_op jit(solution)/shard_map/ppermute | solution.py:268
  209.6 16.9 %all-gather.5 = bf16[2496,128]{1,0:T(8,128)(2,1)} all-gather(bf16[624,128]{1,0:T(8,128)(2,1)S(1)} %shard_map.89), channel_id=7, replica_groups=mesh['sector'=8,'dof'=4] {'dof'}, dimensions={0}, use_global_device_ids=true | all-gather | bytes 798720 | tf_op jit(solution)/shard_map/all_gather | solution.py:228
  226.6 4.8 %shard_map.91 = bf16[8,96,128]{2,1,0:T(8,128)(2,1)} custom-call(bf16[768,3072]{1,0:T(8,128)(2,1)} %matrix_ref.11, bf16[4,624,128]{2,1,0:T(8,128)(2,1)} %bitcast.14), custom_call_target="tpu_custom_call" | custom-call | flops 75497472 | bytes 5357568 | tf_op jit(solution)/shard_map/pallas_call | solution.py:36
  234.7 6.8 %shard_map.90 = (f32[1024,128]{1,0:T(8,128)}, bf16[4,256,128]{2,1,0:T(8,128)(2,1)}, f32[8,128]{1,0:T(8,128)}, f32[1024,128]{1,0:T(8,128)}, f32[1024,128]{1,0:T(8,128)}, /*index=5*/f32[1024,128]{1,0:T(8,128)}) custom-call(bf16[1024,2048]{1,0:T(8,128)(2,1)} %bitcast.11, bf16[4,624,128]{2,1,0:T(8,128)(2,1)} %bitcast.15, ...), custom_call_target="tpu_custom_call" | custom-call | flops 536870912 | bytes 7979008 | tf_op jit(solution)/shard_map/pallas_call | solution.py:36
  244.5 13.4 %all_to_all.50.sums_ref = f32[32,8,128]{2,1,0:T(8,128)} all-to-all(f32[32,8,128]{2,1,0:T(8,128)} %get-tuple-element.70), channel_id=1, replica_groups=mesh['sector'=8,'dof'=4] {'sector','dof'}, dimensions={0} | all-to-all | bytes 262144 | tf_op jit(solution)/shard_map/all_to_all | solution.py:224
  257.9 3.8 %shard_map.93 = (f32[1,1024,128]{2,1,0:T(8,128)}, f32[1,1024,128]{2,1,0:T(8,128)}) custom-call(f32[32,8,128]{2,1,0:T(8,128)} %all_to_all.50.sums_ref, f32[1024,128]{1,0:T(8,128)} %get-tuple-element.71.image_ref, f32[1024,128]{1,0:T(8,128)} %get-tuple-element.69.residual_ref, f32[1024,128]{1,0:T(8,128)} %get-tuple-element.72.precon_ref, ...), custom_call_target="tpu_custom_call" | custom-call | tf_op jit(solution)/shard_map/pallas_call | solution.py:206
  (49 shorter events, 39.9 us)
Async XLA Ops:
  2.5 29.1 %all-to-all-start = ((bf16[4,256,128]{2,1,0:T(8,128)(2,1)}), bf16[4,256,128]{2,1,0:T(8,128)(2,1)S(1)}, u32[]{:S(2)}, u32[]{:S(2)}) async-start(bf16[4,256,128]{2,1,0:T(8,128)(2,1)} %get-tuple-element.39), calls=%async_computation | async-start | bytes 524288 | tf_op jit(solution)/shard_map/all_to_all | solution.py:224
  31.6 0.7 copy-start.3
  39.3 38.7 %copy-start.6 = (f32[1,768]{1,0:T(1,128)S(1)}, f32[1,768]{1,0:T(1,128)}, u32[]{:S(2)}) copy-start(f32[1,768]{1,0:T(1,128)} %springs_ref.11) | copy-start | bytes 9220
  39.3 38.8 %copy-start.7 = (f32[1,1024]{1,0:T(1,128)S(1)}, f32[1,1024]{1,0:T(1,128)}, u32[]{:S(2)}) copy-start(f32[1,1024]{1,0:T(1,128)} %param.7) | copy-start | bytes 12292
  39.3 13.8 %all-to-all-start.1 = ((f32[8,112,128]{2,1,0:T(8,128)}), f32[8,112,128]{2,1,0:T(8,128)S(1)}, u32[]{:S(2)}, u32[]{:S(2)}) async-start(f32[8,112,128]{2,1,0:T(8,128)} %get-tuple-element.42), calls=%async_computation.1 | async-start | bytes 917504 | tf_op jit(solution)/shard_map/all_to_all | solution.py:224
  43.1 10.0 %collective-permute-start = (bf16[256,128]{1,0:T(8,128)(2,1)}, bf16[256,128]{1,0:T(8,128)(2,1)S(1)}, u32[]{:S(2)}, u32[]{:S(2)}) collective-permute-start(bf16[256,128]{1,0:T(8,128)(2,1)} %get-tuple-element.40), channel_id=1, source_target_pairs={{0,4},{4,8},{8,12},{12,16},{16,20},{20,24},{24,28},{28,0},{1,5},{5... | collective-permute-start | bytes 196616 | tf_op jit(solution)/shard_map/ppermute | solution.py:268
  43.6 9.5 %collective-permute-start.1 = (bf16[256,128]{1,0:T(8,128)(2,1)}, bf16[256,128]{1,0:T(8,128)(2,1)S(1)}, u32[]{:S(2)}, u32[]{:S(2)}) collective-permute-start(bf16[256,128]{1,0:T(8,128)(2,1)} %get-tuple-element.41), channel_id=1, source_target_pairs={{4,0},{8,4},{12,8},{16,12},{20,16},{24,20},{28,24},{0,28},{5,1},{9... | collective-permute-start | bytes 196616 | tf_op jit(solution)/shard_map/ppermute | solution.py:269
  74.6 11.7 %all-to-all-start.2 = ((f32[8,96,128]{2,1,0:T(8,128)}), f32[8,96,128]{2,1,0:T(8,128)S(1)}, u32[]{:S(2)}, u32[]{:S(2)}) async-start(f32[8,96,128]{2,1,0:T(8,128)} %shard_map.81), calls=%async_computation.2 | async-start | bytes 786432 | tf_op jit(solution)/shard_map/all_to_all | solution.py:224
  86.3 4.6 %copy-start = (f32[8,96,128]{2,1,0:T(8,128)}, f32[8,96,128]{2,1,0:T(8,128)S(1)}, u32[]{:S(2)}) copy-start(f32[8,96,128]{2,1,0:T(8,128)S(1)} %all-to-all-done.2.hubs_ref) | copy-start | bytes 1179652
  86.3 27.4 %all-to-all-start.3 = ((bf16[4,256,128]{2,1,0:T(8,128)(2,1)}), bf16[4,256,128]{2,1,0:T(8,128)(2,1)S(1)}, u32[]{:S(2)}, u32[]{:S(2)}) async-start(bf16[4,256,128]{2,1,0:T(8,128)(2,1)} %get-tuple-element.47), calls=%async_computation.3 | async-start | bytes 524288 | tf_op jit(solution)/shard_map/all_to_all | solution.py:224
  113.7 0.7 copy-start.1
  121.3 10.9 %all-to-all-start.4 = ((bf16[8,112,128]{2,1,0:T(8,128)(2,1)}), bf16[8,112,128]{2,1,0:T(8,128)(2,1)S(1)}, u32[]{:S(2)}, u32[]{:S(2)}) async-start(bf16[8,112,128]{2,1,0:T(8,128)(2,1)} %get-tuple-element.51), calls=%async_computation.4 | async-start | bytes 458752 | tf_op jit(solution)/shard_map/all_to_all | solution.py:224
  124.7 7.4 %collective-permute-start.2 = (bf16[256,128]{1,0:T(8,128)(2,1)}, bf16[256,128]{1,0:T(8,128)(2,1)S(1)}, u32[]{:S(2)}, u32[]{:S(2)}) collective-permute-start(bf16[256,128]{1,0:T(8,128)(2,1)} %get-tuple-element.49), channel_id=1, source_target_pairs={{0,4},{4,8},{8,12},{12,16},{16,20},{20,24},{24,28},{28,0},{1,5},{5... | collective-permute-start | bytes 196616 | tf_op jit(solution)/shard_map/ppermute | solution.py:268
  125.1 7.0 %collective-permute-start.3 = (bf16[256,128]{1,0:T(8,128)(2,1)}, bf16[256,128]{1,0:T(8,128)(2,1)S(1)}, u32[]{:S(2)}, u32[]{:S(2)}) collective-permute-start(bf16[256,128]{1,0:T(8,128)(2,1)} %get-tuple-element.50), channel_id=1, source_target_pairs={{4,0},{8,4},{12,8},{16,12},{20,16},{24,20},{28,24},{0,28},{5,1},{9... | collective-permute-start | bytes 196616 | tf_op jit(solution)/shard_map/ppermute | solution.py:269
  153.9 10.0 %all-to-all-start.5 = ((bf16[8,96,128]{2,1,0:T(8,128)(2,1)}), bf16[8,96,128]{2,1,0:T(8,128)(2,1)S(1)}, u32[]{:S(2)}, u32[]{:S(2)}) async-start(bf16[8,96,128]{2,1,0:T(8,128)(2,1)} %shard_map.86), calls=%async_computation.5 | async-start | bytes 393216 | tf_op jit(solution)/shard_map/all_to_all | solution.py:224
  164.0 3.4 %copy-start.4 = (bf16[8,96,128]{2,1,0:T(8,128)(2,1)}, bf16[8,96,128]{2,1,0:T(8,128)(2,1)S(1)}, u32[]{:S(2)}) copy-start(bf16[8,96,128]{2,1,0:T(8,128)(2,1)S(1)} %all-to-all-done.5.hubs_ref) | copy-start | bytes 589828
  164.0 26.4 %all-to-all-start.6 = ((bf16[4,256,128]{2,1,0:T(8,128)(2,1)}), bf16[4,256,128]{2,1,0:T(8,128)(2,1)S(1)}, u32[]{:S(2)}, u32[]{:S(2)}) async-start(bf16[4,256,128]{2,1,0:T(8,128)(2,1)} %get-tuple-element.58), calls=%async_computation.6 | async-start | bytes 524288 | tf_op jit(solution)/shard_map/all_to_all | solution.py:224
  190.4 0.7 copy-start.2
  198.1 11.5 %all-to-all-start.7 = ((bf16[8,112,128]{2,1,0:T(8,128)(2,1)}), bf16[8,112,128]{2,1,0:T(8,128)(2,1)S(1)}, u32[]{:S(2)}, u32[]{:S(2)}) async-start(bf16[8,112,128]{2,1,0:T(8,128)(2,1)} %get-tuple-element.62), calls=%async_computation.7 | async-start | bytes 458752 | tf_op jit(solution)/shard_map/all_to_all | solution.py:224
  202.1 7.5 %collective-permute-start.4 = (bf16[256,128]{1,0:T(8,128)(2,1)}, bf16[256,128]{1,0:T(8,128)(2,1)S(1)}, u32[]{:S(2)}, u32[]{:S(2)}) collective-permute-start(bf16[256,128]{1,0:T(8,128)(2,1)} %get-tuple-element.60), channel_id=1, source_target_pairs={{0,4},{4,8},{8,12},{12,16},{16,20},{20,24},{24,28},{28,0},{1,5},{5... | collective-permute-start | bytes 196616 | tf_op jit(solution)/shard_map/ppermute | solution.py:268
  202.6 7.0 %collective-permute-start.5 = (bf16[256,128]{1,0:T(8,128)(2,1)}, bf16[256,128]{1,0:T(8,128)(2,1)S(1)}, u32[]{:S(2)}, u32[]{:S(2)}) collective-permute-start(bf16[256,128]{1,0:T(8,128)(2,1)} %get-tuple-element.61), channel_id=1, source_target_pairs={{4,0},{8,4},{12,8},{16,12},{20,16},{24,20},{28,24},{0,28},{5,1},{9... | collective-permute-start | bytes 196616 | tf_op jit(solution)/shard_map/ppermute | solution.py:269
  231.3 10.2 %all-to-all-start.8 = ((bf16[8,96,128]{2,1,0:T(8,128)(2,1)}), bf16[8,96,128]{2,1,0:T(8,128)(2,1)S(1)}, u32[]{:S(2)}, u32[]{:S(2)}) async-start(bf16[8,96,128]{2,1,0:T(8,128)(2,1)} %shard_map.91), calls=%async_computation.8 | async-start | bytes 393216 | tf_op jit(solution)/shard_map/all_to_all | solution.py:224
  241.5 0.7 copy-start.5

commit v12 on v7

v12 whole, which is shorter than its diff:
```python
import functools

import jax
import jax.numpy as jnp
from jax import lax
from jax.experimental import pallas as pl
from jax.experimental.pallas import tpu as pltpu
from jax.sharding import PartitionSpec as P

ITERS = 3
LANES = 128
MIB = 1024 * 1024
SUM_ROWS = 8
TERM_ROWS = 16
f32 = jnp.float32
bf16 = jnp.bfloat16


def shape(*dims, dtype=f32):
    return jax.ShapeDtypeStruct(dims, dtype)


def call(kernel, outs, operands, flops=0):
    whole = pl.BlockSpec(memory_space=pltpu.VMEM)
    return pl.pallas_call(
        kernel,
        in_specs=[whole] * len(operands),
        out_specs=jax.tree.map(lambda _: whole, outs),
        out_shape=outs,
        compiler_params=pltpu.CompilerParams(vmem_limit_bytes=20 * MIB),
        cost_estimate=pl.CostEstimate(
            flops=flops, bytes_accessed=sum(x.size * x.dtype.itemsize for x in operands), transcendentals=0
        ),
    )(*operands)


def in_terms(sums):
    terms = None
    for at in range(3):
        term = sums.astype(bf16).astype(f32)
        sums = sums - term
        terms = term if at == 0 else terms + pltpu.roll(term, 2 * at, 0)
    return jnp.concatenate([terms, jnp.zeros_like(terms)], axis=0)


def from_terms(terms):
    terms = terms[:SUM_ROWS].astype(f32)
    sums = terms + pltpu.roll(terms, SUM_ROWS - 2, 0) + pltpu.roll(terms, SUM_ROWS - 4, 0)
    return jnp.where(lax.broadcasted_iota(jnp.int32, sums.shape, 0) < 2, sums, 0.0)


def product_kernel(parts, matrix_ref, springs_ref, tops_ref, *refs):
    *refs, out_ref, load_ref, right_ref, left_ref = refs
    here = lax.axis_index("dof")
    _, top, _ = tops_ref.shape
    for part in range(parts):
        end_ref = refs[part]
        end = end_ref.shape[0]
        start = part * (top + end)
        owner = lax.rem(here + part, parts)
        product = jnp.dot(
            matrix_ref[:, start : start + top], tops_ref[part], preferred_element_type=f32
        ) + jnp.dot(
            matrix_ref[:, pl.ds(pl.multiple_of(owner * (top + end) + top, LANES), end)],
            end_ref[...],
            preferred_element_type=f32,
        )
        if part:
            out_ref[...] += product
        else:
            out_ref[...] = product

    sectors, height, _ = load_ref.shape
    cases = out_ref.shape[1] // sectors
    quarter = right_ref.shape[0]
    left_ref[...] = out_ref[:quarter].astype(bf16)
    right_ref[...] = out_ref[quarter : 2 * quarter].astype(bf16)
    for at in range((height - TERM_ROWS) // cases):
        rows = slice(at * LANES, (at + 1) * LANES)
        turned = (out_ref[rows].T * springs_ref[:, rows]).astype(load_ref.dtype)
        for s in range(sectors):
            load_ref[s, at * cases : (at + 1) * cases] = turned[s * cases : (s + 1) * cases]
    terms = in_terms(refs[parts][...]) if refs[parts:] else jnp.zeros((TERM_ROWS, LANES), f32)
    for s in range(sectors):
        load_ref[s, height - TERM_ROWS :] = terms.astype(load_ref.dtype)


def pack_kernel(before_ref, after_ref, *refs):
    *part_refs, out_ref = refs
    quarter = before_ref.shape[0]
    height = part_refs[0].shape[0] - TERM_ROWS
    out_ref[:quarter] = before_ref[...]
    out_ref[quarter : 2 * quarter] = after_ref[...]
    total = sum(ref[...].astype(f32) for ref in part_refs)
    out_ref[2 * quarter : 2 * quarter + height] = total[:height].astype(bf16)
    out_ref[2 * quarter + height :] = in_terms(from_terms(total[height:])).astype(bf16)


def alpha_from(sums):
    return sums[0:1] / (sums[1:2] + 1e-06)


def hub_kernel(cases, matrix_ref, pieces_ref, out_ref):
    parts = pieces_ref.shape[0]
    height = out_ref.shape[0]
    chunks = height // cases
    depth = chunks * LANES
    first = pieces_ref.shape[1] - TERM_ROWS - height
    total = None
    for part in range(parts):
        load = jnp.concatenate(
            [pieces_ref[part, first + c * cases : first + (c + 1) * cases] for c in range(chunks)], axis=1
        )
        product = lax.dot_general(
            load,
            matrix_ref[:, part * depth : (part + 1) * depth],
            (((1,), (1,)), ((), ())),
            preferred_element_type=f32,
        )
        total = product if total is None else total + product
    for c in range(chunks):
        out_ref[c * cases : (c + 1) * cases] = total[:, c * LANES : (c + 1) * LANES].astype(out_ref.dtype)


def base_kernel(first, matrix_ref, pieces_ref, product_ref, stiffness_ref, *refs):
    if first:
        base_ref, end_ref, factor_ref = refs
    else:
        *refs, base_ref, end_ref, factor_ref, left_ref, newer_ref, better_ref = refs
        image_ref, residual_ref, precon_ref = refs[:3]
    parts, height, _ = pieces_ref.shape
    depth = matrix_ref.shape[1] // parts
    base_ref[...] = stiffness_ref[...] * product_ref[...]
    for part in range(parts):
        base_ref[...] += jnp.dot(
            matrix_ref[:, part * depth : (part + 1) * depth],
            pieces_ref[part, :depth],
            preferred_element_type=f32,
        )
    if first:
        factor_ref[...] = jnp.ones_like(factor_ref)
    else:
        alpha = alpha_from(sum(from_terms(pieces_ref[part, height - TERM_ROWS :]) for part in range(parts)))
        factor_ref[...] = jnp.broadcast_to(-alpha, factor_ref.shape)
        base_ref[...] = image_ref[...] - alpha * base_ref[...]
        left_ref[...] = residual_ref[...] - alpha * image_ref[...]
        gain = alpha * precon_ref[...]
        better_ref[...] = refs[3][...] + gain if len(refs) > 3 else gain
        newer_ref[...] = precon_ref[...] - alpha * product_ref[...]
    end_ref[...] = base_ref[base_ref.shape[0] - end_ref.shape[0] :].astype(bf16)


def image_kernel(sectors, base_ref, springs_ref, factor_ref, residual_ref, *refs):
    *hub_refs, image_ref, top_ref, sums_ref, hubs_ref = refs
    here = lax.axis_index("sector")
    for ahead in range(sectors):
        hubs_ref[lax.rem(here + ahead, sectors)] = hub_refs[ahead][...].astype(f32)
    attached = top_ref.shape[0]
    chunks = attached // LANES
    cases = hubs_ref.shape[1] // chunks
    factor = factor_ref[0:1]
    for c in range(chunks):
        at = slice(c * LANES, (c + 1) * LANES)
        hub = jnp.concatenate([hubs_ref[s, c * cases : (c + 1) * cases] for s in range(sectors)], axis=0)
        image = base_ref[at] - factor * (hub * springs_ref[:, at]).T
        image_ref[at] = image
        top_ref[at] = image.astype(bf16)
    image_ref[attached:] = base_ref[attached:]
    image = image_ref[...]
    upper = jnp.sum(image * residual_ref[...], axis=0, keepdims=True)
    lower = jnp.sum(image * image, axis=0, keepdims=True)
    rest = jnp.zeros((SUM_ROWS - 2, image.shape[1]), f32)
    sums = jnp.concatenate([upper, lower, rest], axis=0)
    sums_ref[...] = jnp.broadcast_to(sums, sums_ref.shape)


def last_kernel(sums_ref, image_ref, residual_ref, precon_ref, solution_ref, newer_ref, left_ref):
    alpha = alpha_from(jnp.sum(sums_ref[...], axis=0))
    newer_ref[0] = solution_ref[...] + alpha * precon_ref[...]
    left_ref[0] = residual_ref[...] - alpha * image_ref[...]


def last_update(sums, *state):
    rows, loads = state[0].shape
    height = rows // 4
    block = pl.BlockSpec((height, loads), lambda k: (k, 0))
    out_block = pl.BlockSpec((1, height, loads), lambda k: (0, k, 0))
    out = shape(1, rows, loads)
    return pl.pallas_call(
        last_kernel,
        grid=(4,),
        in_specs=[pl.BlockSpec(sums.shape, lambda k: (0, 0, 0))] + [block] * len(state),
        out_specs=(out_block, out_block),
        out_shape=(out, out),
        compiler_params=pltpu.CompilerParams(vmem_limit_bytes=60 * MIB),
    )(sums, *state)


def round_kernel(field_ref, top_ref, end_ref):
    attached = top_ref.shape[0]
    top_ref[...] = field_ref[0, :attached].astype(bf16)
    end_ref[...] = field_ref[0, attached:].astype(bf16)


def exchange(blocks, axes):
    return lax.all_to_all(blocks, axes, split_axis=0, concat_axis=0)


def from_ahead(cells, axis, distance):
    count = lax.axis_size(axis)
    return lax.ppermute(cells, axis, [((i + distance) % count, i) for i in range(count)])


def one_from_each(cells, axis):
    return [cells] + [from_ahead(cells, axis, d) for d in range(1, lax.axis_size(axis))]


def mine_from_each(blocks, axis):
    count, here = lax.axis_size(axis), lax.axis_index(axis)
    own = [lax.dynamic_index_in_dim(blocks, (here - d) % count, 0, False) for d in range(count)]
    return own[:1] + [from_ahead(own[d], axis, d) for d in range(1, count)]


def gathered(field):
    return lax.all_gather(field, "dof", axis=0)


def around(sectors):
    onward = [(s, (s + 1) % sectors) for s in range(sectors)]
    return onward, [(b, a) for a, b in onward]


def alpha_of(sums):
    return alpha_from(jnp.sum(sums, axis=0))[0]


def tiled_body(rhs, diagonal, coupling, springs, precond, hub_inverse):
    residual = rhs[0]
    rows, loads = residual.shape
    attached = springs.shape[1]
    quarter = rows - attached
    sectors, parts = lax.axis_size("sector"), lax.axis_size("dof")
    cases = loads // sectors
    height = attached // LANES * cases
    onward, backward = around(sectors)
    full, face = shape(rows, loads), shape(quarter, loads, dtype=bf16)
    top_shape = shape(attached, loads, dtype=bf16)

    stiffness = diagonal[0] + jnp.pad(springs[0], (0, quarter))
    stiffness = jnp.broadcast_to(stiffness[:, None], (rows, loads))
    state = sums = ()

    top, end = call(round_kernel, (top_shape, face), (rhs,))
    for step in range(ITERS):
        first, last = step == 0, step == ITERS - 1
        sent = f32 if first else bf16
        product, load, right, left = call(
            functools.partial(product_kernel, parts),
            (full, shape(sectors, height + TERM_ROWS, LANES, dtype=sent), face, face),
            (precond, springs, gathered(top), *one_from_each(end, "dof"), *sums),
            flops=2 * precond.size * loads,
        )
        before = lax.ppermute(right, "sector", onward)
        after = lax.ppermute(left, "sector", backward)
        packed = call(
            pack_kernel,
            shape(2 * quarter + height + TERM_ROWS, loads, dtype=bf16),
            (before, after, *mine_from_each(load, "sector")),
        )
        pieces = gathered(packed)
        hub = call(
            functools.partial(hub_kernel, cases),
            shape(height, LANES, dtype=sent),
            (hub_inverse, pieces),
            flops=2 * hub_inverse.size * cases,
        )
        hubs = one_from_each(hub, "sector")
        base, end, factor, *state = call(
            functools.partial(base_kernel, first),
            (full, face, shape(SUM_ROWS, loads)) + (() if first else (full, full, full)),
            (coupling[0], pieces, product, stiffness, *state),
            flops=2 * coupling.size * loads,
        )
        residual, precon, *solution = (residual, product) if first else state
        sums_shape = shape(sectors * parts, SUM_ROWS, loads) if last else shape(SUM_ROWS, loads)
        image, top, sums, _ = call(
            functools.partial(image_kernel, sectors),
            (full, top_shape, sums_shape, shape(sectors, height, LANES)),
            (base, springs, factor, residual, *hubs),
        )
        state = (image, residual, precon, *solution)
        sums = (sums,)
    out = shape(1, rows, loads)
    return call(last_kernel, (out, out), (exchange(*sums, ("sector", "dof")), *state))


def plain_body(rhs, diagonal, coupling, springs, precond, hub_inverse):
    residual = rhs[0]
    spring_rows = springs[0][:, None]
    rows, loads = residual.shape
    quarter = rows // 4
    sectors = lax.axis_size("sector")
    onward, backward = around(sectors)
    solution = jnp.zeros_like(residual)

    def whole(field):
        return gathered(field.astype(bf16)).reshape(-1, loads)

    def copies(cells, axes):
        count = lax.axis_size(axes)
        return exchange(jnp.broadcast_to(cells[None], (count,) + cells.shape), axes)

    precon = jnp.dot(precond, whole(residual), preferred_element_type=f32)
    for step in range(ITERS):
        faces = precon[: 2 * quarter].astype(bf16)
        before = lax.ppermute(faces[quarter:], "sector", onward)
        after = lax.ppermute(faces[:quarter], "sector", backward)
        couple = jnp.dot(
            coupling[0], whole(jnp.concatenate([before, after])), preferred_element_type=f32
        )
        attached = precon[: 3 * quarter]
        load = (spring_rows * attached).T.reshape(sectors, loads // sectors, -1)
        load = jnp.sum(exchange(load, "sector"), axis=0).astype(bf16)
        load = copies(load, "dof").transpose(0, 2, 1).reshape(hub_inverse.shape[1], -1)
        hub = jnp.dot(hub_inverse, load, preferred_element_type=f32)
        hub = copies(hub.T, "sector").reshape(loads, -1).T
        pull = jnp.pad(spring_rows * (attached - hub), ((0, quarter), (0, 0)))
        image = diagonal[0][:, None] * precon + couple + pull
        sums = jnp.stack([jnp.sum(image * residual, axis=0), jnp.sum(image * image, axis=0)])
        alpha = alpha_of(copies(sums, ("sector", "dof")))
        solution = solution + alpha * precon
        residual = residual - alpha * image
        if step < ITERS - 1:
            change = jnp.dot(precond, whole(image), preferred_element_type=f32)
            precon = precon - alpha * change
    return (solution[None], residual[None])


def body(rhs, *rest):
    rows, loads = rhs.shape[1:]
    cases = loads // lax.axis_size("sector")
    tiled = loads == LANES and (rows // 4) % LANES == 0 and cases % 16 == 0
    return (tiled_body if tiled else plain_body)(rhs, *rest)


def solution(mesh):
    placed = (
        P("sector", "dof", None),
        P("sector", "dof"),
        P("sector", "dof", None),
        P("sector", "dof"),
        P("dof", None),
        P("dof", None),
    )
    return jax.shard_map(
        body,
        mesh=mesh,
        in_specs=placed,
        out_specs=(P("sector", "dof", None), P("sector", "dof", None)),
        check_vma=False,
    )
```

time: 280 us -> 220 us (0.79)
  Pallas kernels: 65.1 us -> 19.4 us
  starting transfers between devices: 45.2 us -> 61.3 us
  waiting for transfers between devices: 22.9 us -> 12 us
  blocking collectives: 126 us -> 116 us
  local copies, waits for them, and re-layouts: 18.1 us -> 9.97 us
    ppermute x0 -> x51, starting transfers between devices: none -> 53.3 us  [from_ahead(): lax.ppermute(cells, axis, [((i + distance) % count, i) for i in range(cou...]
    pallas_call x17, Pallas kernels: 65.1 us -> 19.4 us  [call(): pl.pallas_call(kernel, in_specs=[whole] * len(operands), out_specs=jax.tr...]
    all_to_all x9 -> x0, starting transfers between devices: 37.1 us -> none  [exchange(): return lax.all_to_all(blocks, axes, split_axis=0, concat_axis=0)]
    ppermute x3, waiting for transfers between devices: 20.7 us -> 0.01 us  [tiled_body(): before = lax.ppermute(right, 'sector', onward)]
    ppermute x0 -> x51, waiting for transfers between devices: none -> 12 us  [from_ahead(): lax.ppermute(cells, axis, [((i + distance) % count, i) for i in range(cou...]
    all_gather x6, blocking collectives: 114 us -> 103 us  [gathered(): return lax.all_gather(field, 'dof', axis=0)]
    unnamed x48 -> x26, local copies, waits for them, and re-layouts: 15.6 us -> 9.66 us
  transfers between devices with their start and end apart: 15 -> 57, of which waited for: 6 -> 10; matrix products, arithmetic and copies ran while one was open for 1% -> 0% of each run, Pallas kernels for 8% -> 3%
where the time goes in v12:
time: 220 us; the launch traced here: 219 us
  blocking collectives  116 us (53%)
  starting transfers between devices  61.3 us (28%)
  Pallas kernels  19.4 us (9%)
  waiting for transfers between devices  12 us (5%)
  local copies, waits for them, and re-layouts  9.97 us (5%)
    all_gather x6, blocking collectives, gathered(): return lax.all_gather(field, 'dof', axis=0)  103 us
    ppermute x51, starting transfers between devices, from_ahead(): lax.ppermute(cells, axis, [((i + distance) % count, i) for i in range(cou...  53.3 us
    pallas_call x17, Pallas kernels, call(): pl.pallas_call(kernel, in_specs=[whole] * len(operands), out_specs=jax.tr...  19.4 us
    all_to_all x1, blocking collectives, exchange(): return lax.all_to_all(blocks, axes, split_axis=0, concat_axis=0)  12.3 us
    ppermute x51, waiting for transfers between devices, from_ahead(): lax.ppermute(cells, axis, [((i + distance) % count, i) for i in range(cou...  12 us
    unnamed x26, local copies, waits for them, and re-layouts  9.66 us
    ppermute x3, starting transfers between devices, tiled_body(): after = lax.ppermute(left, 'sector', backward)  6.01 us
  transfers between devices with their start and end apart: 57, of which 10 were waited for; matrix products, arithmetic and copies ran while one was open for 0% of the time, Pallas kernels for 3%

profile of v12, /device:TPU:0, one launch (start us, length us, event | category | flops | bytes accessed | tf_op | source)
XLA Modules:
  0.0 219.3 jit_solution(10095846064920049219)
XLA Ops:
  1.7 3.1 %collective-permute-start.2 = (bf16[256,128]{1,0:T(8,128)(2,1)S(1)}, bf16[256,128]{1,0:T(8,128)(2,1)S(1)}, u32[]{:S(2)}, u32[]{:S(2)}) collective-permute-start(bf16[256,128]{1,0:T(8,128)(2,1)S(1)} %get-tuple-element.39.refs_0_), channel_id=1, source_target_pairs={{3,0},{0,1},{1,2},{2,3},{7,4},{4,5},{5,6},{6,7},{11,8},{8,9},{9,10... | collective-permute-start | bytes 196616 | tf_op jit(solution)/shard_map/ppermute | solution.py:211
  4.8 2.6 %collective-permute-start.1 = (bf16[256,128]{1,0:T(8,128)(2,1)S(1)}, bf16[256,128]{1,0:T(8,128)(2,1)S(1)}, u32[]{:S(2)}, u32[]{:S(2)}) collective-permute-start(bf16[256,128]{1,0:T(8,128)(2,1)S(1)} %get-tuple-element.39.refs_0_), channel_id=1, source_target_pairs={{2,0},{3,1},{0,2},{1,3},{6,4},{7,5},{4,6},{5,7},{10,8},{11,9},{8,1... | collective-permute-start | bytes 196616 | tf_op jit(solution)/shard_map/ppermute | solution.py:211
  8.7 17.6 %all-gather = bf16[3072,128]{1,0:T(8,128)(2,1)S(1)} all-gather(bf16[768,128]{1,0:T(8,128)(2,1)S(1)} %get-tuple-element.38), channel_id=2, replica_groups=mesh['sector'=8,'dof'=4] {'dof'}, dimensions={0}, use_global_device_ids=true | all-gather | bytes 983040 | tf_op jit(solution)/shard_map/all_gather | solution.py:225
  26.3 3.4 %copy-done = bf16[1024,4096]{1,0:T(8,128)(2,1)S(1)} copy-done((bf16[1024,4096]{1,0:T(8,128)(2,1)S(1)}, bf16[1024,4096]{1,0:T(8,128)(2,1)}, u32[]{:S(2)}) %copy-start) | copy-done | bytes 8388632
  30.4 2.3 %shard_map.78 = (f32[1024,128]{1,0:T(8,128)S(1)}, f32[8,112,128]{2,1,0:T(8,128)S(1)}, bf16[256,128]{1,0:T(8,128)(2,1)S(1)}, bf16[256,128]{1,0:T(8,128)(2,1)S(1)}) custom-call(bf16[1024,4096]{1,0:T(8,128)(2,1)S(1)} %copy-done, f32[1,768]{1,0:T(1,128)S(1)} %copy-done.6, bf16[4,768,128]{2,1,0:T(8,128)(2,1)S(1)} %bitcast.74, ...), custom_call_target="tpu_custom_call" | custom-call | flops 1073741824 | bytes 9440256 | tf_op jit(solution)/shard_map/pallas_call | solution.py:25
  34.6 2.4 %collective-permute-start.9 = (f32[112,128]{1,0:T(8,128)S(1)}, f32[112,128]{1,0:T(8,128)S(1)}, u32[]{:S(2)}, u32[]{:S(2)}) collective-permute-start(f32[112,128]{1,0:T(8,128)S(1)} %get-tuple-element.76), channel_id=1, source_target_pairs={{20,0},{24,4},{28,8},{0,12},{4,16},{8,20},{12,24},{16,28},{21,1},{... | collective-permute-start | bytes 172040 | tf_op jit(solution)/shard_map/ppermute | solution.py:211
  37.5 2.6 %collective-permute-start.4 = (bf16[256,128]{1,0:T(8,128)(2,1)S(1)}, bf16[256,128]{1,0:T(8,128)(2,1)S(1)}, u32[]{:S(2)}, u32[]{:S(2)}) collective-permute-start(bf16[256,128]{1,0:T(8,128)(2,1)S(1)} %get-tuple-element.41), channel_id=1, source_target_pairs={{4,0},{8,4},{12,8},{16,12},{20,16},{24,20},{28,24},{0,28},{5,1},{9... | collective-permute-start | bytes 196616 | tf_op jit(solution)/shard_map/ppermute | solution.py:264
  45.0 17.0 %all-gather.1 = bf16[2496,128]{1,0:T(8,128)(2,1)S(1)} all-gather(bf16[624,128]{1,0:T(8,128)(2,1)S(1)} %shard_map.79), channel_id=3, replica_groups=mesh['sector'=8,'dof'=4] {'dof'}, dimensions={0}, use_global_device_ids=true | all-gather | bytes 798720 | tf_op jit(solution)/shard_map/all_gather | solution.py:225
  62.0 2.3 %copy-done.1 = bf16[768,3072]{1,0:T(8,128)(2,1)S(1)} copy-done((bf16[768,3072]{1,0:T(8,128)(2,1)S(1)}, bf16[768,3072]{1,0:T(8,128)(2,1)}, u32[]{:S(2)}) %copy-start.1) | copy-done | bytes 4718616
  65.6 2.3 %collective-permute-start.17 = (f32[96,128]{1,0:T(8,128)S(1)}, f32[96,128]{1,0:T(8,128)S(1)}, u32[]{:S(2)}, u32[]{:S(2)}) collective-permute-start(f32[96,128]{1,0:T(8,128)S(1)} %shard_map.81.refs_0_), channel_id=1, source_target_pairs={{24,0},{28,4},{0,8},{4,12},{8,16},{12,20},{16,24},{20,28},{25,1},{... | collective-permute-start | bytes 147464 | tf_op jit(solution)/shard_map/ppermute | solution.py:211
  74.3 2.2 copy-done.2
  77.8 2.2 %collective-permute-start.20 = (bf16[256,128]{1,0:T(8,128)(2,1)S(1)}, bf16[256,128]{1,0:T(8,128)(2,1)S(1)}, u32[]{:S(2)}, u32[]{:S(2)}) collective-permute-start(bf16[256,128]{1,0:T(8,128)(2,1)S(1)} %get-tuple-element.47.refs_0_), channel_id=1, source_target_pairs={{2,0},{3,1},{0,2},{1,3},{6,4},{7,5},{4,6},{5,7},{10,8},{11,9},{8,1... | collective-permute-start | bytes 196616 | tf_op jit(solution)/shard_map/ppermute | solution.py:211
  82.5 17.0 %all-gather.2 = bf16[3072,128]{1,0:T(8,128)(2,1)S(1)} all-gather(bf16[768,128]{1,0:T(8,128)(2,1)S(1)} %get-tuple-element.46), channel_id=4, replica_groups=mesh['sector'=8,'dof'=4] {'dof'}, dimensions={0}, use_global_device_ids=true | all-gather | bytes 983040 | tf_op jit(solution)/shard_map/all_gather | solution.py:225
  99.6 2.3 %shard_map.83 = (f32[1024,128]{1,0:T(8,128)S(1)}, bf16[8,112,128]{2,1,0:T(8,128)(2,1)S(1)}, bf16[256,128]{1,0:T(8,128)(2,1)S(1)}, bf16[256,128]{1,0:T(8,128)(2,1)S(1)}) custom-call(bf16[1024,4096]{1,0:T(8,128)(2,1)S(1)} %bitcast.58, f32[1,768]{1,0:T(1,128)S(1)} %copy-done.7, bf16[4,768,128]{2,1,0:T(8,128)(2,1)S(1)} %bitcast.72, ...), custom_call_target="tpu_custom_call" | custom-call | flops 1073741824 | bytes 9444352 | tf_op jit(solution)/shard_map/pallas_call | solution.py:25
  106.9 2.5 %collective-permute-done.29.refs_6_ = bf16[112,128]{1,0:T(8,128)(2,1)S(1)} collective-permute-done((bf16[112,128]{1,0:T(8,128)(2,1)S(1)}, bf16[112,128]{1,0:T(8,128)(2,1)S(1)}, u32[]{:S(2)}, u32[]{:S(2)}) %collective-permute-start.29) | collective-permute-done | bytes 28704 | tf_op jit(solution)/shard_map/ppermute | solution.py:211
  113.5 16.9 %all-gather.3 = bf16[2496,128]{1,0:T(8,128)(2,1)S(1)} all-gather(bf16[624,128]{1,0:T(8,128)(2,1)S(1)} %shard_map.84), channel_id=5, replica_groups=mesh['sector'=8,'dof'=4] {'dof'}, dimensions={0}, use_global_device_ids=true | all-gather | bytes 798720 | tf_op jit(solution)/shard_map/all_gather | solution.py:225
  133.4 2.3 %collective-permute-start.35 = (bf16[96,128]{1,0:T(8,128)(2,1)S(1)}, bf16[96,128]{1,0:T(8,128)(2,1)S(1)}, u32[]{:S(2)}, u32[]{:S(2)}) collective-permute-start(bf16[96,128]{1,0:T(8,128)(2,1)S(1)} %shard_map.86.refs_0_), channel_id=1, source_target_pairs={{20,0},{24,4},{28,8},{0,12},{4,16},{8,20},{12,24},{16,28},{21,1},{... | collective-permute-start | bytes 73736 | tf_op jit(solution)/shard_map/ppermute | solution.py:211
  140.7 2.6 %collective-permute-start.39 = (bf16[256,128]{1,0:T(8,128)(2,1)S(1)}, bf16[256,128]{1,0:T(8,128)(2,1)S(1)}, u32[]{:S(2)}, u32[]{:S(2)}) collective-permute-start(bf16[256,128]{1,0:T(8,128)(2,1)S(1)} %get-tuple-element.58.refs_0_), channel_id=1, source_target_pairs={{2,0},{3,1},{0,2},{1,3},{6,4},{7,5},{4,6},{5,7},{10,8},{11,9},{8,1... | collective-permute-start | bytes 196616 | tf_op jit(solution)/shard_map/ppermute | solution.py:211
  145.4 17.9 %all-gather.4 = bf16[3072,128]{1,0:T(8,128)(2,1)S(1)} all-gather(bf16[768,128]{1,0:T(8,128)(2,1)S(1)} %get-tuple-element.57), channel_id=6, replica_groups=mesh['sector'=8,'dof'=4] {'dof'}, dimensions={0}, use_global_device_ids=true | all-gather | bytes 983040 | tf_op jit(solution)/shard_map/all_gather | solution.py:225
  163.3 2.3 %shard_map.88 = (f32[1024,128]{1,0:T(8,128)S(1)}, bf16[8,112,128]{2,1,0:T(8,128)(2,1)S(1)}, bf16[256,128]{1,0:T(8,128)(2,1)S(1)}, bf16[256,128]{1,0:T(8,128)(2,1)S(1)}) custom-call(bf16[1024,4096]{1,0:T(8,128)(2,1)S(1)} %bitcast.58, f32[1,768]{1,0:T(1,128)S(1)} %copy-done.7, bf16[4,768,128]{2,1,0:T(8,128)(2,1)S(1)} %bitcast.73, ...), custom_call_target="tpu_custom_call" | custom-call | flops 1073741824 | bytes 9444352 | tf_op jit(solution)/shard_map/pallas_call | solution.py:25
  170.7 2.5 %collective-permute-done.48.refs_6_ = bf16[112,128]{1,0:T(8,128)(2,1)S(1)} collective-permute-done((bf16[112,128]{1,0:T(8,128)(2,1)S(1)}, bf16[112,128]{1,0:T(8,128)(2,1)S(1)}, u32[]{:S(2)}, u32[]{:S(2)}) %collective-permute-start.48) | collective-permute-done | bytes 28704 | tf_op jit(solution)/shard_map/ppermute | solution.py:211
  177.2 17.0 %all-gather.5 = bf16[2496,128]{1,0:T(8,128)(2,1)S(1)} all-gather(bf16[624,128]{1,0:T(8,128)(2,1)S(1)} %shard_map.89), channel_id=7, replica_groups=mesh['sector'=8,'dof'=4] {'dof'}, dimensions={0}, use_global_device_ids=true | all-gather | bytes 798720 | tf_op jit(solution)/shard_map/all_gather | solution.py:225
  197.2 2.3 %collective-permute-start.54 = (bf16[96,128]{1,0:T(8,128)(2,1)S(1)}, bf16[96,128]{1,0:T(8,128)(2,1)S(1)}, u32[]{:S(2)}, u32[]{:S(2)}) collective-permute-start(bf16[96,128]{1,0:T(8,128)(2,1)S(1)} %shard_map.91.refs_0_), channel_id=1, source_target_pairs={{20,0},{24,4},{28,8},{0,12},{4,16},{8,20},{12,24},{16,28},{21,1},{... | collective-permute-start | bytes 73736 | tf_op jit(solution)/shard_map/ppermute | solution.py:211
  205.9 12.3 %all_to_all.5.sums_ref = f32[32,8,128]{2,1,0:T(8,128)S(1)} all-to-all(f32[32,8,128]{2,1,0:T(8,128)S(1)} %get-tuple-element.70), channel_id=1, replica_groups=mesh['sector'=8,'dof'=4] {'sector','dof'}, dimensions={0} | all-to-all | bytes 262144 | tf_op jit(solution)/shard_map/all_to_all | solution.py:206
  (148 shorter events, 60.4 us)
Async XLA Ops:
  1.7 24.6 %collective-permute-start.2 = (bf16[256,128]{1,0:T(8,128)(2,1)S(1)}, bf16[256,128]{1,0:T(8,128)(2,1)S(1)}, u32[]{:S(2)}, u32[]{:S(2)}) collective-permute-start(bf16[256,128]{1,0:T(8,128)(2,1)S(1)} %get-tuple-element.39.refs_0_), channel_id=1, source_target_pairs={{3,0},{0,1},{1,2},{2,3},{7,4},{4,5},{5,6},{6,7},{11,8},{8,9},{9,10... | collective-permute-start | bytes 196616 | tf_op jit(solution)/shard_map/ppermute | solution.py:211
  4.8 21.5 %collective-permute-start.1 = (bf16[256,128]{1,0:T(8,128)(2,1)S(1)}, bf16[256,128]{1,0:T(8,128)(2,1)S(1)}, u32[]{:S(2)}, u32[]{:S(2)}) collective-permute-start(bf16[256,128]{1,0:T(8,128)(2,1)S(1)} %get-tuple-element.39.refs_0_), channel_id=1, source_target_pairs={{2,0},{3,1},{0,2},{1,3},{6,4},{7,5},{4,6},{5,7},{10,8},{11,9},{8,1... | collective-permute-start | bytes 196616 | tf_op jit(solution)/shard_map/ppermute | solution.py:211
  7.4 18.9 %collective-permute-start = (bf16[256,128]{1,0:T(8,128)(2,1)S(1)}, bf16[256,128]{1,0:T(8,128)(2,1)S(1)}, u32[]{:S(2)}, u32[]{:S(2)}) collective-permute-start(bf16[256,128]{1,0:T(8,128)(2,1)S(1)} %get-tuple-element.39.refs_0_), channel_id=1, source_target_pairs={{1,0},{2,1},{3,2},{0,3},{5,4},{6,5},{7,6},{4,7},{9,8},{10,9},{11,1... | collective-permute-start | bytes 196616 | tf_op jit(solution)/shard_map/ppermute | solution.py:211
  32.9 7.3 %collective-permute-start.10 = (f32[112,128]{1,0:T(8,128)S(1)}, f32[112,128]{1,0:T(8,128)S(1)}, u32[]{:S(2)}, u32[]{:S(2)}) collective-permute-start(f32[112,128]{1,0:T(8,128)S(1)} %get-tuple-element.75), channel_id=1, source_target_pairs={{24,0},{28,4},{0,8},{4,12},{8,16},{12,20},{16,24},{20,28},{25,1},{... | collective-permute-start | bytes 172040 | tf_op jit(solution)/shard_map/ppermute | solution.py:211
  37.5 7.5 %collective-permute-start.3 = (bf16[256,128]{1,0:T(8,128)(2,1)S(1)}, bf16[256,128]{1,0:T(8,128)(2,1)S(1)}, u32[]{:S(2)}, u32[]{:S(2)}) collective-permute-start(bf16[256,128]{1,0:T(8,128)(2,1)S(1)} %get-tuple-element.40), channel_id=1, source_target_pairs={{0,4},{4,8},{8,12},{12,16},{16,20},{20,24},{24,28},{28,0},{1,5},{5... | collective-permute-start | bytes 196616 | tf_op jit(solution)/shard_map/ppermute | solution.py:263
  37.5 7.5 %collective-permute-start.4 = (bf16[256,128]{1,0:T(8,128)(2,1)S(1)}, bf16[256,128]{1,0:T(8,128)(2,1)S(1)}, u32[]{:S(2)}, u32[]{:S(2)}) collective-permute-start(bf16[256,128]{1,0:T(8,128)(2,1)S(1)} %get-tuple-element.41), channel_id=1, source_target_pairs={{4,0},{8,4},{12,8},{16,12},{20,16},{24,20},{28,24},{0,28},{5,1},{9... | collective-permute-start | bytes 196616 | tf_op jit(solution)/shard_map/ppermute | solution.py:264
  68.0 9.7 %collective-permute-start.16 = (f32[96,128]{1,0:T(8,128)S(1)}, f32[96,128]{1,0:T(8,128)S(1)}, u32[]{:S(2)}, u32[]{:S(2)}) collective-permute-start(f32[96,128]{1,0:T(8,128)S(1)} %shard_map.81.refs_0_), channel_id=1, source_target_pairs={{20,0},{24,4},{28,8},{0,12},{4,16},{8,20},{12,24},{16,28},{21,1},{... | collective-permute-start | bytes 147464 | tf_op jit(solution)/shard_map/ppermute | solution.py:211
  69.3 8.5 %collective-permute-start.15 = (f32[96,128]{1,0:T(8,128)S(1)}, f32[96,128]{1,0:T(8,128)S(1)}, u32[]{:S(2)}, u32[]{:S(2)}) collective-permute-start(f32[96,128]{1,0:T(8,128)S(1)} %shard_map.81.refs_0_), channel_id=1, source_target_pairs={{16,0},{20,4},{24,8},{28,12},{0,16},{4,20},{8,24},{12,28},{17,1},{... | collective-permute-start | bytes 147464 | tf_op jit(solution)/shard_map/ppermute | solution.py:211
  70.9 9.1 %collective-permute-start.14 = (f32[96,128]{1,0:T(8,128)S(1)}, f32[96,128]{1,0:T(8,128)S(1)}, u32[]{:S(2)}, u32[]{:S(2)}) collective-permute-start(f32[96,128]{1,0:T(8,128)S(1)} %shard_map.81.refs_0_), channel_id=1, source_target_pairs={{12,0},{16,4},{20,8},{24,12},{28,16},{0,20},{4,24},{8,28},{13,1},{... | collective-permute-start | bytes 147464 | tf_op jit(solution)/shard_map/ppermute | solution.py:211
  70.9 10.8 %collective-permute-start.13 = (f32[96,128]{1,0:T(8,128)S(1)}, f32[96,128]{1,0:T(8,128)S(1)}, u32[]{:S(2)}, u32[]{:S(2)}) collective-permute-start(f32[96,128]{1,0:T(8,128)S(1)} %shard_map.81.refs_0_), channel_id=1, source_target_pairs={{8,0},{12,4},{16,8},{20,12},{24,16},{28,20},{0,24},{4,28},{9,1},{1... | collective-permute-start | bytes 147464 | tf_op jit(solution)/shard_map/ppermute | solution.py:211
  72.1 9.5 %collective-permute-start.12 = (f32[96,128]{1,0:T(8,128)S(1)}, f32[96,128]{1,0:T(8,128)S(1)}, u32[]{:S(2)}, u32[]{:S(2)}) collective-permute-start(f32[96,128]{1,0:T(8,128)S(1)} %shard_map.81.refs_0_), channel_id=1, source_target_pairs={{4,0},{8,4},{12,8},{16,12},{20,16},{24,20},{28,24},{0,28},{5,1},{9... | collective-permute-start | bytes 147464 | tf_op jit(solution)/shard_map/ppermute | solution.py:211
  77.7 21.8 %collective-permute-start.21 = (bf16[256,128]{1,0:T(8,128)(2,1)S(1)}, bf16[256,128]{1,0:T(8,128)(2,1)S(1)}, u32[]{:S(2)}, u32[]{:S(2)}) collective-permute-start(bf16[256,128]{1,0:T(8,128)(2,1)S(1)} %get-tuple-element.47.refs_0_), channel_id=1, source_target_pairs={{3,0},{0,1},{1,2},{2,3},{7,4},{4,5},{5,6},{6,7},{11,8},{8,9},{9,10... | collective-permute-start | bytes 196616 | tf_op jit(solution)/shard_map/ppermute | solution.py:211
  77.8 21.7 %collective-permute-start.20 = (bf16[256,128]{1,0:T(8,128)(2,1)S(1)}, bf16[256,128]{1,0:T(8,128)(2,1)S(1)}, u32[]{:S(2)}, u32[]{:S(2)}) collective-permute-start(bf16[256,128]{1,0:T(8,128)(2,1)S(1)} %get-tuple-element.47.refs_0_), channel_id=1, source_target_pairs={{2,0},{3,1},{0,2},{1,3},{6,4},{7,5},{4,6},{5,7},{10,8},{11,9},{8,1... | collective-permute-start | bytes 196616 | tf_op jit(solution)/shard_map/ppermute | solution.py:211
  80.0 19.5 %collective-permute-start.19 = (bf16[256,128]{1,0:T(8,128)(2,1)S(1)}, bf16[256,128]{1,0:T(8,128)(2,1)S(1)}, u32[]{:S(2)}, u32[]{:S(2)}) collective-permute-start(bf16[256,128]{1,0:T(8,128)(2,1)S(1)} %get-tuple-element.47.refs_0_), channel_id=1, source_target_pairs={{1,0},{2,1},{3,2},{0,3},{5,4},{6,5},{7,6},{4,7},{9,8},{10,9},{11,1... | collective-permute-start | bytes 196616 | tf_op jit(solution)/shard_map/ppermute | solution.py:211
  102.0 11.4 %collective-permute-start.22 = (bf16[256,128]{1,0:T(8,128)(2,1)S(1)}, bf16[256,128]{1,0:T(8,128)(2,1)S(1)}, u32[]{:S(2)}, u32[]{:S(2)}) collective-permute-start(bf16[256,128]{1,0:T(8,128)(2,1)S(1)} %get-tuple-element.49), channel_id=1, source_target_pairs={{0,4},{4,8},{8,12},{12,16},{16,20},{20,24},{24,28},{28,0},{1,5},{5... | collective-permute-start | bytes 196616 | tf_op jit(solution)/shard_map/ppermute | solution.py:263
  102.9 10.5 %collective-permute-start.23 = (bf16[256,128]{1,0:T(8,128)(2,1)S(1)}, bf16[256,128]{1,0:T(8,128)(2,1)S(1)}, u32[]{:S(2)}, u32[]{:S(2)}) collective-permute-start(bf16[256,128]{1,0:T(8,128)(2,1)S(1)} %get-tuple-element.50), channel_id=1, source_target_pairs={{4,0},{8,4},{12,8},{16,12},{20,16},{24,20},{28,24},{0,28},{5,1},{9... | collective-permute-start | bytes 196616 | tf_op jit(solution)/shard_map/ppermute | solution.py:264
  133.4 7.2 %collective-permute-start.35 = (bf16[96,128]{1,0:T(8,128)(2,1)S(1)}, bf16[96,128]{1,0:T(8,128)(2,1)S(1)}, u32[]{:S(2)}, u32[]{:S(2)}) collective-permute-start(bf16[96,128]{1,0:T(8,128)(2,1)S(1)} %shard_map.86.refs_0_), channel_id=1, source_target_pairs={{20,0},{24,4},{28,8},{0,12},{4,16},{8,20},{12,24},{16,28},{21,1},{... | collective-permute-start | bytes 73736 | tf_op jit(solution)/shard_map/ppermute | solution.py:211
  136.4 8.3 %collective-permute-start.32 = (bf16[96,128]{1,0:T(8,128)(2,1)S(1)}, bf16[96,128]{1,0:T(8,128)(2,1)S(1)}, u32[]{:S(2)}, u32[]{:S(2)}) collective-permute-start(bf16[96,128]{1,0:T(8,128)(2,1)S(1)} %shard_map.86.refs_0_), channel_id=1, source_target_pairs={{8,0},{12,4},{16,8},{20,12},{24,16},{28,20},{0,24},{4,28},{9,1},{1... | collective-permute-start | bytes 73736 | tf_op jit(solution)/shard_map/ppermute | solution.py:211
  140.6 22.7 %collective-permute-start.40 = (bf16[256,128]{1,0:T(8,128)(2,1)S(1)}, bf16[256,128]{1,0:T(8,128)(2,1)S(1)}, u32[]{:S(2)}, u32[]{:S(2)}) collective-permute-start(bf16[256,128]{1,0:T(8,128)(2,1)S(1)} %get-tuple-element.58.refs_0_), channel_id=1, source_target_pairs={{3,0},{0,1},{1,2},{2,3},{7,4},{4,5},{5,6},{6,7},{11,8},{8,9},{9,10... | collective-permute-start | bytes 196616 | tf_op jit(solution)/shard_map/ppermute | solution.py:211
  140.7 22.6 %collective-permute-start.39 = (bf16[256,128]{1,0:T(8,128)(2,1)S(1)}, bf16[256,128]{1,0:T(8,128)(2,1)S(1)}, u32[]{:S(2)}, u32[]{:S(2)}) collective-permute-start(bf16[256,128]{1,0:T(8,128)(2,1)S(1)} %get-tuple-element.58.refs_0_), channel_id=1, source_target_pairs={{2,0},{3,1},{0,2},{1,3},{6,4},{7,5},{4,6},{5,7},{10,8},{11,9},{8,1... | collective-permute-start | bytes 196616 | tf_op jit(solution)/shard_map/ppermute | solution.py:211
  143.3 20.0 %collective-permute-start.38 = (bf16[256,128]{1,0:T(8,128)(2,1)S(1)}, bf16[256,128]{1,0:T(8,128)(2,1)S(1)}, u32[]{:S(2)}, u32[]{:S(2)}) collective-permute-start(bf16[256,128]{1,0:T(8,128)(2,1)S(1)} %get-tuple-element.58.refs_0_), channel_id=1, source_target_pairs={{1,0},{2,1},{3,2},{0,3},{5,4},{6,5},{7,6},{4,7},{9,8},{10,9},{11,1... | collective-permute-start | bytes 196616 | tf_op jit(solution)/shard_map/ppermute | solution.py:211
  165.8 11.4 %collective-permute-start.41 = (bf16[256,128]{1,0:T(8,128)(2,1)S(1)}, bf16[256,128]{1,0:T(8,128)(2,1)S(1)}, u32[]{:S(2)}, u32[]{:S(2)}) collective-permute-start(bf16[256,128]{1,0:T(8,128)(2,1)S(1)} %get-tuple-element.60), channel_id=1, source_target_pairs={{0,4},{4,8},{8,12},{12,16},{16,20},{20,24},{24,28},{28,0},{1,5},{5... | collective-permute-start | bytes 196616 | tf_op jit(solution)/shard_map/ppermute | solution.py:263
  167.0 10.2 %collective-permute-start.42 = (bf16[256,128]{1,0:T(8,128)(2,1)S(1)}, bf16[256,128]{1,0:T(8,128)(2,1)S(1)}, u32[]{:S(2)}, u32[]{:S(2)}) collective-permute-start(bf16[256,128]{1,0:T(8,128)(2,1)S(1)} %get-tuple-element.61), channel_id=1, source_target_pairs={{4,0},{8,4},{12,8},{16,12},{20,16},{24,20},{28,24},{0,28},{5,1},{9... | collective-permute-start | bytes 196616 | tf_op jit(solution)/shard_map/ppermute | solution.py:264
  197.2 7.8 %collective-permute-start.54 = (bf16[96,128]{1,0:T(8,128)(2,1)S(1)}, bf16[96,128]{1,0:T(8,128)(2,1)S(1)}, u32[]{:S(2)}, u32[]{:S(2)}) collective-permute-start(bf16[96,128]{1,0:T(8,128)(2,1)S(1)} %shard_map.91.refs_0_), channel_id=1, source_target_pairs={{20,0},{24,4},{28,8},{0,12},{4,16},{8,20},{12,24},{16,28},{21,1},{... | collective-permute-start | bytes 73736 | tf_op jit(solution)/shard_map/ppermute | solution.py:211
  (46 other events, 405.1 us)

commit v13 on v12

--- a/solution.py
+++ b/solution.py
@@ -85,35 +85,40 @@
         load_ref[s, height - TERM_ROWS :] = terms.astype(load_ref.dtype)
 
 
-def pack_kernel(before_ref, after_ref, *refs):
+def join_kernel(before_ref, after_ref, out_ref):
+    quarter = before_ref.shape[0]
+    out_ref[:quarter] = before_ref[...]
+    out_ref[quarter:] = after_ref[...]
+
+
+def slice_kernel(*refs):
     *part_refs, out_ref = refs
-    quarter = before_ref.shape[0]
-    height = part_refs[0].shape[0] - TERM_ROWS
-    out_ref[:quarter] = before_ref[...]
-    out_ref[quarter : 2 * quarter] = after_ref[...]
+    height = out_ref.shape[0] - TERM_ROWS
     total = sum(ref[...].astype(f32) for ref in part_refs)
-    out_ref[2 * quarter : 2 * quarter + height] = total[:height].astype(bf16)
-    out_ref[2 * quarter + height :] = in_terms(from_terms(total[height:])).astype(bf16)
+    out_ref[:height] = total[:height].astype(bf16)
+    out_ref[height:] = in_terms(from_terms(total[height:])).astype(bf16)
 
 
 def alpha_from(sums):
     return sums[0:1] / (sums[1:2] + 1e-06)
 
 
-def hub_kernel(cases, matrix_ref, pieces_ref, out_ref):
-    parts = pieces_ref.shape[0]
-    height = out_ref.shape[0]
-    chunks = height // cases
-    depth = chunks * LANES
-    first = pieces_ref.shape[1] - TERM_ROWS - height
+def block_columns(matrix_ref, parts, ahead):
+    width = matrix_ref.shape[1] // parts
+    owner = lax.rem(lax.axis_index("dof") + ahead, parts)
+    return matrix_ref[:, pl.ds(pl.multiple_of(owner * width, LANES), width)]
+
+
+def hub_kernel(cases, matrix_ref, *refs):
+    *load_refs, out_ref = refs
+    parts = len(load_refs)
+    chunks = out_ref.shape[0] // cases
     total = None
-    for part in range(parts):
-        load = jnp.concatenate(
-            [pieces_ref[part, first + c * cases : first + (c + 1) * cases] for c in range(chunks)], axis=1
-        )
+    for part, ref in enumerate(load_refs):
+        load = jnp.concatenate([ref[c * cases : (c + 1) * cases] for c in range(chunks)], axis=1)
         product = lax.dot_general(
             load,
-            matrix_ref[:, part * depth : (part + 1) * depth],
+            block_columns(matrix_ref, parts, part),
             (((1,), (1,)), ((), ())),
             preferred_element_type=f32,
         )
@@ -122,25 +127,22 @@
         out_ref[c * cases : (c + 1) * cases] = total[:, c * LANES : (c + 1) * LANES].astype(out_ref.dtype)
 
 
-def base_kernel(first, matrix_ref, pieces_ref, product_ref, stiffness_ref, *refs):
+def base_kernel(first, parts, matrix_ref, product_ref, stiffness_ref, *refs):
+    face_refs, load_refs, refs = refs[:parts], refs[parts : 2 * parts], refs[2 * parts :]
     if first:
         base_ref, end_ref, factor_ref = refs
     else:
         *refs, base_ref, end_ref, factor_ref, left_ref, newer_ref, better_ref = refs
         image_ref, residual_ref, precon_ref = refs[:3]
-    parts, height, _ = pieces_ref.shape
-    depth = matrix_ref.shape[1] // parts
     base_ref[...] = stiffness_ref[...] * product_ref[...]
-    for part in range(parts):
+    for part, ref in enumerate(face_refs):
         base_ref[...] += jnp.dot(
-            matrix_ref[:, part * depth : (part + 1) * depth],
-            pieces_ref[part, :depth],
-            preferred_element_type=f32,
+            block_columns(matrix_ref, parts, part), ref[...], preferred_element_type=f32
         )
     if first:
         factor_ref[...] = jnp.ones_like(factor_ref)
     else:
-        alpha = alpha_from(sum(from_terms(pieces_ref[part, height - TERM_ROWS :]) for part in range(parts)))
+        alpha = alpha_from(sum(from_terms(ref[ref.shape[0] - TERM_ROWS :]) for ref in load_refs))
         factor_ref[...] = jnp.broadcast_to(-alpha, factor_ref.shape)
         base_ref[...] = image_ref[...] - alpha * base_ref[...]
         left_ref[...] = residual_ref[...] - alpha * image_ref[...]
@@ -262,23 +264,25 @@
         )
         before = lax.ppermute(right, "sector", onward)
         after = lax.ppermute(left, "sector", backward)
-        packed = call(
-            pack_kernel,
-            shape(2 * quarter + height + TERM_ROWS, loads, dtype=bf16),
-            (before, after, *mine_from_each(load, "sector")),
-        )
-        pieces = gathered(packed)
+        faces = call(join_kernel, shape(2 * quarter, loads, dtype=bf16), (before, after))
+        faces = one_from_each(faces, "dof")
+        load = call(
+            slice_kernel,
+            shape(height + TERM_ROWS, loads, dtype=bf16),
+            mine_from_each(load, "sector"),
+        )
+        slices = one_from_each(load, "dof")
         hub = call(
             functools.partial(hub_kernel, cases),
             shape(height, LANES, dtype=sent),
-            (hub_inverse, pieces),
+            (hub_inverse, *slices),
             flops=2 * hub_inverse.size * cases,
         )
         hubs = one_from_each(hub, "sector")
         base, end, factor, *state = call(
-            functools.partial(base_kernel, first),
+            functools.partial(base_kernel, first, parts),
             (full, face, shape(SUM_ROWS, loads)) + (() if first else (full, full, full)),
-            (coupling[0], pieces, product, stiffness, *state),
+            (coupling[0], product, stiffness, *faces, *slices, *state),
             flops=2 * coupling.size * loads,
         )
         residual, precon, *solution = (residual, product) if first else state

time: 220 us -> 214 us (0.973)
  blocking collectives: 116 us -> 66.7 us
  starting transfers between devices: 61.3 us -> 83.4 us
  waiting for transfers between devices: 12 us -> 31.7 us
    all_gather x6 -> x3, blocking collectives: 103 us -> 53.6 us  [gathered(): return lax.all_gather(field, 'dof', axis=0)]
    ppermute x51 -> x69, starting transfers between devices: 53.3 us -> 75.4 us  [from_ahead(): lax.ppermute(cells, axis, [((i + distance) % count, i) for i in range(cou...]
    ppermute x51 -> x69, waiting for transfers between devices: 12 us -> 31.7 us  [from_ahead(): lax.ppermute(cells, axis, [((i + distance) % count, i) for i in range(cou...]
    pallas_call x17 -> x20, Pallas kernels: 19.4 us -> 19.5 us  [call(): pl.pallas_call(kernel, in_specs=[whole] * len(operands), out_specs=jax.tr...]
  transfers between devices with their start and end apart: 57 -> 75, of which waited for: 10 -> 20; matrix products, arithmetic and copies ran while one was open for 0% -> 0% of each run, Pallas kernels for 3% -> 5%
where the time goes in v13:
time: 214 us; the launch traced here: 213 us
  starting transfers between devices  83.4 us (39%)
  blocking collectives  66.7 us (31%)
  waiting for transfers between devices  31.7 us (15%)
  Pallas kernels  19.5 us (9%)
  local copies, waits for them, and re-layouts  11.1 us (5%)
    ppermute x69, starting transfers between devices, from_ahead(): lax.ppermute(cells, axis, [((i + distance) % count, i) for i in range(cou...  75.4 us
    all_gather x3, blocking collectives, gathered(): return lax.all_gather(field, 'dof', axis=0)  53.6 us
    ppermute x69, waiting for transfers between devices, from_ahead(): lax.ppermute(cells, axis, [((i + distance) % count, i) for i in range(cou...  31.7 us
    pallas_call x20, Pallas kernels, call(): pl.pallas_call(kernel, in_specs=[whole] * len(operands), out_specs=jax.tr...  19.5 us
    all_to_all x1, blocking collectives, exchange(): return lax.all_to_all(blocks, axes, split_axis=0, concat_axis=0)  13.1 us
    unnamed x26, local copies, waits for them, and re-layouts  10.9 us
    ppermute x3, starting transfers between devices, tiled_body(): after = lax.ppermute(left, 'sector', backward)  7.9 us
  transfers between devices with their start and end apart: 75, of which 20 were waited for; matrix products, arithmetic and copies ran while one was open for 0% of the time, Pallas kernels for 5%

profile of v13, /device:TPU:0, one launch (start us, length us, event | category | flops | bytes accessed | tf_op | source)
XLA Modules:
  0.0 213.4 jit_solution(5465940699102670257)
XLA Ops:
  1.7 3.1 %collective-permute-start.2 = (bf16[256,128]{1,0:T(8,128)(2,1)S(1)}, bf16[256,128]{1,0:T(8,128)(2,1)S(1)}, u32[]{:S(2)}, u32[]{:S(2)}) collective-permute-start(bf16[256,128]{1,0:T(8,128)(2,1)S(1)} %get-tuple-element.39.refs_0_), channel_id=1, source_target_pairs={{3,0},{0,1},{1,2},{2,3},{7,4},{4,5},{5,6},{6,7},{11,8},{8,9},{9,10... | collective-permute-start | bytes 196616 | tf_op jit(solution)/shard_map/ppermute | solution.py:213
  4.8 2.6 %collective-permute-start.1 = (bf16[256,128]{1,0:T(8,128)(2,1)S(1)}, bf16[256,128]{1,0:T(8,128)(2,1)S(1)}, u32[]{:S(2)}, u32[]{:S(2)}) collective-permute-start(bf16[256,128]{1,0:T(8,128)(2,1)S(1)} %get-tuple-element.39.refs_0_), channel_id=1, source_target_pairs={{2,0},{3,1},{0,2},{1,3},{6,4},{7,5},{4,6},{5,7},{10,8},{11,9},{8,1... | collective-permute-start | bytes 196616 | tf_op jit(solution)/shard_map/ppermute | solution.py:213
  8.7 17.6 %all-gather = bf16[3072,128]{1,0:T(8,128)(2,1)S(1)} all-gather(bf16[768,128]{1,0:T(8,128)(2,1)S(1)} %get-tuple-element.38), channel_id=2, replica_groups=mesh['sector'=8,'dof'=4] {'dof'}, dimensions={0}, use_global_device_ids=true | all-gather | bytes 983040 | tf_op jit(solution)/shard_map/all_gather | solution.py:227
  26.3 3.4 %copy-done = bf16[1024,4096]{1,0:T(8,128)(2,1)S(1)} copy-done((bf16[1024,4096]{1,0:T(8,128)(2,1)S(1)}, bf16[1024,4096]{1,0:T(8,128)(2,1)}, u32[]{:S(2)}) %copy-start) | copy-done | bytes 8388632
  30.4 2.3 %shard_map.78 = (f32[1024,128]{1,0:T(8,128)S(1)}, f32[8,112,128]{2,1,0:T(8,128)S(1)}, bf16[256,128]{1,0:T(8,128)(2,1)S(1)}, bf16[256,128]{1,0:T(8,128)(2,1)S(1)}) custom-call(bf16[1024,4096]{1,0:T(8,128)(2,1)S(1)} %copy-done, f32[1,768]{1,0:T(1,128)S(1)} %copy-done.6, bf16[4,768,128]{2,1,0:T(8,128)(2,1)S(1)} %bitcast.65, ...), custom_call_target="tpu_custom_call" | custom-call | flops 1073741824 | bytes 9440256 | tf_op jit(solution)/shard_map/pallas_call | solution.py:25
  34.6 2.4 %collective-permute-start.12 = (f32[112,128]{1,0:T(8,128)S(1)}, f32[112,128]{1,0:T(8,128)S(1)}, u32[]{:S(2)}, u32[]{:S(2)}) collective-permute-start(f32[112,128]{1,0:T(8,128)S(1)} %get-tuple-element.76), channel_id=1, source_target_pairs={{20,0},{24,4},{28,8},{0,12},{4,16},{8,20},{12,24},{16,28},{21,1},{... | collective-permute-start | bytes 172040 | tf_op jit(solution)/shard_map/ppermute | solution.py:213
  41.4 2.6 %collective-permute-start.4 = (bf16[256,128]{1,0:T(8,128)(2,1)S(1)}, bf16[256,128]{1,0:T(8,128)(2,1)S(1)}, u32[]{:S(2)}, u32[]{:S(2)}) collective-permute-start(bf16[256,128]{1,0:T(8,128)(2,1)S(1)} %get-tuple-element.42), channel_id=1, source_target_pairs={{4,0},{8,4},{12,8},{16,12},{20,16},{24,20},{28,24},{0,28},{5,1},{9... | collective-permute-start | bytes 196616 | tf_op jit(solution)/shard_map/ppermute | solution.py:266
  50.2 2.8 %collective-permute-start.5 = (bf16[512,128]{1,0:T(8,128)(2,1)S(1)}, bf16[512,128]{1,0:T(8,128)(2,1)S(1)}, u32[]{:S(2)}, u32[]{:S(2)}) collective-permute-start(bf16[512,128]{1,0:T(8,128)(2,1)S(1)} %shard_map.79.refs_0_), channel_id=1, source_target_pairs={{1,0},{2,1},{3,2},{0,3},{5,4},{6,5},{7,6},{4,7},{9,8},{10,9},{11,1... | collective-permute-start | bytes 393224 | tf_op jit(solution)/shard_map/ppermute | solution.py:213
  53.0 2.3 %copy-done.2 = bf16[768,3072]{1,0:T(8,128)(2,1)S(1)} copy-done((bf16[768,3072]{1,0:T(8,128)(2,1)S(1)}, bf16[768,3072]{1,0:T(8,128)(2,1)}, u32[]{:S(2)}) %copy-start.2) | copy-done | bytes 4718616
  57.4 3.7 %collective-permute-done.24.refs_7_ = f32[96,128]{1,0:T(8,128)S(1)} collective-permute-done((f32[96,128]{1,0:T(8,128)S(1)}, f32[96,128]{1,0:T(8,128)S(1)}, u32[]{:S(2)}, u32[]{:S(2)}) %collective-permute-start.24) | collective-permute-done | bytes 49184 | tf_op jit(solution)/shard_map/ppermute | solution.py:213
  66.9 4.0 %collective-permute-start.27 = (bf16[256,128]{1,0:T(8,128)(2,1)S(1)}, bf16[256,128]{1,0:T(8,128)(2,1)S(1)}, u32[]{:S(2)}, u32[]{:S(2)}) collective-permute-start(bf16[256,128]{1,0:T(8,128)(2,1)S(1)} %get-tuple-element.47.refs_0_), channel_id=1, source_target_pairs={{3,0},{0,1},{1,2},{2,3},{7,4},{4,5},{5,6},{6,7},{11,8},{8,9},{9,10... | collective-permute-start | bytes 196616 | tf_op jit(solution)/shard_map/ppermute | solution.py:213
  70.9 2.4 %collective-permute-start.25 = (bf16[256,128]{1,0:T(8,128)(2,1)S(1)}, bf16[256,128]{1,0:T(8,128)(2,1)S(1)}, u32[]{:S(2)}, u32[]{:S(2)}) collective-permute-start(bf16[256,128]{1,0:T(8,128)(2,1)S(1)} %get-tuple-element.47.refs_0_), channel_id=1, source_target_pairs={{1,0},{2,1},{3,2},{0,3},{5,4},{6,5},{7,6},{4,7},{9,8},{10,9},{11,1... | collective-permute-start | bytes 196616 | tf_op jit(solution)/shard_map/ppermute | solution.py:213
  74.2 18.1 %all-gather.1 = bf16[3072,128]{1,0:T(8,128)(2,1)S(1)} all-gather(bf16[768,128]{1,0:T(8,128)(2,1)S(1)} %get-tuple-element.46), channel_id=3, replica_groups=mesh['sector'=8,'dof'=4] {'dof'}, dimensions={0}, use_global_device_ids=true | all-gather | bytes 983040 | tf_op jit(solution)/shard_map/all_gather | solution.py:227
  92.3 3.4 %copy-done.1 = bf16[1024,4096]{1,0:T(8,128)(2,1)S(1)} copy-done((bf16[1024,4096]{1,0:T(8,128)(2,1)S(1)}, bf16[1024,4096]{1,0:T(8,128)(2,1)}, u32[]{:S(2)}) %copy-start.1) | copy-done | bytes 8388632
  98.0 2.6 %collective-permute-start.29 = (bf16[256,128]{1,0:T(8,128)(2,1)S(1)}, bf16[256,128]{1,0:T(8,128)(2,1)S(1)}, u32[]{:S(2)}, u32[]{:S(2)}) collective-permute-start(bf16[256,128]{1,0:T(8,128)(2,1)S(1)} %get-tuple-element.51), channel_id=1, source_target_pairs={{4,0},{8,4},{12,8},{16,12},{20,16},{24,20},{28,24},{0,28},{5,1},{9... | collective-permute-start | bytes 196616 | tf_op jit(solution)/shard_map/ppermute | solution.py:266
  115.1 4.2 %collective-permute-done.42.refs_7_.refs_3_ = bf16[112,128]{1,0:T(8,128)(2,1)S(1)} collective-permute-done((bf16[112,128]{1,0:T(8,128)(2,1)S(1)}, bf16[112,128]{1,0:T(8,128)(2,1)S(1)}, u32[]{:S(2)}, u32[]{:S(2)}) %collective-permute-start.42) | collective-permute-done | bytes 28704 | tf_op jit(solution)/shard_map/ppermute | solution.py:213
  126.1 2.9 %collective-permute-done.49.refs_7_ = bf16[96,128]{1,0:T(8,128)(2,1)S(1)} collective-permute-done((bf16[96,128]{1,0:T(8,128)(2,1)S(1)}, bf16[96,128]{1,0:T(8,128)(2,1)S(1)}, u32[]{:S(2)}, u32[]{:S(2)}) %collective-permute-start.49) | collective-permute-done | bytes 24608 | tf_op jit(solution)/shard_map/ppermute | solution.py:213
  135.2 3.3 %collective-permute-start.51 = (bf16[256,128]{1,0:T(8,128)(2,1)S(1)}, bf16[256,128]{1,0:T(8,128)(2,1)S(1)}, u32[]{:S(2)}, u32[]{:S(2)}) collective-permute-start(bf16[256,128]{1,0:T(8,128)(2,1)S(1)} %get-tuple-element.58.refs_0_), channel_id=1, source_target_pairs={{2,0},{3,1},{0,2},{1,3},{6,4},{7,5},{4,6},{5,7},{10,8},{11,9},{8,1... | collective-permute-start | bytes 196616 | tf_op jit(solution)/shard_map/ppermute | solution.py:213
  140.2 17.9 %all-gather.2 = bf16[3072,128]{1,0:T(8,128)(2,1)S(1)} all-gather(bf16[768,128]{1,0:T(8,128)(2,1)S(1)} %get-tuple-element.57), channel_id=4, replica_groups=mesh['sector'=8,'dof'=4] {'dof'}, dimensions={0}, use_global_device_ids=true | all-gather | bytes 983040 | tf_op jit(solution)/shard_map/all_gather | solution.py:227
  158.2 2.3 %shard_map.90 = (f32[1024,128]{1,0:T(8,128)S(1)}, bf16[8,112,128]{2,1,0:T(8,128)(2,1)S(1)}, bf16[256,128]{1,0:T(8,128)(2,1)S(1)}, bf16[256,128]{1,0:T(8,128)(2,1)S(1)}) custom-call(bf16[1024,4096]{1,0:T(8,128)(2,1)S(1)} %bitcast.55, f32[1,768]{1,0:T(1,128)S(1)} %copy-done.7, bf16[4,768,128]{2,1,0:T(8,128)(2,1)S(1)} %bitcast.64, ...), custom_call_target="tpu_custom_call" | custom-call | flops 1073741824 | bytes 9444352 | tf_op jit(solution)/shard_map/pallas_call | solution.py:25
  160.6 2.6 %collective-permute-start.54 = (bf16[256,128]{1,0:T(8,128)(2,1)S(1)}, bf16[256,128]{1,0:T(8,128)(2,1)S(1)}, u32[]{:S(2)}, u32[]{:S(2)}) collective-permute-start(bf16[256,128]{1,0:T(8,128)(2,1)S(1)} %get-tuple-element.62), channel_id=1, source_target_pairs={{4,0},{8,4},{12,8},{16,12},{20,16},{24,20},{28,24},{0,28},{5,1},{9... | collective-permute-start | bytes 196616 | tf_op jit(solution)/shard_map/ppermute | solution.py:266
  177.7 4.1 %collective-permute-done.67.refs_7_.refs_3_ = bf16[112,128]{1,0:T(8,128)(2,1)S(1)} collective-permute-done((bf16[112,128]{1,0:T(8,128)(2,1)S(1)}, bf16[112,128]{1,0:T(8,128)(2,1)S(1)}, u32[]{:S(2)}, u32[]{:S(2)}) %collective-permute-start.67) | collective-permute-done | bytes 28704 | tf_op jit(solution)/shard_map/ppermute | solution.py:213
  188.6 3.0 %collective-permute-done.74.refs_7_ = bf16[96,128]{1,0:T(8,128)(2,1)S(1)} collective-permute-done((bf16[96,128]{1,0:T(8,128)(2,1)S(1)}, bf16[96,128]{1,0:T(8,128)(2,1)S(1)}, u32[]{:S(2)}, u32[]{:S(2)}) %collective-permute-start.74) | collective-permute-done | bytes 24608 | tf_op jit(solution)/shard_map/ppermute | solution.py:213
  199.3 13.1 %all_to_all.5.sums_ref = f32[32,8,128]{2,1,0:T(8,128)S(1)} all-to-all(f32[32,8,128]{2,1,0:T(8,128)S(1)} %get-tuple-element.70), channel_id=1, replica_groups=mesh['sector'=8,'dof'=4] {'sector','dof'}, dimensions={0} | all-to-all | bytes 262144 | tf_op jit(solution)/shard_map/all_to_all | solution.py:208
  (184 shorter events, 85.6 us)
Async XLA Ops:
  1.7 24.6 %collective-permute-start.2 = (bf16[256,128]{1,0:T(8,128)(2,1)S(1)}, bf16[256,128]{1,0:T(8,128)(2,1)S(1)}, u32[]{:S(2)}, u32[]{:S(2)}) collective-permute-start(bf16[256,128]{1,0:T(8,128)(2,1)S(1)} %get-tuple-element.39.refs_0_), channel_id=1, source_target_pairs={{3,0},{0,1},{1,2},{2,3},{7,4},{4,5},{5,6},{6,7},{11,8},{8,9},{9,10... | collective-permute-start | bytes 196616 | tf_op jit(solution)/shard_map/ppermute | solution.py:213
  4.8 21.5 %collective-permute-start.1 = (bf16[256,128]{1,0:T(8,128)(2,1)S(1)}, bf16[256,128]{1,0:T(8,128)(2,1)S(1)}, u32[]{:S(2)}, u32[]{:S(2)}) collective-permute-start(bf16[256,128]{1,0:T(8,128)(2,1)S(1)} %get-tuple-element.39.refs_0_), channel_id=1, source_target_pairs={{2,0},{3,1},{0,2},{1,3},{6,4},{7,5},{4,6},{5,7},{10,8},{11,9},{8,1... | collective-permute-start | bytes 196616 | tf_op jit(solution)/shard_map/ppermute | solution.py:213
  7.4 18.9 %collective-permute-start = (bf16[256,128]{1,0:T(8,128)(2,1)S(1)}, bf16[256,128]{1,0:T(8,128)(2,1)S(1)}, u32[]{:S(2)}, u32[]{:S(2)}) collective-permute-start(bf16[256,128]{1,0:T(8,128)(2,1)S(1)} %get-tuple-element.39.refs_0_), channel_id=1, source_target_pairs={{1,0},{2,1},{3,2},{0,3},{5,4},{6,5},{7,6},{4,7},{9,8},{10,9},{11,1... | collective-permute-start | bytes 196616 | tf_op jit(solution)/shard_map/ppermute | solution.py:213
  44.1 8.9 %collective-permute-start.16 = (bf16[112,128]{1,0:T(8,128)(2,1)S(1)}, bf16[112,128]{1,0:T(8,128)(2,1)S(1)}, u32[]{:S(2)}, u32[]{:S(2)}) collective-permute-start(bf16[112,128]{1,0:T(8,128)(2,1)S(1)} %shard_map.80.refs_4_.refs_0_), channel_id=1, source_target_pairs={{2,0},{3,1},{0,2},{1,3},{6,4},{7,5},{4,6},{5,7},{10,8},{11,9},{8,1... | collective-permute-start | bytes 86024 | tf_op jit(solution)/shard_map/ppermute | solution.py:213
  48.0 14.9 %collective-permute-start.7 = (bf16[512,128]{1,0:T(8,128)(2,1)S(1)}, bf16[512,128]{1,0:T(8,128)(2,1)S(1)}, u32[]{:S(2)}, u32[]{:S(2)}) collective-permute-start(bf16[512,128]{1,0:T(8,128)(2,1)S(1)} %shard_map.79.refs_0_), channel_id=1, source_target_pairs={{3,0},{0,1},{1,2},{2,3},{7,4},{4,5},{5,6},{6,7},{11,8},{8,9},{9,10... | collective-permute-start | bytes 393224 | tf_op jit(solution)/shard_map/ppermute | solution.py:213
  48.6 15.0 %collective-permute-start.6 = (bf16[512,128]{1,0:T(8,128)(2,1)S(1)}, bf16[512,128]{1,0:T(8,128)(2,1)S(1)}, u32[]{:S(2)}, u32[]{:S(2)}) collective-permute-start(bf16[512,128]{1,0:T(8,128)(2,1)S(1)} %shard_map.79.refs_0_), channel_id=1, source_target_pairs={{2,0},{3,1},{0,2},{1,3},{6,4},{7,5},{4,6},{5,7},{10,8},{11,9},{8,1... | collective-permute-start | bytes 393224 | tf_op jit(solution)/shard_map/ppermute | solution.py:213
  50.2 13.9 %collective-permute-start.5 = (bf16[512,128]{1,0:T(8,128)(2,1)S(1)}, bf16[512,128]{1,0:T(8,128)(2,1)S(1)}, u32[]{:S(2)}, u32[]{:S(2)}) collective-permute-start(bf16[512,128]{1,0:T(8,128)(2,1)S(1)} %shard_map.79.refs_0_), channel_id=1, source_target_pairs={{1,0},{2,1},{3,2},{0,3},{5,4},{6,5},{7,6},{4,7},{9,8},{10,9},{11,1... | collective-permute-start | bytes 393224 | tf_op jit(solution)/shard_map/ppermute | solution.py:213
  62.2 8.7 %collective-permute-start.21 = (f32[96,128]{1,0:T(8,128)S(1)}, f32[96,128]{1,0:T(8,128)S(1)}, u32[]{:S(2)}, u32[]{:S(2)}) collective-permute-start(f32[96,128]{1,0:T(8,128)S(1)} %shard_map.82.refs_0_), channel_id=1, source_target_pairs={{16,0},{20,4},{24,8},{28,12},{0,16},{4,20},{8,24},{12,28},{17,1},{... | collective-permute-start | bytes 147464 | tf_op jit(solution)/shard_map/ppermute | solution.py:213
  63.6 9.8 %collective-permute-start.19 = (f32[96,128]{1,0:T(8,128)S(1)}, f32[96,128]{1,0:T(8,128)S(1)}, u32[]{:S(2)}, u32[]{:S(2)}) collective-permute-start(f32[96,128]{1,0:T(8,128)S(1)} %shard_map.82.refs_0_), channel_id=1, source_target_pairs={{8,0},{12,4},{16,8},{20,12},{24,16},{28,20},{0,24},{4,28},{9,1},{1... | collective-permute-start | bytes 147464 | tf_op jit(solution)/shard_map/ppermute | solution.py:213
  64.0 9.3 %collective-permute-start.18 = (f32[96,128]{1,0:T(8,128)S(1)}, f32[96,128]{1,0:T(8,128)S(1)}, u32[]{:S(2)}, u32[]{:S(2)}) collective-permute-start(f32[96,128]{1,0:T(8,128)S(1)} %shard_map.82.refs_0_), channel_id=1, source_target_pairs={{4,0},{8,4},{12,8},{16,12},{20,16},{24,20},{28,24},{0,28},{5,1},{9... | collective-permute-start | bytes 147464 | tf_op jit(solution)/shard_map/ppermute | solution.py:213
  66.9 25.3 %collective-permute-start.27 = (bf16[256,128]{1,0:T(8,128)(2,1)S(1)}, bf16[256,128]{1,0:T(8,128)(2,1)S(1)}, u32[]{:S(2)}, u32[]{:S(2)}) collective-permute-start(bf16[256,128]{1,0:T(8,128)(2,1)S(1)} %get-tuple-element.47.refs_0_), channel_id=1, source_target_pairs={{3,0},{0,1},{1,2},{2,3},{7,4},{4,5},{5,6},{6,7},{11,8},{8,9},{9,10... | collective-permute-start | bytes 196616 | tf_op jit(solution)/shard_map/ppermute | solution.py:213
  70.9 21.4 %collective-permute-start.26 = (bf16[256,128]{1,0:T(8,128)(2,1)S(1)}, bf16[256,128]{1,0:T(8,128)(2,1)S(1)}, u32[]{:S(2)}, u32[]{:S(2)}) collective-permute-start(bf16[256,128]{1,0:T(8,128)(2,1)S(1)} %get-tuple-element.47.refs_0_), channel_id=1, source_target_pairs={{2,0},{3,1},{0,2},{1,3},{6,4},{7,5},{4,6},{5,7},{10,8},{11,9},{8,1... | collective-permute-start | bytes 196616 | tf_op jit(solution)/shard_map/ppermute | solution.py:213
  70.9 21.4 %collective-permute-start.25 = (bf16[256,128]{1,0:T(8,128)(2,1)S(1)}, bf16[256,128]{1,0:T(8,128)(2,1)S(1)}, u32[]{:S(2)}, u32[]{:S(2)}) collective-permute-start(bf16[256,128]{1,0:T(8,128)(2,1)S(1)} %get-tuple-element.47.refs_0_), channel_id=1, source_target_pairs={{1,0},{2,1},{3,2},{0,3},{5,4},{6,5},{7,6},{4,7},{9,8},{10,9},{11,1... | collective-permute-start | bytes 196616 | tf_op jit(solution)/shard_map/ppermute | solution.py:213
  104.9 25.5 %collective-permute-start.32 = (bf16[512,128]{1,0:T(8,128)(2,1)S(1)}, bf16[512,128]{1,0:T(8,128)(2,1)S(1)}, u32[]{:S(2)}, u32[]{:S(2)}) collective-permute-start(bf16[512,128]{1,0:T(8,128)(2,1)S(1)} %shard_map.85.refs_0_), channel_id=1, source_target_pairs={{3,0},{0,1},{1,2},{2,3},{7,4},{4,5},{5,6},{6,7},{11,8},{8,9},{9,10... | collective-permute-start | bytes 393224 | tf_op jit(solution)/shard_map/ppermute | solution.py:213
  105.6 25.6 %collective-permute-start.31 = (bf16[512,128]{1,0:T(8,128)(2,1)S(1)}, bf16[512,128]{1,0:T(8,128)(2,1)S(1)}, u32[]{:S(2)}, u32[]{:S(2)}) collective-permute-start(bf16[512,128]{1,0:T(8,128)(2,1)S(1)} %shard_map.85.refs_0_), channel_id=1, source_target_pairs={{2,0},{3,1},{0,2},{1,3},{6,4},{7,5},{4,6},{5,7},{10,8},{11,9},{8,1... | collective-permute-start | bytes 393224 | tf_op jit(solution)/shard_map/ppermute | solution.py:213
  107.5 24.7 %collective-permute-start.30 = (bf16[512,128]{1,0:T(8,128)(2,1)S(1)}, bf16[512,128]{1,0:T(8,128)(2,1)S(1)}, u32[]{:S(2)}, u32[]{:S(2)}) collective-permute-start(bf16[512,128]{1,0:T(8,128)(2,1)S(1)} %shard_map.85.refs_0_), channel_id=1, source_target_pairs={{1,0},{2,1},{3,2},{0,3},{5,4},{6,5},{7,6},{4,7},{9,8},{10,9},{11,1... | collective-permute-start | bytes 393224 | tf_op jit(solution)/shard_map/ppermute | solution.py:213
  113.8 9.1 %collective-permute-start.41 = (bf16[112,128]{1,0:T(8,128)(2,1)S(1)}, bf16[112,128]{1,0:T(8,128)(2,1)S(1)}, u32[]{:S(2)}, u32[]{:S(2)}) collective-permute-start(bf16[112,128]{1,0:T(8,128)(2,1)S(1)} %shard_map.86.refs_4_.refs_0_), channel_id=1, source_target_pairs={{2,0},{3,1},{0,2},{1,3},{6,4},{7,5},{4,6},{5,7},{10,8},{11,9},{8,1... | collective-permute-start | bytes 86024 | tf_op jit(solution)/shard_map/ppermute | solution.py:213
  135.0 23.2 %collective-permute-start.52 = (bf16[256,128]{1,0:T(8,128)(2,1)S(1)}, bf16[256,128]{1,0:T(8,128)(2,1)S(1)}, u32[]{:S(2)}, u32[]{:S(2)}) collective-permute-start(bf16[256,128]{1,0:T(8,128)(2,1)S(1)} %get-tuple-element.58.refs_0_), channel_id=1, source_target_pairs={{3,0},{0,1},{1,2},{2,3},{7,4},{4,5},{5,6},{6,7},{11,8},{8,9},{9,10... | collective-permute-start | bytes 196616 | tf_op jit(solution)/shard_map/ppermute | solution.py:213
  135.2 22.9 %collective-permute-start.51 = (bf16[256,128]{1,0:T(8,128)(2,1)S(1)}, bf16[256,128]{1,0:T(8,128)(2,1)S(1)}, u32[]{:S(2)}, u32[]{:S(2)}) collective-permute-start(bf16[256,128]{1,0:T(8,128)(2,1)S(1)} %get-tuple-element.58.refs_0_), channel_id=1, source_target_pairs={{2,0},{3,1},{0,2},{1,3},{6,4},{7,5},{4,6},{5,7},{10,8},{11,9},{8,1... | collective-permute-start | bytes 196616 | tf_op jit(solution)/shard_map/ppermute | solution.py:213
  138.5 19.6 %collective-permute-start.50 = (bf16[256,128]{1,0:T(8,128)(2,1)S(1)}, bf16[256,128]{1,0:T(8,128)(2,1)S(1)}, u32[]{:S(2)}, u32[]{:S(2)}) collective-permute-start(bf16[256,128]{1,0:T(8,128)(2,1)S(1)} %get-tuple-element.58.refs_0_), channel_id=1, source_target_pairs={{1,0},{2,1},{3,2},{0,3},{5,4},{6,5},{7,6},{4,7},{9,8},{10,9},{11,1... | collective-permute-start | bytes 196616 | tf_op jit(solution)/shard_map/ppermute | solution.py:213
  167.5 25.4 %collective-permute-start.57 = (bf16[512,128]{1,0:T(8,128)(2,1)S(1)}, bf16[512,128]{1,0:T(8,128)(2,1)S(1)}, u32[]{:S(2)}, u32[]{:S(2)}) collective-permute-start(bf16[512,128]{1,0:T(8,128)(2,1)S(1)} %shard_map.91.refs_0_), channel_id=1, source_target_pairs={{3,0},{0,1},{1,2},{2,3},{7,4},{4,5},{5,6},{6,7},{11,8},{8,9},{9,10... | collective-permute-start | bytes 393224 | tf_op jit(solution)/shard_map/ppermute | solution.py:213
  168.2 25.5 %collective-permute-start.56 = (bf16[512,128]{1,0:T(8,128)(2,1)S(1)}, bf16[512,128]{1,0:T(8,128)(2,1)S(1)}, u32[]{:S(2)}, u32[]{:S(2)}) collective-permute-start(bf16[512,128]{1,0:T(8,128)(2,1)S(1)} %shard_map.91.refs_0_), channel_id=1, source_target_pairs={{2,0},{3,1},{0,2},{1,3},{6,4},{7,5},{4,6},{5,7},{10,8},{11,9},{8,1... | collective-permute-start | bytes 393224 | tf_op jit(solution)/shard_map/ppermute | solution.py:213
  170.0 24.8 %collective-permute-start.55 = (bf16[512,128]{1,0:T(8,128)(2,1)S(1)}, bf16[512,128]{1,0:T(8,128)(2,1)S(1)}, u32[]{:S(2)}, u32[]{:S(2)}) collective-permute-start(bf16[512,128]{1,0:T(8,128)(2,1)S(1)} %shard_map.91.refs_0_), channel_id=1, source_target_pairs={{1,0},{2,1},{3,2},{0,3},{5,4},{6,5},{7,6},{4,7},{9,8},{10,9},{11,1... | collective-permute-start | bytes 393224 | tf_op jit(solution)/shard_map/ppermute | solution.py:213
  176.2 9.4 %collective-permute-start.66 = (bf16[112,128]{1,0:T(8,128)(2,1)S(1)}, bf16[112,128]{1,0:T(8,128)(2,1)S(1)}, u32[]{:S(2)}, u32[]{:S(2)}) collective-permute-start(bf16[112,128]{1,0:T(8,128)(2,1)S(1)} %shard_map.92.refs_4_.refs_0_), channel_id=1, source_target_pairs={{2,0},{3,1},{0,2},{1,3},{6,4},{7,5},{4,6},{5,7},{10,8},{11,9},{8,1... | collective-permute-start | bytes 86024 | tf_op jit(solution)/shard_map/ppermute | solution.py:213
  (64 other events, 617.3 us)

commit v14 on v13

--- a/solution.py
+++ b/solution.py
@@ -27,7 +27,7 @@
         in_specs=[whole] * len(operands),
         out_specs=jax.tree.map(lambda _: whole, outs),
         out_shape=outs,
-        compiler_params=pltpu.CompilerParams(vmem_limit_bytes=20 * MIB),
+        compiler_params=pltpu.CompilerParams(vmem_limit_bytes=12 * MIB),
         cost_estimate=pl.CostEstimate(
             flops=flops, bytes_accessed=sum(x.size * x.dtype.itemsize for x in operands), transcendentals=0
         ),
@@ -85,7 +85,7 @@
         load_ref[s, height - TERM_ROWS :] = terms.astype(load_ref.dtype)
 
 
-def join_kernel(before_ref, after_ref, out_ref):
+def join_kernel(before_ref, after_ref, _, out_ref):
     quarter = before_ref.shape[0]
     out_ref[:quarter] = before_ref[...]
     out_ref[quarter:] = after_ref[...]
@@ -264,14 +264,14 @@
         )
         before = lax.ppermute(right, "sector", onward)
         after = lax.ppermute(left, "sector", backward)
-        faces = call(join_kernel, shape(2 * quarter, loads, dtype=bf16), (before, after))
-        faces = one_from_each(faces, "dof")
         load = call(
             slice_kernel,
             shape(height + TERM_ROWS, loads, dtype=bf16),
             mine_from_each(load, "sector"),
         )
         slices = one_from_each(load, "dof")
+        faces = call(join_kernel, shape(2 * quarter, loads, dtype=bf16), (before, after, slices[-1]))
+        faces = one_from_each(faces, "dof")
         hub = call(
             functools.partial(hub_kernel, cases),
             shape(height, LANES, dtype=sent),

time: 214 us -> 223 us (1.042)
  waiting for transfers between devices: 31.7 us -> 50.2 us
  starting transfers between devices: 83.4 us -> 70.3 us
  blocking collectives: 66.7 us -> 70.3 us
    ppermute x69, waiting for transfers between devices: 31.7 us -> 50.2 us  [from_ahead(): lax.ppermute(cells, axis, [((i + distance) % count, i) for i in range(cou...]
    ppermute x69, starting transfers between devices: 75.4 us -> 62.7 us  [from_ahead(): lax.ppermute(cells, axis, [((i + distance) % count, i) for i in range(cou...]
    all_gather x3, blocking collectives: 53.6 us -> 57.7 us  [gathered(): return lax.all_gather(field, 'dof', axis=0)]
  transfers between devices with their start and end apart: 75 -> 75, of which waited for: 20 -> 25; matrix products, arithmetic and copies ran while one was open for 0% -> 0% of each run, Pallas kernels for 5% -> 5%
where the time goes in v14:
time: 223 us; the launch traced here: 222 us
  starting transfers between devices  70.3 us (32%)
  blocking collectives  70.3 us (32%)
  waiting for transfers between devices  50.2 us (23%)
  Pallas kernels  19.4 us (9%)
  local copies, waits for them, and re-layouts  11.2 us (5%)
    ppermute x69, starting transfers between devices, from_ahead(): lax.ppermute(cells, axis, [((i + distance) % count, i) for i in range(cou...  62.7 us
    all_gather x3, blocking collectives, gathered(): return lax.all_gather(field, 'dof', axis=0)  57.7 us
    ppermute x69, waiting for transfers between devices, from_ahead(): lax.ppermute(cells, axis, [((i + distance) % count, i) for i in range(cou...  50.2 us
    pallas_call x20, Pallas kernels, call(): pl.pallas_call(kernel, in_specs=[whole] * len(operands), out_specs=jax.tr...  19.4 us
    all_to_all x1, blocking collectives, exchange(): return lax.all_to_all(blocks, axes, split_axis=0, concat_axis=0)  12.6 us
    unnamed x26, local copies, waits for them, and re-layouts  10.8 us
    ppermute x3, starting transfers between devices, tiled_body(): after = lax.ppermute(left, 'sector', backward)  5.79 us
  transfers between devices with their start and end apart: 75, of which 25 were waited for; matrix products, arithmetic and copies ran while one was open for 0% of the time, Pallas kernels for 5%

profile of v14, /device:TPU:0, one launch (start us, length us, event | category | flops | bytes accessed | tf_op | source)
XLA Modules:
  0.0 222.4 jit_solution(16482038470861246270)
XLA Ops:
  1.7 5.1 %collective-permute-start = (bf16[256,128]{1,0:T(8,128)(2,1)S(1)}, bf16[256,128]{1,0:T(8,128)(2,1)S(1)}, u32[]{:S(2)}, u32[]{:S(2)}) collective-permute-start(bf16[256,128]{1,0:T(8,128)(2,1)S(1)} %get-tuple-element.39.refs_0_), channel_id=1, source_target_pairs={{1,0},{2,1},{3,2},{0,3},{5,4},{6,5},{7,6},{4,7},{9,8},{10,9},{11,1... | collective-permute-start | bytes 196616 | tf_op jit(solution)/shard_map/ppermute | solution.py:213
  7.8 19.2 %all-gather = bf16[3072,128]{1,0:T(8,128)(2,1)S(1)} all-gather(bf16[768,128]{1,0:T(8,128)(2,1)S(1)} %get-tuple-element.38), channel_id=2, replica_groups=mesh['sector'=8,'dof'=4] {'dof'}, dimensions={0}, use_global_device_ids=true | all-gather | bytes 983040 | tf_op jit(solution)/shard_map/all_gather | solution.py:227
  27.0 3.4 %copy-done = bf16[1024,4096]{1,0:T(8,128)(2,1)S(1)} copy-done((bf16[1024,4096]{1,0:T(8,128)(2,1)S(1)}, bf16[1024,4096]{1,0:T(8,128)(2,1)}, u32[]{:S(2)}) %copy-start) | copy-done | bytes 8388632
  31.1 2.3 %shard_map.78 = (f32[1024,128]{1,0:T(8,128)S(1)}, f32[8,112,128]{2,1,0:T(8,128)S(1)}, bf16[256,128]{1,0:T(8,128)(2,1)S(1)}, bf16[256,128]{1,0:T(8,128)(2,1)S(1)}) custom-call(bf16[1024,4096]{1,0:T(8,128)(2,1)S(1)} %copy-done, f32[1,768]{1,0:T(1,128)S(1)} %copy-done.6, bf16[4,768,128]{2,1,0:T(8,128)(2,1)S(1)} %bitcast.65, ...), custom_call_target="tpu_custom_call" | custom-call | flops 1073741824 | bytes 9440256 | tf_op jit(solution)/shard_map/pallas_call | solution.py:25
  45.0 3.8 %collective-permute-start.16 = (bf16[112,128]{1,0:T(8,128)(2,1)S(1)}, bf16[112,128]{1,0:T(8,128)(2,1)S(1)}, u32[]{:S(2)}, u32[]{:S(2)}) collective-permute-start(bf16[112,128]{1,0:T(8,128)(2,1)S(1)} %shard_map.79.refs_4_.refs_0_), channel_id=1, source_target_pairs={{1,0},{2,1},{3,2},{0,3},{5,4},{6,5},{7,6},{4,7},{9,8},{10,9},{11,1... | collective-permute-start | bytes 86024 | tf_op jit(solution)/shard_map/ppermute | solution.py:213
  53.9 2.5 %collective-permute-done.17.refs_6_.refs_2_ = bf16[112,128]{1,0:T(8,128)(2,1)S(1)} collective-permute-done((bf16[112,128]{1,0:T(8,128)(2,1)S(1)}, bf16[112,128]{1,0:T(8,128)(2,1)S(1)}, u32[]{:S(2)}, u32[]{:S(2)}) %collective-permute-start.17) | collective-permute-done | bytes 28704 | tf_op jit(solution)/shard_map/ppermute | solution.py:213
  56.4 2.3 %copy-done.2 = bf16[768,3072]{1,0:T(8,128)(2,1)S(1)} copy-done((bf16[768,3072]{1,0:T(8,128)(2,1)S(1)}, bf16[768,3072]{1,0:T(8,128)(2,1)}, u32[]{:S(2)}) %copy-start.2) | copy-done | bytes 4718616
  72.3 19.6 %all-gather.1 = bf16[3072,128]{1,0:T(8,128)(2,1)S(1)} all-gather(bf16[768,128]{1,0:T(8,128)(2,1)S(1)} %get-tuple-element.46), channel_id=3, replica_groups=mesh['sector'=8,'dof'=4] {'dof'}, dimensions={0}, use_global_device_ids=true | all-gather | bytes 983040 | tf_op jit(solution)/shard_map/all_gather | solution.py:227
  92.0 3.4 %copy-done.1 = bf16[1024,4096]{1,0:T(8,128)(2,1)S(1)} copy-done((bf16[1024,4096]{1,0:T(8,128)(2,1)S(1)}, bf16[1024,4096]{1,0:T(8,128)(2,1)}, u32[]{:S(2)}) %copy-start.1) | copy-done | bytes 8388632
  95.3 2.3 %shard_map.84 = (f32[1024,128]{1,0:T(8,128)S(1)}, bf16[8,112,128]{2,1,0:T(8,128)(2,1)S(1)}, bf16[256,128]{1,0:T(8,128)(2,1)S(1)}, bf16[256,128]{1,0:T(8,128)(2,1)S(1)}) custom-call(bf16[1024,4096]{1,0:T(8,128)(2,1)S(1)} %copy-done.1, f32[1,768]{1,0:T(1,128)S(1)} %copy-done.7, bf16[4,768,128]{2,1,0:T(8,128)(2,1)S(1)} %bitcast.63, ...), custom_call_target="tpu_custom_call" | custom-call | flops 1073741824 | bytes 9444352 | tf_op jit(solution)/shard_map/pallas_call | solution.py:25
  101.8 2.6 %collective-permute-start.29 = (bf16[256,128]{1,0:T(8,128)(2,1)S(1)}, bf16[256,128]{1,0:T(8,128)(2,1)S(1)}, u32[]{:S(2)}, u32[]{:S(2)}) collective-permute-start(bf16[256,128]{1,0:T(8,128)(2,1)S(1)} %get-tuple-element.51), channel_id=1, source_target_pairs={{4,0},{8,4},{12,8},{16,12},{20,16},{24,20},{28,24},{0,28},{5,1},{9... | collective-permute-start | bytes 196616 | tf_op jit(solution)/shard_map/ppermute | solution.py:266
  105.4 2.4 %collective-permute-done.34.refs_5_ = bf16[112,128]{1,0:T(8,128)(2,1)S(1)} collective-permute-done((bf16[112,128]{1,0:T(8,128)(2,1)S(1)}, bf16[112,128]{1,0:T(8,128)(2,1)S(1)}, u32[]{:S(2)}, u32[]{:S(2)}) %collective-permute-start.34) | collective-permute-done | bytes 28704 | tf_op jit(solution)/shard_map/ppermute | solution.py:213
  109.6 5.7 %collective-permute-done.37._.refs_7_.refs_3_ = bf16[112,128]{1,0:T(8,128)(2,1)S(1)} collective-permute-done((bf16[112,128]{1,0:T(8,128)(2,1)S(1)}, bf16[112,128]{1,0:T(8,128)(2,1)S(1)}, u32[]{:S(2)}, u32[]{:S(2)}) %collective-permute-start.37) | collective-permute-done | bytes 28704 | tf_op jit(solution)/shard_map/ppermute | solution.py:213
  117.4 2.4 %collective-permute-start.41 = (bf16[112,128]{1,0:T(8,128)(2,1)S(1)}, bf16[112,128]{1,0:T(8,128)(2,1)S(1)}, u32[]{:S(2)}, u32[]{:S(2)}) collective-permute-start(bf16[112,128]{1,0:T(8,128)(2,1)S(1)} %shard_map.85.refs_4_.refs_0_), channel_id=1, source_target_pairs={{1,0},{2,1},{3,2},{0,3},{5,4},{6,5},{7,6},{4,7},{9,8},{10,9},{11,1... | collective-permute-start | bytes 86024 | tf_op jit(solution)/shard_map/ppermute | solution.py:213
  120.5 2.4 %collective-permute-done.41.refs_5_.refs_1_ = bf16[112,128]{1,0:T(8,128)(2,1)S(1)} collective-permute-done((bf16[112,128]{1,0:T(8,128)(2,1)S(1)}, bf16[112,128]{1,0:T(8,128)(2,1)S(1)}, u32[]{:S(2)}, u32[]{:S(2)}) %collective-permute-start.41) | collective-permute-done | bytes 28704 | tf_op jit(solution)/shard_map/ppermute | solution.py:213
  122.9 5.3 %collective-permute-done.42.refs_6_.refs_2_ = bf16[112,128]{1,0:T(8,128)(2,1)S(1)} collective-permute-done((bf16[112,128]{1,0:T(8,128)(2,1)S(1)}, bf16[112,128]{1,0:T(8,128)(2,1)S(1)}, u32[]{:S(2)}, u32[]{:S(2)}) %collective-permute-start.42) | collective-permute-done | bytes 28704 | tf_op jit(solution)/shard_map/ppermute | solution.py:213
  138.1 3.8 %collective-permute-start.50 = (bf16[256,128]{1,0:T(8,128)(2,1)S(1)}, bf16[256,128]{1,0:T(8,128)(2,1)S(1)}, u32[]{:S(2)}, u32[]{:S(2)}) collective-permute-start(bf16[256,128]{1,0:T(8,128)(2,1)S(1)} %get-tuple-element.58.refs_0_), channel_id=1, source_target_pairs={{1,0},{2,1},{3,2},{0,3},{5,4},{6,5},{7,6},{4,7},{9,8},{10,9},{11,1... | collective-permute-start | bytes 196616 | tf_op jit(solution)/shard_map/ppermute | solution.py:213
  143.4 18.9 %all-gather.2 = bf16[3072,128]{1,0:T(8,128)(2,1)S(1)} all-gather(bf16[768,128]{1,0:T(8,128)(2,1)S(1)} %get-tuple-element.57), channel_id=4, replica_groups=mesh['sector'=8,'dof'=4] {'dof'}, dimensions={0}, use_global_device_ids=true | all-gather | bytes 983040 | tf_op jit(solution)/shard_map/all_gather | solution.py:227
  162.3 2.3 %shard_map.90 = (f32[1024,128]{1,0:T(8,128)S(1)}, bf16[8,112,128]{2,1,0:T(8,128)(2,1)S(1)}, bf16[256,128]{1,0:T(8,128)(2,1)S(1)}, bf16[256,128]{1,0:T(8,128)(2,1)S(1)}) custom-call(bf16[1024,4096]{1,0:T(8,128)(2,1)S(1)} %bitcast.55, f32[1,768]{1,0:T(1,128)S(1)} %copy-done.7, bf16[4,768,128]{2,1,0:T(8,128)(2,1)S(1)} %bitcast.64, ...), custom_call_target="tpu_custom_call" | custom-call | flops 1073741824 | bytes 9444352 | tf_op jit(solution)/shard_map/pallas_call | solution.py:25
  169.3 2.3 %collective-permute-start.54 = (bf16[256,128]{1,0:T(8,128)(2,1)S(1)}, bf16[256,128]{1,0:T(8,128)(2,1)S(1)}, u32[]{:S(2)}, u32[]{:S(2)}) collective-permute-start(bf16[256,128]{1,0:T(8,128)(2,1)S(1)} %get-tuple-element.62), channel_id=1, source_target_pairs={{4,0},{8,4},{12,8},{16,12},{20,16},{24,20},{28,24},{0,28},{5,1},{9... | collective-permute-start | bytes 196616 | tf_op jit(solution)/shard_map/ppermute | solution.py:266
  176.9 5.8 %collective-permute-done.62._.refs_7_.refs_3_ = bf16[112,128]{1,0:T(8,128)(2,1)S(1)} collective-permute-done((bf16[112,128]{1,0:T(8,128)(2,1)S(1)}, bf16[112,128]{1,0:T(8,128)(2,1)S(1)}, u32[]{:S(2)}, u32[]{:S(2)}) %collective-permute-start.62) | collective-permute-done | bytes 28704 | tf_op jit(solution)/shard_map/ppermute | solution.py:213
  184.8 2.4 %collective-permute-start.66 = (bf16[112,128]{1,0:T(8,128)(2,1)S(1)}, bf16[112,128]{1,0:T(8,128)(2,1)S(1)}, u32[]{:S(2)}, u32[]{:S(2)}) collective-permute-start(bf16[112,128]{1,0:T(8,128)(2,1)S(1)} %shard_map.91.refs_4_.refs_0_), channel_id=1, source_target_pairs={{1,0},{2,1},{3,2},{0,3},{5,4},{6,5},{7,6},{4,7},{9,8},{10,9},{11,1... | collective-permute-start | bytes 86024 | tf_op jit(solution)/shard_map/ppermute | solution.py:213
  190.1 5.4 %collective-permute-done.67.refs_6_.refs_2_ = bf16[112,128]{1,0:T(8,128)(2,1)S(1)} collective-permute-done((bf16[112,128]{1,0:T(8,128)(2,1)S(1)}, bf16[112,128]{1,0:T(8,128)(2,1)S(1)}, u32[]{:S(2)}, u32[]{:S(2)}) %collective-permute-start.67) | collective-permute-done | bytes 28704 | tf_op jit(solution)/shard_map/ppermute | solution.py:213
  208.7 12.6 %all_to_all.5.sums_ref = f32[32,8,128]{2,1,0:T(8,128)S(1)} all-to-all(f32[32,8,128]{2,1,0:T(8,128)S(1)} %get-tuple-element.70), channel_id=1, replica_groups=mesh['sector'=8,'dof'=4] {'sector','dof'}, dimensions={0} | all-to-all | bytes 262144 | tf_op jit(solution)/shard_map/all_to_all | solution.py:208
  (184 shorter events, 83.2 us)
Async XLA Ops:
  1.7 25.3 %collective-permute-start = (bf16[256,128]{1,0:T(8,128)(2,1)S(1)}, bf16[256,128]{1,0:T(8,128)(2,1)S(1)}, u32[]{:S(2)}, u32[]{:S(2)}) collective-permute-start(bf16[256,128]{1,0:T(8,128)(2,1)S(1)} %get-tuple-element.39.refs_0_), channel_id=1, source_target_pairs={{1,0},{2,1},{3,2},{0,3},{5,4},{6,5},{7,6},{4,7},{9,8},{10,9},{11,1... | collective-permute-start | bytes 196616 | tf_op jit(solution)/shard_map/ppermute | solution.py:213
  6.8 20.2 %collective-permute-start.1 = (bf16[256,128]{1,0:T(8,128)(2,1)S(1)}, bf16[256,128]{1,0:T(8,128)(2,1)S(1)}, u32[]{:S(2)}, u32[]{:S(2)}) collective-permute-start(bf16[256,128]{1,0:T(8,128)(2,1)S(1)} %get-tuple-element.39.refs_0_), channel_id=1, source_target_pairs={{2,0},{3,1},{0,2},{1,3},{6,4},{7,5},{4,6},{5,7},{10,8},{11,9},{8,1... | collective-permute-start | bytes 196616 | tf_op jit(solution)/shard_map/ppermute | solution.py:213
  6.8 20.2 %collective-permute-start.2 = (bf16[256,128]{1,0:T(8,128)(2,1)S(1)}, bf16[256,128]{1,0:T(8,128)(2,1)S(1)}, u32[]{:S(2)}, u32[]{:S(2)}) collective-permute-start(bf16[256,128]{1,0:T(8,128)(2,1)S(1)} %get-tuple-element.39.refs_0_), channel_id=1, source_target_pairs={{3,0},{0,1},{1,2},{2,3},{7,4},{4,5},{5,6},{6,7},{11,8},{8,9},{9,10... | collective-permute-start | bytes 196616 | tf_op jit(solution)/shard_map/ppermute | solution.py:213
  39.6 9.2 %collective-permute-start.3 = (bf16[256,128]{1,0:T(8,128)(2,1)S(1)}, bf16[256,128]{1,0:T(8,128)(2,1)S(1)}, u32[]{:S(2)}, u32[]{:S(2)}) collective-permute-start(bf16[256,128]{1,0:T(8,128)(2,1)S(1)} %get-tuple-element.41), channel_id=1, source_target_pairs={{0,4},{4,8},{8,12},{12,16},{16,20},{20,24},{24,28},{28,0},{1,5},{5... | collective-permute-start | bytes 196616 | tf_op jit(solution)/shard_map/ppermute | solution.py:265
  45.0 8.9 %collective-permute-start.16 = (bf16[112,128]{1,0:T(8,128)(2,1)S(1)}, bf16[112,128]{1,0:T(8,128)(2,1)S(1)}, u32[]{:S(2)}, u32[]{:S(2)}) collective-permute-start(bf16[112,128]{1,0:T(8,128)(2,1)S(1)} %shard_map.79.refs_4_.refs_0_), channel_id=1, source_target_pairs={{1,0},{2,1},{3,2},{0,3},{5,4},{6,5},{7,6},{4,7},{9,8},{10,9},{11,1... | collective-permute-start | bytes 86024 | tf_op jit(solution)/shard_map/ppermute | solution.py:213
  50.8 13.4 %collective-permute-start.13 = (bf16[512,128]{1,0:T(8,128)(2,1)S(1)}, bf16[512,128]{1,0:T(8,128)(2,1)S(1)}, u32[]{:S(2)}, u32[]{:S(2)}) collective-permute-start(bf16[512,128]{1,0:T(8,128)(2,1)S(1)} %shard_map.80.refs_0_), channel_id=1, source_target_pairs={{1,0},{2,1},{3,2},{0,3},{5,4},{6,5},{7,6},{4,7},{9,8},{10,9},{11,1... | collective-permute-start | bytes 393224 | tf_op jit(solution)/shard_map/ppermute | solution.py:213
  50.9 14.6 %collective-permute-start.14 = (bf16[512,128]{1,0:T(8,128)(2,1)S(1)}, bf16[512,128]{1,0:T(8,128)(2,1)S(1)}, u32[]{:S(2)}, u32[]{:S(2)}) collective-permute-start(bf16[512,128]{1,0:T(8,128)(2,1)S(1)} %shard_map.80.refs_0_), channel_id=1, source_target_pairs={{2,0},{3,1},{0,2},{1,3},{6,4},{7,5},{4,6},{5,7},{10,8},{11,9},{8,1... | collective-permute-start | bytes 393224 | tf_op jit(solution)/shard_map/ppermute | solution.py:213
  51.9 15.1 %collective-permute-start.15 = (bf16[512,128]{1,0:T(8,128)(2,1)S(1)}, bf16[512,128]{1,0:T(8,128)(2,1)S(1)}, u32[]{:S(2)}, u32[]{:S(2)}) collective-permute-start(bf16[512,128]{1,0:T(8,128)(2,1)S(1)} %shard_map.80.refs_0_), channel_id=1, source_target_pairs={{3,0},{0,1},{1,2},{2,3},{7,4},{4,5},{5,6},{6,7},{11,8},{8,9},{9,10... | collective-permute-start | bytes 393224 | tf_op jit(solution)/shard_map/ppermute | solution.py:213
  69.1 22.9 %collective-permute-start.25 = (bf16[256,128]{1,0:T(8,128)(2,1)S(1)}, bf16[256,128]{1,0:T(8,128)(2,1)S(1)}, u32[]{:S(2)}, u32[]{:S(2)}) collective-permute-start(bf16[256,128]{1,0:T(8,128)(2,1)S(1)} %get-tuple-element.47.refs_0_), channel_id=1, source_target_pairs={{1,0},{2,1},{3,2},{0,3},{5,4},{6,5},{7,6},{4,7},{9,8},{10,9},{11,1... | collective-permute-start | bytes 196616 | tf_op jit(solution)/shard_map/ppermute | solution.py:213
  69.9 22.1 %collective-permute-start.26 = (bf16[256,128]{1,0:T(8,128)(2,1)S(1)}, bf16[256,128]{1,0:T(8,128)(2,1)S(1)}, u32[]{:S(2)}, u32[]{:S(2)}) collective-permute-start(bf16[256,128]{1,0:T(8,128)(2,1)S(1)} %get-tuple-element.47.refs_0_), channel_id=1, source_target_pairs={{2,0},{3,1},{0,2},{1,3},{6,4},{7,5},{4,6},{5,7},{10,8},{11,9},{8,1... | collective-permute-start | bytes 196616 | tf_op jit(solution)/shard_map/ppermute | solution.py:213
  69.9 22.1 %collective-permute-start.27 = (bf16[256,128]{1,0:T(8,128)(2,1)S(1)}, bf16[256,128]{1,0:T(8,128)(2,1)S(1)}, u32[]{:S(2)}, u32[]{:S(2)}) collective-permute-start(bf16[256,128]{1,0:T(8,128)(2,1)S(1)} %get-tuple-element.47.refs_0_), channel_id=1, source_target_pairs={{3,0},{0,1},{1,2},{2,3},{7,4},{4,5},{5,6},{6,7},{11,8},{8,9},{9,10... | collective-permute-start | bytes 196616 | tf_op jit(solution)/shard_map/ppermute | solution.py:213
  101.8 13.5 %collective-permute-start.28 = (bf16[256,128]{1,0:T(8,128)(2,1)S(1)}, bf16[256,128]{1,0:T(8,128)(2,1)S(1)}, u32[]{:S(2)}, u32[]{:S(2)}) collective-permute-start(bf16[256,128]{1,0:T(8,128)(2,1)S(1)} %get-tuple-element.50), channel_id=1, source_target_pairs={{0,4},{4,8},{8,12},{12,16},{16,20},{20,24},{24,28},{28,0},{1,5},{5... | collective-permute-start | bytes 196616 | tf_op jit(solution)/shard_map/ppermute | solution.py:265
  101.8 13.5 %collective-permute-start.29 = (bf16[256,128]{1,0:T(8,128)(2,1)S(1)}, bf16[256,128]{1,0:T(8,128)(2,1)S(1)}, u32[]{:S(2)}, u32[]{:S(2)}) collective-permute-start(bf16[256,128]{1,0:T(8,128)(2,1)S(1)} %get-tuple-element.51), channel_id=1, source_target_pairs={{4,0},{8,4},{12,8},{16,12},{20,16},{24,20},{28,24},{0,28},{5,1},{9... | collective-permute-start | bytes 196616 | tf_op jit(solution)/shard_map/ppermute | solution.py:266
  115.3 19.4 %collective-permute-start.38 = (bf16[512,128]{1,0:T(8,128)(2,1)S(1)}, bf16[512,128]{1,0:T(8,128)(2,1)S(1)}, u32[]{:S(2)}, u32[]{:S(2)}) collective-permute-start(bf16[512,128]{1,0:T(8,128)(2,1)S(1)} %shard_map.86.refs_0_), channel_id=1, source_target_pairs={{1,0},{2,1},{3,2},{0,3},{5,4},{6,5},{7,6},{4,7},{9,8},{10,9},{11,1... | collective-permute-start | bytes 393224 | tf_op jit(solution)/shard_map/ppermute | solution.py:213
  115.6 19.1 %collective-permute-start.39 = (bf16[512,128]{1,0:T(8,128)(2,1)S(1)}, bf16[512,128]{1,0:T(8,128)(2,1)S(1)}, u32[]{:S(2)}, u32[]{:S(2)}) collective-permute-start(bf16[512,128]{1,0:T(8,128)(2,1)S(1)} %shard_map.86.refs_0_), channel_id=1, source_target_pairs={{2,0},{3,1},{0,2},{1,3},{6,4},{7,5},{4,6},{5,7},{10,8},{11,9},{8,1... | collective-permute-start | bytes 393224 | tf_op jit(solution)/shard_map/ppermute | solution.py:213
  115.6 20.8 %collective-permute-start.40 = (bf16[512,128]{1,0:T(8,128)(2,1)S(1)}, bf16[512,128]{1,0:T(8,128)(2,1)S(1)}, u32[]{:S(2)}, u32[]{:S(2)}) collective-permute-start(bf16[512,128]{1,0:T(8,128)(2,1)S(1)} %shard_map.86.refs_0_), channel_id=1, source_target_pairs={{3,0},{0,1},{1,2},{2,3},{7,4},{4,5},{5,6},{6,7},{11,8},{8,9},{9,10... | collective-permute-start | bytes 393224 | tf_op jit(solution)/shard_map/ppermute | solution.py:213
  138.1 24.2 %collective-permute-start.50 = (bf16[256,128]{1,0:T(8,128)(2,1)S(1)}, bf16[256,128]{1,0:T(8,128)(2,1)S(1)}, u32[]{:S(2)}, u32[]{:S(2)}) collective-permute-start(bf16[256,128]{1,0:T(8,128)(2,1)S(1)} %get-tuple-element.58.refs_0_), channel_id=1, source_target_pairs={{1,0},{2,1},{3,2},{0,3},{5,4},{6,5},{7,6},{4,7},{9,8},{10,9},{11,1... | collective-permute-start | bytes 196616 | tf_op jit(solution)/shard_map/ppermute | solution.py:213
  141.9 20.4 %collective-permute-start.51 = (bf16[256,128]{1,0:T(8,128)(2,1)S(1)}, bf16[256,128]{1,0:T(8,128)(2,1)S(1)}, u32[]{:S(2)}, u32[]{:S(2)}) collective-permute-start(bf16[256,128]{1,0:T(8,128)(2,1)S(1)} %get-tuple-element.58.refs_0_), channel_id=1, source_target_pairs={{2,0},{3,1},{0,2},{1,3},{6,4},{7,5},{4,6},{5,7},{10,8},{11,9},{8,1... | collective-permute-start | bytes 196616 | tf_op jit(solution)/shard_map/ppermute | solution.py:213
  142.0 20.4 %collective-permute-start.52 = (bf16[256,128]{1,0:T(8,128)(2,1)S(1)}, bf16[256,128]{1,0:T(8,128)(2,1)S(1)}, u32[]{:S(2)}, u32[]{:S(2)}) collective-permute-start(bf16[256,128]{1,0:T(8,128)(2,1)S(1)} %get-tuple-element.58.refs_0_), channel_id=1, source_target_pairs={{3,0},{0,1},{1,2},{2,3},{7,4},{4,5},{5,6},{6,7},{11,8},{8,9},{9,10... | collective-permute-start | bytes 196616 | tf_op jit(solution)/shard_map/ppermute | solution.py:213
  168.9 13.8 %collective-permute-start.53 = (bf16[256,128]{1,0:T(8,128)(2,1)S(1)}, bf16[256,128]{1,0:T(8,128)(2,1)S(1)}, u32[]{:S(2)}, u32[]{:S(2)}) collective-permute-start(bf16[256,128]{1,0:T(8,128)(2,1)S(1)} %get-tuple-element.61), channel_id=1, source_target_pairs={{0,4},{4,8},{8,12},{12,16},{16,20},{20,24},{24,28},{28,0},{1,5},{5... | collective-permute-start | bytes 196616 | tf_op jit(solution)/shard_map/ppermute | solution.py:265
  169.3 13.5 %collective-permute-start.54 = (bf16[256,128]{1,0:T(8,128)(2,1)S(1)}, bf16[256,128]{1,0:T(8,128)(2,1)S(1)}, u32[]{:S(2)}, u32[]{:S(2)}) collective-permute-start(bf16[256,128]{1,0:T(8,128)(2,1)S(1)} %get-tuple-element.62), channel_id=1, source_target_pairs={{4,0},{8,4},{12,8},{16,12},{20,16},{24,20},{28,24},{0,28},{5,1},{9... | collective-permute-start | bytes 196616 | tf_op jit(solution)/shard_map/ppermute | solution.py:266
  182.8 19.2 %collective-permute-start.63 = (bf16[512,128]{1,0:T(8,128)(2,1)S(1)}, bf16[512,128]{1,0:T(8,128)(2,1)S(1)}, u32[]{:S(2)}, u32[]{:S(2)}) collective-permute-start(bf16[512,128]{1,0:T(8,128)(2,1)S(1)} %shard_map.92.refs_0_), channel_id=1, source_target_pairs={{1,0},{2,1},{3,2},{0,3},{5,4},{6,5},{7,6},{4,7},{9,8},{10,9},{11,1... | collective-permute-start | bytes 393224 | tf_op jit(solution)/shard_map/ppermute | solution.py:213
  182.9 19.0 %collective-permute-start.64 = (bf16[512,128]{1,0:T(8,128)(2,1)S(1)}, bf16[512,128]{1,0:T(8,128)(2,1)S(1)}, u32[]{:S(2)}, u32[]{:S(2)}) collective-permute-start(bf16[512,128]{1,0:T(8,128)(2,1)S(1)} %shard_map.92.refs_0_), channel_id=1, source_target_pairs={{2,0},{3,1},{0,2},{1,3},{6,4},{7,5},{4,6},{5,7},{10,8},{11,9},{8,1... | collective-permute-start | bytes 393224 | tf_op jit(solution)/shard_map/ppermute | solution.py:213
  182.9 20.8 %collective-permute-start.65 = (bf16[512,128]{1,0:T(8,128)(2,1)S(1)}, bf16[512,128]{1,0:T(8,128)(2,1)S(1)}, u32[]{:S(2)}, u32[]{:S(2)}) collective-permute-start(bf16[512,128]{1,0:T(8,128)(2,1)S(1)} %shard_map.92.refs_0_), channel_id=1, source_target_pairs={{3,0},{0,1},{1,2},{2,3},{7,4},{4,5},{5,6},{6,7},{11,8},{8,9},{9,10... | collective-permute-start | bytes 393224 | tf_op jit(solution)/shard_map/ppermute | solution.py:213
  (64 other events, 521.4 us)

commit v15 on v14

--- a/solution.py
+++ b/solution.py
@@ -27,7 +27,7 @@
         in_specs=[whole] * len(operands),
         out_specs=jax.tree.map(lambda _: whole, outs),
         out_shape=outs,
-        compiler_params=pltpu.CompilerParams(vmem_limit_bytes=12 * MIB),
+        compiler_params=pltpu.CompilerParams(vmem_limit_bytes=20 * MIB),
         cost_estimate=pl.CostEstimate(
             flops=flops, bytes_accessed=sum(x.size * x.dtype.itemsize for x in operands), transcendentals=0
         ),
@@ -85,7 +85,8 @@
         load_ref[s, height - TERM_ROWS :] = terms.astype(load_ref.dtype)
 
 
-def join_kernel(before_ref, after_ref, _, out_ref):
+def join_kernel(before_ref, after_ref, *refs):
+    out_ref = refs[-1]
     quarter = before_ref.shape[0]
     out_ref[:quarter] = before_ref[...]
     out_ref[quarter:] = after_ref[...]
@@ -270,7 +271,7 @@
             mine_from_each(load, "sector"),
         )
         slices = one_from_each(load, "dof")
-        faces = call(join_kernel, shape(2 * quarter, loads, dtype=bf16), (before, after, slices[-1]))
+        faces = call(join_kernel, shape(2 * quarter, loads, dtype=bf16), (before, after, *slices[1:]))
         faces = one_from_each(faces, "dof")
         hub = call(
             functools.partial(hub_kernel, cases),

time: 223 us -> 204 us (0.915)
  waiting for transfers between devices: 50.2 us -> 36.3 us
  blocking collectives: 70.3 us -> 65.7 us
    ppermute x69, waiting for transfers between devices: 50.2 us -> 36.3 us  [from_ahead(): lax.ppermute(cells, axis, [((i + distance) % count, i) for i in range(cou...]
    all_to_all x1, blocking collectives: 12.6 us -> 10.1 us  [exchange(): return lax.all_to_all(blocks, axes, split_axis=0, concat_axis=0)]
  transfers between devices with their start and end apart: 75 -> 75, of which waited for: 25 -> 27; matrix products, arithmetic and copies ran while one was open for 0% -> 0% of each run, Pallas kernels for 5% -> 5%
where the time goes in v15:
time: 204 us
  starting transfers between devices  70.2 us (34%)
  blocking collectives  65.7 us (32%)
  waiting for transfers between devices  36.3 us (18%)
  Pallas kernels  19.5 us (10%)
  local copies, waits for them, and re-layouts  11.2 us (5%)
    ppermute x69, starting transfers between devices, from_ahead(): lax.ppermute(cells, axis, [((i + distance) % count, i) for i in range(cou...  62.6 us
    all_gather x3, blocking collectives, gathered(): return lax.all_gather(field, 'dof', axis=0)  55.6 us
    ppermute x69, waiting for transfers between devices, from_ahead(): lax.ppermute(cells, axis, [((i + distance) % count, i) for i in range(cou...  36.3 us
    pallas_call x20, Pallas kernels, call(): pl.pallas_call(kernel, in_specs=[whole] * len(operands), out_specs=jax.tr...  19.5 us
    unnamed x26, local copies, waits for them, and re-layouts  10.9 us
    all_to_all x1, blocking collectives, exchange(): return lax.all_to_all(blocks, axes, split_axis=0, concat_axis=0)  10.1 us
    ppermute x3, starting transfers between devices, tiled_body(): after = lax.ppermute(left, 'sector', backward)  5.88 us
  transfers between devices with their start and end apart: 75, of which 27 were waited for; matrix products, arithmetic and copies ran while one was open for 0% of the time, Pallas kernels for 5%

profile of v15, /device:TPU:0, one launch (start us, length us, event | category | flops | bytes accessed | tf_op | source)
XLA Modules:
  0.0 204.0 jit_solution(12780438241559895380)
XLA Ops:
  1.7 5.1 %collective-permute-start = (bf16[256,128]{1,0:T(8,128)(2,1)S(1)}, bf16[256,128]{1,0:T(8,128)(2,1)S(1)}, u32[]{:S(2)}, u32[]{:S(2)}) collective-permute-start(bf16[256,128]{1,0:T(8,128)(2,1)S(1)} %get-tuple-element.39.refs_0_), channel_id=1, source_target_pairs={{1,0},{2,1},{3,2},{0,3},{5,4},{6,5},{7,6},{4,7},{9,8},{10,9},{11,1... | collective-permute-start | bytes 196616 | tf_op jit(solution)/shard_map/ppermute | solution.py:214
  7.8 19.2 %all-gather = bf16[3072,128]{1,0:T(8,128)(2,1)S(1)} all-gather(bf16[768,128]{1,0:T(8,128)(2,1)S(1)} %get-tuple-element.38), channel_id=2, replica_groups=mesh['sector'=8,'dof'=4] {'dof'}, dimensions={0}, use_global_device_ids=true | all-gather | bytes 983040 | tf_op jit(solution)/shard_map/all_gather | solution.py:228
  27.0 3.4 %copy-done = bf16[1024,4096]{1,0:T(8,128)(2,1)S(1)} copy-done((bf16[1024,4096]{1,0:T(8,128)(2,1)S(1)}, bf16[1024,4096]{1,0:T(8,128)(2,1)}, u32[]{:S(2)}) %copy-start) | copy-done | bytes 8388632
  31.1 2.3 %shard_map.78 = (f32[1024,128]{1,0:T(8,128)S(1)}, f32[8,112,128]{2,1,0:T(8,128)S(1)}, bf16[256,128]{1,0:T(8,128)(2,1)S(1)}, bf16[256,128]{1,0:T(8,128)(2,1)S(1)}) custom-call(bf16[1024,4096]{1,0:T(8,128)(2,1)S(1)} %copy-done, f32[1,768]{1,0:T(1,128)S(1)} %copy-done.6, bf16[4,768,128]{2,1,0:T(8,128)(2,1)S(1)} %bitcast.65, ...), custom_call_target="tpu_custom_call" | custom-call | flops 1073741824 | bytes 9440256 | tf_op jit(solution)/shard_map/pallas_call | solution.py:25
  33.8 2.2 %collective-permute-start.6 = (f32[112,128]{1,0:T(8,128)S(1)}, f32[112,128]{1,0:T(8,128)S(1)}, u32[]{:S(2)}, u32[]{:S(2)}) collective-permute-start(f32[112,128]{1,0:T(8,128)S(1)} %get-tuple-element.79), channel_id=1, source_target_pairs={{8,0},{12,4},{16,8},{20,12},{24,16},{28,20},{0,24},{4,28},{9,1},{1... | collective-permute-start | bytes 172040 | tf_op jit(solution)/shard_map/ppermute | solution.py:214
  42.9 2.0 collective-permute-done.9.refs_5_
  48.9 2.9 %collective-permute-done.13.refs_1_.refs_6_.refs_2_ = bf16[112,128]{1,0:T(8,128)(2,1)S(1)} collective-permute-done((bf16[112,128]{1,0:T(8,128)(2,1)S(1)}, bf16[112,128]{1,0:T(8,128)(2,1)S(1)}, u32[]{:S(2)}, u32[]{:S(2)}) %collective-permute-start.13) | collective-permute-done | bytes 28704 | tf_op jit(solution)/shard_map/ppermute | solution.py:214
  55.3 2.3 %copy-done.2 = bf16[768,3072]{1,0:T(8,128)(2,1)S(1)} copy-done((bf16[768,3072]{1,0:T(8,128)(2,1)S(1)}, bf16[768,3072]{1,0:T(8,128)(2,1)}, u32[]{:S(2)}) %copy-start.2) | copy-done | bytes 4718616
  73.2 17.8 %all-gather.1 = bf16[3072,128]{1,0:T(8,128)(2,1)S(1)} all-gather(bf16[768,128]{1,0:T(8,128)(2,1)S(1)} %get-tuple-element.46), channel_id=3, replica_groups=mesh['sector'=8,'dof'=4] {'dof'}, dimensions={0}, use_global_device_ids=true | all-gather | bytes 983040 | tf_op jit(solution)/shard_map/all_gather | solution.py:228
  91.0 3.4 %copy-done.1 = bf16[1024,4096]{1,0:T(8,128)(2,1)S(1)} copy-done((bf16[1024,4096]{1,0:T(8,128)(2,1)S(1)}, bf16[1024,4096]{1,0:T(8,128)(2,1)}, u32[]{:S(2)}) %copy-start.1) | copy-done | bytes 8388632
  94.3 2.3 %shard_map.84 = (f32[1024,128]{1,0:T(8,128)S(1)}, bf16[8,112,128]{2,1,0:T(8,128)(2,1)S(1)}, bf16[256,128]{1,0:T(8,128)(2,1)S(1)}, bf16[256,128]{1,0:T(8,128)(2,1)S(1)}) custom-call(bf16[1024,4096]{1,0:T(8,128)(2,1)S(1)} %copy-done.1, f32[1,768]{1,0:T(1,128)S(1)} %copy-done.7, bf16[4,768,128]{2,1,0:T(8,128)(2,1)S(1)} %bitcast.63, ...), custom_call_target="tpu_custom_call" | custom-call | flops 1073741824 | bytes 9444352 | tf_op jit(solution)/shard_map/pallas_call | solution.py:25
  101.0 2.4 %collective-permute-start.29 = (bf16[256,128]{1,0:T(8,128)(2,1)S(1)}, bf16[256,128]{1,0:T(8,128)(2,1)S(1)}, u32[]{:S(2)}, u32[]{:S(2)}) collective-permute-start(bf16[256,128]{1,0:T(8,128)(2,1)S(1)} %get-tuple-element.51), channel_id=1, source_target_pairs={{4,0},{8,4},{12,8},{16,12},{20,16},{24,20},{28,24},{0,28},{5,1},{9... | collective-permute-start | bytes 196616 | tf_op jit(solution)/shard_map/ppermute | solution.py:267
  112.8 2.8 %collective-permute-done.38.refs_1_.refs_6_.refs_2_ = bf16[112,128]{1,0:T(8,128)(2,1)S(1)} collective-permute-done((bf16[112,128]{1,0:T(8,128)(2,1)S(1)}, bf16[112,128]{1,0:T(8,128)(2,1)S(1)}, u32[]{:S(2)}, u32[]{:S(2)}) %collective-permute-start.38) | collective-permute-done | bytes 28704 | tf_op jit(solution)/shard_map/ppermute | solution.py:214
  126.2 2.2 %collective-permute-done.41.refs_2_ = bf16[512,128]{1,0:T(8,128)(2,1)S(1)} collective-permute-done((bf16[512,128]{1,0:T(8,128)(2,1)S(1)}, bf16[512,128]{1,0:T(8,128)(2,1)S(1)}, u32[]{:S(2)}, u32[]{:S(2)}) %collective-permute-start.41) | collective-permute-done | bytes 131104 | tf_op jit(solution)/shard_map/ppermute | solution.py:214
  134.5 18.7 %all-gather.2 = bf16[3072,128]{1,0:T(8,128)(2,1)S(1)} all-gather(bf16[768,128]{1,0:T(8,128)(2,1)S(1)} %get-tuple-element.57), channel_id=4, replica_groups=mesh['sector'=8,'dof'=4] {'dof'}, dimensions={0}, use_global_device_ids=true | all-gather | bytes 983040 | tf_op jit(solution)/shard_map/all_gather | solution.py:228
  153.2 2.3 %shard_map.90 = (f32[1024,128]{1,0:T(8,128)S(1)}, bf16[8,112,128]{2,1,0:T(8,128)(2,1)S(1)}, bf16[256,128]{1,0:T(8,128)(2,1)S(1)}, bf16[256,128]{1,0:T(8,128)(2,1)S(1)}) custom-call(bf16[1024,4096]{1,0:T(8,128)(2,1)S(1)} %bitcast.55, f32[1,768]{1,0:T(1,128)S(1)} %copy-done.7, bf16[4,768,128]{2,1,0:T(8,128)(2,1)S(1)} %bitcast.64, ...), custom_call_target="tpu_custom_call" | custom-call | flops 1073741824 | bytes 9444352 | tf_op jit(solution)/shard_map/pallas_call | solution.py:25
  155.7 2.2 %collective-permute-start.56 = (bf16[112,128]{1,0:T(8,128)(2,1)S(1)}, bf16[112,128]{1,0:T(8,128)(2,1)S(1)}, u32[]{:S(2)}, u32[]{:S(2)}) collective-permute-start(bf16[112,128]{1,0:T(8,128)(2,1)S(1)} %get-tuple-element.87), channel_id=1, source_target_pairs={{8,0},{12,4},{16,8},{20,12},{24,16},{28,20},{0,24},{4,28},{9,1},{1... | collective-permute-start | bytes 86024 | tf_op jit(solution)/shard_map/ppermute | solution.py:214
  159.7 2.6 %collective-permute-start.54 = (bf16[256,128]{1,0:T(8,128)(2,1)S(1)}, bf16[256,128]{1,0:T(8,128)(2,1)S(1)}, u32[]{:S(2)}, u32[]{:S(2)}) collective-permute-start(bf16[256,128]{1,0:T(8,128)(2,1)S(1)} %get-tuple-element.62), channel_id=1, source_target_pairs={{4,0},{8,4},{12,8},{16,12},{20,16},{24,20},{28,24},{0,28},{5,1},{9... | collective-permute-start | bytes 196616 | tf_op jit(solution)/shard_map/ppermute | solution.py:267
  163.2 2.4 %collective-permute-done.59.refs_5_ = bf16[112,128]{1,0:T(8,128)(2,1)S(1)} collective-permute-done((bf16[112,128]{1,0:T(8,128)(2,1)S(1)}, bf16[112,128]{1,0:T(8,128)(2,1)S(1)}, u32[]{:S(2)}, u32[]{:S(2)}) %collective-permute-start.59) | collective-permute-done | bytes 28704 | tf_op jit(solution)/shard_map/ppermute | solution.py:214
  171.5 2.8 %collective-permute-done.63.refs_1_.refs_6_.refs_2_ = bf16[112,128]{1,0:T(8,128)(2,1)S(1)} collective-permute-done((bf16[112,128]{1,0:T(8,128)(2,1)S(1)}, bf16[112,128]{1,0:T(8,128)(2,1)S(1)}, u32[]{:S(2)}, u32[]{:S(2)}) %collective-permute-start.63) | collective-permute-done | bytes 28704 | tf_op jit(solution)/shard_map/ppermute | solution.py:214
  185.1 2.0 collective-permute-done.66.refs_2_
  187.2 2.1 %shard_map.93 = (f32[1024,128]{1,0:T(8,128)S(1)}, bf16[256,128]{1,0:T(8,128)(2,1)}, f32[8,128]{1,0:T(8,128)S(1)}, f32[1024,128]{1,0:T(8,128)S(1)}, f32[1024,128]{1,0:T(8,128)S(1)}, /*index=5*/f32[1024,128]{1,0:T(8,128)S(1)}) custom-call(bf16[1024,2048]{1,0:T(8,128)(2,1)S(1)} %bitcast.60, f32[1024,128]{1,0:T(8,128)S(1)} %get-tuple-element.60.product_ref, ...), custom_call_target="tpu_custom_call" | custom-call | flops 536870912 | bytes 7979008 | tf_op jit(solution)/shard_map/pallas_call | solution.py:25
  189.2 2.6 %collective-permute-done.73.refs_6_ = bf16[96,128]{1,0:T(8,128)(2,1)S(1)} collective-permute-done((bf16[96,128]{1,0:T(8,128)(2,1)S(1)}, bf16[96,128]{1,0:T(8,128)(2,1)S(1)}, u32[]{:S(2)}, u32[]{:S(2)}) %collective-permute-start.73) | collective-permute-done | bytes 24608 | tf_op jit(solution)/shard_map/ppermute | solution.py:214
  192.8 10.1 %all_to_all.5.sums_ref = f32[32,8,128]{2,1,0:T(8,128)S(1)} all-to-all(f32[32,8,128]{2,1,0:T(8,128)S(1)} %get-tuple-element.70), channel_id=1, replica_groups=mesh['sector'=8,'dof'=4] {'sector','dof'}, dimensions={0} | all-to-all | bytes 262144 | tf_op jit(solution)/shard_map/all_to_all | solution.py:209
  (184 shorter events, 84.8 us)
Async XLA Ops:
  1.7 25.3 %collective-permute-start = (bf16[256,128]{1,0:T(8,128)(2,1)S(1)}, bf16[256,128]{1,0:T(8,128)(2,1)S(1)}, u32[]{:S(2)}, u32[]{:S(2)}) collective-permute-start(bf16[256,128]{1,0:T(8,128)(2,1)S(1)} %get-tuple-element.39.refs_0_), channel_id=1, source_target_pairs={{1,0},{2,1},{3,2},{0,3},{5,4},{6,5},{7,6},{4,7},{9,8},{10,9},{11,1... | collective-permute-start | bytes 196616 | tf_op jit(solution)/shard_map/ppermute | solution.py:214
  6.8 20.2 %collective-permute-start.1 = (bf16[256,128]{1,0:T(8,128)(2,1)S(1)}, bf16[256,128]{1,0:T(8,128)(2,1)S(1)}, u32[]{:S(2)}, u32[]{:S(2)}) collective-permute-start(bf16[256,128]{1,0:T(8,128)(2,1)S(1)} %get-tuple-element.39.refs_0_), channel_id=1, source_target_pairs={{2,0},{3,1},{0,2},{1,3},{6,4},{7,5},{4,6},{5,7},{10,8},{11,9},{8,1... | collective-permute-start | bytes 196616 | tf_op jit(solution)/shard_map/ppermute | solution.py:214
  6.8 20.2 %collective-permute-start.2 = (bf16[256,128]{1,0:T(8,128)(2,1)S(1)}, bf16[256,128]{1,0:T(8,128)(2,1)S(1)}, u32[]{:S(2)}, u32[]{:S(2)}) collective-permute-start(bf16[256,128]{1,0:T(8,128)(2,1)S(1)} %get-tuple-element.39.refs_0_), channel_id=1, source_target_pairs={{3,0},{0,1},{1,2},{2,3},{7,4},{4,5},{5,6},{6,7},{11,8},{8,9},{9,10... | collective-permute-start | bytes 196616 | tf_op jit(solution)/shard_map/ppermute | solution.py:214
  39.6 8.2 %collective-permute-start.3 = (bf16[256,128]{1,0:T(8,128)(2,1)S(1)}, bf16[256,128]{1,0:T(8,128)(2,1)S(1)}, u32[]{:S(2)}, u32[]{:S(2)}) collective-permute-start(bf16[256,128]{1,0:T(8,128)(2,1)S(1)} %get-tuple-element.41), channel_id=1, source_target_pairs={{0,4},{4,8},{8,12},{12,16},{16,20},{20,24},{24,28},{28,0},{1,5},{5... | collective-permute-start | bytes 196616 | tf_op jit(solution)/shard_map/ppermute | solution.py:266
  52.2 12.5 %collective-permute-start.15 = (bf16[512,128]{1,0:T(8,128)(2,1)S(1)}, bf16[512,128]{1,0:T(8,128)(2,1)S(1)}, u32[]{:S(2)}, u32[]{:S(2)}) collective-permute-start(bf16[512,128]{1,0:T(8,128)(2,1)S(1)} %shard_map.80.refs_0_), channel_id=1, source_target_pairs={{1,0},{2,1},{3,2},{0,3},{5,4},{6,5},{7,6},{4,7},{9,8},{10,9},{11,1... | collective-permute-start | bytes 393224 | tf_op jit(solution)/shard_map/ppermute | solution.py:214
  53.3 11.6 %collective-permute-start.16 = (bf16[512,128]{1,0:T(8,128)(2,1)S(1)}, bf16[512,128]{1,0:T(8,128)(2,1)S(1)}, u32[]{:S(2)}, u32[]{:S(2)}) collective-permute-start(bf16[512,128]{1,0:T(8,128)(2,1)S(1)} %shard_map.80.refs_0_), channel_id=1, source_target_pairs={{2,0},{3,1},{0,2},{1,3},{6,4},{7,5},{4,6},{5,7},{10,8},{11,9},{8,1... | collective-permute-start | bytes 393224 | tf_op jit(solution)/shard_map/ppermute | solution.py:214
  53.4 12.6 %collective-permute-start.17 = (bf16[512,128]{1,0:T(8,128)(2,1)S(1)}, bf16[512,128]{1,0:T(8,128)(2,1)S(1)}, u32[]{:S(2)}, u32[]{:S(2)}) collective-permute-start(bf16[512,128]{1,0:T(8,128)(2,1)S(1)} %shard_map.80.refs_0_), channel_id=1, source_target_pairs={{3,0},{0,1},{1,2},{2,3},{7,4},{4,5},{5,6},{6,7},{11,8},{8,9},{9,10... | collective-permute-start | bytes 393224 | tf_op jit(solution)/shard_map/ppermute | solution.py:214
  68.3 22.7 %collective-permute-start.25 = (bf16[256,128]{1,0:T(8,128)(2,1)S(1)}, bf16[256,128]{1,0:T(8,128)(2,1)S(1)}, u32[]{:S(2)}, u32[]{:S(2)}) collective-permute-start(bf16[256,128]{1,0:T(8,128)(2,1)S(1)} %get-tuple-element.47.refs_0_), channel_id=1, source_target_pairs={{1,0},{2,1},{3,2},{0,3},{5,4},{6,5},{7,6},{4,7},{9,8},{10,9},{11,1... | collective-permute-start | bytes 196616 | tf_op jit(solution)/shard_map/ppermute | solution.py:214
  70.2 20.7 %collective-permute-start.26 = (bf16[256,128]{1,0:T(8,128)(2,1)S(1)}, bf16[256,128]{1,0:T(8,128)(2,1)S(1)}, u32[]{:S(2)}, u32[]{:S(2)}) collective-permute-start(bf16[256,128]{1,0:T(8,128)(2,1)S(1)} %get-tuple-element.47.refs_0_), channel_id=1, source_target_pairs={{2,0},{3,1},{0,2},{1,3},{6,4},{7,5},{4,6},{5,7},{10,8},{11,9},{8,1... | collective-permute-start | bytes 196616 | tf_op jit(solution)/shard_map/ppermute | solution.py:214
  70.7 20.2 %collective-permute-start.27 = (bf16[256,128]{1,0:T(8,128)(2,1)S(1)}, bf16[256,128]{1,0:T(8,128)(2,1)S(1)}, u32[]{:S(2)}, u32[]{:S(2)}) collective-permute-start(bf16[256,128]{1,0:T(8,128)(2,1)S(1)} %get-tuple-element.47.refs_0_), channel_id=1, source_target_pairs={{3,0},{0,1},{1,2},{2,3},{7,4},{4,5},{5,6},{6,7},{11,8},{8,9},{9,10... | collective-permute-start | bytes 196616 | tf_op jit(solution)/shard_map/ppermute | solution.py:214
  100.7 15.8 %collective-permute-start.28 = (bf16[256,128]{1,0:T(8,128)(2,1)S(1)}, bf16[256,128]{1,0:T(8,128)(2,1)S(1)}, u32[]{:S(2)}, u32[]{:S(2)}) collective-permute-start(bf16[256,128]{1,0:T(8,128)(2,1)S(1)} %get-tuple-element.50), channel_id=1, source_target_pairs={{0,4},{4,8},{8,12},{12,16},{16,20},{20,24},{24,28},{28,0},{1,5},{5... | collective-permute-start | bytes 196616 | tf_op jit(solution)/shard_map/ppermute | solution.py:266
  101.0 15.5 %collective-permute-start.29 = (bf16[256,128]{1,0:T(8,128)(2,1)S(1)}, bf16[256,128]{1,0:T(8,128)(2,1)S(1)}, u32[]{:S(2)}, u32[]{:S(2)}) collective-permute-start(bf16[256,128]{1,0:T(8,128)(2,1)S(1)} %get-tuple-element.51), channel_id=1, source_target_pairs={{4,0},{8,4},{12,8},{16,12},{20,16},{24,20},{28,24},{0,28},{5,1},{9... | collective-permute-start | bytes 196616 | tf_op jit(solution)/shard_map/ppermute | solution.py:267
  116.5 9.6 %collective-permute-start.40 = (bf16[512,128]{1,0:T(8,128)(2,1)S(1)}, bf16[512,128]{1,0:T(8,128)(2,1)S(1)}, u32[]{:S(2)}, u32[]{:S(2)}) collective-permute-start(bf16[512,128]{1,0:T(8,128)(2,1)S(1)} %shard_map.86.refs_0_), channel_id=1, source_target_pairs={{1,0},{2,1},{3,2},{0,3},{5,4},{6,5},{7,6},{4,7},{9,8},{10,9},{11,1... | collective-permute-start | bytes 393224 | tf_op jit(solution)/shard_map/ppermute | solution.py:214
  117.3 11.0 %collective-permute-start.41 = (bf16[512,128]{1,0:T(8,128)(2,1)S(1)}, bf16[512,128]{1,0:T(8,128)(2,1)S(1)}, u32[]{:S(2)}, u32[]{:S(2)}) collective-permute-start(bf16[512,128]{1,0:T(8,128)(2,1)S(1)} %shard_map.86.refs_0_), channel_id=1, source_target_pairs={{2,0},{3,1},{0,2},{1,3},{6,4},{7,5},{4,6},{5,7},{10,8},{11,9},{8,1... | collective-permute-start | bytes 393224 | tf_op jit(solution)/shard_map/ppermute | solution.py:214
  117.8 10.6 %collective-permute-start.42 = (bf16[512,128]{1,0:T(8,128)(2,1)S(1)}, bf16[512,128]{1,0:T(8,128)(2,1)S(1)}, u32[]{:S(2)}, u32[]{:S(2)}) collective-permute-start(bf16[512,128]{1,0:T(8,128)(2,1)S(1)} %shard_map.86.refs_0_), channel_id=1, source_target_pairs={{3,0},{0,1},{1,2},{2,3},{7,4},{4,5},{5,6},{6,7},{11,8},{8,9},{9,10... | collective-permute-start | bytes 393224 | tf_op jit(solution)/shard_map/ppermute | solution.py:214
  129.8 23.4 %collective-permute-start.50 = (bf16[256,128]{1,0:T(8,128)(2,1)S(1)}, bf16[256,128]{1,0:T(8,128)(2,1)S(1)}, u32[]{:S(2)}, u32[]{:S(2)}) collective-permute-start(bf16[256,128]{1,0:T(8,128)(2,1)S(1)} %get-tuple-element.58.refs_0_), channel_id=1, source_target_pairs={{1,0},{2,1},{3,2},{0,3},{5,4},{6,5},{7,6},{4,7},{9,8},{10,9},{11,1... | collective-permute-start | bytes 196616 | tf_op jit(solution)/shard_map/ppermute | solution.py:214
  131.6 21.6 %collective-permute-start.51 = (bf16[256,128]{1,0:T(8,128)(2,1)S(1)}, bf16[256,128]{1,0:T(8,128)(2,1)S(1)}, u32[]{:S(2)}, u32[]{:S(2)}) collective-permute-start(bf16[256,128]{1,0:T(8,128)(2,1)S(1)} %get-tuple-element.58.refs_0_), channel_id=1, source_target_pairs={{2,0},{3,1},{0,2},{1,3},{6,4},{7,5},{4,6},{5,7},{10,8},{11,9},{8,1... | collective-permute-start | bytes 196616 | tf_op jit(solution)/shard_map/ppermute | solution.py:214
  132.3 20.8 %collective-permute-start.52 = (bf16[256,128]{1,0:T(8,128)(2,1)S(1)}, bf16[256,128]{1,0:T(8,128)(2,1)S(1)}, u32[]{:S(2)}, u32[]{:S(2)}) collective-permute-start(bf16[256,128]{1,0:T(8,128)(2,1)S(1)} %get-tuple-element.58.refs_0_), channel_id=1, source_target_pairs={{3,0},{0,1},{1,2},{2,3},{7,4},{4,5},{5,6},{6,7},{11,8},{8,9},{9,10... | collective-permute-start | bytes 196616 | tf_op jit(solution)/shard_map/ppermute | solution.py:214
  159.7 15.6 %collective-permute-start.53 = (bf16[256,128]{1,0:T(8,128)(2,1)S(1)}, bf16[256,128]{1,0:T(8,128)(2,1)S(1)}, u32[]{:S(2)}, u32[]{:S(2)}) collective-permute-start(bf16[256,128]{1,0:T(8,128)(2,1)S(1)} %get-tuple-element.61), channel_id=1, source_target_pairs={{0,4},{4,8},{8,12},{12,16},{16,20},{20,24},{24,28},{28,0},{1,5},{5... | collective-permute-start | bytes 196616 | tf_op jit(solution)/shard_map/ppermute | solution.py:266
  159.7 15.6 %collective-permute-start.54 = (bf16[256,128]{1,0:T(8,128)(2,1)S(1)}, bf16[256,128]{1,0:T(8,128)(2,1)S(1)}, u32[]{:S(2)}, u32[]{:S(2)}) collective-permute-start(bf16[256,128]{1,0:T(8,128)(2,1)S(1)} %get-tuple-element.62), channel_id=1, source_target_pairs={{4,0},{8,4},{12,8},{16,12},{20,16},{24,20},{28,24},{0,28},{5,1},{9... | collective-permute-start | bytes 196616 | tf_op jit(solution)/shard_map/ppermute | solution.py:267
  175.3 9.4 %collective-permute-start.65 = (bf16[512,128]{1,0:T(8,128)(2,1)S(1)}, bf16[512,128]{1,0:T(8,128)(2,1)S(1)}, u32[]{:S(2)}, u32[]{:S(2)}) collective-permute-start(bf16[512,128]{1,0:T(8,128)(2,1)S(1)} %shard_map.92.refs_0_), channel_id=1, source_target_pairs={{1,0},{2,1},{3,2},{0,3},{5,4},{6,5},{7,6},{4,7},{9,8},{10,9},{11,1... | collective-permute-start | bytes 393224 | tf_op jit(solution)/shard_map/ppermute | solution.py:214
  176.0 11.1 %collective-permute-start.66 = (bf16[512,128]{1,0:T(8,128)(2,1)S(1)}, bf16[512,128]{1,0:T(8,128)(2,1)S(1)}, u32[]{:S(2)}, u32[]{:S(2)}) collective-permute-start(bf16[512,128]{1,0:T(8,128)(2,1)S(1)} %shard_map.92.refs_0_), channel_id=1, source_target_pairs={{2,0},{3,1},{0,2},{1,3},{6,4},{7,5},{4,6},{5,7},{10,8},{11,9},{8,1... | collective-permute-start | bytes 393224 | tf_op jit(solution)/shard_map/ppermute | solution.py:214
  176.5 10.6 %collective-permute-start.67 = (bf16[512,128]{1,0:T(8,128)(2,1)S(1)}, bf16[512,128]{1,0:T(8,128)(2,1)S(1)}, u32[]{:S(2)}, u32[]{:S(2)}) collective-permute-start(bf16[512,128]{1,0:T(8,128)(2,1)S(1)} %shard_map.92.refs_0_), channel_id=1, source_target_pairs={{3,0},{0,1},{1,2},{2,3},{7,4},{4,5},{5,6},{6,7},{11,8},{8,9},{9,10... | collective-permute-start | bytes 393224 | tf_op jit(solution)/shard_map/ppermute | solution.py:214
  181.3 7.9 %collective-permute-start.70 = (bf16[96,128]{1,0:T(8,128)(2,1)S(1)}, bf16[96,128]{1,0:T(8,128)(2,1)S(1)}, u32[]{:S(2)}, u32[]{:S(2)}) collective-permute-start(bf16[96,128]{1,0:T(8,128)(2,1)S(1)} %shard_map.94.refs_0_), channel_id=1, source_target_pairs={{12,0},{16,4},{20,8},{24,12},{28,16},{0,20},{4,24},{8,28},{13,1},{... | collective-permute-start | bytes 73736 | tf_op jit(solution)/shard_map/ppermute | solution.py:214
  (64 other events, 492.5 us)

commit v16 on v15

--- a/solution.py
+++ b/solution.py
@@ -199,10 +199,16 @@
     )(sums, *state)
 
 
-def round_kernel(field_ref, top_ref, end_ref):
+def round_kernel(field_ref, diagonal_ref, springs_ref, top_ref, end_ref, stiffness_ref):
     attached = top_ref.shape[0]
     top_ref[...] = field_ref[0, :attached].astype(bf16)
     end_ref[...] = field_ref[0, attached:].astype(bf16)
+    for start in range(0, stiffness_ref.shape[0], LANES):
+        rows = slice(start, start + LANES)
+        row = diagonal_ref[:, rows]
+        if start < attached:
+            row = row + springs_ref[:, rows]
+        stiffness_ref[rows] = jnp.broadcast_to(row, (LANES, LANES)).T
 
 
 def exchange(blocks, axes):
@@ -249,11 +255,9 @@
     full, face = shape(rows, loads), shape(quarter, loads, dtype=bf16)
     top_shape = shape(attached, loads, dtype=bf16)
 
-    stiffness = diagonal[0] + jnp.pad(springs[0], (0, quarter))
-    stiffness = jnp.broadcast_to(stiffness[:, None], (rows, loads))
     state = sums = ()
 
-    top, end = call(round_kernel, (top_shape, face), (rhs,))
+    top, end, stiffness = call(round_kernel, (top_shape, face, full), (rhs, diagonal, springs))
     for step in range(ITERS):
         first, last = step == 0, step == ITERS - 1
         sent = f32 if first else bf16

time: 204 us -> 200 us (0.980)
  local copies, waits for them, and re-layouts: 11.2 us -> 6.62 us
    unnamed x26 -> x22, local copies, waits for them, and re-layouts: 10.9 us -> 6.5 us
  transfers between devices with their start and end apart: 75 -> 75, of which waited for: 27 -> 29; matrix products, arithmetic and copies ran while one was open for 0% -> 0% of each run, Pallas kernels for 5% -> 5%
where the time goes in v16:
time: 200 us
  starting transfers between devices  68.4 us (34%)
  blocking collectives  66.4 us (33%)
  waiting for transfers between devices  37.8 us (19%)
  Pallas kernels  19.6 us (10%)
  local copies, waits for them, and re-layouts  6.62 us (3%)
    ppermute x69, starting transfers between devices, from_ahead(): lax.ppermute(cells, axis, [((i + distance) % count, i) for i in range(cou...  60.7 us
    all_gather x3, blocking collectives, gathered(): return lax.all_gather(field, 'dof', axis=0)  56.1 us
    ppermute x69, waiting for transfers between devices, from_ahead(): lax.ppermute(cells, axis, [((i + distance) % count, i) for i in range(cou...  37.8 us
    pallas_call x20, Pallas kernels, call(): pl.pallas_call(kernel, in_specs=[whole] * len(operands), out_specs=jax.tr...  19.6 us
    all_to_all x1, blocking collectives, exchange(): return lax.all_to_all(blocks, axes, split_axis=0, concat_axis=0)  10.3 us
    unnamed x22, local copies, waits for them, and re-layouts  6.5 us
    ppermute x3, starting transfers between devices, tiled_body(): after = lax.ppermute(left, 'sector', backward)  5.79 us
  transfers between devices with their start and end apart: 75, of which 29 were waited for; matrix products, arithmetic and copies ran while one was open for 0% of the time, Pallas kernels for 5%

profile of v16, /device:TPU:0, one launch (start us, length us, event | category | flops | bytes accessed | tf_op | source)
XLA Modules:
  0.0 199.8 jit_solution(1862284509618806119)
XLA Ops:
  3.2 5.1 %collective-permute-start = (bf16[256,128]{1,0:T(8,128)(2,1)S(1)}, bf16[256,128]{1,0:T(8,128)(2,1)S(1)}, u32[]{:S(2)}, u32[]{:S(2)}) collective-permute-start(bf16[256,128]{1,0:T(8,128)(2,1)S(1)} %get-tuple-element.40.refs_0_), channel_id=1, source_target_pairs={{1,0},{2,1},{3,2},{0,3},{5,4},{6,5},{7,6},{4,7},{9,8},{10,9},{11,1... | collective-permute-start | bytes 196616 | tf_op jit(solution)/shard_map/ppermute | solution.py:220
  9.4 19.2 %all-gather = bf16[3072,128]{1,0:T(8,128)(2,1)S(1)} all-gather(bf16[768,128]{1,0:T(8,128)(2,1)S(1)} %get-tuple-element.39), channel_id=2, replica_groups=mesh['sector'=8,'dof'=4] {'dof'}, dimensions={0}, use_global_device_ids=true | all-gather | bytes 983040 | tf_op jit(solution)/shard_map/all_gather | solution.py:234
  28.5 3.4 %copy-done = bf16[1024,4096]{1,0:T(8,128)(2,1)S(1)} copy-done((bf16[1024,4096]{1,0:T(8,128)(2,1)S(1)}, bf16[1024,4096]{1,0:T(8,128)(2,1)}, u32[]{:S(2)}) %copy-start) | copy-done | bytes 8388632
  32.6 2.3 %shard_map.78 = (f32[1024,128]{1,0:T(8,128)S(1)}, f32[8,112,128]{2,1,0:T(8,128)S(1)}, bf16[256,128]{1,0:T(8,128)(2,1)S(1)}, bf16[256,128]{1,0:T(8,128)(2,1)S(1)}) custom-call(bf16[1024,4096]{1,0:T(8,128)(2,1)S(1)} %copy-done, f32[1,768]{1,0:T(1,128)S(1)} %copy-done.6, bf16[4,768,128]{2,1,0:T(8,128)(2,1)S(1)} %bitcast.62, ...), custom_call_target="tpu_custom_call" | custom-call | flops 1073741824 | bytes 9440256 | tf_op jit(solution)/shard_map/pallas_call | solution.py:25
  35.4 2.2 %collective-permute-start.6 = (f32[112,128]{1,0:T(8,128)S(1)}, f32[112,128]{1,0:T(8,128)S(1)}, u32[]{:S(2)}, u32[]{:S(2)}) collective-permute-start(f32[112,128]{1,0:T(8,128)S(1)} %get-tuple-element.81), channel_id=1, source_target_pairs={{8,0},{12,4},{16,8},{20,12},{24,16},{28,20},{0,24},{4,28},{9,1},{1... | collective-permute-start | bytes 172040 | tf_op jit(solution)/shard_map/ppermute | solution.py:220
  44.4 2.0 %collective-permute-done.9.refs_5_ = f32[112,128]{1,0:T(8,128)S(1)} collective-permute-done((f32[112,128]{1,0:T(8,128)S(1)}, f32[112,128]{1,0:T(8,128)S(1)}, u32[]{:S(2)}, u32[]{:S(2)}) %collective-permute-start.9) | collective-permute-done | bytes 57376 | tf_op jit(solution)/shard_map/ppermute | solution.py:220
  50.4 2.8 %collective-permute-done.13.refs_1_.refs_6_.refs_2_ = bf16[112,128]{1,0:T(8,128)(2,1)S(1)} collective-permute-done((bf16[112,128]{1,0:T(8,128)(2,1)S(1)}, bf16[112,128]{1,0:T(8,128)(2,1)S(1)}, u32[]{:S(2)}, u32[]{:S(2)}) %collective-permute-start.13) | collective-permute-done | bytes 28704 | tf_op jit(solution)/shard_map/ppermute | solution.py:220
  72.2 18.8 %all-gather.1 = bf16[3072,128]{1,0:T(8,128)(2,1)S(1)} all-gather(bf16[768,128]{1,0:T(8,128)(2,1)S(1)} %get-tuple-element.48), channel_id=3, replica_groups=mesh['sector'=8,'dof'=4] {'dof'}, dimensions={0}, use_global_device_ids=true | all-gather | bytes 983040 | tf_op jit(solution)/shard_map/all_gather | solution.py:234
  91.0 2.3 %shard_map.84 = (f32[1024,128]{1,0:T(8,128)S(1)}, bf16[8,112,128]{2,1,0:T(8,128)(2,1)S(1)}, bf16[256,128]{1,0:T(8,128)(2,1)S(1)}, bf16[256,128]{1,0:T(8,128)(2,1)S(1)}) custom-call(bf16[1024,4096]{1,0:T(8,128)(2,1)S(1)} %bitcast.54, f32[1,768]{1,0:T(1,128)S(1)} %copy-done.7, bf16[4,768,128]{2,1,0:T(8,128)(2,1)S(1)} %bitcast.60, ...), custom_call_target="tpu_custom_call" | custom-call | flops 1073741824 | bytes 9444352 | tf_op jit(solution)/shard_map/pallas_call | solution.py:25
  96.9 2.3 %collective-permute-start.29 = (bf16[256,128]{1,0:T(8,128)(2,1)S(1)}, bf16[256,128]{1,0:T(8,128)(2,1)S(1)}, u32[]{:S(2)}, u32[]{:S(2)}) collective-permute-start(bf16[256,128]{1,0:T(8,128)(2,1)S(1)} %get-tuple-element.53), channel_id=1, source_target_pairs={{4,0},{8,4},{12,8},{16,12},{20,16},{24,20},{28,24},{0,28},{5,1},{9... | collective-permute-start | bytes 196616 | tf_op jit(solution)/shard_map/ppermute | solution.py:271
  104.6 2.0 %collective-permute-start.37 = (bf16[112,128]{1,0:T(8,128)(2,1)S(1)}, bf16[112,128]{1,0:T(8,128)(2,1)S(1)}, u32[]{:S(2)}, u32[]{:S(2)}) collective-permute-start(bf16[112,128]{1,0:T(8,128)(2,1)S(1)} %shard_map.85.refs_4_.refs_0_), channel_id=1, source_target_pairs={{1,0},{2,1},{3,2},{0,3},{5,4},{6,5},{7,6},{4,7},{9,8},{10,9},{11,1... | collective-permute-start | bytes 86024 | tf_op jit(solution)/shard_map/ppermute | solution.py:220
  108.5 2.9 %collective-permute-done.38.refs_1_.refs_6_.refs_2_ = bf16[112,128]{1,0:T(8,128)(2,1)S(1)} collective-permute-done((bf16[112,128]{1,0:T(8,128)(2,1)S(1)}, bf16[112,128]{1,0:T(8,128)(2,1)S(1)}, u32[]{:S(2)}, u32[]{:S(2)}) %collective-permute-start.38) | collective-permute-done | bytes 28704 | tf_op jit(solution)/shard_map/ppermute | solution.py:220
  122.0 2.3 %collective-permute-done.41.refs_2_ = bf16[512,128]{1,0:T(8,128)(2,1)S(1)} collective-permute-done((bf16[512,128]{1,0:T(8,128)(2,1)S(1)}, bf16[512,128]{1,0:T(8,128)(2,1)S(1)}, u32[]{:S(2)}, u32[]{:S(2)}) %collective-permute-start.41) | collective-permute-done | bytes 131104 | tf_op jit(solution)/shard_map/ppermute | solution.py:220
  130.4 18.1 %all-gather.2 = bf16[3072,128]{1,0:T(8,128)(2,1)S(1)} all-gather(bf16[768,128]{1,0:T(8,128)(2,1)S(1)} %get-tuple-element.59), channel_id=4, replica_groups=mesh['sector'=8,'dof'=4] {'dof'}, dimensions={0}, use_global_device_ids=true | all-gather | bytes 983040 | tf_op jit(solution)/shard_map/all_gather | solution.py:234
  148.5 2.3 %shard_map.90 = (f32[1024,128]{1,0:T(8,128)S(1)}, bf16[8,112,128]{2,1,0:T(8,128)(2,1)S(1)}, bf16[256,128]{1,0:T(8,128)(2,1)S(1)}, bf16[256,128]{1,0:T(8,128)(2,1)S(1)}) custom-call(bf16[1024,4096]{1,0:T(8,128)(2,1)S(1)} %bitcast.54, f32[1,768]{1,0:T(1,128)S(1)} %copy-done.7, bf16[4,768,128]{2,1,0:T(8,128)(2,1)S(1)} %bitcast.61, ...), custom_call_target="tpu_custom_call" | custom-call | flops 1073741824 | bytes 9444352 | tf_op jit(solution)/shard_map/pallas_call | solution.py:25
  151.0 2.5 %collective-permute-start.56 = (bf16[112,128]{1,0:T(8,128)(2,1)S(1)}, bf16[112,128]{1,0:T(8,128)(2,1)S(1)}, u32[]{:S(2)}, u32[]{:S(2)}) collective-permute-start(bf16[112,128]{1,0:T(8,128)(2,1)S(1)} %get-tuple-element.89), channel_id=1, source_target_pairs={{8,0},{12,4},{16,8},{20,12},{24,16},{28,20},{0,24},{4,28},{9,1},{1... | collective-permute-start | bytes 86024 | tf_op jit(solution)/shard_map/ppermute | solution.py:220
  155.3 2.6 %collective-permute-start.54 = (bf16[256,128]{1,0:T(8,128)(2,1)S(1)}, bf16[256,128]{1,0:T(8,128)(2,1)S(1)}, u32[]{:S(2)}, u32[]{:S(2)}) collective-permute-start(bf16[256,128]{1,0:T(8,128)(2,1)S(1)} %get-tuple-element.64), channel_id=1, source_target_pairs={{4,0},{8,4},{12,8},{16,12},{20,16},{24,20},{28,24},{0,28},{5,1},{9... | collective-permute-start | bytes 196616 | tf_op jit(solution)/shard_map/ppermute | solution.py:271
  159.2 2.0 collective-permute-done.59.refs_5_
  163.4 1.9 collective-permute-start.62
  167.3 2.8 %collective-permute-done.63.refs_1_.refs_6_.refs_2_ = bf16[112,128]{1,0:T(8,128)(2,1)S(1)} collective-permute-done((bf16[112,128]{1,0:T(8,128)(2,1)S(1)}, bf16[112,128]{1,0:T(8,128)(2,1)S(1)}, u32[]{:S(2)}, u32[]{:S(2)}) %collective-permute-start.63) | collective-permute-done | bytes 28704 | tf_op jit(solution)/shard_map/ppermute | solution.py:220
  180.6 2.2 %collective-permute-done.66.refs_2_ = bf16[512,128]{1,0:T(8,128)(2,1)S(1)} collective-permute-done((bf16[512,128]{1,0:T(8,128)(2,1)S(1)}, bf16[512,128]{1,0:T(8,128)(2,1)S(1)}, u32[]{:S(2)}, u32[]{:S(2)}) %collective-permute-start.66) | collective-permute-done | bytes 131104 | tf_op jit(solution)/shard_map/ppermute | solution.py:220
  182.8 2.1 %shard_map.93 = (f32[1024,128]{1,0:T(8,128)S(1)}, bf16[256,128]{1,0:T(8,128)(2,1)}, f32[8,128]{1,0:T(8,128)S(1)}, f32[1024,128]{1,0:T(8,128)S(1)}, f32[1024,128]{1,0:T(8,128)S(1)}, /*index=5*/f32[1024,128]{1,0:T(8,128)S(1)}) custom-call(bf16[1024,2048]{1,0:T(8,128)(2,1)S(1)} %bitcast.57, f32[1024,128]{1,0:T(8,128)S(1)} %get-tuple-element.62.product_ref, ...), custom_call_target="tpu_custom_call" | custom-call | flops 536870912 | bytes 7979008 | tf_op jit(solution)/shard_map/pallas_call | solution.py:25
  184.9 2.6 %collective-permute-done.73.refs_6_ = bf16[96,128]{1,0:T(8,128)(2,1)S(1)} collective-permute-done((bf16[96,128]{1,0:T(8,128)(2,1)S(1)}, bf16[96,128]{1,0:T(8,128)(2,1)S(1)}, u32[]{:S(2)}, u32[]{:S(2)}) %collective-permute-start.73) | collective-permute-done | bytes 24608 | tf_op jit(solution)/shard_map/ppermute | solution.py:220
  188.4 10.3 %all_to_all.5.sums_ref = f32[32,8,128]{2,1,0:T(8,128)S(1)} all-to-all(f32[32,8,128]{2,1,0:T(8,128)S(1)} %get-tuple-element.72), channel_id=1, replica_groups=mesh['sector'=8,'dof'=4] {'sector','dof'}, dimensions={0} | all-to-all | bytes 262144 | tf_op jit(solution)/shard_map/all_to_all | solution.py:215
  (176 shorter events, 81.7 us)
Async XLA Ops:
  3.2 25.3 %collective-permute-start = (bf16[256,128]{1,0:T(8,128)(2,1)S(1)}, bf16[256,128]{1,0:T(8,128)(2,1)S(1)}, u32[]{:S(2)}, u32[]{:S(2)}) collective-permute-start(bf16[256,128]{1,0:T(8,128)(2,1)S(1)} %get-tuple-element.40.refs_0_), channel_id=1, source_target_pairs={{1,0},{2,1},{3,2},{0,3},{5,4},{6,5},{7,6},{4,7},{9,8},{10,9},{11,1... | collective-permute-start | bytes 196616 | tf_op jit(solution)/shard_map/ppermute | solution.py:220
  8.3 20.2 %collective-permute-start.1 = (bf16[256,128]{1,0:T(8,128)(2,1)S(1)}, bf16[256,128]{1,0:T(8,128)(2,1)S(1)}, u32[]{:S(2)}, u32[]{:S(2)}) collective-permute-start(bf16[256,128]{1,0:T(8,128)(2,1)S(1)} %get-tuple-element.40.refs_0_), channel_id=1, source_target_pairs={{2,0},{3,1},{0,2},{1,3},{6,4},{7,5},{4,6},{5,7},{10,8},{11,9},{8,1... | collective-permute-start | bytes 196616 | tf_op jit(solution)/shard_map/ppermute | solution.py:220
  8.3 20.2 %collective-permute-start.2 = (bf16[256,128]{1,0:T(8,128)(2,1)S(1)}, bf16[256,128]{1,0:T(8,128)(2,1)S(1)}, u32[]{:S(2)}, u32[]{:S(2)}) collective-permute-start(bf16[256,128]{1,0:T(8,128)(2,1)S(1)} %get-tuple-element.40.refs_0_), channel_id=1, source_target_pairs={{3,0},{0,1},{1,2},{2,3},{7,4},{4,5},{5,6},{6,7},{11,8},{8,9},{9,10... | collective-permute-start | bytes 196616 | tf_op jit(solution)/shard_map/ppermute | solution.py:220
  41.2 8.2 %collective-permute-start.3 = (bf16[256,128]{1,0:T(8,128)(2,1)S(1)}, bf16[256,128]{1,0:T(8,128)(2,1)S(1)}, u32[]{:S(2)}, u32[]{:S(2)}) collective-permute-start(bf16[256,128]{1,0:T(8,128)(2,1)S(1)} %get-tuple-element.43), channel_id=1, source_target_pairs={{0,4},{4,8},{8,12},{12,16},{16,20},{20,24},{24,28},{28,0},{1,5},{5... | collective-permute-start | bytes 196616 | tf_op jit(solution)/shard_map/ppermute | solution.py:270
  53.7 10.2 %collective-permute-start.15 = (bf16[512,128]{1,0:T(8,128)(2,1)S(1)}, bf16[512,128]{1,0:T(8,128)(2,1)S(1)}, u32[]{:S(2)}, u32[]{:S(2)}) collective-permute-start(bf16[512,128]{1,0:T(8,128)(2,1)S(1)} %shard_map.80.refs_0_), channel_id=1, source_target_pairs={{1,0},{2,1},{3,2},{0,3},{5,4},{6,5},{7,6},{4,7},{9,8},{10,9},{11,1... | collective-permute-start | bytes 393224 | tf_op jit(solution)/shard_map/ppermute | solution.py:220
  54.9 9.7 %collective-permute-start.16 = (bf16[512,128]{1,0:T(8,128)(2,1)S(1)}, bf16[512,128]{1,0:T(8,128)(2,1)S(1)}, u32[]{:S(2)}, u32[]{:S(2)}) collective-permute-start(bf16[512,128]{1,0:T(8,128)(2,1)S(1)} %shard_map.80.refs_0_), channel_id=1, source_target_pairs={{2,0},{3,1},{0,2},{1,3},{6,4},{7,5},{4,6},{5,7},{10,8},{11,9},{8,1... | collective-permute-start | bytes 393224 | tf_op jit(solution)/shard_map/ppermute | solution.py:220
  55.0 10.8 %collective-permute-start.17 = (bf16[512,128]{1,0:T(8,128)(2,1)S(1)}, bf16[512,128]{1,0:T(8,128)(2,1)S(1)}, u32[]{:S(2)}, u32[]{:S(2)}) collective-permute-start(bf16[512,128]{1,0:T(8,128)(2,1)S(1)} %shard_map.80.refs_0_), channel_id=1, source_target_pairs={{3,0},{0,1},{1,2},{2,3},{7,4},{4,5},{5,6},{6,7},{11,8},{8,9},{9,10... | collective-permute-start | bytes 393224 | tf_op jit(solution)/shard_map/ppermute | solution.py:220
  67.3 23.7 %collective-permute-start.25 = (bf16[256,128]{1,0:T(8,128)(2,1)S(1)}, bf16[256,128]{1,0:T(8,128)(2,1)S(1)}, u32[]{:S(2)}, u32[]{:S(2)}) collective-permute-start(bf16[256,128]{1,0:T(8,128)(2,1)S(1)} %get-tuple-element.49.refs_0_), channel_id=1, source_target_pairs={{1,0},{2,1},{3,2},{0,3},{5,4},{6,5},{7,6},{4,7},{9,8},{10,9},{11,1... | collective-permute-start | bytes 196616 | tf_op jit(solution)/shard_map/ppermute | solution.py:220
  69.2 21.8 %collective-permute-start.26 = (bf16[256,128]{1,0:T(8,128)(2,1)S(1)}, bf16[256,128]{1,0:T(8,128)(2,1)S(1)}, u32[]{:S(2)}, u32[]{:S(2)}) collective-permute-start(bf16[256,128]{1,0:T(8,128)(2,1)S(1)} %get-tuple-element.49.refs_0_), channel_id=1, source_target_pairs={{2,0},{3,1},{0,2},{1,3},{6,4},{7,5},{4,6},{5,7},{10,8},{11,9},{8,1... | collective-permute-start | bytes 196616 | tf_op jit(solution)/shard_map/ppermute | solution.py:220
  69.7 21.3 %collective-permute-start.27 = (bf16[256,128]{1,0:T(8,128)(2,1)S(1)}, bf16[256,128]{1,0:T(8,128)(2,1)S(1)}, u32[]{:S(2)}, u32[]{:S(2)}) collective-permute-start(bf16[256,128]{1,0:T(8,128)(2,1)S(1)} %get-tuple-element.49.refs_0_), channel_id=1, source_target_pairs={{3,0},{0,1},{1,2},{2,3},{7,4},{4,5},{5,6},{6,7},{11,8},{8,9},{9,10... | collective-permute-start | bytes 196616 | tf_op jit(solution)/shard_map/ppermute | solution.py:220
  96.5 15.9 %collective-permute-start.28 = (bf16[256,128]{1,0:T(8,128)(2,1)S(1)}, bf16[256,128]{1,0:T(8,128)(2,1)S(1)}, u32[]{:S(2)}, u32[]{:S(2)}) collective-permute-start(bf16[256,128]{1,0:T(8,128)(2,1)S(1)} %get-tuple-element.52), channel_id=1, source_target_pairs={{0,4},{4,8},{8,12},{12,16},{16,20},{20,24},{24,28},{28,0},{1,5},{5... | collective-permute-start | bytes 196616 | tf_op jit(solution)/shard_map/ppermute | solution.py:270
  96.9 15.5 %collective-permute-start.29 = (bf16[256,128]{1,0:T(8,128)(2,1)S(1)}, bf16[256,128]{1,0:T(8,128)(2,1)S(1)}, u32[]{:S(2)}, u32[]{:S(2)}) collective-permute-start(bf16[256,128]{1,0:T(8,128)(2,1)S(1)} %get-tuple-element.53), channel_id=1, source_target_pairs={{4,0},{8,4},{12,8},{16,12},{20,16},{24,20},{28,24},{0,28},{5,1},{9... | collective-permute-start | bytes 196616 | tf_op jit(solution)/shard_map/ppermute | solution.py:271
  112.3 9.4 %collective-permute-start.40 = (bf16[512,128]{1,0:T(8,128)(2,1)S(1)}, bf16[512,128]{1,0:T(8,128)(2,1)S(1)}, u32[]{:S(2)}, u32[]{:S(2)}) collective-permute-start(bf16[512,128]{1,0:T(8,128)(2,1)S(1)} %shard_map.86.refs_0_), channel_id=1, source_target_pairs={{1,0},{2,1},{3,2},{0,3},{5,4},{6,5},{7,6},{4,7},{9,8},{10,9},{11,1... | collective-permute-start | bytes 393224 | tf_op jit(solution)/shard_map/ppermute | solution.py:220
  113.0 11.4 %collective-permute-start.41 = (bf16[512,128]{1,0:T(8,128)(2,1)S(1)}, bf16[512,128]{1,0:T(8,128)(2,1)S(1)}, u32[]{:S(2)}, u32[]{:S(2)}) collective-permute-start(bf16[512,128]{1,0:T(8,128)(2,1)S(1)} %shard_map.86.refs_0_), channel_id=1, source_target_pairs={{2,0},{3,1},{0,2},{1,3},{6,4},{7,5},{4,6},{5,7},{10,8},{11,9},{8,1... | collective-permute-start | bytes 393224 | tf_op jit(solution)/shard_map/ppermute | solution.py:220
  113.6 10.8 %collective-permute-start.42 = (bf16[512,128]{1,0:T(8,128)(2,1)S(1)}, bf16[512,128]{1,0:T(8,128)(2,1)S(1)}, u32[]{:S(2)}, u32[]{:S(2)}) collective-permute-start(bf16[512,128]{1,0:T(8,128)(2,1)S(1)} %shard_map.86.refs_0_), channel_id=1, source_target_pairs={{3,0},{0,1},{1,2},{2,3},{7,4},{4,5},{5,6},{6,7},{11,8},{8,9},{9,10... | collective-permute-start | bytes 393224 | tf_op jit(solution)/shard_map/ppermute | solution.py:220
  125.8 22.7 %collective-permute-start.50 = (bf16[256,128]{1,0:T(8,128)(2,1)S(1)}, bf16[256,128]{1,0:T(8,128)(2,1)S(1)}, u32[]{:S(2)}, u32[]{:S(2)}) collective-permute-start(bf16[256,128]{1,0:T(8,128)(2,1)S(1)} %get-tuple-element.60.refs_0_), channel_id=1, source_target_pairs={{1,0},{2,1},{3,2},{0,3},{5,4},{6,5},{7,6},{4,7},{9,8},{10,9},{11,1... | collective-permute-start | bytes 196616 | tf_op jit(solution)/shard_map/ppermute | solution.py:220
  127.2 21.3 %collective-permute-start.51 = (bf16[256,128]{1,0:T(8,128)(2,1)S(1)}, bf16[256,128]{1,0:T(8,128)(2,1)S(1)}, u32[]{:S(2)}, u32[]{:S(2)}) collective-permute-start(bf16[256,128]{1,0:T(8,128)(2,1)S(1)} %get-tuple-element.60.refs_0_), channel_id=1, source_target_pairs={{2,0},{3,1},{0,2},{1,3},{6,4},{7,5},{4,6},{5,7},{10,8},{11,9},{8,1... | collective-permute-start | bytes 196616 | tf_op jit(solution)/shard_map/ppermute | solution.py:220
  128.0 20.5 %collective-permute-start.52 = (bf16[256,128]{1,0:T(8,128)(2,1)S(1)}, bf16[256,128]{1,0:T(8,128)(2,1)S(1)}, u32[]{:S(2)}, u32[]{:S(2)}) collective-permute-start(bf16[256,128]{1,0:T(8,128)(2,1)S(1)} %get-tuple-element.60.refs_0_), channel_id=1, source_target_pairs={{3,0},{0,1},{1,2},{2,3},{7,4},{4,5},{5,6},{6,7},{11,8},{8,9},{9,10... | collective-permute-start | bytes 196616 | tf_op jit(solution)/shard_map/ppermute | solution.py:220
  155.2 15.8 %collective-permute-start.53 = (bf16[256,128]{1,0:T(8,128)(2,1)S(1)}, bf16[256,128]{1,0:T(8,128)(2,1)S(1)}, u32[]{:S(2)}, u32[]{:S(2)}) collective-permute-start(bf16[256,128]{1,0:T(8,128)(2,1)S(1)} %get-tuple-element.63), channel_id=1, source_target_pairs={{0,4},{4,8},{8,12},{12,16},{16,20},{20,24},{24,28},{28,0},{1,5},{5... | collective-permute-start | bytes 196616 | tf_op jit(solution)/shard_map/ppermute | solution.py:270
  155.3 15.8 %collective-permute-start.54 = (bf16[256,128]{1,0:T(8,128)(2,1)S(1)}, bf16[256,128]{1,0:T(8,128)(2,1)S(1)}, u32[]{:S(2)}, u32[]{:S(2)}) collective-permute-start(bf16[256,128]{1,0:T(8,128)(2,1)S(1)} %get-tuple-element.64), channel_id=1, source_target_pairs={{4,0},{8,4},{12,8},{16,12},{20,16},{24,20},{28,24},{0,28},{5,1},{9... | collective-permute-start | bytes 196616 | tf_op jit(solution)/shard_map/ppermute | solution.py:271
  171.0 9.4 %collective-permute-start.65 = (bf16[512,128]{1,0:T(8,128)(2,1)S(1)}, bf16[512,128]{1,0:T(8,128)(2,1)S(1)}, u32[]{:S(2)}, u32[]{:S(2)}) collective-permute-start(bf16[512,128]{1,0:T(8,128)(2,1)S(1)} %shard_map.92.refs_0_), channel_id=1, source_target_pairs={{1,0},{2,1},{3,2},{0,3},{5,4},{6,5},{7,6},{4,7},{9,8},{10,9},{11,1... | collective-permute-start | bytes 393224 | tf_op jit(solution)/shard_map/ppermute | solution.py:220
  171.8 11.0 %collective-permute-start.66 = (bf16[512,128]{1,0:T(8,128)(2,1)S(1)}, bf16[512,128]{1,0:T(8,128)(2,1)S(1)}, u32[]{:S(2)}, u32[]{:S(2)}) collective-permute-start(bf16[512,128]{1,0:T(8,128)(2,1)S(1)} %shard_map.92.refs_0_), channel_id=1, source_target_pairs={{2,0},{3,1},{0,2},{1,3},{6,4},{7,5},{4,6},{5,7},{10,8},{11,9},{8,1... | collective-permute-start | bytes 393224 | tf_op jit(solution)/shard_map/ppermute | solution.py:220
  172.3 10.5 %collective-permute-start.67 = (bf16[512,128]{1,0:T(8,128)(2,1)S(1)}, bf16[512,128]{1,0:T(8,128)(2,1)S(1)}, u32[]{:S(2)}, u32[]{:S(2)}) collective-permute-start(bf16[512,128]{1,0:T(8,128)(2,1)S(1)} %shard_map.92.refs_0_), channel_id=1, source_target_pairs={{3,0},{0,1},{1,2},{2,3},{7,4},{4,5},{5,6},{6,7},{11,8},{8,9},{9,10... | collective-permute-start | bytes 393224 | tf_op jit(solution)/shard_map/ppermute | solution.py:220
  177.1 7.8 %collective-permute-start.70 = (bf16[96,128]{1,0:T(8,128)(2,1)S(1)}, bf16[96,128]{1,0:T(8,128)(2,1)S(1)}, u32[]{:S(2)}, u32[]{:S(2)}) collective-permute-start(bf16[96,128]{1,0:T(8,128)(2,1)S(1)} %shard_map.94.refs_0_), channel_id=1, source_target_pairs={{12,0},{16,4},{20,8},{24,12},{28,16},{0,20},{4,24},{8,28},{13,1},{... | collective-permute-start | bytes 73736 | tf_op jit(solution)/shard_map/ppermute | solution.py:220
  (62 other events, 443.9 us)

commit v17 on v15

--- a/solution.py
+++ b/solution.py
@@ -174,7 +174,7 @@
     lower = jnp.sum(image * image, axis=0, keepdims=True)
     rest = jnp.zeros((SUM_ROWS - 2, image.shape[1]), f32)
     sums = jnp.concatenate([upper, lower, rest], axis=0)
-    sums_ref[...] = jnp.broadcast_to(sums, sums_ref.shape)
+    sums_ref[...] = jnp.broadcast_to(sums[: sums_ref.shape[-2]], sums_ref.shape)
 
 
 def last_kernel(sums_ref, image_ref, residual_ref, precon_ref, solution_ref, newer_ref, left_ref):
@@ -205,6 +205,15 @@
     end_ref[...] = field_ref[0, attached:].astype(bf16)
 
 
+def stiffness_kernel(diagonal_ref, springs_ref, out_ref):
+    for start in range(0, out_ref.shape[0], LANES):
+        rows = slice(start, start + LANES)
+        row = diagonal_ref[:, rows]
+        if start < springs_ref.shape[1]:
+            row = row + springs_ref[:, rows]
+        out_ref[rows] = jnp.broadcast_to(row, (LANES, LANES)).T
+
+
 def exchange(blocks, axes):
     return lax.all_to_all(blocks, axes, split_axis=0, concat_axis=0)
 
@@ -249,11 +258,10 @@
     full, face = shape(rows, loads), shape(quarter, loads, dtype=bf16)
     top_shape = shape(attached, loads, dtype=bf16)
 
-    stiffness = diagonal[0] + jnp.pad(springs[0], (0, quarter))
-    stiffness = jnp.broadcast_to(stiffness[:, None], (rows, loads))
     state = sums = ()
 
     top, end = call(round_kernel, (top_shape, face), (rhs,))
+    stiffness = call(stiffness_kernel, full, (diagonal, springs))
     for step in range(ITERS):
         first, last = step == 0, step == ITERS - 1
         sent = f32 if first else bf16
@@ -287,7 +295,7 @@
             flops=2 * coupling.size * loads,
         )
         residual, precon, *solution = (residual, product) if first else state
-        sums_shape = shape(sectors * parts, SUM_ROWS, loads) if last else shape(SUM_ROWS, loads)
+        sums_shape = shape(sectors * parts, 2, loads) if last else shape(SUM_ROWS, loads)
         image, top, sums, _ = call(
             functools.partial(image_kernel, sectors),
             (full, top_shape, sums_shape, shape(sectors, height, LANES)),

time: 204 us -> 197 us (0.966)
  local copies, waits for them, and re-layouts: 11.2 us -> 5.26 us
  starting transfers between devices: 70.2 us -> 68 us
    unnamed x26 -> x22, local copies, waits for them, and re-layouts: 10.9 us -> 5.14 us
    ppermute x69, starting transfers between devices: 62.6 us -> 60.4 us  [from_ahead(): lax.ppermute(cells, axis, [((i + distance) % count, i) for i in range(cou...]
    pallas_call x20 -> x21, Pallas kernels: 19.5 us -> 19.7 us  [call(): pl.pallas_call(kernel, in_specs=[whole] * len(operands), out_specs=jax.tr...]
  transfers between devices with their start and end apart: 75 -> 75, of which waited for: 27 -> 28; matrix products, arithmetic and copies ran while one was open for 0% -> 0% of each run, Pallas kernels for 5% -> 5%
where the time goes in v17:
time: 197 us; the launch traced here: 196 us
  starting transfers between devices  68 us (35%)
  blocking collectives  65.4 us (33%)
  waiting for transfers between devices  37.1 us (19%)
  Pallas kernels  19.7 us (10%)
  local copies, waits for them, and re-layouts  5.26 us (3%)
    ppermute x69, starting transfers between devices, from_ahead(): lax.ppermute(cells, axis, [((i + distance) % count, i) for i in range(cou...  60.4 us
    all_gather x3, blocking collectives, gathered(): return lax.all_gather(field, 'dof', axis=0)  56.3 us
    ppermute x69, waiting for transfers between devices, from_ahead(): lax.ppermute(cells, axis, [((i + distance) % count, i) for i in range(cou...  37.1 us
    pallas_call x21, Pallas kernels, call(): pl.pallas_call(kernel, in_specs=[whole] * len(operands), out_specs=jax.tr...  19.7 us
    all_to_all x1, blocking collectives, exchange(): return lax.all_to_all(blocks, axes, split_axis=0, concat_axis=0)  9.09 us
    ppermute x3, starting transfers between devices, tiled_body(): after = lax.ppermute(left, 'sector', backward)  5.44 us
    unnamed x22, local copies, waits for them, and re-layouts  5.14 us
  transfers between devices with their start and end apart: 75, of which 28 were waited for; matrix products, arithmetic and copies ran while one was open for 0% of the time, Pallas kernels for 5%

profile of v17, /device:TPU:0, one launch (start us, length us, event | category | flops | bytes accessed | tf_op | source)
XLA Modules:
  0.0 196.5 jit_solution(14578925357396691890)
XLA Ops:
  1.7 5.1 %collective-permute-start = (bf16[256,128]{1,0:T(8,128)(2,1)S(1)}, bf16[256,128]{1,0:T(8,128)(2,1)S(1)}, u32[]{:S(2)}, u32[]{:S(2)}) collective-permute-start(bf16[256,128]{1,0:T(8,128)(2,1)S(1)} %get-tuple-element.39.refs_0_), channel_id=1, source_target_pairs={{1,0},{2,1},{3,2},{0,3},{5,4},{6,5},{7,6},{4,7},{9,8},{10,9},{11,1... | collective-permute-start | bytes 196616 | tf_op jit(solution)/shard_map/ppermute | solution.py:223
  7.8 19.0 %all-gather = bf16[3072,128]{1,0:T(8,128)(2,1)S(1)} all-gather(bf16[768,128]{1,0:T(8,128)(2,1)S(1)} %get-tuple-element.38), channel_id=2, replica_groups=mesh['sector'=8,'dof'=4] {'dof'}, dimensions={0}, use_global_device_ids=true | all-gather | bytes 983040 | tf_op jit(solution)/shard_map/all_gather | solution.py:237
  26.8 3.4 %copy-done = bf16[1024,4096]{1,0:T(8,128)(2,1)S(1)} copy-done((bf16[1024,4096]{1,0:T(8,128)(2,1)S(1)}, bf16[1024,4096]{1,0:T(8,128)(2,1)}, u32[]{:S(2)}) %copy-start) | copy-done | bytes 8388632
  30.9 2.3 %shard_map.78 = (f32[1024,128]{1,0:T(8,128)S(1)}, f32[8,112,128]{2,1,0:T(8,128)S(1)}, bf16[256,128]{1,0:T(8,128)(2,1)S(1)}, bf16[256,128]{1,0:T(8,128)(2,1)S(1)}) custom-call(bf16[1024,4096]{1,0:T(8,128)(2,1)S(1)} %copy-done, f32[1,768]{1,0:T(1,128)S(1)} %copy-done.4, bf16[4,768,128]{2,1,0:T(8,128)(2,1)S(1)} %bitcast.64, ...), custom_call_target="tpu_custom_call" | custom-call | flops 1073741824 | bytes 9440256 | tf_op jit(solution)/shard_map/pallas_call | solution.py:25
  33.6 2.2 %collective-permute-start.6 = (f32[112,128]{1,0:T(8,128)S(1)}, f32[112,128]{1,0:T(8,128)S(1)}, u32[]{:S(2)}, u32[]{:S(2)}) collective-permute-start(f32[112,128]{1,0:T(8,128)S(1)} %get-tuple-element.79), channel_id=1, source_target_pairs={{8,0},{12,4},{16,8},{20,12},{24,16},{28,20},{0,24},{4,28},{9,1},{1... | collective-permute-start | bytes 172040 | tf_op jit(solution)/shard_map/ppermute | solution.py:223
  42.7 2.0 %collective-permute-done.9.refs_5_ = f32[112,128]{1,0:T(8,128)S(1)} collective-permute-done((f32[112,128]{1,0:T(8,128)S(1)}, f32[112,128]{1,0:T(8,128)S(1)}, u32[]{:S(2)}, u32[]{:S(2)}) %collective-permute-start.9) | collective-permute-done | bytes 57376 | tf_op jit(solution)/shard_map/ppermute | solution.py:223
  65.1 2.0 %collective-permute-start.25 = (bf16[256,128]{1,0:T(8,128)(2,1)S(1)}, bf16[256,128]{1,0:T(8,128)(2,1)S(1)}, u32[]{:S(2)}, u32[]{:S(2)}) collective-permute-start(bf16[256,128]{1,0:T(8,128)(2,1)S(1)} %get-tuple-element.47.refs_0_), channel_id=1, source_target_pairs={{1,0},{2,1},{3,2},{0,3},{5,4},{6,5},{7,6},{4,7},{9,8},{10,9},{11,1... | collective-permute-start | bytes 196616 | tf_op jit(solution)/shard_map/ppermute | solution.py:223
  70.2 18.8 %all-gather.1 = bf16[3072,128]{1,0:T(8,128)(2,1)S(1)} all-gather(bf16[768,128]{1,0:T(8,128)(2,1)S(1)} %get-tuple-element.46), channel_id=3, replica_groups=mesh['sector'=8,'dof'=4] {'dof'}, dimensions={0}, use_global_device_ids=true | all-gather | bytes 983040 | tf_op jit(solution)/shard_map/all_gather | solution.py:237
  89.0 2.3 %shard_map.85 = (f32[1024,128]{1,0:T(8,128)S(1)}, bf16[8,112,128]{2,1,0:T(8,128)(2,1)S(1)}, bf16[256,128]{1,0:T(8,128)(2,1)S(1)}, bf16[256,128]{1,0:T(8,128)(2,1)S(1)}) custom-call(bf16[1024,4096]{1,0:T(8,128)(2,1)S(1)} %bitcast.54, f32[1,768]{1,0:T(1,128)S(1)} %copy-done.5, bf16[4,768,128]{2,1,0:T(8,128)(2,1)S(1)} %bitcast.62, ...), custom_call_target="tpu_custom_call" | custom-call | flops 1073741824 | bytes 9444352 | tf_op jit(solution)/shard_map/pallas_call | solution.py:25
  94.9 2.4 %collective-permute-start.29 = (bf16[256,128]{1,0:T(8,128)(2,1)S(1)}, bf16[256,128]{1,0:T(8,128)(2,1)S(1)}, u32[]{:S(2)}, u32[]{:S(2)}) collective-permute-start(bf16[256,128]{1,0:T(8,128)(2,1)S(1)} %get-tuple-element.51), channel_id=1, source_target_pairs={{4,0},{8,4},{12,8},{16,12},{20,16},{24,20},{28,24},{0,28},{5,1},{9... | collective-permute-start | bytes 196616 | tf_op jit(solution)/shard_map/ppermute | solution.py:275
  98.2 2.3 %collective-permute-done.34.refs_5_ = bf16[112,128]{1,0:T(8,128)(2,1)S(1)} collective-permute-done((bf16[112,128]{1,0:T(8,128)(2,1)S(1)}, bf16[112,128]{1,0:T(8,128)(2,1)S(1)}, u32[]{:S(2)}, u32[]{:S(2)}) %collective-permute-start.34) | collective-permute-done | bytes 28704 | tf_op jit(solution)/shard_map/ppermute | solution.py:223
  102.6 2.0 %collective-permute-start.37 = (bf16[112,128]{1,0:T(8,128)(2,1)S(1)}, bf16[112,128]{1,0:T(8,128)(2,1)S(1)}, u32[]{:S(2)}, u32[]{:S(2)}) collective-permute-start(bf16[112,128]{1,0:T(8,128)(2,1)S(1)} %shard_map.86.refs_4_.refs_0_), channel_id=1, source_target_pairs={{1,0},{2,1},{3,2},{0,3},{5,4},{6,5},{7,6},{4,7},{9,8},{10,9},{11,1... | collective-permute-start | bytes 86024 | tf_op jit(solution)/shard_map/ppermute | solution.py:223
  106.5 2.8 %collective-permute-done.38.refs_1_.refs_6_.refs_2_ = bf16[112,128]{1,0:T(8,128)(2,1)S(1)} collective-permute-done((bf16[112,128]{1,0:T(8,128)(2,1)S(1)}, bf16[112,128]{1,0:T(8,128)(2,1)S(1)}, u32[]{:S(2)}, u32[]{:S(2)}) %collective-permute-start.38) | collective-permute-done | bytes 28704 | tf_op jit(solution)/shard_map/ppermute | solution.py:223
  111.5 1.9 collective-permute-start.42
  128.1 18.6 %all-gather.2 = bf16[3072,128]{1,0:T(8,128)(2,1)S(1)} all-gather(bf16[768,128]{1,0:T(8,128)(2,1)S(1)} %get-tuple-element.57), channel_id=4, replica_groups=mesh['sector'=8,'dof'=4] {'dof'}, dimensions={0}, use_global_device_ids=true | all-gather | bytes 983040 | tf_op jit(solution)/shard_map/all_gather | solution.py:237
  146.6 2.3 %shard_map.91 = (f32[1024,128]{1,0:T(8,128)S(1)}, bf16[8,112,128]{2,1,0:T(8,128)(2,1)S(1)}, bf16[256,128]{1,0:T(8,128)(2,1)S(1)}, bf16[256,128]{1,0:T(8,128)(2,1)S(1)}) custom-call(bf16[1024,4096]{1,0:T(8,128)(2,1)S(1)} %bitcast.54, f32[1,768]{1,0:T(1,128)S(1)} %copy-done.5, bf16[4,768,128]{2,1,0:T(8,128)(2,1)S(1)} %bitcast.63, ...), custom_call_target="tpu_custom_call" | custom-call | flops 1073741824 | bytes 9444352 | tf_op jit(solution)/shard_map/pallas_call | solution.py:25
  152.9 2.2 %collective-permute-start.54 = (bf16[256,128]{1,0:T(8,128)(2,1)S(1)}, bf16[256,128]{1,0:T(8,128)(2,1)S(1)}, u32[]{:S(2)}, u32[]{:S(2)}) collective-permute-start(bf16[256,128]{1,0:T(8,128)(2,1)S(1)} %get-tuple-element.62), channel_id=1, source_target_pairs={{4,0},{8,4},{12,8},{16,12},{20,16},{24,20},{28,24},{0,28},{5,1},{9... | collective-permute-start | bytes 196616 | tf_op jit(solution)/shard_map/ppermute | solution.py:275
  160.9 2.1 %collective-permute-start.62 = (bf16[112,128]{1,0:T(8,128)(2,1)S(1)}, bf16[112,128]{1,0:T(8,128)(2,1)S(1)}, u32[]{:S(2)}, u32[]{:S(2)}) collective-permute-start(bf16[112,128]{1,0:T(8,128)(2,1)S(1)} %shard_map.92.refs_4_.refs_0_), channel_id=1, source_target_pairs={{1,0},{2,1},{3,2},{0,3},{5,4},{6,5},{7,6},{4,7},{9,8},{10,9},{11,1... | collective-permute-start | bytes 86024 | tf_op jit(solution)/shard_map/ppermute | solution.py:223
  164.9 3.0 %collective-permute-done.63.refs_1_.refs_6_.refs_2_ = bf16[112,128]{1,0:T(8,128)(2,1)S(1)} collective-permute-done((bf16[112,128]{1,0:T(8,128)(2,1)S(1)}, bf16[112,128]{1,0:T(8,128)(2,1)S(1)}, u32[]{:S(2)}, u32[]{:S(2)}) %collective-permute-start.63) | collective-permute-done | bytes 28704 | tf_op jit(solution)/shard_map/ppermute | solution.py:223
  170.0 1.9 collective-permute-start.67
  178.4 2.3 %collective-permute-done.66.refs_2_ = bf16[512,128]{1,0:T(8,128)(2,1)S(1)} collective-permute-done((bf16[512,128]{1,0:T(8,128)(2,1)S(1)}, bf16[512,128]{1,0:T(8,128)(2,1)S(1)}, u32[]{:S(2)}, u32[]{:S(2)}) %collective-permute-start.66) | collective-permute-done | bytes 131104 | tf_op jit(solution)/shard_map/ppermute | solution.py:223
  180.7 2.1 %shard_map.94 = (f32[1024,128]{1,0:T(8,128)S(1)}, bf16[256,128]{1,0:T(8,128)(2,1)}, f32[8,128]{1,0:T(8,128)S(1)}, f32[1024,128]{1,0:T(8,128)S(1)}, f32[1024,128]{1,0:T(8,128)S(1)}, /*index=5*/f32[1024,128]{1,0:T(8,128)S(1)}) custom-call(bf16[1024,2048]{1,0:T(8,128)(2,1)S(1)} %bitcast.59, f32[1024,128]{1,0:T(8,128)S(1)} %get-tuple-element.60.product_ref, ...), custom_call_target="tpu_custom_call" | custom-call | flops 536870912 | bytes 7979008 | tf_op jit(solution)/shard_map/pallas_call | solution.py:25
  182.8 2.6 %collective-permute-done.73.refs_6_ = bf16[96,128]{1,0:T(8,128)(2,1)S(1)} collective-permute-done((bf16[96,128]{1,0:T(8,128)(2,1)S(1)}, bf16[96,128]{1,0:T(8,128)(2,1)S(1)}, u32[]{:S(2)}, u32[]{:S(2)}) %collective-permute-start.73) | collective-permute-done | bytes 24608 | tf_op jit(solution)/shard_map/ppermute | solution.py:223
  186.3 9.1 %all_to_all.5.sums_ref = f32[32,2,128]{2,1,0:T(2,128)S(1)} all-to-all(f32[32,2,128]{2,1,0:T(2,128)S(1)} %get-tuple-element.70), channel_id=1, replica_groups=mesh['sector'=8,'dof'=4] {'sector','dof'}, dimensions={0} | all-to-all | bytes 65536 | tf_op jit(solution)/shard_map/all_to_all | solution.py:218
  (178 shorter events, 80.6 us)
Async XLA Ops:
  1.7 25.1 %collective-permute-start = (bf16[256,128]{1,0:T(8,128)(2,1)S(1)}, bf16[256,128]{1,0:T(8,128)(2,1)S(1)}, u32[]{:S(2)}, u32[]{:S(2)}) collective-permute-start(bf16[256,128]{1,0:T(8,128)(2,1)S(1)} %get-tuple-element.39.refs_0_), channel_id=1, source_target_pairs={{1,0},{2,1},{3,2},{0,3},{5,4},{6,5},{7,6},{4,7},{9,8},{10,9},{11,1... | collective-permute-start | bytes 196616 | tf_op jit(solution)/shard_map/ppermute | solution.py:223
  6.8 20.0 %collective-permute-start.1 = (bf16[256,128]{1,0:T(8,128)(2,1)S(1)}, bf16[256,128]{1,0:T(8,128)(2,1)S(1)}, u32[]{:S(2)}, u32[]{:S(2)}) collective-permute-start(bf16[256,128]{1,0:T(8,128)(2,1)S(1)} %get-tuple-element.39.refs_0_), channel_id=1, source_target_pairs={{2,0},{3,1},{0,2},{1,3},{6,4},{7,5},{4,6},{5,7},{10,8},{11,9},{8,1... | collective-permute-start | bytes 196616 | tf_op jit(solution)/shard_map/ppermute | solution.py:223
  6.8 20.0 %collective-permute-start.2 = (bf16[256,128]{1,0:T(8,128)(2,1)S(1)}, bf16[256,128]{1,0:T(8,128)(2,1)S(1)}, u32[]{:S(2)}, u32[]{:S(2)}) collective-permute-start(bf16[256,128]{1,0:T(8,128)(2,1)S(1)} %get-tuple-element.39.refs_0_), channel_id=1, source_target_pairs={{3,0},{0,1},{1,2},{2,3},{7,4},{4,5},{5,6},{6,7},{11,8},{8,9},{9,10... | collective-permute-start | bytes 196616 | tf_op jit(solution)/shard_map/ppermute | solution.py:223
  39.5 8.3 %collective-permute-start.3 = (bf16[256,128]{1,0:T(8,128)(2,1)S(1)}, bf16[256,128]{1,0:T(8,128)(2,1)S(1)}, u32[]{:S(2)}, u32[]{:S(2)}) collective-permute-start(bf16[256,128]{1,0:T(8,128)(2,1)S(1)} %get-tuple-element.41), channel_id=1, source_target_pairs={{0,4},{4,8},{8,12},{12,16},{16,20},{20,24},{24,28},{28,0},{1,5},{5... | collective-permute-start | bytes 196616 | tf_op jit(solution)/shard_map/ppermute | solution.py:274
  52.4 9.1 %collective-permute-start.15 = (bf16[512,128]{1,0:T(8,128)(2,1)S(1)}, bf16[512,128]{1,0:T(8,128)(2,1)S(1)}, u32[]{:S(2)}, u32[]{:S(2)}) collective-permute-start(bf16[512,128]{1,0:T(8,128)(2,1)S(1)} %shard_map.81.refs_0_), channel_id=1, source_target_pairs={{1,0},{2,1},{3,2},{0,3},{5,4},{6,5},{7,6},{4,7},{9,8},{10,9},{11,1... | collective-permute-start | bytes 393224 | tf_op jit(solution)/shard_map/ppermute | solution.py:223
  53.2 9.7 %collective-permute-start.16 = (bf16[512,128]{1,0:T(8,128)(2,1)S(1)}, bf16[512,128]{1,0:T(8,128)(2,1)S(1)}, u32[]{:S(2)}, u32[]{:S(2)}) collective-permute-start(bf16[512,128]{1,0:T(8,128)(2,1)S(1)} %shard_map.81.refs_0_), channel_id=1, source_target_pairs={{2,0},{3,1},{0,2},{1,3},{6,4},{7,5},{4,6},{5,7},{10,8},{11,9},{8,1... | collective-permute-start | bytes 393224 | tf_op jit(solution)/shard_map/ppermute | solution.py:223
  53.2 10.4 %collective-permute-start.17 = (bf16[512,128]{1,0:T(8,128)(2,1)S(1)}, bf16[512,128]{1,0:T(8,128)(2,1)S(1)}, u32[]{:S(2)}, u32[]{:S(2)}) collective-permute-start(bf16[512,128]{1,0:T(8,128)(2,1)S(1)} %shard_map.81.refs_0_), channel_id=1, source_target_pairs={{3,0},{0,1},{1,2},{2,3},{7,4},{4,5},{5,6},{6,7},{11,8},{8,9},{9,10... | collective-permute-start | bytes 393224 | tf_op jit(solution)/shard_map/ppermute | solution.py:223
  65.1 23.9 %collective-permute-start.25 = (bf16[256,128]{1,0:T(8,128)(2,1)S(1)}, bf16[256,128]{1,0:T(8,128)(2,1)S(1)}, u32[]{:S(2)}, u32[]{:S(2)}) collective-permute-start(bf16[256,128]{1,0:T(8,128)(2,1)S(1)} %get-tuple-element.47.refs_0_), channel_id=1, source_target_pairs={{1,0},{2,1},{3,2},{0,3},{5,4},{6,5},{7,6},{4,7},{9,8},{10,9},{11,1... | collective-permute-start | bytes 196616 | tf_op jit(solution)/shard_map/ppermute | solution.py:223
  67.1 21.9 %collective-permute-start.26 = (bf16[256,128]{1,0:T(8,128)(2,1)S(1)}, bf16[256,128]{1,0:T(8,128)(2,1)S(1)}, u32[]{:S(2)}, u32[]{:S(2)}) collective-permute-start(bf16[256,128]{1,0:T(8,128)(2,1)S(1)} %get-tuple-element.47.refs_0_), channel_id=1, source_target_pairs={{2,0},{3,1},{0,2},{1,3},{6,4},{7,5},{4,6},{5,7},{10,8},{11,9},{8,1... | collective-permute-start | bytes 196616 | tf_op jit(solution)/shard_map/ppermute | solution.py:223
  68.2 20.8 %collective-permute-start.27 = (bf16[256,128]{1,0:T(8,128)(2,1)S(1)}, bf16[256,128]{1,0:T(8,128)(2,1)S(1)}, u32[]{:S(2)}, u32[]{:S(2)}) collective-permute-start(bf16[256,128]{1,0:T(8,128)(2,1)S(1)} %get-tuple-element.47.refs_0_), channel_id=1, source_target_pairs={{3,0},{0,1},{1,2},{2,3},{7,4},{4,5},{5,6},{6,7},{11,8},{8,9},{9,10... | collective-permute-start | bytes 196616 | tf_op jit(solution)/shard_map/ppermute | solution.py:223
  94.6 15.7 %collective-permute-start.28 = (bf16[256,128]{1,0:T(8,128)(2,1)S(1)}, bf16[256,128]{1,0:T(8,128)(2,1)S(1)}, u32[]{:S(2)}, u32[]{:S(2)}) collective-permute-start(bf16[256,128]{1,0:T(8,128)(2,1)S(1)} %get-tuple-element.50), channel_id=1, source_target_pairs={{0,4},{4,8},{8,12},{12,16},{16,20},{20,24},{24,28},{28,0},{1,5},{5... | collective-permute-start | bytes 196616 | tf_op jit(solution)/shard_map/ppermute | solution.py:274
  94.9 15.4 %collective-permute-start.29 = (bf16[256,128]{1,0:T(8,128)(2,1)S(1)}, bf16[256,128]{1,0:T(8,128)(2,1)S(1)}, u32[]{:S(2)}, u32[]{:S(2)}) collective-permute-start(bf16[256,128]{1,0:T(8,128)(2,1)S(1)} %get-tuple-element.51), channel_id=1, source_target_pairs={{4,0},{8,4},{12,8},{16,12},{20,16},{24,20},{28,24},{0,28},{5,1},{9... | collective-permute-start | bytes 196616 | tf_op jit(solution)/shard_map/ppermute | solution.py:275
  110.3 9.6 %collective-permute-start.40 = (bf16[512,128]{1,0:T(8,128)(2,1)S(1)}, bf16[512,128]{1,0:T(8,128)(2,1)S(1)}, u32[]{:S(2)}, u32[]{:S(2)}) collective-permute-start(bf16[512,128]{1,0:T(8,128)(2,1)S(1)} %shard_map.87.refs_0_), channel_id=1, source_target_pairs={{1,0},{2,1},{3,2},{0,3},{5,4},{6,5},{7,6},{4,7},{9,8},{10,9},{11,1... | collective-permute-start | bytes 393224 | tf_op jit(solution)/shard_map/ppermute | solution.py:223
  111.1 10.9 %collective-permute-start.41 = (bf16[512,128]{1,0:T(8,128)(2,1)S(1)}, bf16[512,128]{1,0:T(8,128)(2,1)S(1)}, u32[]{:S(2)}, u32[]{:S(2)}) collective-permute-start(bf16[512,128]{1,0:T(8,128)(2,1)S(1)} %shard_map.87.refs_0_), channel_id=1, source_target_pairs={{2,0},{3,1},{0,2},{1,3},{6,4},{7,5},{4,6},{5,7},{10,8},{11,9},{8,1... | collective-permute-start | bytes 393224 | tf_op jit(solution)/shard_map/ppermute | solution.py:223
  111.5 10.9 %collective-permute-start.42 = (bf16[512,128]{1,0:T(8,128)(2,1)S(1)}, bf16[512,128]{1,0:T(8,128)(2,1)S(1)}, u32[]{:S(2)}, u32[]{:S(2)}) collective-permute-start(bf16[512,128]{1,0:T(8,128)(2,1)S(1)} %shard_map.87.refs_0_), channel_id=1, source_target_pairs={{3,0},{0,1},{1,2},{2,3},{7,4},{4,5},{5,6},{6,7},{11,8},{8,9},{9,10... | collective-permute-start | bytes 393224 | tf_op jit(solution)/shard_map/ppermute | solution.py:223
  123.8 22.8 %collective-permute-start.50 = (bf16[256,128]{1,0:T(8,128)(2,1)S(1)}, bf16[256,128]{1,0:T(8,128)(2,1)S(1)}, u32[]{:S(2)}, u32[]{:S(2)}) collective-permute-start(bf16[256,128]{1,0:T(8,128)(2,1)S(1)} %get-tuple-element.58.refs_0_), channel_id=1, source_target_pairs={{1,0},{2,1},{3,2},{0,3},{5,4},{6,5},{7,6},{4,7},{9,8},{10,9},{11,1... | collective-permute-start | bytes 196616 | tf_op jit(solution)/shard_map/ppermute | solution.py:223
  125.3 21.3 %collective-permute-start.51 = (bf16[256,128]{1,0:T(8,128)(2,1)S(1)}, bf16[256,128]{1,0:T(8,128)(2,1)S(1)}, u32[]{:S(2)}, u32[]{:S(2)}) collective-permute-start(bf16[256,128]{1,0:T(8,128)(2,1)S(1)} %get-tuple-element.58.refs_0_), channel_id=1, source_target_pairs={{2,0},{3,1},{0,2},{1,3},{6,4},{7,5},{4,6},{5,7},{10,8},{11,9},{8,1... | collective-permute-start | bytes 196616 | tf_op jit(solution)/shard_map/ppermute | solution.py:223
  125.8 20.8 %collective-permute-start.52 = (bf16[256,128]{1,0:T(8,128)(2,1)S(1)}, bf16[256,128]{1,0:T(8,128)(2,1)S(1)}, u32[]{:S(2)}, u32[]{:S(2)}) collective-permute-start(bf16[256,128]{1,0:T(8,128)(2,1)S(1)} %get-tuple-element.58.refs_0_), channel_id=1, source_target_pairs={{3,0},{0,1},{1,2},{2,3},{7,4},{4,5},{5,6},{6,7},{11,8},{8,9},{9,10... | collective-permute-start | bytes 196616 | tf_op jit(solution)/shard_map/ppermute | solution.py:223
  152.5 16.2 %collective-permute-start.53 = (bf16[256,128]{1,0:T(8,128)(2,1)S(1)}, bf16[256,128]{1,0:T(8,128)(2,1)S(1)}, u32[]{:S(2)}, u32[]{:S(2)}) collective-permute-start(bf16[256,128]{1,0:T(8,128)(2,1)S(1)} %get-tuple-element.61), channel_id=1, source_target_pairs={{0,4},{4,8},{8,12},{12,16},{16,20},{20,24},{24,28},{28,0},{1,5},{5... | collective-permute-start | bytes 196616 | tf_op jit(solution)/shard_map/ppermute | solution.py:274
  152.9 15.8 %collective-permute-start.54 = (bf16[256,128]{1,0:T(8,128)(2,1)S(1)}, bf16[256,128]{1,0:T(8,128)(2,1)S(1)}, u32[]{:S(2)}, u32[]{:S(2)}) collective-permute-start(bf16[256,128]{1,0:T(8,128)(2,1)S(1)} %get-tuple-element.62), channel_id=1, source_target_pairs={{4,0},{8,4},{12,8},{16,12},{20,16},{24,20},{28,24},{0,28},{5,1},{9... | collective-permute-start | bytes 196616 | tf_op jit(solution)/shard_map/ppermute | solution.py:275
  168.8 9.5 %collective-permute-start.65 = (bf16[512,128]{1,0:T(8,128)(2,1)S(1)}, bf16[512,128]{1,0:T(8,128)(2,1)S(1)}, u32[]{:S(2)}, u32[]{:S(2)}) collective-permute-start(bf16[512,128]{1,0:T(8,128)(2,1)S(1)} %shard_map.93.refs_0_), channel_id=1, source_target_pairs={{1,0},{2,1},{3,2},{0,3},{5,4},{6,5},{7,6},{4,7},{9,8},{10,9},{11,1... | collective-permute-start | bytes 393224 | tf_op jit(solution)/shard_map/ppermute | solution.py:223
  169.6 11.1 %collective-permute-start.66 = (bf16[512,128]{1,0:T(8,128)(2,1)S(1)}, bf16[512,128]{1,0:T(8,128)(2,1)S(1)}, u32[]{:S(2)}, u32[]{:S(2)}) collective-permute-start(bf16[512,128]{1,0:T(8,128)(2,1)S(1)} %shard_map.93.refs_0_), channel_id=1, source_target_pairs={{2,0},{3,1},{0,2},{1,3},{6,4},{7,5},{4,6},{5,7},{10,8},{11,9},{8,1... | collective-permute-start | bytes 393224 | tf_op jit(solution)/shard_map/ppermute | solution.py:223
  170.0 10.7 %collective-permute-start.67 = (bf16[512,128]{1,0:T(8,128)(2,1)S(1)}, bf16[512,128]{1,0:T(8,128)(2,1)S(1)}, u32[]{:S(2)}, u32[]{:S(2)}) collective-permute-start(bf16[512,128]{1,0:T(8,128)(2,1)S(1)} %shard_map.93.refs_0_), channel_id=1, source_target_pairs={{3,0},{0,1},{1,2},{2,3},{7,4},{4,5},{5,6},{6,7},{11,8},{8,9},{9,10... | collective-permute-start | bytes 393224 | tf_op jit(solution)/shard_map/ppermute | solution.py:223
  174.8 7.9 %collective-permute-start.70 = (bf16[96,128]{1,0:T(8,128)(2,1)S(1)}, bf16[96,128]{1,0:T(8,128)(2,1)S(1)}, u32[]{:S(2)}, u32[]{:S(2)}) collective-permute-start(bf16[96,128]{1,0:T(8,128)(2,1)S(1)} %shard_map.95.refs_0_), channel_id=1, source_target_pairs={{12,0},{16,4},{20,8},{24,12},{28,16},{0,20},{4,24},{8,28},{13,1},{... | collective-permute-start | bytes 73736 | tf_op jit(solution)/shard_map/ppermute | solution.py:223
  (62 other events, 511.1 us)

commit v18 on v17

--- a/solution.py
+++ b/solution.py
@@ -92,8 +92,10 @@
     out_ref[quarter:] = after_ref[...]
 
 
-def slice_kernel(*refs):
-    *part_refs, out_ref = refs
+def slice_kernel(right_ref, left_ref, *refs):
+    *part_refs, out_ref, right_out, left_out = refs
+    right_out[...] = right_ref[...]
+    left_out[...] = left_ref[...]
     height = out_ref.shape[0] - TERM_ROWS
     total = sum(ref[...].astype(f32) for ref in part_refs)
     out_ref[:height] = total[:height].astype(bf16)
@@ -271,13 +273,13 @@
             (precond, springs, gathered(top), *one_from_each(end, "dof"), *sums),
             flops=2 * precond.size * loads,
         )
+        load, right, left = call(
+            slice_kernel,
+            (shape(height + TERM_ROWS, loads, dtype=bf16), face, face),
+            (right, left, *mine_from_each(load, "sector")),
+        )
         before = lax.ppermute(right, "sector", onward)
         after = lax.ppermute(left, "sector", backward)
-        load = call(
-            slice_kernel,
-            shape(height + TERM_ROWS, loads, dtype=bf16),
-            mine_from_each(load, "sector"),
-        )
         slices = one_from_each(load, "dof")
         faces = call(join_kernel, shape(2 * quarter, loads, dtype=bf16), (before, after, *slices[1:]))
         faces = one_from_each(faces, "dof")

time: 197 us -> 210 us (1.066)
  starting transfers between devices: 68 us -> 73.5 us
  waiting for transfers between devices: 37.1 us -> 41 us
  blocking collectives: 65.4 us -> 68.8 us
    ppermute x69, starting transfers between devices: 60.4 us -> 65.4 us  [from_ahead(): lax.ppermute(cells, axis, [((i + distance) % count, i) for i in range(cou...]
    ppermute x69, waiting for transfers between devices: 37.1 us -> 40.9 us  [from_ahead(): lax.ppermute(cells, axis, [((i + distance) % count, i) for i in range(cou...]
    all_gather x3, blocking collectives: 56.3 us -> 59.2 us  [gathered(): return lax.all_gather(field, 'dof', axis=0)]
    ppermute x3, starting transfers between devices: 5.44 us -> 7.89 us  [tiled_body(): after = lax.ppermute(left, 'sector', backward)]
  transfers between devices with their start and end apart: 75 -> 75, of which waited for: 28 -> 29; matrix products, arithmetic and copies ran while one was open for 0% -> 0% of each run, Pallas kernels for 5% -> 5%
where the time goes in v18:
time: 210 us; the launch traced here: 209 us
  starting transfers between devices  73.5 us (35%)
  blocking collectives  68.8 us (33%)
  waiting for transfers between devices  41 us (20%)
  Pallas kernels  19.7 us (9%)
  local copies, waits for them, and re-layouts  5.26 us (3%)
    ppermute x69, starting transfers between devices, from_ahead(): lax.ppermute(cells, axis, [((i + distance) % count, i) for i in range(cou...  65.4 us
    all_gather x3, blocking collectives, gathered(): return lax.all_gather(field, 'dof', axis=0)  59.2 us
    ppermute x69, waiting for transfers between devices, from_ahead(): lax.ppermute(cells, axis, [((i + distance) % count, i) for i in range(cou...  40.9 us
    pallas_call x21, Pallas kernels, call(): pl.pallas_call(kernel, in_specs=[whole] * len(operands), out_specs=jax.tr...  19.7 us
    all_to_all x1, blocking collectives, exchange(): return lax.all_to_all(blocks, axes, split_axis=0, concat_axis=0)  9.55 us
    ppermute x3, starting transfers between devices, tiled_body(): after = lax.ppermute(left, 'sector', backward)  7.89 us
    unnamed x22, local copies, waits for them, and re-layouts  5.14 us
  transfers between devices with their start and end apart: 75, of which 29 were waited for; matrix products, arithmetic and copies ran while one was open for 0% of the time, Pallas kernels for 5%

profile of v18, /device:TPU:0, one launch (start us, length us, event | category | flops | bytes accessed | tf_op | source)
XLA Modules:
  0.0 209.2 jit_solution(6322780324970890801)
XLA Ops:
  1.7 5.1 %collective-permute-start = (bf16[256,128]{1,0:T(8,128)(2,1)S(1)}, bf16[256,128]{1,0:T(8,128)(2,1)S(1)}, u32[]{:S(2)}, u32[]{:S(2)}) collective-permute-start(bf16[256,128]{1,0:T(8,128)(2,1)S(1)} %get-tuple-element.48.refs_0_), channel_id=1, source_target_pairs={{1,0},{2,1},{3,2},{0,3},{5,4},{6,5},{7,6},{4,7},{9,8},{10,9},{11,1... | collective-permute-start | bytes 196616 | tf_op jit(solution)/shard_map/ppermute | solution.py:225
  7.8 19.0 %all-gather = bf16[3072,128]{1,0:T(8,128)(2,1)S(1)} all-gather(bf16[768,128]{1,0:T(8,128)(2,1)S(1)} %get-tuple-element.47), channel_id=2, replica_groups=mesh['sector'=8,'dof'=4] {'dof'}, dimensions={0}, use_global_device_ids=true | all-gather | bytes 983040 | tf_op jit(solution)/shard_map/all_gather | solution.py:239
  26.8 3.4 %copy-done = bf16[1024,4096]{1,0:T(8,128)(2,1)S(1)} copy-done((bf16[1024,4096]{1,0:T(8,128)(2,1)S(1)}, bf16[1024,4096]{1,0:T(8,128)(2,1)}, u32[]{:S(2)}) %copy-start) | copy-done | bytes 8388632
  30.9 2.3 %shard_map.78 = (f32[1024,128]{1,0:T(8,128)S(1)}, f32[8,112,128]{2,1,0:T(8,128)S(1)}, bf16[256,128]{1,0:T(8,128)(2,1)S(1)}, bf16[256,128]{1,0:T(8,128)(2,1)S(1)}) custom-call(bf16[1024,4096]{1,0:T(8,128)(2,1)S(1)} %copy-done, f32[1,768]{1,0:T(1,128)S(1)} %copy-done.4, bf16[4,768,128]{2,1,0:T(8,128)(2,1)S(1)} %bitcast.64, ...), custom_call_target="tpu_custom_call" | custom-call | flops 1073741824 | bytes 9440256 | tf_op jit(solution)/shard_map/pallas_call | solution.py:25
  33.6 2.2 %collective-permute-start.4 = (f32[112,128]{1,0:T(8,128)S(1)}, f32[112,128]{1,0:T(8,128)S(1)}, u32[]{:S(2)}, u32[]{:S(2)}) collective-permute-start(f32[112,128]{1,0:T(8,128)S(1)} %get-tuple-element.97), channel_id=1, source_target_pairs={{8,0},{12,4},{16,8},{20,12},{24,16},{28,20},{0,24},{4,28},{9,1},{1... | collective-permute-start | bytes 172040 | tf_op jit(solution)/shard_map/ppermute | solution.py:225
  39.5 2.4 %collective-permute-done.6.refs_4_ = f32[112,128]{1,0:T(8,128)S(1)} collective-permute-done((f32[112,128]{1,0:T(8,128)S(1)}, f32[112,128]{1,0:T(8,128)S(1)}, u32[]{:S(2)}, u32[]{:S(2)}) %collective-permute-start.6) | collective-permute-done | bytes 57376 | tf_op jit(solution)/shard_map/ppermute | solution.py:225
  41.9 2.2 %collective-permute-done.7.refs_5_ = f32[112,128]{1,0:T(8,128)S(1)} collective-permute-done((f32[112,128]{1,0:T(8,128)S(1)}, f32[112,128]{1,0:T(8,128)S(1)}, u32[]{:S(2)}, u32[]{:S(2)}) %collective-permute-start.7) | collective-permute-done | bytes 57376 | tf_op jit(solution)/shard_map/ppermute | solution.py:225
  44.2 2.6 %collective-permute-start.11 = (bf16[256,128]{1,0:T(8,128)(2,1)S(1)}, bf16[256,128]{1,0:T(8,128)(2,1)S(1)}, u32[]{:S(2)}, u32[]{:S(2)}) collective-permute-start(bf16[256,128]{1,0:T(8,128)(2,1)S(1)} %get-tuple-element.54), channel_id=1, source_target_pairs={{4,0},{8,4},{12,8},{16,12},{20,16},{24,20},{28,24},{0,28},{5,1},{9... | collective-permute-start | bytes 196616 | tf_op jit(solution)/shard_map/ppermute | solution.py:282
  50.7 3.1 %collective-permute-done.13.refs_1_.refs_6_.refs_2_ = bf16[112,128]{1,0:T(8,128)(2,1)S(1)} collective-permute-done((bf16[112,128]{1,0:T(8,128)(2,1)S(1)}, bf16[112,128]{1,0:T(8,128)(2,1)S(1)}, u32[]{:S(2)}, u32[]{:S(2)}) %collective-permute-start.13) | collective-permute-done | bytes 28704 | tf_op jit(solution)/shard_map/ppermute | solution.py:225
  55.1 3.4 %collective-permute-start.16 = (bf16[512,128]{1,0:T(8,128)(2,1)S(1)}, bf16[512,128]{1,0:T(8,128)(2,1)S(1)}, u32[]{:S(2)}, u32[]{:S(2)}) collective-permute-start(bf16[512,128]{1,0:T(8,128)(2,1)S(1)} %shard_map.81.refs_0_), channel_id=1, source_target_pairs={{2,0},{3,1},{0,2},{1,3},{6,4},{7,5},{4,6},{5,7},{10,8},{11,9},{8,1... | collective-permute-start | bytes 393224 | tf_op jit(solution)/shard_map/ppermute | solution.py:225
  74.0 19.8 %all-gather.1 = bf16[3072,128]{1,0:T(8,128)(2,1)S(1)} all-gather(bf16[768,128]{1,0:T(8,128)(2,1)S(1)} %get-tuple-element.58), channel_id=3, replica_groups=mesh['sector'=8,'dof'=4] {'dof'}, dimensions={0}, use_global_device_ids=true | all-gather | bytes 983040 | tf_op jit(solution)/shard_map/all_gather | solution.py:239
  93.9 2.3 %shard_map.85 = (f32[1024,128]{1,0:T(8,128)S(1)}, bf16[8,112,128]{2,1,0:T(8,128)(2,1)S(1)}, bf16[256,128]{1,0:T(8,128)(2,1)S(1)}, bf16[256,128]{1,0:T(8,128)(2,1)S(1)}) custom-call(bf16[1024,4096]{1,0:T(8,128)(2,1)S(1)} %bitcast.54, f32[1,768]{1,0:T(1,128)S(1)} %copy-done.5, bf16[4,768,128]{2,1,0:T(8,128)(2,1)S(1)} %bitcast.62, ...), custom_call_target="tpu_custom_call" | custom-call | flops 1073741824 | bytes 9444352 | tf_op jit(solution)/shard_map/pallas_call | solution.py:25
  103.2 2.2 %collective-permute-done.33.refs_6_ = bf16[112,128]{1,0:T(8,128)(2,1)S(1)} collective-permute-done((bf16[112,128]{1,0:T(8,128)(2,1)S(1)}, bf16[112,128]{1,0:T(8,128)(2,1)S(1)}, u32[]{:S(2)}, u32[]{:S(2)}) %collective-permute-start.33) | collective-permute-done | bytes 28704 | tf_op jit(solution)/shard_map/ppermute | solution.py:225
  106.2 2.6 %collective-permute-start.36 = (bf16[256,128]{1,0:T(8,128)(2,1)S(1)}, bf16[256,128]{1,0:T(8,128)(2,1)S(1)}, u32[]{:S(2)}, u32[]{:S(2)}) collective-permute-start(bf16[256,128]{1,0:T(8,128)(2,1)S(1)} %get-tuple-element.66), channel_id=1, source_target_pairs={{4,0},{8,4},{12,8},{16,12},{20,16},{24,20},{28,24},{0,28},{5,1},{9... | collective-permute-start | bytes 196616 | tf_op jit(solution)/shard_map/ppermute | solution.py:282
  108.9 2.7 %collective-permute-start.37 = (bf16[112,128]{1,0:T(8,128)(2,1)S(1)}, bf16[112,128]{1,0:T(8,128)(2,1)S(1)}, u32[]{:S(2)}, u32[]{:S(2)}) collective-permute-start(bf16[112,128]{1,0:T(8,128)(2,1)S(1)} %get-tuple-element.67.refs_4_.refs_0_), channel_id=1, source_target_pairs={{1,0},{2,1},{3,2},{0,3},{5,4},{6,5},{7,6},{4,7},{9,8},{10,9},{11,1... | collective-permute-start | bytes 86024 | tf_op jit(solution)/shard_map/ppermute | solution.py:225
  113.1 3.4 %collective-permute-done.38.refs_1_.refs_6_.refs_2_ = bf16[112,128]{1,0:T(8,128)(2,1)S(1)} collective-permute-done((bf16[112,128]{1,0:T(8,128)(2,1)S(1)}, bf16[112,128]{1,0:T(8,128)(2,1)S(1)}, u32[]{:S(2)}, u32[]{:S(2)}) %collective-permute-start.38) | collective-permute-done | bytes 28704 | tf_op jit(solution)/shard_map/ppermute | solution.py:225
  117.9 3.6 %collective-permute-start.41 = (bf16[512,128]{1,0:T(8,128)(2,1)S(1)}, bf16[512,128]{1,0:T(8,128)(2,1)S(1)}, u32[]{:S(2)}, u32[]{:S(2)}) collective-permute-start(bf16[512,128]{1,0:T(8,128)(2,1)S(1)} %shard_map.87.refs_0_), channel_id=1, source_target_pairs={{2,0},{3,1},{0,2},{1,3},{6,4},{7,5},{4,6},{5,7},{10,8},{11,9},{8,1... | collective-permute-start | bytes 393224 | tf_op jit(solution)/shard_map/ppermute | solution.py:225
  136.2 20.4 %all-gather.2 = bf16[3072,128]{1,0:T(8,128)(2,1)S(1)} all-gather(bf16[768,128]{1,0:T(8,128)(2,1)S(1)} %get-tuple-element.72), channel_id=4, replica_groups=mesh['sector'=8,'dof'=4] {'dof'}, dimensions={0}, use_global_device_ids=true | all-gather | bytes 983040 | tf_op jit(solution)/shard_map/all_gather | solution.py:239
  156.6 2.3 %shard_map.91 = (f32[1024,128]{1,0:T(8,128)S(1)}, bf16[8,112,128]{2,1,0:T(8,128)(2,1)S(1)}, bf16[256,128]{1,0:T(8,128)(2,1)S(1)}, bf16[256,128]{1,0:T(8,128)(2,1)S(1)}) custom-call(bf16[1024,4096]{1,0:T(8,128)(2,1)S(1)} %bitcast.54, f32[1,768]{1,0:T(1,128)S(1)} %copy-done.5, bf16[4,768,128]{2,1,0:T(8,128)(2,1)S(1)} %bitcast.63, ...), custom_call_target="tpu_custom_call" | custom-call | flops 1073741824 | bytes 9444352 | tf_op jit(solution)/shard_map/pallas_call | solution.py:25
  168.8 2.6 %collective-permute-start.61 = (bf16[256,128]{1,0:T(8,128)(2,1)S(1)}, bf16[256,128]{1,0:T(8,128)(2,1)S(1)}, u32[]{:S(2)}, u32[]{:S(2)}) collective-permute-start(bf16[256,128]{1,0:T(8,128)(2,1)S(1)} %get-tuple-element.80), channel_id=1, source_target_pairs={{4,0},{8,4},{12,8},{16,12},{20,16},{24,20},{28,24},{0,28},{5,1},{9... | collective-permute-start | bytes 196616 | tf_op jit(solution)/shard_map/ppermute | solution.py:282
  171.4 2.7 %collective-permute-start.62 = (bf16[112,128]{1,0:T(8,128)(2,1)S(1)}, bf16[112,128]{1,0:T(8,128)(2,1)S(1)}, u32[]{:S(2)}, u32[]{:S(2)}) collective-permute-start(bf16[112,128]{1,0:T(8,128)(2,1)S(1)} %get-tuple-element.81.refs_4_.refs_0_), channel_id=1, source_target_pairs={{1,0},{2,1},{3,2},{0,3},{5,4},{6,5},{7,6},{4,7},{9,8},{10,9},{11,1... | collective-permute-start | bytes 86024 | tf_op jit(solution)/shard_map/ppermute | solution.py:225
  175.6 3.4 %collective-permute-done.63.refs_1_.refs_6_.refs_2_ = bf16[112,128]{1,0:T(8,128)(2,1)S(1)} collective-permute-done((bf16[112,128]{1,0:T(8,128)(2,1)S(1)}, bf16[112,128]{1,0:T(8,128)(2,1)S(1)}, u32[]{:S(2)}, u32[]{:S(2)}) %collective-permute-start.63) | collective-permute-done | bytes 28704 | tf_op jit(solution)/shard_map/ppermute | solution.py:225
  180.4 3.6 %collective-permute-start.66 = (bf16[512,128]{1,0:T(8,128)(2,1)S(1)}, bf16[512,128]{1,0:T(8,128)(2,1)S(1)}, u32[]{:S(2)}, u32[]{:S(2)}) collective-permute-start(bf16[512,128]{1,0:T(8,128)(2,1)S(1)} %shard_map.93.refs_0_), channel_id=1, source_target_pairs={{2,0},{3,1},{0,2},{1,3},{6,4},{7,5},{4,6},{5,7},{10,8},{11,9},{8,1... | collective-permute-start | bytes 393224 | tf_op jit(solution)/shard_map/ppermute | solution.py:225
  198.6 9.6 %all_to_all.5.sums_ref = f32[32,2,128]{2,1,0:T(2,128)S(1)} all-to-all(f32[32,2,128]{2,1,0:T(2,128)S(1)} %get-tuple-element.88), channel_id=1, replica_groups=mesh['sector'=8,'dof'=4] {'sector','dof'}, dimensions={0} | all-to-all | bytes 65536 | tf_op jit(solution)/shard_map/all_to_all | solution.py:220
  (178 shorter events, 81.2 us)
Async XLA Ops:
  1.7 25.1 %collective-permute-start = (bf16[256,128]{1,0:T(8,128)(2,1)S(1)}, bf16[256,128]{1,0:T(8,128)(2,1)S(1)}, u32[]{:S(2)}, u32[]{:S(2)}) collective-permute-start(bf16[256,128]{1,0:T(8,128)(2,1)S(1)} %get-tuple-element.48.refs_0_), channel_id=1, source_target_pairs={{1,0},{2,1},{3,2},{0,3},{5,4},{6,5},{7,6},{4,7},{9,8},{10,9},{11,1... | collective-permute-start | bytes 196616 | tf_op jit(solution)/shard_map/ppermute | solution.py:225
  6.8 20.0 %collective-permute-start.1 = (bf16[256,128]{1,0:T(8,128)(2,1)S(1)}, bf16[256,128]{1,0:T(8,128)(2,1)S(1)}, u32[]{:S(2)}, u32[]{:S(2)}) collective-permute-start(bf16[256,128]{1,0:T(8,128)(2,1)S(1)} %get-tuple-element.48.refs_0_), channel_id=1, source_target_pairs={{2,0},{3,1},{0,2},{1,3},{6,4},{7,5},{4,6},{5,7},{10,8},{11,9},{8,1... | collective-permute-start | bytes 196616 | tf_op jit(solution)/shard_map/ppermute | solution.py:225
  6.8 20.0 %collective-permute-start.2 = (bf16[256,128]{1,0:T(8,128)(2,1)S(1)}, bf16[256,128]{1,0:T(8,128)(2,1)S(1)}, u32[]{:S(2)}, u32[]{:S(2)}) collective-permute-start(bf16[256,128]{1,0:T(8,128)(2,1)S(1)} %get-tuple-element.48.refs_0_), channel_id=1, source_target_pairs={{3,0},{0,1},{1,2},{2,3},{7,4},{4,5},{5,6},{6,7},{11,8},{8,9},{9,10... | collective-permute-start | bytes 196616 | tf_op jit(solution)/shard_map/ppermute | solution.py:225
  44.1 10.6 %collective-permute-start.10 = (bf16[256,128]{1,0:T(8,128)(2,1)S(1)}, bf16[256,128]{1,0:T(8,128)(2,1)S(1)}, u32[]{:S(2)}, u32[]{:S(2)}) collective-permute-start(bf16[256,128]{1,0:T(8,128)(2,1)S(1)} %get-tuple-element.53), channel_id=1, source_target_pairs={{0,4},{4,8},{8,12},{12,16},{16,20},{20,24},{24,28},{28,0},{1,5},{5... | collective-permute-start | bytes 196616 | tf_op jit(solution)/shard_map/ppermute | solution.py:281
  44.2 10.5 %collective-permute-start.11 = (bf16[256,128]{1,0:T(8,128)(2,1)S(1)}, bf16[256,128]{1,0:T(8,128)(2,1)S(1)}, u32[]{:S(2)}, u32[]{:S(2)}) collective-permute-start(bf16[256,128]{1,0:T(8,128)(2,1)S(1)} %get-tuple-element.54), channel_id=1, source_target_pairs={{4,0},{8,4},{12,8},{16,12},{20,16},{24,20},{28,24},{0,28},{5,1},{9... | collective-permute-start | bytes 196616 | tf_op jit(solution)/shard_map/ppermute | solution.py:282
  54.7 12.4 %collective-permute-start.15 = (bf16[512,128]{1,0:T(8,128)(2,1)S(1)}, bf16[512,128]{1,0:T(8,128)(2,1)S(1)}, u32[]{:S(2)}, u32[]{:S(2)}) collective-permute-start(bf16[512,128]{1,0:T(8,128)(2,1)S(1)} %shard_map.81.refs_0_), channel_id=1, source_target_pairs={{1,0},{2,1},{3,2},{0,3},{5,4},{6,5},{7,6},{4,7},{9,8},{10,9},{11,1... | collective-permute-start | bytes 393224 | tf_op jit(solution)/shard_map/ppermute | solution.py:225
  55.1 12.0 %collective-permute-start.16 = (bf16[512,128]{1,0:T(8,128)(2,1)S(1)}, bf16[512,128]{1,0:T(8,128)(2,1)S(1)}, u32[]{:S(2)}, u32[]{:S(2)}) collective-permute-start(bf16[512,128]{1,0:T(8,128)(2,1)S(1)} %shard_map.81.refs_0_), channel_id=1, source_target_pairs={{2,0},{3,1},{0,2},{1,3},{6,4},{7,5},{4,6},{5,7},{10,8},{11,9},{8,1... | collective-permute-start | bytes 393224 | tf_op jit(solution)/shard_map/ppermute | solution.py:225
  58.6 9.9 %collective-permute-start.17 = (bf16[512,128]{1,0:T(8,128)(2,1)S(1)}, bf16[512,128]{1,0:T(8,128)(2,1)S(1)}, u32[]{:S(2)}, u32[]{:S(2)}) collective-permute-start(bf16[512,128]{1,0:T(8,128)(2,1)S(1)} %shard_map.81.refs_0_), channel_id=1, source_target_pairs={{3,0},{0,1},{1,2},{2,3},{7,4},{4,5},{5,6},{6,7},{11,8},{8,9},{9,10... | collective-permute-start | bytes 393224 | tf_op jit(solution)/shard_map/ppermute | solution.py:225
  70.5 23.4 %collective-permute-start.25 = (bf16[256,128]{1,0:T(8,128)(2,1)S(1)}, bf16[256,128]{1,0:T(8,128)(2,1)S(1)}, u32[]{:S(2)}, u32[]{:S(2)}) collective-permute-start(bf16[256,128]{1,0:T(8,128)(2,1)S(1)} %get-tuple-element.59.refs_0_), channel_id=1, source_target_pairs={{1,0},{2,1},{3,2},{0,3},{5,4},{6,5},{7,6},{4,7},{9,8},{10,9},{11,1... | collective-permute-start | bytes 196616 | tf_op jit(solution)/shard_map/ppermute | solution.py:225
  72.4 21.5 %collective-permute-start.26 = (bf16[256,128]{1,0:T(8,128)(2,1)S(1)}, bf16[256,128]{1,0:T(8,128)(2,1)S(1)}, u32[]{:S(2)}, u32[]{:S(2)}) collective-permute-start(bf16[256,128]{1,0:T(8,128)(2,1)S(1)} %get-tuple-element.59.refs_0_), channel_id=1, source_target_pairs={{2,0},{3,1},{0,2},{1,3},{6,4},{7,5},{4,6},{5,7},{10,8},{11,9},{8,1... | collective-permute-start | bytes 196616 | tf_op jit(solution)/shard_map/ppermute | solution.py:225
  72.4 21.5 %collective-permute-start.27 = (bf16[256,128]{1,0:T(8,128)(2,1)S(1)}, bf16[256,128]{1,0:T(8,128)(2,1)S(1)}, u32[]{:S(2)}, u32[]{:S(2)}) collective-permute-start(bf16[256,128]{1,0:T(8,128)(2,1)S(1)} %get-tuple-element.59.refs_0_), channel_id=1, source_target_pairs={{3,0},{0,1},{1,2},{2,3},{7,4},{4,5},{5,6},{6,7},{11,8},{8,9},{9,10... | collective-permute-start | bytes 196616 | tf_op jit(solution)/shard_map/ppermute | solution.py:225
  106.2 11.4 %collective-permute-start.35 = (bf16[256,128]{1,0:T(8,128)(2,1)S(1)}, bf16[256,128]{1,0:T(8,128)(2,1)S(1)}, u32[]{:S(2)}, u32[]{:S(2)}) collective-permute-start(bf16[256,128]{1,0:T(8,128)(2,1)S(1)} %get-tuple-element.65), channel_id=1, source_target_pairs={{0,4},{4,8},{8,12},{12,16},{16,20},{20,24},{24,28},{28,0},{1,5},{5... | collective-permute-start | bytes 196616 | tf_op jit(solution)/shard_map/ppermute | solution.py:281
  106.2 11.3 %collective-permute-start.36 = (bf16[256,128]{1,0:T(8,128)(2,1)S(1)}, bf16[256,128]{1,0:T(8,128)(2,1)S(1)}, u32[]{:S(2)}, u32[]{:S(2)}) collective-permute-start(bf16[256,128]{1,0:T(8,128)(2,1)S(1)} %get-tuple-element.66), channel_id=1, source_target_pairs={{4,0},{8,4},{12,8},{16,12},{20,16},{24,20},{28,24},{0,28},{5,1},{9... | collective-permute-start | bytes 196616 | tf_op jit(solution)/shard_map/ppermute | solution.py:282
  117.5 12.0 %collective-permute-start.40 = (bf16[512,128]{1,0:T(8,128)(2,1)S(1)}, bf16[512,128]{1,0:T(8,128)(2,1)S(1)}, u32[]{:S(2)}, u32[]{:S(2)}) collective-permute-start(bf16[512,128]{1,0:T(8,128)(2,1)S(1)} %shard_map.87.refs_0_), channel_id=1, source_target_pairs={{1,0},{2,1},{3,2},{0,3},{5,4},{6,5},{7,6},{4,7},{9,8},{10,9},{11,1... | collective-permute-start | bytes 393224 | tf_op jit(solution)/shard_map/ppermute | solution.py:225
  117.9 11.7 %collective-permute-start.41 = (bf16[512,128]{1,0:T(8,128)(2,1)S(1)}, bf16[512,128]{1,0:T(8,128)(2,1)S(1)}, u32[]{:S(2)}, u32[]{:S(2)}) collective-permute-start(bf16[512,128]{1,0:T(8,128)(2,1)S(1)} %shard_map.87.refs_0_), channel_id=1, source_target_pairs={{2,0},{3,1},{0,2},{1,3},{6,4},{7,5},{4,6},{5,7},{10,8},{11,9},{8,1... | collective-permute-start | bytes 393224 | tf_op jit(solution)/shard_map/ppermute | solution.py:225
  121.4 9.6 %collective-permute-start.42 = (bf16[512,128]{1,0:T(8,128)(2,1)S(1)}, bf16[512,128]{1,0:T(8,128)(2,1)S(1)}, u32[]{:S(2)}, u32[]{:S(2)}) collective-permute-start(bf16[512,128]{1,0:T(8,128)(2,1)S(1)} %shard_map.87.refs_0_), channel_id=1, source_target_pairs={{3,0},{0,1},{1,2},{2,3},{7,4},{4,5},{5,6},{6,7},{11,8},{8,9},{9,10... | collective-permute-start | bytes 393224 | tf_op jit(solution)/shard_map/ppermute | solution.py:225
  133.1 23.5 %collective-permute-start.50 = (bf16[256,128]{1,0:T(8,128)(2,1)S(1)}, bf16[256,128]{1,0:T(8,128)(2,1)S(1)}, u32[]{:S(2)}, u32[]{:S(2)}) collective-permute-start(bf16[256,128]{1,0:T(8,128)(2,1)S(1)} %get-tuple-element.73.refs_0_), channel_id=1, source_target_pairs={{1,0},{2,1},{3,2},{0,3},{5,4},{6,5},{7,6},{4,7},{9,8},{10,9},{11,1... | collective-permute-start | bytes 196616 | tf_op jit(solution)/shard_map/ppermute | solution.py:225
  134.7 21.9 %collective-permute-start.51 = (bf16[256,128]{1,0:T(8,128)(2,1)S(1)}, bf16[256,128]{1,0:T(8,128)(2,1)S(1)}, u32[]{:S(2)}, u32[]{:S(2)}) collective-permute-start(bf16[256,128]{1,0:T(8,128)(2,1)S(1)} %get-tuple-element.73.refs_0_), channel_id=1, source_target_pairs={{2,0},{3,1},{0,2},{1,3},{6,4},{7,5},{4,6},{5,7},{10,8},{11,9},{8,1... | collective-permute-start | bytes 196616 | tf_op jit(solution)/shard_map/ppermute | solution.py:225
  134.8 21.9 %collective-permute-start.52 = (bf16[256,128]{1,0:T(8,128)(2,1)S(1)}, bf16[256,128]{1,0:T(8,128)(2,1)S(1)}, u32[]{:S(2)}, u32[]{:S(2)}) collective-permute-start(bf16[256,128]{1,0:T(8,128)(2,1)S(1)} %get-tuple-element.73.refs_0_), channel_id=1, source_target_pairs={{3,0},{0,1},{1,2},{2,3},{7,4},{4,5},{5,6},{6,7},{11,8},{8,9},{9,10... | collective-permute-start | bytes 196616 | tf_op jit(solution)/shard_map/ppermute | solution.py:225
  168.7 11.4 %collective-permute-start.60 = (bf16[256,128]{1,0:T(8,128)(2,1)S(1)}, bf16[256,128]{1,0:T(8,128)(2,1)S(1)}, u32[]{:S(2)}, u32[]{:S(2)}) collective-permute-start(bf16[256,128]{1,0:T(8,128)(2,1)S(1)} %get-tuple-element.79), channel_id=1, source_target_pairs={{0,4},{4,8},{8,12},{12,16},{16,20},{20,24},{24,28},{28,0},{1,5},{5... | collective-permute-start | bytes 196616 | tf_op jit(solution)/shard_map/ppermute | solution.py:281
  168.8 11.3 %collective-permute-start.61 = (bf16[256,128]{1,0:T(8,128)(2,1)S(1)}, bf16[256,128]{1,0:T(8,128)(2,1)S(1)}, u32[]{:S(2)}, u32[]{:S(2)}) collective-permute-start(bf16[256,128]{1,0:T(8,128)(2,1)S(1)} %get-tuple-element.80), channel_id=1, source_target_pairs={{4,0},{8,4},{12,8},{16,12},{20,16},{24,20},{28,24},{0,28},{5,1},{9... | collective-permute-start | bytes 196616 | tf_op jit(solution)/shard_map/ppermute | solution.py:282
  180.1 12.1 %collective-permute-start.65 = (bf16[512,128]{1,0:T(8,128)(2,1)S(1)}, bf16[512,128]{1,0:T(8,128)(2,1)S(1)}, u32[]{:S(2)}, u32[]{:S(2)}) collective-permute-start(bf16[512,128]{1,0:T(8,128)(2,1)S(1)} %shard_map.93.refs_0_), channel_id=1, source_target_pairs={{1,0},{2,1},{3,2},{0,3},{5,4},{6,5},{7,6},{4,7},{9,8},{10,9},{11,1... | collective-permute-start | bytes 393224 | tf_op jit(solution)/shard_map/ppermute | solution.py:225
  180.4 11.8 %collective-permute-start.66 = (bf16[512,128]{1,0:T(8,128)(2,1)S(1)}, bf16[512,128]{1,0:T(8,128)(2,1)S(1)}, u32[]{:S(2)}, u32[]{:S(2)}) collective-permute-start(bf16[512,128]{1,0:T(8,128)(2,1)S(1)} %shard_map.93.refs_0_), channel_id=1, source_target_pairs={{2,0},{3,1},{0,2},{1,3},{6,4},{7,5},{4,6},{5,7},{10,8},{11,9},{8,1... | collective-permute-start | bytes 393224 | tf_op jit(solution)/shard_map/ppermute | solution.py:225
  183.9 9.6 %collective-permute-start.67 = (bf16[512,128]{1,0:T(8,128)(2,1)S(1)}, bf16[512,128]{1,0:T(8,128)(2,1)S(1)}, u32[]{:S(2)}, u32[]{:S(2)}) collective-permute-start(bf16[512,128]{1,0:T(8,128)(2,1)S(1)} %shard_map.93.refs_0_), channel_id=1, source_target_pairs={{3,0},{0,1},{1,2},{2,3},{7,4},{4,5},{5,6},{6,7},{11,8},{8,9},{9,10... | collective-permute-start | bytes 393224 | tf_op jit(solution)/shard_map/ppermute | solution.py:225
  (62 other events, 530.0 us)
